TPU v7x, 32 devices: a whole 2x2x4 slice. The times are simulated.
32 devices in a mesh: gx: 2 (over y), gy: 4 (over z), gz: 4 (over x, core).
Axes of the slice: x: 2, y: 2, z: 4, core: 2. Of those that a mesh axis runs over, the one named last changes fastest.
Arguments:
- pops: float32 [27, 16, 32, 256], P(None, 'gz', 'gy', 'gx')
- solid: int32 [16, 32, 256], P('gz', 'gy', 'gx'), may hold values from 0 to 1, as said below
- profile_table: float32 [8, 16], P(None, 'gz'), as said below
- profile_index: int32 [32], P('gy'), may hold values from 0 to 7
Outputs:
- updated: float32 [27, 16, 32, 256], P(None, 'gz', 'gy', 'gx')
Inputs may be any that keep to these rules, and one draw needn't show every extreme that they name: `solid`: buildings are vertical columns on footprints of 4 x 4 cells aligned to multiples of 4; every cell with z index 15 is 0. `profile_table`: every profile's speeds lie in a band of positive values.
All inputs are finite; a program needn't handle non-finite values.
Results may differ from a plain program's by a relative error of at most 0.0003.
Values sent between devices are 32-bit elements; how exact they have to be, the bound alone decides.
No kernel may reach another device: no remote copies, remote signals or barrier semaphores. Data moves between devices by JAX's collectives and lax.ppermute only.
A program may use at most 64 MiB of HBM per device.

v0:
```python
import jax
import jax.numpy as jnp
import numpy as np
from jax import lax
from jax.sharding import PartitionSpec as P

STEPS = 2
SPONGE = 32


tau_base = 0.52
smag_const = 0.17
root_two = 1.4142135623730951


def padded_2(array, sides, width):
    for axis, dim in sides:
        size, length = (lax.axis_size(axis), array.shape[dim])
        up = [(i, (i + 1) % size) for i in range(size)]
        down = [(j, i) for i, j in up]
        last = lax.slice_in_dim(array, length - width, length, axis=dim)
        initial = lax.slice_in_dim(array, 0, width, axis=dim)
        before = lax.ppermute(last, axis, up)
        after = lax.ppermute(initial, axis, down)
        array = jnp.concatenate([before, array, after], axis=dim)
    return array


def lattice():
    velocity = np.array(
        [[cx, cy, cz] for cz in (-1, 0, 1) for cy in (-1, 0, 1) for cx in (-1, 0, 1)]
    )
    lengths_sq = (velocity * velocity).sum(1)
    weights = np.array([8.0 / 27.0, 2.0 / 27.0, 1.0 / 54.0, 1.0 / 216.0])[lengths_sq]
    return (velocity, weights)


def mirror_of(number):
    velocity, weights = lattice()
    cx, cy, cz = velocity[number]
    return int((1 - cz) * 9 + (cy + 1) * 3 + (cx + 1))


def equilibrium(density, speed_x, speed_y, speed_z):
    velocity, weights = lattice()
    comp_x = jnp.asarray(velocity[:, 0], jnp.float32).reshape(27, 1, 1, 1)
    comp_y = jnp.asarray(velocity[:, 1], jnp.float32).reshape(27, 1, 1, 1)
    comp_z = jnp.asarray(velocity[:, 2], jnp.float32).reshape(27, 1, 1, 1)
    factor = jnp.asarray(weights, jnp.float32).reshape(27, 1, 1, 1)
    along = comp_x * speed_x + comp_y * speed_y + comp_z * speed_z
    square = speed_x * speed_x + speed_y * speed_y + speed_z * speed_z
    return factor * density * (1.0 + 3.0 * along + 4.5 * along * along - 1.5 * square)


def collide(pops):
    velocity, weights = lattice()
    first_table = np.concatenate([np.ones((27, 1)), velocity], axis=1)
    moments = jnp.einsum(
        "qm,qzyx->mzyx",
        jnp.asarray(first_table, jnp.float32),
        pops,
        precision=lax.Precision.HIGHEST,
    )
    density = moments[0]
    speed_x = moments[1] / density
    speed_y = moments[2] / density
    speed_z = moments[3] / density
    nonequil = pops - equilibrium(density, speed_x, speed_y, speed_z)
    pair_table = np.stack(
        [
            velocity[:, 0] * velocity[:, 0],
            velocity[:, 1] * velocity[:, 1],
            velocity[:, 2] * velocity[:, 2],
            velocity[:, 0] * velocity[:, 1],
            velocity[:, 0] * velocity[:, 2],
            velocity[:, 1] * velocity[:, 2],
        ],
        axis=1,
    )
    stress = jnp.einsum(
        "qm,qzyx->mzyx",
        jnp.asarray(pair_table, jnp.float32),
        nonequil,
        precision=lax.Precision.HIGHEST,
    )
    strain_sq = (
        stress[0] ** 2
        + stress[1] ** 2
        + stress[2] ** 2
        + 2.0 * (stress[3] ** 2 + stress[4] ** 2 + stress[5] ** 2)
    )
    magnitude = jnp.sqrt(2.0 * strain_sq)
    relax = 0.5 * (
        tau_base
        + jnp.sqrt(
            tau_base * tau_base + 18.0 * root_two * smag_const * smag_const * magnitude / density
        )
    )
    return (pops - nonequil / relax, density)


def shards(pops, solid, profile_table, profile_index):
    velocity, weights = lattice()
    planes, span_cells, stream_cells = solid.shape
    profiles = profile_table.shape[0]
    walls = padded_2(solid, (("gx", 2), ("gy", 1), ("gz", 0)), 1)
    height = lax.axis_index("gz") * planes + jnp.arange(planes, dtype=jnp.int32)[:, None, None]
    depth = planes * lax.axis_size("gz")
    stream_pos = lax.axis_index("gx") * stream_cells + jnp.arange(stream_cells, dtype=jnp.int32)
    sponge = (stream_pos < SPONGE)[None, None, None, :]
    onehot = (profile_index[:, None] == jnp.arange(profiles, dtype=jnp.int32)[None, :]).astype(
        jnp.float32
    )
    target = jnp.einsum("yp,pz->zy", onehot, profile_table, precision=lax.Precision.HIGHEST)[
        :, :, None
    ]
    fluid = (solid == 0)[None]
    rest = jnp.asarray(weights, jnp.float32).reshape(27, 1, 1, 1)
    for step in range(STEPS):
        post, density = collide(pops)
        zeros = jnp.zeros_like(density)
        pinned = equilibrium(density, target + zeros, zeros, zeros)
        post = jnp.where(sponge, pinned, post)
        padded = padded_2(post, (("gx", 3), ("gy", 2), ("gz", 1)), 1)
        pieces = []
        for number in range(27):
            cx, cy, cz = [int(value) for value in velocity[number]]
            source = padded[
                number,
                1 - cz : 1 - cz + planes,
                1 - cy : 1 - cy + span_cells,
                1 - cx : 1 - cx + stream_cells,
            ]
            blocked = (
                walls[
                    1 - cz : 1 - cz + planes,
                    1 - cy : 1 - cy + span_cells,
                    1 - cx : 1 - cx + stream_cells,
                ]
                == 1
            )
            bounce = post[26 - number]
            mirror = padded[
                mirror_of(number),
                1 : 1 + planes,
                1 - cy : 1 - cy + span_cells,
                1 - cx : 1 - cx + stream_cells,
            ]
            value = jnp.where(blocked, bounce, source)
            value = jnp.where(height - cz < 0, bounce, value)
            value = jnp.where(height - cz > depth - 1, mirror, value)
            pieces.append(value)
        pops = jnp.where(fluid, jnp.stack(pieces), rest)
    return pops


def solution(mesh):
    return jax.shard_map(
        shards,
        mesh=mesh,
        in_specs=(P(None, "gz", "gy", "gx"), P("gz", "gy", "gx"), P(None, "gz"), P("gy")),
        out_specs=P(None, "gz", "gy", "gx"),
        check_vma=False,
    )
```

profile of v0, /device:TPU:1, one launch (start us, length us, event | category | flops | bytes accessed | tf_op | source)
XLA Modules:
  0.0 108.7 jit_solution(10461660243468349066)
XLA Ops:
  0.0 0.7 copy-done.5
  0.7 1.6 %fusion.6 = f32[4,4,8,128]{3,0,2,1:T(4,128)S(1)} fusion(f32[27,4,1,1]{0,1,3,2:T(4,128)S(1)} %copy-done.5, f32[27,4,8,128]{3,2,1,0:T(8,128)} %param.25), kind=kOutput, calls=%fused_computation.14 | convolution fusion | flops 5308416 | bytes 508336 | tf_op jit(solution)/shard_map/qm,qzyx->mzyx/dot_general | solution.py:58
  2.4 0.6 copy-done.8
  3.1 0.3 fusion.9
  3.4 0.3 copy-done.4
  3.8 0.6 fusion.4
  4.5 0.6 copy-done.11
  5.1 0.2 multiply_multiply_fusion.7
  5.4 0.6 copy-done.9
  6.0 0.8 fusion.8
  6.8 0.2 fusion.148
  7.0 2.1 %collective-permute-start.1 = (f32[27,4,8,1]{3,2,1,0:T(8,128)S(1)}, f32[27,4,8,1]{3,2,1,0:T(8,128)S(1)}, u32[]{:S(2)}, u32[]{:S(2)}) collective-permute-start(f32[27,4,8,1]{3,2,1,0:T(8,128)S(1)} %get-tuple-element.68), channel_id=1, source_target_pairs={{16,0},{0,16},{17,1},{1,17},{18,2},{2,18},{19,3},{3,19},{20,4},{4,... | collective-permute-start | bytes 10376 | tf_op jit(solution)/shard_map/ppermute | solution.py:24
  9.3 1.4 %collective-permute-start.4 = (s32[4,8,1]{2,1,0:T(8,128)S(1)}, s32[4,8,1]{2,1,0:T(8,128)S(1)}, u32[]{:S(2)}, u32[]{:S(2)}) collective-permute-start(s32[4,8,1]{2,1,0:T(8,128)S(1)} %get-tuple-element.104), channel_id=1, source_target_pairs={{16,0},{0,16},{17,1},{1,17},{18,2},{2,18},{19,3},{3,19},{20,4},{4,... | collective-permute-start | bytes 392 | tf_op jit(solution)/shard_map/ppermute | solution.py:24
  10.8 18.1 %collective-permute-done.4 = s32[4,8,1]{2,1,0:T(8,128)S(1)} collective-permute-done((s32[4,8,1]{2,1,0:T(8,128)S(1)}, s32[4,8,1]{2,1,0:T(8,128)S(1)}, u32[]{:S(2)}, u32[]{:S(2)}) %collective-permute-start.4) | collective-permute-done | bytes 160 | tf_op jit(solution)/shard_map/ppermute | solution.py:24
  28.9 0.4 collective-permute-done.3
  29.3 3.3 %collective-permute-start.6 = (s32[4,1,130]{2,1,0:T(1,128)S(1)}, s32[4,1,130]{2,1,0:T(1,128)S(1)}, u32[]{:S(2)}, u32[]{:S(2)}) collective-permute-start(s32[4,1,130]{2,1,0:T(1,128)S(1)} %get-tuple-element.94), channel_id=1, source_target_pairs={{4,0},{8,4},{12,8},{0,12},{5,1},{9,5},{13,9},{1,13},{6,2},{10,6},{... | collective-permute-start | bytes 6248 | tf_op jit(solution)/shard_map/ppermute | solution.py:24
  32.6 0.8 pad_maximum_fusion.13
  33.4 3.3 %collective-permute-start.2 = (f32[27,4,1,130]{3,2,1,0:T(1,128)S(1)}, f32[27,4,1,130]{3,2,1,0:T(1,128)S(1)}, u32[]{:S(2)}, u32[]{:S(2)}) collective-permute-start(f32[27,4,1,130]{3,2,1,0:T(1,128)S(1)} %get-tuple-element.64), channel_id=1, source_target_pairs={{4,0},{8,4},{12,8},{0,12},{5,1},{9,5},{13,9},{1,13},{6,2},{10,6},{... | collective-permute-start | bytes 168488 | tf_op jit(solution)/shard_map/ppermute | solution.py:24
  36.7 0.3 collective-permute-done.5
  37.1 4.1 %collective-permute-start.10 = (s32[1,10,130]{2,1,0:T(8,128)S(1)}, s32[1,10,130]{2,1,0:T(8,128)S(1)}, u32[]{:S(2)}, u32[]{:S(2)}) collective-permute-start(s32[1,10,130]{2,1,0:T(8,128)S(1)} %get-tuple-element.91), channel_id=1, source_target_pairs={{0,1},{1,2},{2,3},{3,0},{4,5},{5,6},{6,7},{7,4},{8,9},{9,10},{10,1... | collective-permute-start | bytes 15608 | tf_op jit(solution)/shard_map/ppermute | solution.py:23
  41.2 1.1 %collective-permute-done.8 = f32[27,4,1,130]{3,2,1,0:T(1,128)S(1)} collective-permute-done((f32[27,4,1,130]{3,2,1,0:T(1,128)S(1)}, f32[27,4,1,130]{3,2,1,0:T(1,128)S(1)}, u32[]{:S(2)}, u32[]{:S(2)}) %collective-permute-start.8) | collective-permute-done | bytes 56192 | tf_op jit(solution)/shard_map/ppermute | solution.py:23
  42.3 0.4 pad_maximum_fusion.5
  42.7 3.4 %collective-permute-start.9 = (f32[27,1,10,130]{3,2,1,0:T(8,128)S(1)}, f32[27,1,10,130]{3,2,1,0:T(8,128)S(1)}, u32[]{:S(2)}, u32[]{:S(2)}) collective-permute-start(f32[27,1,10,130]{3,2,1,0:T(8,128)S(1)} %get-tuple-element.60), channel_id=1, source_target_pairs={{1,0},{2,1},{3,2},{0,3},{5,4},{6,5},{7,6},{4,7},{9,8},{10,9},{11,1... | collective-permute-start | bytes 421208 | tf_op jit(solution)/shard_map/ppermute | solution.py:24
  46.1 0.1 add_add_fusion
  46.3 1.2 %collective-permute-start.11 = (f32[27,1,10,130]{3,2,1,0:T(8,128)S(1)}, f32[27,1,10,130]{3,2,1,0:T(8,128)S(1)}, u32[]{:S(2)}, u32[]{:S(2)}) collective-permute-start(f32[27,1,10,130]{3,2,1,0:T(8,128)S(1)} %get-tuple-element.59), channel_id=1, source_target_pairs={{0,1},{1,2},{2,3},{3,0},{4,5},{5,6},{6,7},{7,4},{8,9},{9,10},{10,1... | collective-permute-start | bytes 421208 | tf_op jit(solution)/shard_map/ppermute | solution.py:23
  47.4 10.6 %collective-permute-done.9 = f32[27,1,10,130]{3,2,1,0:T(8,128)S(1)} collective-permute-done((f32[27,1,10,130]{3,2,1,0:T(8,128)S(1)}, f32[27,1,10,130]{3,2,1,0:T(8,128)S(1)}, u32[]{:S(2)}, u32[]{:S(2)}) %collective-permute-start.9) | collective-permute-done | bytes 140432 | tf_op jit(solution)/shard_map/ppermute | solution.py:24
  58.1 0.1 constant_dynamic-update-slice_fusion.26
  58.7 0.1 constant_dynamic-update-slice_fusion.20
  59.5 0.1 constant_dynamic-update-slice_fusion.11
  59.9 0.1 constant_dynamic-update-slice_fusion.8
  60.5 0.1 constant_dynamic-update-slice_fusion.2
  60.9 0.6 fusion.2
  61.6 0.3 fusion.11
  61.9 0.6 fusion
  62.6 0.7 fusion.10
  63.3 0.2 fusion.147
  63.5 1.3 %collective-permute-start.13 = (f32[27,4,8,1]{3,2,1,0:T(8,128)S(1)}, f32[27,4,8,1]{3,2,1,0:T(8,128)S(1)}, u32[]{:S(2)}, u32[]{:S(2)}) collective-permute-start(f32[27,4,8,1]{3,2,1,0:T(8,128)S(1)} %get-tuple-element.66), channel_id=1, source_target_pairs={{16,0},{0,16},{17,1},{1,17},{18,2},{2,18},{19,3},{3,19},{20,4},{4,... | collective-permute-start | bytes 10376 | tf_op jit(solution)/shard_map/ppermute | solution.py:24
  64.8 0.2 collective-permute-start.12
  65.0 10.7 %collective-permute-done.13 = f32[27,4,8,1]{3,2,1,0:T(8,128)S(1)} collective-permute-done((f32[27,4,8,1]{3,2,1,0:T(8,128)S(1)}, f32[27,4,8,1]{3,2,1,0:T(8,128)S(1)}, u32[]{:S(2)}, u32[]{:S(2)}) %collective-permute-start.13) | collective-permute-done | bytes 3488 | tf_op jit(solution)/shard_map/ppermute | solution.py:24
  75.7 8.4 %collective-permute-done.12 = f32[27,4,8,1]{3,2,1,0:T(8,128)S(1)} collective-permute-done((f32[27,4,8,1]{3,2,1,0:T(8,128)S(1)}, f32[27,4,8,1]{3,2,1,0:T(8,128)S(1)}, u32[]{:S(2)}, u32[]{:S(2)}) %collective-permute-start.12) | collective-permute-done | bytes 3488 | tf_op jit(solution)/shard_map/ppermute | solution.py:23
  84.1 0.7 pad_maximum_fusion.10
  85.0 1.5 %collective-permute-start.15 = (f32[27,4,1,130]{3,2,1,0:T(1,128)S(1)}, f32[27,4,1,130]{3,2,1,0:T(1,128)S(1)}, u32[]{:S(2)}, u32[]{:S(2)}) collective-permute-start(f32[27,4,1,130]{3,2,1,0:T(1,128)S(1)} %get-tuple-element.61), channel_id=1, source_target_pairs={{0,4},{4,8},{8,12},{12,0},{1,5},{5,9},{9,13},{13,1},{2,6},{6,10},{... | collective-permute-start | bytes 168488 | tf_op jit(solution)/shard_map/ppermute | solution.py:23
  86.4 5.7 %collective-permute-done.14 = f32[27,4,1,130]{3,2,1,0:T(1,128)S(1)} collective-permute-done((f32[27,4,1,130]{3,2,1,0:T(1,128)S(1)}, f32[27,4,1,130]{3,2,1,0:T(1,128)S(1)}, u32[]{:S(2)}, u32[]{:S(2)}) %collective-permute-start.14) | collective-permute-done | bytes 56192 | tf_op jit(solution)/shard_map/ppermute | solution.py:24
  92.1 0.4 pad_maximum_fusion
  92.5 0.8 collective-permute-start.16
  93.3 1.0 collective-permute-start.17
  94.3 10.9 %collective-permute-done.16 = f32[27,1,10,130]{3,2,1,0:T(8,128)S(1)} collective-permute-done((f32[27,1,10,130]{3,2,1,0:T(8,128)S(1)}, f32[27,1,10,130]{3,2,1,0:T(8,128)S(1)}, u32[]{:S(2)}, u32[]{:S(2)}) %collective-permute-start.16) | collective-permute-done | bytes 140432 | tf_op jit(solution)/shard_map/ppermute | solution.py:24
  107.8 0.9 broadcast_select_fusion
  (100 shorter events, 5.5 us)
Async XLA Ops:
  0.0 4.5 %copy-start = (f32[8,4]{0,1:T(4,128)S(1)}, f32[8,4]{0,1:T(4,128)}, u32[]{:S(2)}) copy-start(f32[8,4]{0,1:T(4,128)} %param.27) | copy-start | bytes 388
  0.0 0.7 copy-start.5
  0.0 2.4 %copy-start.1 = (f32[27,4,8,128]{3,2,1,0:T(8,128)S(1)}, f32[27,4,8,128]{3,2,1,0:T(8,128)}, u32[]{:S(2)}) copy-start(f32[27,4,8,128]{3,2,1,0:T(8,128)} %param.25) | copy-start | bytes 1327108
  2.4 0.7 copy-start.8
  2.4 0.7 copy-start.3
  2.4 0.7 copy-start.6
  2.4 0.7 copy-start.7
  3.1 0.7 copy-start.4
  4.5 0.7 copy-start.11
  5.3 0.7 copy-start.9
  5.4 0.7 copy-start.10
  6.8 2.4 %copy-start.2 = (s32[4,8,128]{2,1,0:T(8,128)S(1)}, s32[4,8,128]{2,1,0:T(8,128)}, u32[]{:S(2)}) copy-start(s32[4,8,128]{2,1,0:T(8,128)} %param.26) | copy-start | bytes 49156
  7.0 25.6 %collective-permute-start.1 = (f32[27,4,8,1]{3,2,1,0:T(8,128)S(1)}, f32[27,4,8,1]{3,2,1,0:T(8,128)S(1)}, u32[]{:S(2)}, u32[]{:S(2)}) collective-permute-start(f32[27,4,8,1]{3,2,1,0:T(8,128)S(1)} %get-tuple-element.68), channel_id=1, source_target_pairs={{16,0},{0,16},{17,1},{1,17},{18,2},{2,18},{19,3},{3,19},{20,4},{4,... | collective-permute-start | bytes 10376 | tf_op jit(solution)/shard_map/ppermute | solution.py:24
  9.2 23.5 %collective-permute-start = (f32[27,4,8,1]{3,2,1,0:T(8,128)S(1)}, f32[27,4,8,1]{3,2,1,0:T(8,128)S(1)}, u32[]{:S(2)}, u32[]{:S(2)}) collective-permute-start(f32[27,4,8,1]{3,2,1,0:T(8,128)S(1)} %get-tuple-element.67), channel_id=1, source_target_pairs={{0,16},{16,0},{1,17},{17,1},{2,18},{18,2},{3,19},{19,3},{4,20},{20... | collective-permute-start | bytes 10376 | tf_op jit(solution)/shard_map/ppermute | solution.py:23
  9.3 19.6 %collective-permute-start.4 = (s32[4,8,1]{2,1,0:T(8,128)S(1)}, s32[4,8,1]{2,1,0:T(8,128)S(1)}, u32[]{:S(2)}, u32[]{:S(2)}) collective-permute-start(s32[4,8,1]{2,1,0:T(8,128)S(1)} %get-tuple-element.104), channel_id=1, source_target_pairs={{16,0},{0,16},{17,1},{1,17},{18,2},{2,18},{19,3},{3,19},{20,4},{4,... | collective-permute-start | bytes 392 | tf_op jit(solution)/shard_map/ppermute | solution.py:24
  10.7 18.5 %collective-permute-start.3 = (s32[4,8,1]{2,1,0:T(8,128)S(1)}, s32[4,8,1]{2,1,0:T(8,128)S(1)}, u32[]{:S(2)}, u32[]{:S(2)}) collective-permute-start(s32[4,8,1]{2,1,0:T(8,128)S(1)} %get-tuple-element.103), channel_id=1, source_target_pairs={{0,16},{16,0},{1,17},{17,1},{2,18},{18,2},{3,19},{19,3},{4,20},{20... | collective-permute-start | bytes 392 | tf_op jit(solution)/shard_map/ppermute | solution.py:23
  29.3 7.4 %collective-permute-start.6 = (s32[4,1,130]{2,1,0:T(1,128)S(1)}, s32[4,1,130]{2,1,0:T(1,128)S(1)}, u32[]{:S(2)}, u32[]{:S(2)}) collective-permute-start(s32[4,1,130]{2,1,0:T(1,128)S(1)} %get-tuple-element.94), channel_id=1, source_target_pairs={{4,0},{8,4},{12,8},{0,12},{5,1},{9,5},{13,9},{1,13},{6,2},{10,6},{... | collective-permute-start | bytes 6248 | tf_op jit(solution)/shard_map/ppermute | solution.py:24
  32.6 4.4 %collective-permute-start.5 = (s32[4,1,130]{2,1,0:T(1,128)S(1)}, s32[4,1,130]{2,1,0:T(1,128)S(1)}, u32[]{:S(2)}, u32[]{:S(2)}) collective-permute-start(s32[4,1,130]{2,1,0:T(1,128)S(1)} %get-tuple-element.93), channel_id=1, source_target_pairs={{0,4},{4,8},{8,12},{12,0},{1,5},{5,9},{9,13},{13,1},{2,6},{6,10},{... | collective-permute-start | bytes 6248 | tf_op jit(solution)/shard_map/ppermute | solution.py:23
  33.4 7.8 %collective-permute-start.2 = (f32[27,4,1,130]{3,2,1,0:T(1,128)S(1)}, f32[27,4,1,130]{3,2,1,0:T(1,128)S(1)}, u32[]{:S(2)}, u32[]{:S(2)}) collective-permute-start(f32[27,4,1,130]{3,2,1,0:T(1,128)S(1)} %get-tuple-element.64), channel_id=1, source_target_pairs={{4,0},{8,4},{12,8},{0,12},{5,1},{9,5},{13,9},{1,13},{6,2},{10,6},{... | collective-permute-start | bytes 168488 | tf_op jit(solution)/shard_map/ppermute | solution.py:24
  36.7 5.6 %collective-permute-start.8 = (f32[27,4,1,130]{3,2,1,0:T(1,128)S(1)}, f32[27,4,1,130]{3,2,1,0:T(1,128)S(1)}, u32[]{:S(2)}, u32[]{:S(2)}) collective-permute-start(f32[27,4,1,130]{3,2,1,0:T(1,128)S(1)} %get-tuple-element.63), channel_id=1, source_target_pairs={{0,4},{4,8},{8,12},{12,0},{1,5},{5,9},{9,13},{13,1},{2,6},{6,10},{... | collective-permute-start | bytes 168488 | tf_op jit(solution)/shard_map/ppermute | solution.py:23
  37.1 9.1 %collective-permute-start.10 = (s32[1,10,130]{2,1,0:T(8,128)S(1)}, s32[1,10,130]{2,1,0:T(8,128)S(1)}, u32[]{:S(2)}, u32[]{:S(2)}) collective-permute-start(s32[1,10,130]{2,1,0:T(8,128)S(1)} %get-tuple-element.91), channel_id=1, source_target_pairs={{0,1},{1,2},{2,3},{3,0},{4,5},{5,6},{6,7},{7,4},{8,9},{9,10},{10,1... | collective-permute-start | bytes 15608 | tf_op jit(solution)/shard_map/ppermute | solution.py:23
  41.2 4.9 %collective-permute-start.7 = (s32[1,10,130]{2,1,0:T(8,128)S(1)}, s32[1,10,130]{2,1,0:T(8,128)S(1)}, u32[]{:S(2)}, u32[]{:S(2)}) collective-permute-start(s32[1,10,130]{2,1,0:T(8,128)S(1)} %get-tuple-element.92), channel_id=1, source_target_pairs={{1,0},{2,1},{3,2},{0,3},{5,4},{6,5},{7,6},{4,7},{9,8},{10,9},{11,1... | collective-permute-start | bytes 15608 | tf_op jit(solution)/shard_map/ppermute | solution.py:24
  42.7 15.3 %collective-permute-start.9 = (f32[27,1,10,130]{3,2,1,0:T(8,128)S(1)}, f32[27,1,10,130]{3,2,1,0:T(8,128)S(1)}, u32[]{:S(2)}, u32[]{:S(2)}) collective-permute-start(f32[27,1,10,130]{3,2,1,0:T(8,128)S(1)} %get-tuple-element.60), channel_id=1, source_target_pairs={{1,0},{2,1},{3,2},{0,3},{5,4},{6,5},{7,6},{4,7},{9,8},{10,9},{11,1... | collective-permute-start | bytes 421208 | tf_op jit(solution)/shard_map/ppermute | solution.py:24
  46.3 13.6 %collective-permute-start.11 = (f32[27,1,10,130]{3,2,1,0:T(8,128)S(1)}, f32[27,1,10,130]{3,2,1,0:T(8,128)S(1)}, u32[]{:S(2)}, u32[]{:S(2)}) collective-permute-start(f32[27,1,10,130]{3,2,1,0:T(8,128)S(1)} %get-tuple-element.59), channel_id=1, source_target_pairs={{0,1},{1,2},{2,3},{3,0},{4,5},{5,6},{6,7},{7,4},{8,9},{9,10},{10,1... | collective-permute-start | bytes 421208 | tf_op jit(solution)/shard_map/ppermute | solution.py:23
  63.5 12.2 %collective-permute-start.13 = (f32[27,4,8,1]{3,2,1,0:T(8,128)S(1)}, f32[27,4,8,1]{3,2,1,0:T(8,128)S(1)}, u32[]{:S(2)}, u32[]{:S(2)}) collective-permute-start(f32[27,4,8,1]{3,2,1,0:T(8,128)S(1)} %get-tuple-element.66), channel_id=1, source_target_pairs={{16,0},{0,16},{17,1},{1,17},{18,2},{2,18},{19,3},{3,19},{20,4},{4,... | collective-permute-start | bytes 10376 | tf_op jit(solution)/shard_map/ppermute | solution.py:24
  64.8 19.4 %collective-permute-start.12 = (f32[27,4,8,1]{3,2,1,0:T(8,128)S(1)}, f32[27,4,8,1]{3,2,1,0:T(8,128)S(1)}, u32[]{:S(2)}, u32[]{:S(2)}) collective-permute-start(f32[27,4,8,1]{3,2,1,0:T(8,128)S(1)} %get-tuple-element.65), channel_id=1, source_target_pairs={{0,16},{16,0},{1,17},{17,1},{2,18},{18,2},{3,19},{19,3},{4,20},{20... | collective-permute-start | bytes 10376 | tf_op jit(solution)/shard_map/ppermute | solution.py:23
  84.9 7.2 %collective-permute-start.14 = (f32[27,4,1,130]{3,2,1,0:T(1,128)S(1)}, f32[27,4,1,130]{3,2,1,0:T(1,128)S(1)}, u32[]{:S(2)}, u32[]{:S(2)}) collective-permute-start(f32[27,4,1,130]{3,2,1,0:T(1,128)S(1)} %get-tuple-element.62), channel_id=1, source_target_pairs={{4,0},{8,4},{12,8},{0,12},{5,1},{9,5},{13,9},{1,13},{6,2},{10,6},{... | collective-permute-start | bytes 168488 | tf_op jit(solution)/shard_map/ppermute | solution.py:24
  85.0 7.1 %collective-permute-start.15 = (f32[27,4,1,130]{3,2,1,0:T(1,128)S(1)}, f32[27,4,1,130]{3,2,1,0:T(1,128)S(1)}, u32[]{:S(2)}, u32[]{:S(2)}) collective-permute-start(f32[27,4,1,130]{3,2,1,0:T(1,128)S(1)} %get-tuple-element.61), channel_id=1, source_target_pairs={{0,4},{4,8},{8,12},{12,0},{1,5},{5,9},{9,13},{13,1},{2,6},{6,10},{... | collective-permute-start | bytes 168488 | tf_op jit(solution)/shard_map/ppermute | solution.py:23
  92.5 12.7 %collective-permute-start.16 = (f32[27,1,10,130]{3,2,1,0:T(8,128)S(1)}, f32[27,1,10,130]{3,2,1,0:T(8,128)S(1)}, u32[]{:S(2)}, u32[]{:S(2)}) collective-permute-start(f32[27,1,10,130]{3,2,1,0:T(8,128)S(1)} %get-tuple-element.58), channel_id=1, source_target_pairs={{1,0},{2,1},{3,2},{0,3},{5,4},{6,5},{7,6},{4,7},{9,8},{10,9},{11,1... | collective-permute-start | bytes 421208 | tf_op jit(solution)/shard_map/ppermute | solution.py:24
  93.3 13.6 %collective-permute-start.17 = (f32[27,1,10,130]{3,2,1,0:T(8,128)S(1)}, f32[27,1,10,130]{3,2,1,0:T(8,128)S(1)}, u32[]{:S(2)}, u32[]{:S(2)}) collective-permute-start(f32[27,1,10,130]{3,2,1,0:T(8,128)S(1)} %get-tuple-element.57), channel_id=1, source_target_pairs={{0,1},{1,2},{2,3},{3,0},{4,5},{5,6},{6,7},{7,4},{8,9},{9,10},{10,1... | collective-permute-start | bytes 421208 | tf_op jit(solution)/shard_map/ppermute | solution.py:23
where the time goes:
time: 109 us
  waiting for transfers between devices  66.2 us (61%)
  starting transfers between devices  23.8 us (22%)
  other arithmetic  10.8 us (10%)
  local copies, waits for them, and re-layouts  3.69 us (3%)
  matrix products  3.57 us (3%)
    ppermute x9, waiting for transfers between devices, padded_2(): after = lax.ppermute(initial, axis, down)  56 us
    ppermute x9, starting transfers between devices, padded_2(): after = lax.ppermute(initial, axis, down)  15.6 us
    ppermute x9, waiting for transfers between devices, padded_2(): before = lax.ppermute(last, axis, up)  10.2 us
    ppermute x9, starting transfers between devices, padded_2(): before = lax.ppermute(last, axis, up)  8.17 us
    unnamed x50, other arithmetic  4.77 us
    unnamed x26, local copies, waits for them, and re-layouts  2.99 us
    concatenate x6, other arithmetic, padded_2(): array = jnp.concatenate([before, array, after], axis=dim)  2.56 us
    dot_general x2, matrix products, collide(): jnp.einsum('qm,qzyx->mzyx', jnp.asarray(first_table, jnp.float32), pops,...  2.2 us
  transfers between devices with their start and end apart: 18, of which 9 were waited for; matrix products, arithmetic and copies ran while one was open for 4% of the time, Pallas kernels for 0%

commit v1 on v0

v1 whole, which is shorter than its diff:
```python
import jax
import jax.numpy as jnp
import numpy as np
from jax import lax
from jax.experimental import pallas as pl
from jax.experimental.pallas import tpu as pltpu
from jax.sharding import PartitionSpec as P

SPONGE = 32
TAU = 0.52
SMAG = 18.0 * 1.4142135623730951 * 0.17 * 0.17

VEL = [(cx, cy, cz) for cz in (-1, 0, 1) for cy in (-1, 0, 1) for cx in (-1, 0, 1)]
WEIGHT = [
    float(np.array([8.0 / 27.0, 2.0 / 27.0, 1.0 / 54.0, 1.0 / 216.0])[cx * cx + cy * cy + cz * cz])
    for cx, cy, cz in VEL
]
WALL, AIM, CHANNELS = 27, 28, 29
NZ, NY, NX = 4, 8, 128
PITCH = NY + 4
FLAT = (NZ + 4) * PITCH
PAD = 8
ROWS = PAD + FLAT + PAD
UNITS = (NZ + 2) * PITCH // 8

VMEM = pl.BlockSpec(memory_space=pltpu.VMEM)
SMEM = pl.BlockSpec(memory_space=pltpu.SMEM)
F32 = jnp.float32

Y_ROWS = (CHANNELS + 9) * NZ
Z_BLOCKS = CHANNELS + 10
Z_ROWS = -(-Z_BLOCKS * PITCH // 8) * 8


def relaxed(f, sponge, aim):
    quad = {}
    for cz in (-1, 0, 1):
        line = {}
        for cy in (-1, 0, 1):
            base = 9 * (cz + 1) + 3 * (cy + 1)
            both = f[base + 2] + f[base]
            line[cy] = (both + f[base + 1], f[base + 2] - f[base], both)
        s = line[1][0] + line[-1][0]
        sx = line[1][1] + line[-1][1]
        quad[cz] = dict(
            n=s + line[0][0],
            y=line[1][0] - line[-1][0],
            yy=s,
            x=sx + line[0][1],
            xy=line[1][1] - line[-1][1],
            xx=line[1][2] + line[-1][2] + line[0][2],
        )
    up, mid, down = quad[1], quad[0], quad[-1]
    zz = up["n"] + down["n"]
    rho = zz + mid["n"]
    jz = up["n"] - down["n"]
    jy = up["y"] + down["y"] + mid["y"]
    jx = up["x"] + down["x"] + mid["x"]
    inverse = 1.0 / rho
    ux, uy, uz = jx * inverse, jy * inverse, jz * inverse
    third = rho * (1.0 / 3.0)
    pxx = (up["xx"] + down["xx"] + mid["xx"]) - (third + jx * ux)
    pyy = (up["yy"] + down["yy"] + mid["yy"]) - (third + jy * uy)
    pzz = zz - (third + jz * uz)
    pxy = (up["xy"] + down["xy"] + mid["xy"]) - jx * uy
    pxz = (up["x"] - down["x"]) - jx * uz
    pyz = (up["y"] - down["y"]) - jy * uz
    strain = pxx * pxx + pyy * pyy + pzz * pzz + 2.0 * (pxy * pxy + pxz * pxz + pyz * pyz)
    size = jnp.sqrt(2.0 * strain)
    tau = 0.5 * (TAU + jnp.sqrt(TAU * TAU + SMAG * size * inverse))
    omega = 1.0 / tau
    keep = 1.0 - omega
    if sponge is not None:
        keep = jnp.where(sponge, 0.0, keep)
        omega = jnp.where(sponge, 1.0, omega)
        ux = jnp.where(sponge, aim, ux)
        uy = jnp.where(sponge, 0.0, uy)
        uz = jnp.where(sponge, 0.0, uz)
    square = 1.0 - 1.5 * (ux * ux + uy * uy + uz * uz)
    vx, vy, vz = 3.0 * ux, 3.0 * uy, 3.0 * uz
    share = rho * omega
    weighted = {w: share * w for w in sorted(set(WEIGHT))}
    post = [None] * 27
    for q in range(14):
        cx, cy, cz = VEL[q]
        along = None
        for c, v in ((cx, vx), (cy, vy), (cz, vz)):
            if c:
                along = (v if c > 0 else -v) if along is None else (along + v if c > 0 else along - v)
        scale = weighted[WEIGHT[q]]
        if along is None:
            post[q] = keep * f[q] + scale * square
            continue
        even = square + 0.5 * along * along
        post[q] = keep * f[q] + scale * (even + along)
        post[26 - q] = keep * f[26 - q] + scale * (even - along)
    return post


def lane_ids():
    return lax.broadcasted_iota(jnp.int32, (8, 128), 1)


def row_ids():
    return lax.broadcasted_iota(jnp.int32, (8, 128), 0)


def first_kernel(pops, solid, table, index, own, yup, ydown):
    lanes, rows = lane_ids(), row_ids()
    sponge = (lax.axis_index("gx") * NX + lanes) < SPONGE
    for z in range(NZ):
        aim = jnp.zeros((8, 128), F32)
        for y in range(NY):
            aim = jnp.where(rows == y, table[index[y], z], aim)
        post = relaxed([pops[q, z] for q in range(27)], sponge, aim)
        for q in range(27):
            own[pl.ds((q * NZ + z) * 8, 8), :] = post[q]
        own[pl.ds((WALL * NZ + z) * 8, 8), :] = solid[z].astype(F32)
        own[pl.ds((AIM * NZ + z) * 8, 8), :] = aim
    for out, edge, second, part in ((yup, 7, 6, 6), (ydown, 0, 1, 0)):
        out[pl.ds(0, CHANNELS * NZ), :] = own[pl.ds(edge, CHANNELS * NZ, stride=8), :]
        for a in range(3):
            out[pl.ds((CHANNELS + 3 * a) * NZ, 3 * NZ), :] = own[
                pl.ds((9 * a + part) * NZ * 8 + second, 3 * NZ, stride=8), :
            ]


def second_kernel(own, below, above, zup, zdown):
    for out, first, second, part in ((zup, NZ - 1, NZ - 2, 2), (zdown, 0, 1, 0)):
        for k in range(Z_BLOCKS):
            channel, z = (k, first) if k < CHANNELS else (9 * part + k - CHANNELS, second)
            if k == Z_BLOCKS - 1:
                channel = WALL
            out[pl.ds(k * PITCH + 2, 8), :] = own[pl.ds((channel * NZ + z) * 8, 8), :]
        for halo, near, far, group in ((below, 1, 0, 6), (above, PITCH - 2, PITCH - 1, 0)):
            out[pl.ds(near, CHANNELS, stride=PITCH), :] = halo[pl.ds(first, CHANNELS, stride=NZ), :]
            out[pl.ds(CHANNELS * PITCH + near, 9, stride=PITCH), :] = halo[
                pl.ds(9 * part * NZ + second, 9, stride=NZ), :
            ]
            wall_first = halo[pl.ds(WALL * NZ + first, 1), :]
            wall_second = halo[pl.ds(WALL * NZ + second, 1), :]
            out[pl.ds((Z_BLOCKS - 1) * PITCH + near, 1), :] = wall_second
            for a in range(3):
                out[pl.ds((9 * a + group) * PITCH + far, 3, stride=PITCH), :] = halo[
                    pl.ds((CHANNELS + 3 * a) * NZ + first, 3, stride=NZ), :
                ]
            out[pl.ds((CHANNELS + group) * PITCH + far, 3, stride=PITCH), :] = halo[
                pl.ds((CHANNELS + 3 * part) * NZ + second, 3, stride=NZ), :
            ]
            out[pl.ds(WALL * PITCH + far, 1), :] = wall_first
            out[pl.ds((Z_BLOCKS - 1) * PITCH + far, 1), :] = wall_second


def plane_at(z):
    return PAD + (z + 2) * PITCH


def third_kernel(own, below, above, floor, ceiling, full, pack):
    last = lax.axis_size("gz") - 1
    here = lax.axis_index("gz")
    for c in range(CHANNELS):
        for z in range(NZ):
            full[c, pl.ds(plane_at(z) + 2, 8), :] = own[pl.ds((c * NZ + z) * 8, 8), :]
        for halo, near in ((below, 1), (above, PITCH - 2)):
            full[c, pl.ds(plane_at(0) + near, NZ, stride=PITCH), :] = halo[pl.ds(c * NZ, NZ), :]
        full[c, pl.ds(plane_at(-1), PITCH), :] = floor[pl.ds(c * PITCH, PITCH), :]
        full[c, pl.ds(plane_at(NZ), PITCH), :] = ceiling[pl.ds(c * PITCH, PITCH), :]
    for halo, far, group in ((below, 0, 6), (above, PITCH - 1, 0)):
        for k in range(9):
            q = 9 * (k // 3) + group + k % 3
            full[q, pl.ds(plane_at(0) + far, NZ, stride=PITCH), :] = halo[
                pl.ds((CHANNELS + k) * NZ, NZ), :
            ]
        full[WALL, pl.ds(plane_at(0) + far, NZ, stride=PITCH), :] = halo[pl.ds(WALL * NZ, NZ), :]
    for halo, far, group in ((floor, -2, 18), (ceiling, NZ + 1, 0)):
        for k in range(10):
            q = group + k if k < 9 else WALL
            full[q, pl.ds(plane_at(far), PITCH), :] = halo[pl.ds((CHANNELS + k) * PITCH, PITCH), :]

    @pl.when(here == 0)
    def _():
        full[WALL, pl.ds(plane_at(-1), PITCH), :] = jnp.ones((PITCH, 128), F32)

    @pl.when(here == last)
    def _():
        for q in range(9):
            full[q, pl.ds(plane_at(NZ), PITCH), :] = full[q + 18, pl.ds(plane_at(NZ - 1), PITCH), :]

    slot = lane_ids() // 4
    for t in range(FLAT // 8):
        packed = jnp.zeros((8, 128), F32)
        for c in range(CHANNELS):
            moved = pltpu.roll(full[c, pl.ds(PAD + 8 * t, 8), :], (4 * c + 2) % 128, 1)
            packed = jnp.where(slot == c, moved, packed)
        pack[pl.ds(8 * t, 8), :] = packed


def last_kernel(full, mine, left, right, out, post, west, east, turn, walls, back):
    here_x, size_x = lax.axis_index("gx"), lax.axis_size("gx")
    top = lax.axis_index("gz") == lax.axis_size("gz") - 1
    lanes, rows = lane_ids(), row_ids()

    west[pl.ds(PAD, FLAT), :] = left[...]
    east[pl.ds(PAD, FLAT), :] = right[...]

    def edged(value, cx, channel, start):
        if cx == 0:
            return value
        if cx > 0:
            column = pltpu.roll(west[pl.ds(start, 8), :], (128 - 4 * channel - 1) % 128, 1)
            return jnp.where(lanes == 0, column, pltpu.roll(value, 1, 1))
        column = pltpu.roll(east[pl.ds(start, 8), :], (127 - 4 * channel - 2) % 128, 1)
        return jnp.where(lanes == 127, column, pltpu.roll(value, 127, 1))

    for cx in (-1, 0, 1):
        for t in range(FLAT // 8):
            start = PAD + 8 * t
            walls[cx + 1, pl.ds(start, 8), :] = edged(full[WALL, pl.ds(start, 8), :], cx, WALL, start)

    for i, source in enumerate((mine, left, right)):
        block = jnp.concatenate([source[...], jnp.zeros((128 - FLAT, 128), F32)], axis=0)
        turn[i, pl.ds(PAD, 128), :] = block.T
    strip = []
    for c in range(CHANNELS):
        a = turn[1, pl.ds(PAD + 4 * c, 8), :]
        b = turn[0, pl.ds(PAD + 4 * c, 8), :]
        d = turn[0, pl.ds(PAD + 4 * c - 4, 8), :]
        e = turn[2, pl.ds(PAD + 4 * c - 4, 8), :]
        strip.append(jnp.where(rows < 2, a, jnp.where(rows < 4, b, jnp.where(rows < 6, d, e))))

    def shifted(value, q):
        cx, cy, cz = VEL[q]
        if cx:
            value = pltpu.roll(value, cx % 8, 0)
        step = (PITCH * cz + cy) % 128
        return pltpu.roll(value, step, 1) if step else value

    moved = []
    for q in range(27):
        value = shifted(strip[q], q)
        if q != 13:
            value = jnp.where(shifted(strip[WALL], q) != 0.0, strip[26 - q], value)
        moved.append(jnp.where(strip[WALL] != 0.0, WEIGHT[q], value))
    column = here_x * NX + jnp.where(rows < 4, rows - 2, rows + (NX - 6))
    column = lax.rem(column + size_x * NX, size_x * NX)
    sides = relaxed(moved, column < SPONGE, strip[AIM])
    lid = top & (lanes >= (NZ + 2) * PITCH) & (lanes < (NZ + 3) * PITCH)
    for q in range(9):
        sides[q] = jnp.where(lid, pltpu.roll(sides[q + 18], PITCH, 1), sides[q])
    merged = []
    for k in range(9):
        merged.append(jnp.where(rows < 4, sides[3 * k + 2], sides[3 * k]))
    merged = jnp.concatenate(merged + [jnp.zeros((128 - 72, 128), F32)], axis=0)
    back[...] = merged.T

    sponge = (here_x * NX + lanes) < SPONGE
    for u in range(UNITS):
        cell = PAD + PITCH + 8 * u
        f = []
        solid = walls[1, pl.ds(cell, 8), :] != 0.0
        for q in range(27):
            cx, cy, cz = VEL[q]
            start = cell - PITCH * cz - cy
            value = edged(full[q, pl.ds(start, 8), :], cx, q, start)
            if q != 13:
                blocked = walls[cx + 1, pl.ds(start, 8), :] != 0.0
                value = jnp.where(blocked, full[26 - q, pl.ds(cell, 8), :], value)
            f.append(jnp.where(solid, WEIGHT[q], value))
        done = relaxed(f, sponge, full[AIM, pl.ds(cell, 8), :])
        for q in range(27):
            post[q, pl.ds(8 * u, 8), :] = done[q]

    @pl.when(top)
    def _():
        for q in range(9):
            post[q, pl.ds((NZ + 1) * PITCH, PITCH), :] = post[q + 18, pl.ds(NZ * PITCH, PITCH), :]

    for z in range(NZ):
        cell = (z + 1) * PITCH + 2
        solid = walls[1, pl.ds(PAD + PITCH + cell, 8), :] != 0.0
        for q in range(27):
            cx, cy, cz = VEL[q]
            start = cell - PITCH * cz - cy
            value = post[q, pl.ds(start, 8), :]
            if cx:
                lane = 8 * (q // 3) + (1 if cx > 0 else 6)
                edge = 0 if cx > 0 else 127
                side = pltpu.roll(back[pl.ds(PITCH + start, 8), :], (edge - lane) % 128, 1)
                value = jnp.where(lanes == edge, side, pltpu.roll(value, cx % 128, 1))
            if q != 13:
                blocked = walls[cx + 1, pl.ds(PAD + PITCH + start, 8), :] != 0.0
                value = jnp.where(blocked, post[26 - q, pl.ds(cell, 8), :], value)
            out[q, z] = jnp.where(solid, WEIGHT[q], value)


def both_ways(axis, ahead, back, wrap):
    size = lax.axis_size(axis)
    up = [(i, (i + 1) % size) for i in range(size if wrap else size - 1)]
    down = [(j, i) for i, j in up]
    return lax.ppermute(ahead, axis, up), lax.ppermute(back, axis, down)


def shape(*dims):
    return jax.ShapeDtypeStruct(dims, F32)


def shards(pops, solid, profile_table, profile_index):
    own, yup, ydown = pl.pallas_call(
        first_kernel,
        out_shape=[shape(CHANNELS * NZ * 8, 128), shape(Y_ROWS, 128), shape(Y_ROWS, 128)],
        in_specs=[VMEM, VMEM, SMEM, SMEM],
        out_specs=[VMEM] * 3,
        name="collide",
    )(pops, solid, profile_table, profile_index)
    below, above = both_ways("gy", yup, ydown, True)
    zup, zdown = pl.pallas_call(
        second_kernel,
        out_shape=[shape(Z_ROWS, 128)] * 2,
        in_specs=[VMEM] * 3,
        out_specs=[VMEM] * 2,
        name="pack_z",
    )(own, below, above)
    floor, ceiling = both_ways("gz", zup, zdown, False)
    full, pack = pl.pallas_call(
        third_kernel,
        out_shape=[shape(CHANNELS, ROWS, 128), shape(FLAT, 128)],
        in_specs=[VMEM] * 5,
        out_specs=[VMEM] * 2,
        name="pack_x",
    )(own, below, above, floor, ceiling)
    if lax.axis_size("gx") == 2:
        left = lax.ppermute(pack, "gx", [(0, 1), (1, 0)])
        right = left
    else:
        left, right = both_ways("gx", pack, pack, True)
    return pl.pallas_call(
        last_kernel,
        out_shape=shape(27, NZ, NY, NX),
        in_specs=[VMEM] * 4,
        out_specs=VMEM,
        scratch_shapes=[
            pltpu.VMEM((27, UNITS * 8, 128), F32),
            pltpu.VMEM((ROWS, 128), F32),
            pltpu.VMEM((ROWS, 128), F32),
            pltpu.VMEM((3, PAD + 128 + PAD, 128), F32),
            pltpu.VMEM((3, ROWS, 128), F32),
            pltpu.VMEM((128, 128), F32),
        ],
        name="finish",
    )(full, pack, left, right)


def solution(mesh):
    return jax.shard_map(
        shards,
        mesh=mesh,
        in_specs=(P(None, "gz", "gy", "gx"), P("gz", "gy", "gx"), P(None, "gz"), P("gy")),
        out_specs=P(None, "gz", "gy", "gx"),
        check_vma=False,
    )
```

time: 109 us -> 36.5 us (0.33)
  waiting for transfers between devices: 66.2 us -> 11.2 us
  starting transfers between devices: 23.8 us -> 11.4 us
  other arithmetic: 10.8 us -> 0 us
  Pallas kernels: 0 us -> 10.3 us
  matrix products: 3.57 us -> 0 us
    ppermute x18 -> x5, waiting for transfers between devices: 66.2 us -> 11.2 us  [the longest x4 9.26 us: both_ways(): return (lax.ppermute(ahead, axis, up), lax.ppermute(back, axis, down))]
    ppermute x18 -> x5, starting transfers between devices: 23.8 us -> 11.4 us  [the longest x4 10.2 us: both_ways(): return (lax.ppermute(ahead, axis, up), lax.ppermute(back, axis, down))]
    pallas_call x0 -> x4, Pallas kernels: none -> 10.3 us  [the longest x1 3.43 us: shards(): pl.pallas_call(last_kernel, out_shape=shape(27, NZ, NY, NX), in_specs=[VM...]
    unnamed x50 -> x0, other arithmetic: 4.77 us -> none
    dot_general x5 -> x0, matrix products: 3.57 us -> none  [the longest x2 2.2 us: collide(): jnp.einsum('qm,qzyx->mzyx', jnp.asarray(first_table, jnp.float32), pops,...]
    concatenate x6 -> x0, other arithmetic: 2.56 us -> none  [padded_2(): array = jnp.concatenate([before, array, after], axis=dim)]
    select_n x4 -> x0, other arithmetic: 2.42 us -> none  [the longest x2 1.46 us: shards(): post = jnp.where(sponge, pinned, post)]
    unnamed x26 -> x11, local copies, waits for them, and re-layouts: 2.99 us -> 3.26 us
  transfers between devices with their start and end apart: 18 -> 5, of which waited for: 9 -> 5; matrix products, arithmetic and copies ran while one was open for 4% -> 0% of each run, Pallas kernels for 0% -> 0%
where the time goes in v1:
time: 36.5 us; the launch traced here: 36.2 us
  starting transfers between devices  11.4 us (31%)
  waiting for transfers between devices  11.2 us (31%)
  Pallas kernels  10.3 us (28%)
  local copies, waits for them, and re-layouts  3.26 us (9%)
    ppermute x4, starting transfers between devices, both_ways(): return (lax.ppermute(ahead, axis, up), lax.ppermute(back, axis, down))  10.2 us
    ppermute x4, waiting for transfers between devices, both_ways(): return (lax.ppermute(ahead, axis, up), lax.ppermute(back, axis, down))  9.26 us
    pallas_call x1, Pallas kernels, shards(): pl.pallas_call(last_kernel, out_shape=shape(27, NZ, NY, NX), in_specs=[VM...  3.43 us
    unnamed x11, local copies, waits for them, and re-layouts  3.26 us
    pallas_call x1, Pallas kernels, shards(): pl.pallas_call(third_kernel, out_shape=[shape(CHANNELS, ROWS, 128), shape...  2.97 us
    pallas_call x1, Pallas kernels, shards(): pl.pallas_call(first_kernel, out_shape=[shape(CHANNELS * NZ * 8, 128), sh...  2.06 us
    ppermute x1, waiting for transfers between devices, shards(): left = lax.ppermute(pack, 'gx', [(0, 1), (1, 0)])  1.91 us
    pallas_call x1, Pallas kernels, shards(): pl.pallas_call(second_kernel, out_shape=[shape(Z_ROWS, 128)] * 2, in_spec...  1.87 us
  transfers between devices with their start and end apart: 5, of which 5 were waited for; matrix products, arithmetic and copies ran while one was open for 0% of the time, Pallas kernels for 0%

profile of v1, /device:TPU:1, one launch (start us, length us, event | category | flops | bytes accessed | tf_op | source)
XLA Modules:
  0.0 36.2 jit_solution(5477471522596226675)
XLA Ops:
  0.0 1.3 %copy.5.table = f32[8,4]{1,0:T(8,128)} copy(f32[8,4]{0,1:T(4,128)} %param.6) | data formatting | bytes 256 | tf_op args[2]
  1.3 2.1 %collide.1 = (f32[928,128]{1,0:T(8,128)}, f32[152,128]{1,0:T(8,128)}, f32[152,128]{1,0:T(8,128)}) custom-call(f32[27,4,8,128]{3,2,1,0:T(8,128)} %pops.1, s32[4,8,128]{2,1,0:T(8,128)} %solid.1, f32[8,4]{1,0:T(8,128)} %copy.5.table, s32[8]{0:T(128)} %index.1), custom_call_target="tpu_custom_call" | custom-call | tf_op jit(solution)/shard_map/collide/pallas_call | solution.py:308
  3.4 2.1 %collective-permute-start = (f32[152,128]{1,0:T(8,128)}, f32[152,128]{1,0:T(8,128)S(1)}, u32[]{:S(2)}, u32[]{:S(2)}) collective-permute-start(f32[152,128]{1,0:T(8,128)} %get-tuple-element.13), channel_id=1, source_target_pairs={{0,4},{4,8},{8,12},{12,0},{1,5},{5,9},{9,13},{13,1},{2,6},{6,10},{... | collective-permute-start | bytes 233480 | tf_op jit(solution)/shard_map/ppermute | solution.py:300
  5.5 2.0 %collective-permute-start.1 = (f32[152,128]{1,0:T(8,128)}, f32[152,128]{1,0:T(8,128)S(1)}, u32[]{:S(2)}, u32[]{:S(2)}) collective-permute-start(f32[152,128]{1,0:T(8,128)} %get-tuple-element.14), channel_id=1, source_target_pairs={{4,0},{8,4},{12,8},{0,12},{5,1},{9,5},{13,9},{1,13},{6,2},{10,6},{... | collective-permute-start | bytes 233480 | tf_op jit(solution)/shard_map/ppermute | solution.py:300
  7.6 2.1 %collective-permute-done.below = f32[152,128]{1,0:T(8,128)S(1)} collective-permute-done((f32[152,128]{1,0:T(8,128)}, f32[152,128]{1,0:T(8,128)S(1)}, u32[]{:S(2)}, u32[]{:S(2)}) %collective-permute-start) | collective-permute-done | bytes 77856 | tf_op jit(solution)/shard_map/ppermute | solution.py:300
  9.6 0.0 copy-start
  9.6 1.4 %collective-permute-done.1.above = f32[152,128]{1,0:T(8,128)S(1)} collective-permute-done((f32[152,128]{1,0:T(8,128)}, f32[152,128]{1,0:T(8,128)S(1)}, u32[]{:S(2)}, u32[]{:S(2)}) %collective-permute-start.1) | collective-permute-done | bytes 77856 | tf_op jit(solution)/shard_map/ppermute | solution.py:300
  11.1 0.0 copy-start.1
  11.1 0.0 copy-done
  11.1 0.6 %copy-done.1 = f32[152,128]{1,0:T(8,128)} copy-done((f32[152,128]{1,0:T(8,128)}, f32[152,128]{1,0:T(8,128)S(1)}, u32[]{:S(2)}) %copy-start.1) | copy-done | bytes 77848
  11.7 1.9 %pack_z.1 = (f32[472,128]{1,0:T(8,128)}, f32[472,128]{1,0:T(8,128)}) custom-call(f32[928,128]{1,0:T(8,128)} %get-tuple-element.12.own, f32[152,128]{1,0:T(8,128)} %copy-done, f32[152,128]{1,0:T(8,128)} %copy-done.1), custom_call_target="tpu_custom_call" | custom-call | tf_op jit(solution)/shard_map/pack_z/pallas_call | solution.py:316
  13.5 4.1 %collective-permute-start.2 = (f32[472,128]{1,0:T(8,128)}, f32[472,128]{1,0:T(8,128)S(1)}, u32[]{:S(2)}, u32[]{:S(2)}) collective-permute-start(f32[472,128]{1,0:T(8,128)} %get-tuple-element.15), channel_id=1, source_target_pairs={{0,1},{1,2},{2,3},{4,5},{5,6},{6,7},{8,9},{9,10},{10,11},{12,13},{... | collective-permute-start | bytes 725000 | tf_op jit(solution)/shard_map/ppermute | solution.py:300
  17.7 1.9 %collective-permute-start.3 = (f32[472,128]{1,0:T(8,128)}, f32[472,128]{1,0:T(8,128)S(1)}, u32[]{:S(2)}, u32[]{:S(2)}) collective-permute-start(f32[472,128]{1,0:T(8,128)} %get-tuple-element.16), channel_id=1, source_target_pairs={{1,0},{2,1},{3,2},{5,4},{6,5},{7,6},{9,8},{10,9},{11,10},{13,12},{... | collective-permute-start | bytes 725000 | tf_op jit(solution)/shard_map/ppermute | solution.py:300
  19.6 1.5 %collective-permute-done.2.floor = f32[472,128]{1,0:T(8,128)S(1)} collective-permute-done((f32[472,128]{1,0:T(8,128)}, f32[472,128]{1,0:T(8,128)S(1)}, u32[]{:S(2)}, u32[]{:S(2)}) %collective-permute-start.2) | collective-permute-done | bytes 241696 | tf_op jit(solution)/shard_map/ppermute | solution.py:300
  21.1 0.0 copy-start.2
  21.1 4.3 %collective-permute-done.3.ceiling = f32[472,128]{1,0:T(8,128)S(1)} collective-permute-done((f32[472,128]{1,0:T(8,128)}, f32[472,128]{1,0:T(8,128)S(1)}, u32[]{:S(2)}, u32[]{:S(2)}) %collective-permute-start.3) | collective-permute-done | bytes 241696 | tf_op jit(solution)/shard_map/ppermute | solution.py:300
  25.3 0.0 copy-done.2
  25.3 0.0 copy-start.3
  25.3 0.7 %copy-done.3 = f32[472,128]{1,0:T(8,128)} copy-done((f32[472,128]{1,0:T(8,128)}, f32[472,128]{1,0:T(8,128)S(1)}, u32[]{:S(2)}) %copy-start.3) | copy-done | bytes 241688
  26.0 3.0 %pack_x.1 = (f32[29,112,128]{2,1,0:T(8,128)}, f32[96,128]{1,0:T(8,128)}) custom-call(f32[928,128]{1,0:T(8,128)} %get-tuple-element.12.own, f32[152,128]{1,0:T(8,128)} %copy-done, f32[152,128]{1,0:T(8,128)} %copy-done.1, f32[472,128]{1,0:T(8,128)} %copy-done.2, f32[472,128]{1,0:T(8,128)} %copy-done.3), custom_call_target="tpu_custom_call" | custom-call | tf_op jit(solution)/shard_map/pack_x/pallas_call | solution.py:324
  29.0 1.2 %collective-permute-start.4 = (f32[96,128]{1,0:T(8,128)}, f32[96,128]{1,0:T(8,128)S(1)}, u32[]{:S(2)}, u32[]{:S(2)}) collective-permute-start(f32[96,128]{1,0:T(8,128)} %get-tuple-element.18.mine), channel_id=1, source_target_pairs={{0,16},{16,0},{1,17},{17,1},{2,18},{18,2},{3,19},{19,3},{4,20},{20... | collective-permute-start | bytes 147464 | tf_op jit(solution)/shard_map/ppermute | solution.py:332
  30.2 1.9 %collective-permute-done.4.left.right = f32[96,128]{1,0:T(8,128)S(1)} collective-permute-done((f32[96,128]{1,0:T(8,128)}, f32[96,128]{1,0:T(8,128)S(1)}, u32[]{:S(2)}, u32[]{:S(2)}) %collective-permute-start.4) | collective-permute-done | bytes 49184 | tf_op jit(solution)/shard_map/ppermute | solution.py:332
  32.2 0.0 copy-start.4
  32.2 0.6 %copy-done.4 = f32[96,128]{1,0:T(8,128)} copy-done((f32[96,128]{1,0:T(8,128)}, f32[96,128]{1,0:T(8,128)S(1)}, u32[]{:S(2)}) %copy-start.4) | copy-done | bytes 49176
  32.8 3.4 %finish.1 = f32[27,4,8,128]{3,2,1,0:T(8,128)} custom-call(f32[29,112,128]{2,1,0:T(8,128)} %get-tuple-element.17.full, f32[96,128]{1,0:T(8,128)} %get-tuple-element.18.mine, f32[96,128]{1,0:T(8,128)} %copy-done.4, f32[96,128]{1,0:T(8,128)} %copy-done.4), custom_call_target="tpu_custom_call" | custom-call | tf_op jit(solution)/shard_map/finish/pallas_call | solution.py:336
Async XLA Ops:
  3.4 6.2 %collective-permute-start = (f32[152,128]{1,0:T(8,128)}, f32[152,128]{1,0:T(8,128)S(1)}, u32[]{:S(2)}, u32[]{:S(2)}) collective-permute-start(f32[152,128]{1,0:T(8,128)} %get-tuple-element.13), channel_id=1, source_target_pairs={{0,4},{4,8},{8,12},{12,0},{1,5},{5,9},{9,13},{13,1},{2,6},{6,10},{... | collective-permute-start | bytes 233480 | tf_op jit(solution)/shard_map/ppermute | solution.py:300
  5.5 5.5 %collective-permute-start.1 = (f32[152,128]{1,0:T(8,128)}, f32[152,128]{1,0:T(8,128)S(1)}, u32[]{:S(2)}, u32[]{:S(2)}) collective-permute-start(f32[152,128]{1,0:T(8,128)} %get-tuple-element.14), channel_id=1, source_target_pairs={{4,0},{8,4},{12,8},{0,12},{5,1},{9,5},{13,9},{1,13},{6,2},{10,6},{... | collective-permute-start | bytes 233480 | tf_op jit(solution)/shard_map/ppermute | solution.py:300
  9.6 1.4 %copy-start = (f32[152,128]{1,0:T(8,128)}, f32[152,128]{1,0:T(8,128)S(1)}, u32[]{:S(2)}) copy-start(f32[152,128]{1,0:T(8,128)S(1)} %collective-permute-done.below) | copy-start | bytes 233476
  11.1 0.6 %copy-start.1 = (f32[152,128]{1,0:T(8,128)}, f32[152,128]{1,0:T(8,128)S(1)}, u32[]{:S(2)}) copy-start(f32[152,128]{1,0:T(8,128)S(1)} %collective-permute-done.1.above) | copy-start | bytes 233476
  13.5 7.5 %collective-permute-start.2 = (f32[472,128]{1,0:T(8,128)}, f32[472,128]{1,0:T(8,128)S(1)}, u32[]{:S(2)}, u32[]{:S(2)}) collective-permute-start(f32[472,128]{1,0:T(8,128)} %get-tuple-element.15), channel_id=1, source_target_pairs={{0,1},{1,2},{2,3},{4,5},{5,6},{6,7},{8,9},{9,10},{10,11},{12,13},{... | collective-permute-start | bytes 725000 | tf_op jit(solution)/shard_map/ppermute | solution.py:300
  17.7 7.7 %collective-permute-start.3 = (f32[472,128]{1,0:T(8,128)}, f32[472,128]{1,0:T(8,128)S(1)}, u32[]{:S(2)}, u32[]{:S(2)}) collective-permute-start(f32[472,128]{1,0:T(8,128)} %get-tuple-element.16), channel_id=1, source_target_pairs={{1,0},{2,1},{3,2},{5,4},{6,5},{7,6},{9,8},{10,9},{11,10},{13,12},{... | collective-permute-start | bytes 725000 | tf_op jit(solution)/shard_map/ppermute | solution.py:300
  21.1 4.3 %copy-start.2 = (f32[472,128]{1,0:T(8,128)}, f32[472,128]{1,0:T(8,128)S(1)}, u32[]{:S(2)}) copy-start(f32[472,128]{1,0:T(8,128)S(1)} %collective-permute-done.2.floor) | copy-start | bytes 724996
  25.3 0.7 %copy-start.3 = (f32[472,128]{1,0:T(8,128)}, f32[472,128]{1,0:T(8,128)S(1)}, u32[]{:S(2)}) copy-start(f32[472,128]{1,0:T(8,128)S(1)} %collective-permute-done.3.ceiling) | copy-start | bytes 724996
  29.0 3.2 %collective-permute-start.4 = (f32[96,128]{1,0:T(8,128)}, f32[96,128]{1,0:T(8,128)S(1)}, u32[]{:S(2)}, u32[]{:S(2)}) collective-permute-start(f32[96,128]{1,0:T(8,128)} %get-tuple-element.18.mine), channel_id=1, source_target_pairs={{0,16},{16,0},{1,17},{17,1},{2,18},{18,2},{3,19},{19,3},{4,20},{20... | collective-permute-start | bytes 147464 | tf_op jit(solution)/shard_map/ppermute | solution.py:332
  32.2 0.6 %copy-start.4 = (f32[96,128]{1,0:T(8,128)}, f32[96,128]{1,0:T(8,128)S(1)}, u32[]{:S(2)}) copy-start(f32[96,128]{1,0:T(8,128)S(1)} %collective-permute-done.4.left.right) | copy-start | bytes 147460

commit v2 on v1

--- a/solution.py
+++ b/solution.py
@@ -23,6 +23,7 @@
 ROWS = PAD + FLAT + PAD
 UNITS = (NZ + 2) * PITCH // 8
 
+PARAMS = pltpu.CompilerParams(vmem_limit_bytes=12 * 2**20)
 VMEM = pl.BlockSpec(memory_space=pltpu.VMEM)
 SMEM = pl.BlockSpec(memory_space=pltpu.SMEM)
 F32 = jnp.float32
@@ -111,7 +112,7 @@
     for z in range(NZ):
         aim = jnp.zeros((8, 128), F32)
         for y in range(NY):
-            aim = jnp.where(rows == y, table[index[y], z], aim)
+            aim = jnp.where(rows == y, table[z, index[y]], aim)
         post = relaxed([pops[q, z] for q in range(27)], sponge, aim)
         for q in range(27):
             own[pl.ds((q * NZ + z) * 8, 8), :] = post[q]
@@ -310,14 +311,16 @@
         out_shape=[shape(CHANNELS * NZ * 8, 128), shape(Y_ROWS, 128), shape(Y_ROWS, 128)],
         in_specs=[VMEM, VMEM, SMEM, SMEM],
         out_specs=[VMEM] * 3,
+        compiler_params=PARAMS,
         name="collide",
-    )(pops, solid, profile_table, profile_index)
+    )(pops, solid, profile_table.T, profile_index)
     below, above = both_ways("gy", yup, ydown, True)
     zup, zdown = pl.pallas_call(
         second_kernel,
         out_shape=[shape(Z_ROWS, 128)] * 2,
         in_specs=[VMEM] * 3,
         out_specs=[VMEM] * 2,
+        compiler_params=PARAMS,
         name="pack_z",
     )(own, below, above)
     floor, ceiling = both_ways("gz", zup, zdown, False)
@@ -326,6 +329,7 @@
         out_shape=[shape(CHANNELS, ROWS, 128), shape(FLAT, 128)],
         in_specs=[VMEM] * 5,
         out_specs=[VMEM] * 2,
+        compiler_params=PARAMS,
         name="pack_x",
     )(own, below, above, floor, ceiling)
     if lax.axis_size("gx") == 2:
@@ -346,6 +350,7 @@
             pltpu.VMEM((3, ROWS, 128), F32),
             pltpu.VMEM((128, 128), F32),
         ],
+        compiler_params=PARAMS,
         name="finish",
     )(full, pack, left, right)
 

time: 36.5 us -> 29.2 us (0.80)
  Pallas kernels: 10.3 us -> 3.47 us
  waiting for transfers between devices: 11.2 us -> 10.7 us
    pallas_call x1, Pallas kernels: 2.97 us -> 0.55 us  [shards(): pl.pallas_call(third_kernel, out_shape=[shape(CHANNELS, ROWS, 128), shape...]
    pallas_call x1, Pallas kernels: 1.87 us -> 0.05 us  [shards(): pl.pallas_call(second_kernel, out_shape=[shape(Z_ROWS, 128)] * 2, in_spec...]
    pallas_call x1, Pallas kernels: 3.43 us -> 2.07 us  [shards(): pl.pallas_call(last_kernel, out_shape=shape(27, NZ, NY, NX), in_specs=[VM...]
    pallas_call x1, Pallas kernels: 2.06 us -> 0.81 us  [shards(): pl.pallas_call(first_kernel, out_shape=[shape(CHANNELS * NZ * 8, 128), sh...]
    unnamed x11 -> x8, local copies, waits for them, and re-layouts: 3.26 us -> 3.07 us
where the time goes in v2:
time: 29.2 us; the launch traced here: 28.9 us
  starting transfers between devices  11.6 us (40%)
  waiting for transfers between devices  10.7 us (37%)
  Pallas kernels  3.47 us (12%)
  local copies, waits for them, and re-layouts  3.07 us (11%)
    ppermute x4, starting transfers between devices, both_ways(): return (lax.ppermute(ahead, axis, up), lax.ppermute(back, axis, down))  10.3 us
    ppermute x4, waiting for transfers between devices, both_ways(): return (lax.ppermute(ahead, axis, up), lax.ppermute(back, axis, down))  9.03 us
    unnamed x8, local copies, waits for them, and re-layouts  3.07 us
    pallas_call x1, Pallas kernels, shards(): pl.pallas_call(last_kernel, out_shape=shape(27, NZ, NY, NX), in_specs=[VM...  2.07 us
    ppermute x1, waiting for transfers between devices, shards(): left = lax.ppermute(pack, 'gx', [(0, 1), (1, 0)])  1.7 us
    ppermute x1, starting transfers between devices, shards(): left = lax.ppermute(pack, 'gx', [(0, 1), (1, 0)])  1.31 us
    pallas_call x1, Pallas kernels, shards(): pl.pallas_call(first_kernel, out_shape=[shape(CHANNELS * NZ * 8, 128), sh...  0.81 us
  transfers between devices with their start and end apart: 5, of which 5 were waited for; matrix products, arithmetic and copies ran while one was open for 0% of the time, Pallas kernels for 0%

profile of v2, /device:TPU:1, one launch (start us, length us, event | category | flops | bytes accessed | tf_op | source)
XLA Modules:
  0.0 28.9 jit_solution(4870086408092564441)
XLA Ops:
  0.0 0.0 copy-start
  0.0 1.0 %copy-done = f32[27,4,8,128]{3,2,1,0:T(8,128)S(1)} copy-done((f32[27,4,8,128]{3,2,1,0:T(8,128)S(1)}, f32[27,4,8,128]{3,2,1,0:T(8,128)}, u32[]{:S(2)}) %copy-start) | copy-done | bytes 442392
  1.0 0.0 copy-start.1
  1.0 0.7 %copy-done.1 = s32[4,8,128]{2,1,0:T(8,128)S(1)} copy-done((s32[4,8,128]{2,1,0:T(8,128)S(1)}, s32[4,8,128]{2,1,0:T(8,128)}, u32[]{:S(2)}) %copy-start.1) | copy-done | bytes 16408
  1.7 0.0 copy-start.2
  1.7 0.7 %copy-done.2 = f32[8,4]{0,1:T(4,128)S(1)} copy-done((f32[8,4]{0,1:T(4,128)S(1)}, f32[8,4]{0,1:T(4,128)}, u32[]{:S(2)}) %copy-start.2) | copy-done | bytes 152
  2.4 0.0 copy-start.3
  2.4 0.7 %copy-done.3 = s32[8]{0:T(128)S(1)} copy-done((s32[8]{0:T(128)S(1)}, s32[8]{0:T(128)}, u32[]{:S(2)}) %copy-start.3) | copy-done | bytes 56
  3.1 0.8 %collide.1 = (f32[928,128]{1,0:T(8,128)S(1)}, f32[152,128]{1,0:T(8,128)S(1)}, f32[152,128]{1,0:T(8,128)S(1)}) custom-call(f32[27,4,8,128]{3,2,1,0:T(8,128)S(1)} %copy-done, s32[4,8,128]{2,1,0:T(8,128)S(1)} %copy-done.1, f32[4,8]{1,0:T(4,128)S(1)} %bitcast.1, s32[8]{0:T(128)S(1)} %copy-done.3), custom_call_target="tpu_custom_call" | custom-call | tf_op jit(solution)/shard_map/collide/pallas_call | solution.py:309
  3.9 2.2 %collective-permute-start = (f32[152,128]{1,0:T(8,128)S(1)}, f32[152,128]{1,0:T(8,128)S(1)}, u32[]{:S(2)}, u32[]{:S(2)}) collective-permute-start(f32[152,128]{1,0:T(8,128)S(1)} %get-tuple-element.13), channel_id=1, source_target_pairs={{0,4},{4,8},{8,12},{12,0},{1,5},{5,9},{9,13},{13,1},{2,6},{6,10},{... | collective-permute-start | bytes 233480 | tf_op jit(solution)/shard_map/ppermute | solution.py:301
  6.1 2.1 %collective-permute-start.1 = (f32[152,128]{1,0:T(8,128)S(1)}, f32[152,128]{1,0:T(8,128)S(1)}, u32[]{:S(2)}, u32[]{:S(2)}) collective-permute-start(f32[152,128]{1,0:T(8,128)S(1)} %get-tuple-element.14), channel_id=1, source_target_pairs={{4,0},{8,4},{12,8},{0,12},{5,1},{9,5},{13,9},{1,13},{6,2},{10,6},{... | collective-permute-start | bytes 233480 | tf_op jit(solution)/shard_map/ppermute | solution.py:301
  8.2 1.8 %collective-permute-done.below = f32[152,128]{1,0:T(8,128)S(1)} collective-permute-done((f32[152,128]{1,0:T(8,128)S(1)}, f32[152,128]{1,0:T(8,128)S(1)}, u32[]{:S(2)}, u32[]{:S(2)}) %collective-permute-start) | collective-permute-done | bytes 77856 | tf_op jit(solution)/shard_map/ppermute | solution.py:301
  10.0 1.4 %collective-permute-done.1.above = f32[152,128]{1,0:T(8,128)S(1)} collective-permute-done((f32[152,128]{1,0:T(8,128)S(1)}, f32[152,128]{1,0:T(8,128)S(1)}, u32[]{:S(2)}, u32[]{:S(2)}) %collective-permute-start.1) | collective-permute-done | bytes 77856 | tf_op jit(solution)/shard_map/ppermute | solution.py:301
  11.4 4.1 %collective-permute-start.2 = (f32[472,128]{1,0:T(8,128)S(1)}, f32[472,128]{1,0:T(8,128)S(1)}, u32[]{:S(2)}, u32[]{:S(2)}) collective-permute-start(f32[472,128]{1,0:T(8,128)S(1)} %get-tuple-element.15), channel_id=1, source_target_pairs={{0,1},{1,2},{2,3},{4,5},{5,6},{6,7},{8,9},{9,10},{10,11},{12,13},{... | collective-permute-start | bytes 725000 | tf_op jit(solution)/shard_map/ppermute | solution.py:301
  15.6 1.9 %collective-permute-start.3 = (f32[472,128]{1,0:T(8,128)S(1)}, f32[472,128]{1,0:T(8,128)S(1)}, u32[]{:S(2)}, u32[]{:S(2)}) collective-permute-start(f32[472,128]{1,0:T(8,128)S(1)} %get-tuple-element.16), channel_id=1, source_target_pairs={{1,0},{2,1},{3,2},{5,4},{6,5},{7,6},{9,8},{10,9},{11,10},{13,12},{... | collective-permute-start | bytes 725000 | tf_op jit(solution)/shard_map/ppermute | solution.py:301
  17.5 1.1 %collective-permute-done.2.floor = f32[472,128]{1,0:T(8,128)S(1)} collective-permute-done((f32[472,128]{1,0:T(8,128)S(1)}, f32[472,128]{1,0:T(8,128)S(1)}, u32[]{:S(2)}, u32[]{:S(2)}) %collective-permute-start.2) | collective-permute-done | bytes 241696 | tf_op jit(solution)/shard_map/ppermute | solution.py:301
  18.6 4.6 %collective-permute-done.3.ceiling = f32[472,128]{1,0:T(8,128)S(1)} collective-permute-done((f32[472,128]{1,0:T(8,128)S(1)}, f32[472,128]{1,0:T(8,128)S(1)}, u32[]{:S(2)}, u32[]{:S(2)}) %collective-permute-start.3) | collective-permute-done | bytes 241696 | tf_op jit(solution)/shard_map/ppermute | solution.py:301
  23.3 0.5 %pack_x.1 = (f32[29,112,128]{2,1,0:T(8,128)S(1)}, f32[96,128]{1,0:T(8,128)S(1)}) custom-call(f32[928,128]{1,0:T(8,128)S(1)} %get-tuple-element.12.own, f32[152,128]{1,0:T(8,128)S(1)} %collective-permute-done.below, f32[152,128]{1,0:T(8,128)S(1)} %collective-permute-done.1.above, f32[472,128]{1,0:T(8,128)S(1)} %collective-permute-done.2.floor, ...), custom_call_target="tpu_custom_call" | custom-call | tf_op jit(solution)/shard_map/pack_x/pallas_call | solution.py:327
  23.8 1.3 %collective-permute-start.4 = (f32[96,128]{1,0:T(8,128)S(1)}, f32[96,128]{1,0:T(8,128)S(1)}, u32[]{:S(2)}, u32[]{:S(2)}) collective-permute-start(f32[96,128]{1,0:T(8,128)S(1)} %get-tuple-element.18.mine), channel_id=1, source_target_pairs={{0,16},{16,0},{1,17},{17,1},{2,18},{18,2},{3,19},{19,3},{4,20},{20... | collective-permute-start | bytes 147464 | tf_op jit(solution)/shard_map/ppermute | solution.py:336
  25.2 1.7 %collective-permute-done.4.left.right = f32[96,128]{1,0:T(8,128)S(1)} collective-permute-done((f32[96,128]{1,0:T(8,128)S(1)}, f32[96,128]{1,0:T(8,128)S(1)}, u32[]{:S(2)}, u32[]{:S(2)}) %collective-permute-start.4) | collective-permute-done | bytes 49184 | tf_op jit(solution)/shard_map/ppermute | solution.py:336
  26.9 2.1 %finish.1 = f32[27,4,8,128]{3,2,1,0:T(8,128)} custom-call(f32[29,112,128]{2,1,0:T(8,128)S(1)} %get-tuple-element.17.full, f32[96,128]{1,0:T(8,128)S(1)} %get-tuple-element.18.mine, f32[96,128]{1,0:T(8,128)S(1)} %collective-permute-done.4.left.right, f32[96,128]{1,0:T(8,128)S(1)} %collective-permute-done.4.left.right), custom_call_target="tpu_custom_call" | custom-call | tf_op jit(solution)/shard_map/finish/pallas_call | solution.py:340
  (1 shorter events, 0.0 us)
Async XLA Ops:
  0.0 1.0 %copy-start = (f32[27,4,8,128]{3,2,1,0:T(8,128)S(1)}, f32[27,4,8,128]{3,2,1,0:T(8,128)}, u32[]{:S(2)}) copy-start(f32[27,4,8,128]{3,2,1,0:T(8,128)} %pops.1) | copy-start | bytes 1327108
  1.0 0.7 %copy-start.1 = (s32[4,8,128]{2,1,0:T(8,128)S(1)}, s32[4,8,128]{2,1,0:T(8,128)}, u32[]{:S(2)}) copy-start(s32[4,8,128]{2,1,0:T(8,128)} %solid.1) | copy-start | bytes 49156
  1.7 0.7 %copy-start.2 = (f32[8,4]{0,1:T(4,128)S(1)}, f32[8,4]{0,1:T(4,128)}, u32[]{:S(2)}) copy-start(f32[8,4]{0,1:T(4,128)} %param.6) | copy-start | bytes 388
  2.4 0.7 %copy-start.3 = (s32[8]{0:T(128)S(1)}, s32[8]{0:T(128)}, u32[]{:S(2)}) copy-start(s32[8]{0:T(128)} %index.1) | copy-start | bytes 100
  3.9 6.1 %collective-permute-start = (f32[152,128]{1,0:T(8,128)S(1)}, f32[152,128]{1,0:T(8,128)S(1)}, u32[]{:S(2)}, u32[]{:S(2)}) collective-permute-start(f32[152,128]{1,0:T(8,128)S(1)} %get-tuple-element.13), channel_id=1, source_target_pairs={{0,4},{4,8},{8,12},{12,0},{1,5},{5,9},{9,13},{13,1},{2,6},{6,10},{... | collective-permute-start | bytes 233480 | tf_op jit(solution)/shard_map/ppermute | solution.py:301
  6.1 5.3 %collective-permute-start.1 = (f32[152,128]{1,0:T(8,128)S(1)}, f32[152,128]{1,0:T(8,128)S(1)}, u32[]{:S(2)}, u32[]{:S(2)}) collective-permute-start(f32[152,128]{1,0:T(8,128)S(1)} %get-tuple-element.14), channel_id=1, source_target_pairs={{4,0},{8,4},{12,8},{0,12},{5,1},{9,5},{13,9},{1,13},{6,2},{10,6},{... | collective-permute-start | bytes 233480 | tf_op jit(solution)/shard_map/ppermute | solution.py:301
  11.4 7.2 %collective-permute-start.2 = (f32[472,128]{1,0:T(8,128)S(1)}, f32[472,128]{1,0:T(8,128)S(1)}, u32[]{:S(2)}, u32[]{:S(2)}) collective-permute-start(f32[472,128]{1,0:T(8,128)S(1)} %get-tuple-element.15), channel_id=1, source_target_pairs={{0,1},{1,2},{2,3},{4,5},{5,6},{6,7},{8,9},{9,10},{10,11},{12,13},{... | collective-permute-start | bytes 725000 | tf_op jit(solution)/shard_map/ppermute | solution.py:301
  15.6 7.7 %collective-permute-start.3 = (f32[472,128]{1,0:T(8,128)S(1)}, f32[472,128]{1,0:T(8,128)S(1)}, u32[]{:S(2)}, u32[]{:S(2)}) collective-permute-start(f32[472,128]{1,0:T(8,128)S(1)} %get-tuple-element.16), channel_id=1, source_target_pairs={{1,0},{2,1},{3,2},{5,4},{6,5},{7,6},{9,8},{10,9},{11,10},{13,12},{... | collective-permute-start | bytes 725000 | tf_op jit(solution)/shard_map/ppermute | solution.py:301
  23.8 3.0 %collective-permute-start.4 = (f32[96,128]{1,0:T(8,128)S(1)}, f32[96,128]{1,0:T(8,128)S(1)}, u32[]{:S(2)}, u32[]{:S(2)}) collective-permute-start(f32[96,128]{1,0:T(8,128)S(1)} %get-tuple-element.18.mine), channel_id=1, source_target_pairs={{0,16},{16,0},{1,17},{17,1},{2,18},{18,2},{3,19},{19,3},{4,20},{20... | collective-permute-start | bytes 147464 | tf_op jit(solution)/shard_map/ppermute | solution.py:336

commit v3 on v2

--- a/solution.py
+++ b/solution.py
@@ -1,3 +1,5 @@
+import functools
+
 import jax
 import jax.numpy as jnp
 import numpy as np
@@ -25,7 +27,7 @@
 
 PARAMS = pltpu.CompilerParams(vmem_limit_bytes=12 * 2**20)
 VMEM = pl.BlockSpec(memory_space=pltpu.VMEM)
-SMEM = pl.BlockSpec(memory_space=pltpu.SMEM)
+HBM = pl.BlockSpec(memory_space=pltpu.HBM)
 F32 = jnp.float32
 
 Y_ROWS = (CHANNELS + 9) * NZ
@@ -106,7 +108,23 @@
     return lax.broadcasted_iota(jnp.int32, (8, 128), 0)
 
 
-def first_kernel(pops, solid, table, index, own, yup, ydown):
+def by_parity(axis, one, two, body):
+    even = lax.rem(lax.axis_index(axis), 2) == 0
+    pl.when(even)(lambda: body(one, two))
+    pl.when(jnp.logical_not(even))(lambda: body(two, one))
+
+
+def first_kernel(pops_at, solid_at, table_at, index_at, own, one, two, pops, solid, table, index, sems):
+    copies = [
+        pltpu.make_async_copy(source, target, sems.at[i])
+        for i, (source, target) in enumerate(
+            ((pops_at, pops), (solid_at, solid), (table_at, table), (index_at, index))
+        )
+    ]
+    for copy in copies:
+        copy.start()
+    for copy in copies:
+        copy.wait()
     lanes, rows = lane_ids(), row_ids()
     sponge = (lax.axis_index("gx") * NX + lanes) < SPONGE
     for z in range(NZ):
@@ -118,15 +136,30 @@
             own[pl.ds((q * NZ + z) * 8, 8), :] = post[q]
         own[pl.ds((WALL * NZ + z) * 8, 8), :] = solid[z].astype(F32)
         own[pl.ds((AIM * NZ + z) * 8, 8), :] = aim
-    for out, edge, second, part in ((yup, 7, 6, 6), (ydown, 0, 1, 0)):
-        out[pl.ds(0, CHANNELS * NZ), :] = own[pl.ds(edge, CHANNELS * NZ, stride=8), :]
-        for a in range(3):
-            out[pl.ds((CHANNELS + 3 * a) * NZ, 3 * NZ), :] = own[
-                pl.ds((9 * a + part) * NZ * 8 + second, 3 * NZ, stride=8), :
-            ]
-
-
-def second_kernel(own, below, above, zup, zdown):
+
+    def pack(yup, ydown):
+        for out, edge, second, part in ((yup, 7, 6, 6), (ydown, 0, 1, 0)):
+            out[pl.ds(0, CHANNELS * NZ), :] = own[pl.ds(edge, CHANNELS * NZ, stride=8), :]
+            for a in range(3):
+                out[pl.ds((CHANNELS + 3 * a) * NZ, 3 * NZ), :] = own[
+                    pl.ds((9 * a + part) * NZ * 8 + second, 3 * NZ, stride=8), :
+                ]
+
+    by_parity("gy", one, two, pack)
+
+
+def second_kernel(own, y_one, y_two, z_one, z_two):
+    by_parity(
+        "gy",
+        y_one,
+        y_two,
+        lambda above, below: by_parity(
+            "gz", z_one, z_two, lambda zup, zdown: pack_planes(own, below, above, zup, zdown)
+        ),
+    )
+
+
+def pack_planes(own, below, above, zup, zdown):
     for out, first, second, part in ((zup, NZ - 1, NZ - 2, 2), (zdown, 0, 1, 0)):
         for k in range(Z_BLOCKS):
             channel, z = (k, first) if k < CHANNELS else (9 * part + k - CHANNELS, second)
@@ -156,16 +189,10 @@
     return PAD + (z + 2) * PITCH
 
 
-def third_kernel(own, below, above, floor, ceiling, full, pack):
-    last = lax.axis_size("gz") - 1
-    here = lax.axis_index("gz")
+def add_rows(full, above, below):
     for c in range(CHANNELS):
-        for z in range(NZ):
-            full[c, pl.ds(plane_at(z) + 2, 8), :] = own[pl.ds((c * NZ + z) * 8, 8), :]
         for halo, near in ((below, 1), (above, PITCH - 2)):
             full[c, pl.ds(plane_at(0) + near, NZ, stride=PITCH), :] = halo[pl.ds(c * NZ, NZ), :]
-        full[c, pl.ds(plane_at(-1), PITCH), :] = floor[pl.ds(c * PITCH, PITCH), :]
-        full[c, pl.ds(plane_at(NZ), PITCH), :] = ceiling[pl.ds(c * PITCH, PITCH), :]
     for halo, far, group in ((below, 0, 6), (above, PITCH - 1, 0)):
         for k in range(9):
             q = 9 * (k // 3) + group + k % 3
@@ -173,10 +200,26 @@
                 pl.ds((CHANNELS + k) * NZ, NZ), :
             ]
         full[WALL, pl.ds(plane_at(0) + far, NZ, stride=PITCH), :] = halo[pl.ds(WALL * NZ, NZ), :]
+
+
+def add_planes(full, ceiling, floor):
+    for c in range(CHANNELS):
+        full[c, pl.ds(plane_at(-1), PITCH), :] = floor[pl.ds(c * PITCH, PITCH), :]
+        full[c, pl.ds(plane_at(NZ), PITCH), :] = ceiling[pl.ds(c * PITCH, PITCH), :]
     for halo, far, group in ((floor, -2, 18), (ceiling, NZ + 1, 0)):
         for k in range(10):
             q = group + k if k < 9 else WALL
             full[q, pl.ds(plane_at(far), PITCH), :] = halo[pl.ds((CHANNELS + k) * PITCH, PITCH), :]
+
+
+def third_kernel(own, y_one, y_two, z_one, z_two, full, pack):
+    last = lax.axis_size("gz") - 1
+    here = lax.axis_index("gz")
+    for c in range(CHANNELS):
+        for z in range(NZ):
+            full[c, pl.ds(plane_at(z) + 2, 8), :] = own[pl.ds((c * NZ + z) * 8, 8), :]
+    by_parity("gy", y_one, y_two, functools.partial(add_rows, full))
+    by_parity("gz", z_one, z_two, functools.partial(add_planes, full))
 
     @pl.when(here == 0)
     def _():
@@ -196,13 +239,16 @@
         pack[pl.ds(8 * t, 8), :] = packed
 
 
-def last_kernel(full, mine, left, right, out, post, west, east, turn, walls, back):
+def last_kernel(full, mine, x_one, x_two, out, post, west, east, turn, walls, back):
     here_x, size_x = lax.axis_index("gx"), lax.axis_size("gx")
     top = lax.axis_index("gz") == lax.axis_size("gz") - 1
     lanes, rows = lane_ids(), row_ids()
 
-    west[pl.ds(PAD, FLAT), :] = left[...]
-    east[pl.ds(PAD, FLAT), :] = right[...]
+    def spread(right, left):
+        west[pl.ds(PAD, FLAT), :] = left[...]
+        east[pl.ds(PAD, FLAT), :] = right[...]
+
+    by_parity("gx", x_one, x_two, spread)
 
     def edged(value, cx, channel, start):
         if cx == 0:
@@ -218,8 +264,8 @@
             start = PAD + 8 * t
             walls[cx + 1, pl.ds(start, 8), :] = edged(full[WALL, pl.ds(start, 8), :], cx, WALL, start)
 
-    for i, source in enumerate((mine, left, right)):
-        block = jnp.concatenate([source[...], jnp.zeros((128 - FLAT, 128), F32)], axis=0)
+    for i, source in enumerate((mine[...], west[pl.ds(PAD, FLAT), :], east[pl.ds(PAD, FLAT), :])):
+        block = jnp.concatenate([source, jnp.zeros((128 - FLAT, 128), F32)], axis=0)
         turn[i, pl.ds(PAD, 128), :] = block.T
     strip = []
     for c in range(CHANNELS):
@@ -294,11 +340,10 @@
             out[q, z] = jnp.where(solid, WEIGHT[q], value)
 
 
-def both_ways(axis, ahead, back, wrap):
+def swap(value, axis, turn, wrap):
     size = lax.axis_size(axis)
-    up = [(i, (i + 1) % size) for i in range(size if wrap else size - 1)]
-    down = [(j, i) for i, j in up]
-    return lax.ppermute(ahead, axis, up), lax.ppermute(back, axis, down)
+    pairs = [(i, (i + 1) % size) for i in range(turn, size if wrap else size - 1, 2)]
+    return lax.ppermute(value, axis, pairs + [(j, i) for i, j in pairs])
 
 
 def shape(*dims):
@@ -306,37 +351,43 @@
 
 
 def shards(pops, solid, profile_table, profile_index):
-    own, yup, ydown = pl.pallas_call(
+    own, y_one, y_two = pl.pallas_call(
         first_kernel,
         out_shape=[shape(CHANNELS * NZ * 8, 128), shape(Y_ROWS, 128), shape(Y_ROWS, 128)],
-        in_specs=[VMEM, VMEM, SMEM, SMEM],
+        in_specs=[HBM] * 4,
         out_specs=[VMEM] * 3,
+        scratch_shapes=[
+            pltpu.VMEM(pops.shape, F32),
+            pltpu.VMEM(solid.shape, jnp.int32),
+            pltpu.SMEM(profile_table.shape[::-1], F32),
+            pltpu.SMEM(profile_index.shape, jnp.int32),
+            pltpu.SemaphoreType.DMA((4,)),
+        ],
         compiler_params=PARAMS,
         name="collide",
     )(pops, solid, profile_table.T, profile_index)
-    below, above = both_ways("gy", yup, ydown, True)
-    zup, zdown = pl.pallas_call(
+    y_two = swap(y_two, "gy", 1, True)
+    y_one = swap(y_one, "gy", 0, True)
+    z_one, z_two = pl.pallas_call(
         second_kernel,
         out_shape=[shape(Z_ROWS, 128)] * 2,
         in_specs=[VMEM] * 3,
         out_specs=[VMEM] * 2,
         compiler_params=PARAMS,
         name="pack_z",
-    )(own, below, above)
-    floor, ceiling = both_ways("gz", zup, zdown, False)
-    full, pack = pl.pallas_call(
+    )(own, y_one, y_two)
+    z_two = swap(z_two, "gz", 1, False)
+    z_one = swap(z_one, "gz", 0, False)
+    full, mine = pl.pallas_call(
         third_kernel,
         out_shape=[shape(CHANNELS, ROWS, 128), shape(FLAT, 128)],
         in_specs=[VMEM] * 5,
         out_specs=[VMEM] * 2,
         compiler_params=PARAMS,
         name="pack_x",
-    )(own, below, above, floor, ceiling)
-    if lax.axis_size("gx") == 2:
-        left = lax.ppermute(pack, "gx", [(0, 1), (1, 0)])
-        right = left
-    else:
-        left, right = both_ways("gx", pack, pack, True)
+    )(own, y_one, y_two, z_one, z_two)
+    x_one = swap(mine, "gx", 0, True)
+    x_two = x_one if lax.axis_size("gx") == 2 else swap(mine, "gx", 1, True)
     return pl.pallas_call(
         last_kernel,
         out_shape=shape(27, NZ, NY, NX),
@@ -352,7 +403,7 @@
         ],
         compiler_params=PARAMS,
         name="finish",
-    )(full, pack, left, right)
+    )(full, mine, x_one, x_two)
 
 
 def solution(mesh):

time: 29.2 us -> 27.4 us (0.938)
  starting transfers between devices: 11.6 us -> 10.4 us
  waiting for transfers between devices: 10.7 us -> 9.74 us
  Pallas kernels: 3.47 us -> 3.82 us
    ppermute x5, starting transfers between devices: 11.6 us -> 10.4 us  [swap(): return lax.ppermute(value, axis, pairs + [(j, i) for i, j in pairs])]
    ppermute x5, waiting for transfers between devices: 10.7 us -> 9.74 us  [swap(): return lax.ppermute(value, axis, pairs + [(j, i) for i, j in pairs])]
    pallas_call x1, Pallas kernels: 0.81 us -> 1.14 us  [shards(): pl.pallas_call(first_kernel, out_shape=[shape(CHANNELS * NZ * 8, 128), sh...]
  transfers between devices with their start and end apart: 5 -> 5, of which waited for: 5 -> 3; matrix products, arithmetic and copies ran while one was open for 0% -> 0% of each run, Pallas kernels for 0% -> 0%
where the time goes in v3:
time: 27.4 us; the launch traced here: 27.1 us
  starting transfers between devices  10.4 us (38%)
  waiting for transfers between devices  9.74 us (36%)
  Pallas kernels  3.82 us (14%)
  local copies, waits for them, and re-layouts  3.07 us (11%)
    ppermute x5, starting transfers between devices, swap(): return lax.ppermute(value, axis, pairs + [(j, i) for i, j in pairs])  10.4 us
    ppermute x5, waiting for transfers between devices, swap(): return lax.ppermute(value, axis, pairs + [(j, i) for i, j in pairs])  9.74 us
    unnamed x8, local copies, waits for them, and re-layouts  3.07 us
    pallas_call x1, Pallas kernels, shards(): pl.pallas_call(last_kernel, out_shape=shape(27, NZ, NY, NX), in_specs=[VM...  2.08 us
    pallas_call x1, Pallas kernels, shards(): pl.pallas_call(first_kernel, out_shape=[shape(CHANNELS * NZ * 8, 128), sh...  1.14 us
    pallas_call x1, Pallas kernels, shards(): pl.pallas_call(third_kernel, out_shape=[shape(CHANNELS, ROWS, 128), shape...  0.56 us
  transfers between devices with their start and end apart: 5, of which 3 were waited for; matrix products, arithmetic and copies ran while one was open for 0% of the time, Pallas kernels for 0%

profile of v3, /device:TPU:1, one launch (start us, length us, event | category | flops | bytes accessed | tf_op | source)
XLA Modules:
  0.0 27.1 jit_solution(16839498383425327001)
XLA Ops:
  0.0 0.0 copy-start
  0.0 1.0 %copy-done = f32[27,4,8,128]{3,2,1,0:T(8,128)S(1)} copy-done((f32[27,4,8,128]{3,2,1,0:T(8,128)S(1)}, f32[27,4,8,128]{3,2,1,0:T(8,128)}, u32[]{:S(2)}) %copy-start) | copy-done | bytes 442392
  1.0 0.0 copy-start.1
  1.0 0.7 %copy-done.1 = s32[4,8,128]{2,1,0:T(8,128)S(1)} copy-done((s32[4,8,128]{2,1,0:T(8,128)S(1)}, s32[4,8,128]{2,1,0:T(8,128)}, u32[]{:S(2)}) %copy-start.1) | copy-done | bytes 16408
  1.7 0.0 copy-start.2
  1.7 0.7 %copy-done.2 = f32[8,4]{0,1:T(4,128)S(1)} copy-done((f32[8,4]{0,1:T(4,128)S(1)}, f32[8,4]{0,1:T(4,128)}, u32[]{:S(2)}) %copy-start.2) | copy-done | bytes 152
  2.4 0.0 copy-start.3
  2.4 0.7 %copy-done.3 = s32[8]{0:T(128)S(1)} copy-done((s32[8]{0:T(128)S(1)}, s32[8]{0:T(128)}, u32[]{:S(2)}) %copy-start.3) | copy-done | bytes 56
  3.1 1.1 %collide.1 = (f32[928,128]{1,0:T(8,128)S(1)}, f32[152,128]{1,0:T(8,128)S(1)}, f32[152,128]{1,0:T(8,128)S(1)}) custom-call(f32[27,4,8,128]{3,2,1,0:T(8,128)S(1)} %copy-done, s32[4,8,128]{2,1,0:T(8,128)S(1)} %copy-done.1, f32[4,8]{1,0:T(4,128)S(1)} %bitcast.1, s32[8]{0:T(128)S(1)} %copy-done.3), custom_call_target="tpu_custom_call" | custom-call | tf_op jit(solution)/shard_map/collide/pallas_call | solution.py:354
  4.2 2.2 %collective-permute-start = (f32[152,128]{1,0:T(8,128)S(1)}, f32[152,128]{1,0:T(8,128)S(1)}, u32[]{:S(2)}, u32[]{:S(2)}) collective-permute-start(f32[152,128]{1,0:T(8,128)S(1)} %get-tuple-element.13), channel_id=1, source_target_pairs={{0,4},{8,12},{4,0},{12,8},{1,5},{9,13},{5,1},{13,9},{2,6},{10,14},... | collective-permute-start | bytes 233480 | tf_op jit(solution)/shard_map/ppermute | solution.py:346
  6.4 2.2 %collective-permute-start.1 = (f32[152,128]{1,0:T(8,128)S(1)}, f32[152,128]{1,0:T(8,128)S(1)}, u32[]{:S(2)}, u32[]{:S(2)}) collective-permute-start(f32[152,128]{1,0:T(8,128)S(1)} %get-tuple-element.14), channel_id=1, source_target_pairs={{4,8},{12,0},{8,4},{0,12},{5,9},{13,1},{9,5},{1,13},{6,10},{14,2},... | collective-permute-start | bytes 233480 | tf_op jit(solution)/shard_map/ppermute | solution.py:346
  8.6 0.0 collective-permute-done.y_one
  8.6 3.6 %collective-permute-done.1.y_two = f32[152,128]{1,0:T(8,128)S(1)} collective-permute-done((f32[152,128]{1,0:T(8,128)S(1)}, f32[152,128]{1,0:T(8,128)S(1)}, u32[]{:S(2)}, u32[]{:S(2)}) %collective-permute-start.1) | collective-permute-done | bytes 77856 | tf_op jit(solution)/shard_map/ppermute | solution.py:346
  12.3 1.7 %collective-permute-start.2 = (f32[472,128]{1,0:T(8,128)S(1)}, f32[472,128]{1,0:T(8,128)S(1)}, u32[]{:S(2)}, u32[]{:S(2)}) collective-permute-start(f32[472,128]{1,0:T(8,128)S(1)} %get-tuple-element.15), channel_id=1, source_target_pairs={{0,1},{2,3},{1,0},{3,2},{4,5},{6,7},{5,4},{7,6},{8,9},{10,11},{9,8... | collective-permute-start | bytes 725000 | tf_op jit(solution)/shard_map/ppermute | solution.py:346
  14.0 3.0 %collective-permute-start.3 = (f32[472,128]{1,0:T(8,128)S(1)}, f32[472,128]{1,0:T(8,128)S(1)}, u32[]{:S(2)}, u32[]{:S(2)}) collective-permute-start(f32[472,128]{1,0:T(8,128)S(1)} %get-tuple-element.16), channel_id=1, source_target_pairs={{1,2},{2,1},{5,6},{6,5},{9,10},{10,9},{13,14},{14,13},{17,18},{18,... | collective-permute-start | bytes 725000 | tf_op jit(solution)/shard_map/ppermute | solution.py:346
  17.0 0.0 collective-permute-done.2.z_one
  17.0 4.4 %collective-permute-done.3.z_two = f32[472,128]{1,0:T(8,128)S(1)} collective-permute-done((f32[472,128]{1,0:T(8,128)S(1)}, f32[472,128]{1,0:T(8,128)S(1)}, u32[]{:S(2)}, u32[]{:S(2)}) %collective-permute-start.3) | collective-permute-done | bytes 241696 | tf_op jit(solution)/shard_map/ppermute | solution.py:346
  21.4 0.6 %pack_x.1 = (f32[29,112,128]{2,1,0:T(8,128)S(1)}, f32[96,128]{1,0:T(8,128)S(1)}) custom-call(f32[928,128]{1,0:T(8,128)S(1)} %get-tuple-element.12.own, f32[152,128]{1,0:T(8,128)S(1)} %collective-permute-done.y_one, f32[152,128]{1,0:T(8,128)S(1)} %collective-permute-done.1.y_two, f32[472,128]{1,0:T(8,128)S(1)} %collective-permute-done.2.z_one, ...), custom_call_target="tpu_custom_call" | custom-call | tf_op jit(solution)/shard_map/pack_x/pallas_call | solution.py:381
  22.0 1.3 %collective-permute-start.4 = (f32[96,128]{1,0:T(8,128)S(1)}, f32[96,128]{1,0:T(8,128)S(1)}, u32[]{:S(2)}, u32[]{:S(2)}) collective-permute-start(f32[96,128]{1,0:T(8,128)S(1)} %get-tuple-element.18.mine), channel_id=1, source_target_pairs={{0,16},{16,0},{1,17},{17,1},{2,18},{18,2},{3,19},{19,3},{4,20},{20... | collective-permute-start | bytes 147464 | tf_op jit(solution)/shard_map/ppermute | solution.py:346
  23.3 1.7 %collective-permute-done.4.x_one.x_two = f32[96,128]{1,0:T(8,128)S(1)} collective-permute-done((f32[96,128]{1,0:T(8,128)S(1)}, f32[96,128]{1,0:T(8,128)S(1)}, u32[]{:S(2)}, u32[]{:S(2)}) %collective-permute-start.4) | collective-permute-done | bytes 49184 | tf_op jit(solution)/shard_map/ppermute | solution.py:346
  25.0 2.1 %finish.1 = f32[27,4,8,128]{3,2,1,0:T(8,128)} custom-call(f32[29,112,128]{2,1,0:T(8,128)S(1)} %get-tuple-element.17.full, f32[96,128]{1,0:T(8,128)S(1)} %get-tuple-element.18.mine, f32[96,128]{1,0:T(8,128)S(1)} %collective-permute-done.4.x_one.x_two, f32[96,128]{1,0:T(8,128)S(1)} %collective-permute-done.4.x_one.x_two), custom_call_target="tpu_custom_call" | custom-call | tf_op jit(solution)/shard_map/finish/pallas_call | solution.py:391
  (1 shorter events, 0.0 us)
Async XLA Ops:
  0.0 1.0 %copy-start = (f32[27,4,8,128]{3,2,1,0:T(8,128)S(1)}, f32[27,4,8,128]{3,2,1,0:T(8,128)}, u32[]{:S(2)}) copy-start(f32[27,4,8,128]{3,2,1,0:T(8,128)} %pops_at.1) | copy-start | bytes 1327108
  1.0 0.7 %copy-start.1 = (s32[4,8,128]{2,1,0:T(8,128)S(1)}, s32[4,8,128]{2,1,0:T(8,128)}, u32[]{:S(2)}) copy-start(s32[4,8,128]{2,1,0:T(8,128)} %solid_at.1) | copy-start | bytes 49156
  1.7 0.7 %copy-start.2 = (f32[8,4]{0,1:T(4,128)S(1)}, f32[8,4]{0,1:T(4,128)}, u32[]{:S(2)}) copy-start(f32[8,4]{0,1:T(4,128)} %param.6) | copy-start | bytes 388
  2.4 0.7 %copy-start.3 = (s32[8]{0:T(128)S(1)}, s32[8]{0:T(128)}, u32[]{:S(2)}) copy-start(s32[8]{0:T(128)} %index_at.1) | copy-start | bytes 100
  4.2 4.4 %collective-permute-start = (f32[152,128]{1,0:T(8,128)S(1)}, f32[152,128]{1,0:T(8,128)S(1)}, u32[]{:S(2)}, u32[]{:S(2)}) collective-permute-start(f32[152,128]{1,0:T(8,128)S(1)} %get-tuple-element.13), channel_id=1, source_target_pairs={{0,4},{8,12},{4,0},{12,8},{1,5},{9,13},{5,1},{13,9},{2,6},{10,14},... | collective-permute-start | bytes 233480 | tf_op jit(solution)/shard_map/ppermute | solution.py:346
  6.4 5.8 %collective-permute-start.1 = (f32[152,128]{1,0:T(8,128)S(1)}, f32[152,128]{1,0:T(8,128)S(1)}, u32[]{:S(2)}, u32[]{:S(2)}) collective-permute-start(f32[152,128]{1,0:T(8,128)S(1)} %get-tuple-element.14), channel_id=1, source_target_pairs={{4,8},{12,0},{8,4},{0,12},{5,9},{13,1},{9,5},{1,13},{6,10},{14,2},... | collective-permute-start | bytes 233480 | tf_op jit(solution)/shard_map/ppermute | solution.py:346
  12.3 4.7 %collective-permute-start.2 = (f32[472,128]{1,0:T(8,128)S(1)}, f32[472,128]{1,0:T(8,128)S(1)}, u32[]{:S(2)}, u32[]{:S(2)}) collective-permute-start(f32[472,128]{1,0:T(8,128)S(1)} %get-tuple-element.15), channel_id=1, source_target_pairs={{0,1},{2,3},{1,0},{3,2},{4,5},{6,7},{5,4},{7,6},{8,9},{10,11},{9,8... | collective-permute-start | bytes 725000 | tf_op jit(solution)/shard_map/ppermute | solution.py:346
  14.0 7.5 %collective-permute-start.3 = (f32[472,128]{1,0:T(8,128)S(1)}, f32[472,128]{1,0:T(8,128)S(1)}, u32[]{:S(2)}, u32[]{:S(2)}) collective-permute-start(f32[472,128]{1,0:T(8,128)S(1)} %get-tuple-element.16), channel_id=1, source_target_pairs={{1,2},{2,1},{5,6},{6,5},{9,10},{10,9},{13,14},{14,13},{17,18},{18,... | collective-permute-start | bytes 725000 | tf_op jit(solution)/shard_map/ppermute | solution.py:346
  22.0 3.0 %collective-permute-start.4 = (f32[96,128]{1,0:T(8,128)S(1)}, f32[96,128]{1,0:T(8,128)S(1)}, u32[]{:S(2)}, u32[]{:S(2)}) collective-permute-start(f32[96,128]{1,0:T(8,128)S(1)} %get-tuple-element.18.mine), channel_id=1, source_target_pairs={{0,16},{16,0},{1,17},{17,1},{2,18},{18,2},{3,19},{19,3},{4,20},{20... | collective-permute-start | bytes 147464 | tf_op jit(solution)/shard_map/ppermute | solution.py:346

commit v4 on v3

--- a/solution.py
+++ b/solution.py
@@ -32,7 +32,9 @@
 
 Y_ROWS = (CHANNELS + 9) * NZ
 Z_BLOCKS = CHANNELS + 10
-Z_ROWS = -(-Z_BLOCKS * PITCH // 8) * 8
+Z_PITCH = NY + 2
+Z_FAR = Z_BLOCKS * Z_PITCH
+Z_ROWS = -(-(Z_FAR + 2 * 12) // 8) * 8
 
 
 def relaxed(f, sponge, aim):
@@ -148,7 +150,7 @@
     by_parity("gy", one, two, pack)
 
 
-def second_kernel(own, y_one, y_two, z_one, z_two):
+def second_kernel(own, y_one, y_two, z_two, z_one):
     by_parity(
         "gy",
         y_one,
@@ -165,24 +167,22 @@
             channel, z = (k, first) if k < CHANNELS else (9 * part + k - CHANNELS, second)
             if k == Z_BLOCKS - 1:
                 channel = WALL
-            out[pl.ds(k * PITCH + 2, 8), :] = own[pl.ds((channel * NZ + z) * 8, 8), :]
-        for halo, near, far, group in ((below, 1, 0, 6), (above, PITCH - 2, PITCH - 1, 0)):
-            out[pl.ds(near, CHANNELS, stride=PITCH), :] = halo[pl.ds(first, CHANNELS, stride=NZ), :]
-            out[pl.ds(CHANNELS * PITCH + near, 9, stride=PITCH), :] = halo[
+            out[pl.ds(k * Z_PITCH + 1, 8), :] = own[pl.ds((channel * NZ + z) * 8, 8), :]
+        for side, (halo, near, group) in enumerate(((below, 0, 2), (above, Z_PITCH - 1, 0))):
+            out[pl.ds(near, CHANNELS, stride=Z_PITCH), :] = halo[
+                pl.ds(first, CHANNELS, stride=NZ), :
+            ]
+            out[pl.ds(CHANNELS * Z_PITCH + near, 9, stride=Z_PITCH), :] = halo[
                 pl.ds(9 * part * NZ + second, 9, stride=NZ), :
             ]
-            wall_first = halo[pl.ds(WALL * NZ + first, 1), :]
-            wall_second = halo[pl.ds(WALL * NZ + second, 1), :]
-            out[pl.ds((Z_BLOCKS - 1) * PITCH + near, 1), :] = wall_second
-            for a in range(3):
-                out[pl.ds((9 * a + group) * PITCH + far, 3, stride=PITCH), :] = halo[
-                    pl.ds((CHANNELS + 3 * a) * NZ + first, 3, stride=NZ), :
-                ]
-            out[pl.ds((CHANNELS + group) * PITCH + far, 3, stride=PITCH), :] = halo[
+            out[pl.ds((Z_BLOCKS - 1) * Z_PITCH + near, 1), :] = halo[
+                pl.ds(WALL * NZ + second, 1), :
+            ]
+            far = Z_FAR + 12 * side
+            out[pl.ds(far, 9), :] = halo[pl.ds(CHANNELS * NZ + first, 9, stride=NZ), :]
+            out[pl.ds(far + 9, 3), :] = halo[
                 pl.ds((CHANNELS + 3 * part) * NZ + second, 3, stride=NZ), :
             ]
-            out[pl.ds(WALL * PITCH + far, 1), :] = wall_first
-            out[pl.ds((Z_BLOCKS - 1) * PITCH + far, 1), :] = wall_second
 
 
 def plane_at(z):
@@ -203,16 +203,25 @@
 
 
 def add_planes(full, ceiling, floor):
-    for c in range(CHANNELS):
-        full[c, pl.ds(plane_at(-1), PITCH), :] = floor[pl.ds(c * PITCH, PITCH), :]
-        full[c, pl.ds(plane_at(NZ), PITCH), :] = ceiling[pl.ds(c * PITCH, PITCH), :]
-    for halo, far, group in ((floor, -2, 18), (ceiling, NZ + 1, 0)):
-        for k in range(10):
-            q = group + k if k < 9 else WALL
-            full[q, pl.ds(plane_at(far), PITCH), :] = halo[pl.ds((CHANNELS + k) * PITCH, PITCH), :]
-
-
-def third_kernel(own, y_one, y_two, z_one, z_two, full, pack):
+    for halo, near, far, part in ((floor, -1, -2, 2), (ceiling, NZ, NZ + 1, 0)):
+        blocks = [(c, near) for c in range(CHANNELS)]
+        blocks += [(9 * part + k, far) for k in range(9)] + [(WALL, far)]
+        for k, (c, z) in enumerate(blocks):
+            full[c, pl.ds(plane_at(z) + 1, Z_PITCH), :] = halo[pl.ds(k * Z_PITCH, Z_PITCH), :]
+        for side, (row, group) in enumerate(((0, 2), (PITCH - 1, 0))):
+            start = Z_FAR + 12 * side
+            for k in range(9):
+                q = 9 * (k // 3) + 3 * group + k % 3
+                full[q, pl.ds(plane_at(near) + row, 1), :] = halo[pl.ds(start + k, 1), :]
+            for k in range(3):
+                q = 9 * part + 3 * group + k
+                full[q, pl.ds(plane_at(far) + row, 1), :] = halo[pl.ds(start + 9 + k, 1), :]
+            first = 0 if side == 0 else Z_PITCH - 1
+            for k, z in ((WALL, near), (Z_BLOCKS - 1, far)):
+                full[WALL, pl.ds(plane_at(z) + row, 1), :] = halo[pl.ds(k * Z_PITCH + first, 1), :]
+
+
+def third_kernel(own, y_one, y_two, z_two, z_one, full, pack):
     last = lax.axis_size("gz") - 1
     here = lax.axis_index("gz")
     for c in range(CHANNELS):
@@ -365,10 +374,10 @@
         ],
         compiler_params=PARAMS,
         name="collide",
-    )(pops, solid, profile_table.T, profile_index)
+    )(*(pltpu.with_memory_space_constraint(a, pltpu.HBM) for a in (pops, solid, profile_table.T, profile_index)))
     y_two = swap(y_two, "gy", 1, True)
     y_one = swap(y_one, "gy", 0, True)
-    z_one, z_two = pl.pallas_call(
+    z_two, z_one = pl.pallas_call(
         second_kernel,
         out_shape=[shape(Z_ROWS, 128)] * 2,
         in_specs=[VMEM] * 3,
@@ -385,7 +394,7 @@
         out_specs=[VMEM] * 2,
         compiler_params=PARAMS,
         name="pack_x",
-    )(own, y_one, y_two, z_one, z_two)
+    )(own, y_one, y_two, z_two, z_one)
     x_one = swap(mine, "gx", 0, True)
     x_two = x_one if lax.axis_size("gx") == 2 else swap(mine, "gx", 1, True)
     return pl.pallas_call(

time: 27.4 us -> 23.6 us (0.86)
  local copies, waits for them, and re-layouts: 3.07 us -> 0 us
  waiting for transfers between devices: 9.74 us -> 8.75 us
    unnamed x8 -> x0, local copies, waits for them, and re-layouts: 3.07 us -> none
    ppermute x5, waiting for transfers between devices: 9.74 us -> 8.75 us  [swap(): return lax.ppermute(value, axis, pairs + [(j, i) for i, j in pairs])]
where the time goes in v4:
time: 23.6 us; the launch traced here: 23.1 us
  starting transfers between devices  10.4 us (44%)
  waiting for transfers between devices  8.75 us (37%)
  Pallas kernels  3.92 us (17%)
    ppermute x5, starting transfers between devices, swap(): return lax.ppermute(value, axis, pairs + [(j, i) for i, j in pairs])  10.4 us
    ppermute x5, waiting for transfers between devices, swap(): return lax.ppermute(value, axis, pairs + [(j, i) for i, j in pairs])  8.75 us
    pallas_call x1, Pallas kernels, shards(): pl.pallas_call(last_kernel, out_shape=shape(27, NZ, NY, NX), in_specs=[VM...  1.97 us
    pallas_call x1, Pallas kernels, shards(): pl.pallas_call(first_kernel, out_shape=[shape(CHANNELS * NZ * 8, 128), sh...  1.32 us
    pallas_call x1, Pallas kernels, shards(): pl.pallas_call(third_kernel, out_shape=[shape(CHANNELS, ROWS, 128), shape...  0.58 us
  transfers between devices with their start and end apart: 5, of which 3 were waited for; matrix products, arithmetic and copies ran while one was open for 0% of the time, Pallas kernels for 0%

profile of v4, /device:TPU:1, one launch (start us, length us, event | category | flops | bytes accessed | tf_op | source)
XLA Modules:
  0.0 23.1 jit_solution(4439728190101939157)
XLA Ops:
  0.0 1.3 %collide.1 = (f32[928,128]{1,0:T(8,128)S(1)}, f32[152,128]{1,0:T(8,128)S(1)}, f32[152,128]{1,0:T(8,128)S(1)}) custom-call(f32[27,4,8,128]{3,2,1,0:T(8,128)} %pops_at.1, s32[4,8,128]{2,1,0:T(8,128)} %solid_at.1, f32[4,8]{1,0:T(4,128)} %bitcast.1, s32[8]{0:T(128)} %index_at.1), custom_call_target="tpu_custom_call" | custom-call | tf_op jit(solution)/shard_map/collide/pallas_call | solution.py:363
  1.3 2.2 %collective-permute-start = (f32[152,128]{1,0:T(8,128)S(1)}, f32[152,128]{1,0:T(8,128)S(1)}, u32[]{:S(2)}, u32[]{:S(2)}) collective-permute-start(f32[152,128]{1,0:T(8,128)S(1)} %get-tuple-element.13), channel_id=1, source_target_pairs={{0,4},{8,12},{4,0},{12,8},{1,5},{9,13},{5,1},{13,9},{2,6},{10,14},... | collective-permute-start | bytes 233480 | tf_op jit(solution)/shard_map/ppermute | solution.py:355
  3.5 2.2 %collective-permute-start.1 = (f32[152,128]{1,0:T(8,128)S(1)}, f32[152,128]{1,0:T(8,128)S(1)}, u32[]{:S(2)}, u32[]{:S(2)}) collective-permute-start(f32[152,128]{1,0:T(8,128)S(1)} %get-tuple-element.14), channel_id=1, source_target_pairs={{4,8},{12,0},{8,4},{0,12},{5,9},{13,1},{9,5},{1,13},{6,10},{14,2},... | collective-permute-start | bytes 233480 | tf_op jit(solution)/shard_map/ppermute | solution.py:355
  5.7 0.0 collective-permute-done.y_one
  5.7 3.6 %collective-permute-done.1.y_two = f32[152,128]{1,0:T(8,128)S(1)} collective-permute-done((f32[152,128]{1,0:T(8,128)S(1)}, f32[152,128]{1,0:T(8,128)S(1)}, u32[]{:S(2)}, u32[]{:S(2)}) %collective-permute-start.1) | collective-permute-done | bytes 77856 | tf_op jit(solution)/shard_map/ppermute | solution.py:355
  9.4 4.7 %collective-permute-start.2 = (f32[416,128]{1,0:T(8,128)S(1)}, f32[416,128]{1,0:T(8,128)S(1)}, u32[]{:S(2)}, u32[]{:S(2)}) collective-permute-start(f32[416,128]{1,0:T(8,128)S(1)} %get-tuple-element.15), channel_id=1, source_target_pairs={{1,2},{2,1},{5,6},{6,5},{9,10},{10,9},{13,14},{14,13},{17,18},{18,... | collective-permute-start | bytes 638984 | tf_op jit(solution)/shard_map/ppermute | solution.py:355
  14.0 0.1 collective-permute-start.3
  14.1 3.4 %collective-permute-done.2.z_two = f32[416,128]{1,0:T(8,128)S(1)} collective-permute-done((f32[416,128]{1,0:T(8,128)S(1)}, f32[416,128]{1,0:T(8,128)S(1)}, u32[]{:S(2)}, u32[]{:S(2)}) %collective-permute-start.2) | collective-permute-done | bytes 213024 | tf_op jit(solution)/shard_map/ppermute | solution.py:355
  17.6 0.0 collective-permute-done.3.z_one
  17.6 0.6 %pack_x.1 = (f32[29,112,128]{2,1,0:T(8,128)S(1)}, f32[96,128]{1,0:T(8,128)S(1)}) custom-call(f32[928,128]{1,0:T(8,128)S(1)} %get-tuple-element.12.own, f32[152,128]{1,0:T(8,128)S(1)} %collective-permute-done.y_one, f32[152,128]{1,0:T(8,128)S(1)} %collective-permute-done.1.y_two, f32[416,128]{1,0:T(8,128)S(1)} %collective-permute-done.2.z_two, ...), custom_call_target="tpu_custom_call" | custom-call | tf_op jit(solution)/shard_map/pack_x/pallas_call | solution.py:390
  18.2 1.3 %collective-permute-start.4 = (f32[96,128]{1,0:T(8,128)S(1)}, f32[96,128]{1,0:T(8,128)S(1)}, u32[]{:S(2)}, u32[]{:S(2)}) collective-permute-start(f32[96,128]{1,0:T(8,128)S(1)} %get-tuple-element.18.mine), channel_id=1, source_target_pairs={{0,16},{16,0},{1,17},{17,1},{2,18},{18,2},{3,19},{19,3},{4,20},{20... | collective-permute-start | bytes 147464 | tf_op jit(solution)/shard_map/ppermute | solution.py:355
  19.5 1.7 %collective-permute-done.4.x_one.x_two = f32[96,128]{1,0:T(8,128)S(1)} collective-permute-done((f32[96,128]{1,0:T(8,128)S(1)}, f32[96,128]{1,0:T(8,128)S(1)}, u32[]{:S(2)}, u32[]{:S(2)}) %collective-permute-start.4) | collective-permute-done | bytes 49184 | tf_op jit(solution)/shard_map/ppermute | solution.py:355
  21.2 2.0 %finish.1 = f32[27,4,8,128]{3,2,1,0:T(8,128)} custom-call(f32[29,112,128]{2,1,0:T(8,128)S(1)} %get-tuple-element.17.full, f32[96,128]{1,0:T(8,128)S(1)} %get-tuple-element.18.mine, f32[96,128]{1,0:T(8,128)S(1)} %collective-permute-done.4.x_one.x_two, f32[96,128]{1,0:T(8,128)S(1)} %collective-permute-done.4.x_one.x_two), custom_call_target="tpu_custom_call" | custom-call | tf_op jit(solution)/shard_map/finish/pallas_call | solution.py:400
  (1 shorter events, 0.0 us)
Async XLA Ops:
  1.3 4.4 %collective-permute-start = (f32[152,128]{1,0:T(8,128)S(1)}, f32[152,128]{1,0:T(8,128)S(1)}, u32[]{:S(2)}, u32[]{:S(2)}) collective-permute-start(f32[152,128]{1,0:T(8,128)S(1)} %get-tuple-element.13), channel_id=1, source_target_pairs={{0,4},{8,12},{4,0},{12,8},{1,5},{9,13},{5,1},{13,9},{2,6},{10,14},... | collective-permute-start | bytes 233480 | tf_op jit(solution)/shard_map/ppermute | solution.py:355
  3.5 5.8 %collective-permute-start.1 = (f32[152,128]{1,0:T(8,128)S(1)}, f32[152,128]{1,0:T(8,128)S(1)}, u32[]{:S(2)}, u32[]{:S(2)}) collective-permute-start(f32[152,128]{1,0:T(8,128)S(1)} %get-tuple-element.14), channel_id=1, source_target_pairs={{4,8},{12,0},{8,4},{0,12},{5,9},{13,1},{9,5},{1,13},{6,10},{14,2},... | collective-permute-start | bytes 233480 | tf_op jit(solution)/shard_map/ppermute | solution.py:355
  9.4 8.2 %collective-permute-start.2 = (f32[416,128]{1,0:T(8,128)S(1)}, f32[416,128]{1,0:T(8,128)S(1)}, u32[]{:S(2)}, u32[]{:S(2)}) collective-permute-start(f32[416,128]{1,0:T(8,128)S(1)} %get-tuple-element.15), channel_id=1, source_target_pairs={{1,2},{2,1},{5,6},{6,5},{9,10},{10,9},{13,14},{14,13},{17,18},{18,... | collective-permute-start | bytes 638984 | tf_op jit(solution)/shard_map/ppermute | solution.py:355
  14.0 3.5 %collective-permute-start.3 = (f32[416,128]{1,0:T(8,128)S(1)}, f32[416,128]{1,0:T(8,128)S(1)}, u32[]{:S(2)}, u32[]{:S(2)}) collective-permute-start(f32[416,128]{1,0:T(8,128)S(1)} %get-tuple-element.16), channel_id=1, source_target_pairs={{0,1},{2,3},{1,0},{3,2},{4,5},{6,7},{5,4},{7,6},{8,9},{10,11},{9,8... | collective-permute-start | bytes 638984 | tf_op jit(solution)/shard_map/ppermute | solution.py:355
  18.2 3.0 %collective-permute-start.4 = (f32[96,128]{1,0:T(8,128)S(1)}, f32[96,128]{1,0:T(8,128)S(1)}, u32[]{:S(2)}, u32[]{:S(2)}) collective-permute-start(f32[96,128]{1,0:T(8,128)S(1)} %get-tuple-element.18.mine), channel_id=1, source_target_pairs={{0,16},{16,0},{1,17},{17,1},{2,18},{18,2},{3,19},{19,3},{4,20},{20... | collective-permute-start | bytes 147464 | tf_op jit(solution)/shard_map/ppermute | solution.py:355

commit v5 on v4

--- a/solution.py
+++ b/solution.py
@@ -35,6 +35,8 @@
 Z_PITCH = NY + 2
 Z_FAR = Z_BLOCKS * Z_PITCH
 Z_ROWS = -(-(Z_FAR + 2 * 12) // 8) * 8
+
+X_ROWS = 2 * (WALL + 1)
 
 
 def relaxed(f, sponge, aim):
@@ -221,7 +223,7 @@
                 full[WALL, pl.ds(plane_at(z) + row, 1), :] = halo[pl.ds(k * Z_PITCH + first, 1), :]
 
 
-def third_kernel(own, y_one, y_two, z_two, z_one, full, pack):
+def third_kernel(own, y_one, y_two, z_two, z_one, full, columns, message, pack):
     last = lax.axis_size("gz") - 1
     here = lax.axis_index("gz")
     for c in range(CHANNELS):
@@ -240,49 +242,92 @@
             full[q, pl.ds(plane_at(NZ), PITCH), :] = full[q + 18, pl.ds(plane_at(NZ - 1), PITCH), :]
 
     slot = lane_ids() // 4
+    pack[pl.ds(FLAT, 128 - FLAT), :] = jnp.zeros((128 - FLAT, 128), F32)
     for t in range(FLAT // 8):
         packed = jnp.zeros((8, 128), F32)
         for c in range(CHANNELS):
             moved = pltpu.roll(full[c, pl.ds(PAD + 8 * t, 8), :], (4 * c + 2) % 128, 1)
             packed = jnp.where(slot == c, moved, packed)
         pack[pl.ds(8 * t, 8), :] = packed
-
-
-def last_kernel(full, mine, x_one, x_two, out, post, west, east, turn, walls, back):
+    columns[pl.ds(PAD, 128), :] = pack[...].T
+
+    def row(c, i, count):
+        return columns[pl.ds(PAD + 4 * c + i, count), :]
+
+    def returned(q, near, far):
+        cx, cy, cz = VEL[q]
+        step = (-PITCH * cz - cy) % 128
+        value = row(26 - q, near, 8)
+        value = pltpu.roll(value, step, 1) if step else value
+        return jnp.where(row(WALL, far, 8) != 0.0, value, row(q, far, 8))[:1]
+
+    for c in range(WALL + 1):
+        cx = VEL[c][0] if c < 27 else 0
+        if cx == 0:
+            message[pl.ds(2 * c, 2), :] = row(c, 1, 2)
+        elif cx > 0:
+            message[pl.ds(2 * c, 1), :] = returned(c, 1, 0)
+            message[pl.ds(2 * c + 1, 1), :] = row(c, 1, 1)
+        else:
+            message[pl.ds(2 * c, 1), :] = row(c, 2, 1)
+            message[pl.ds(2 * c + 1, 1), :] = returned(c, 2, 3)
+
+
+def block_kernel(full, post, walls):
+    top = lax.axis_index("gz") == lax.axis_size("gz") - 1
+    sponge = (lax.axis_index("gx") * NX + lane_ids()) < SPONGE
+    for t in range(ROWS // 8):
+        rows = pl.ds(8 * t, 8)
+        flags = full[WALL, rows, :]
+        for cx in (-1, 0, 1):
+            walls[cx + 1, rows, :] = pltpu.roll(flags, cx % 128, 1) if cx else flags
+    for u in range(UNITS):
+        cell = PAD + PITCH + 8 * u
+        f = []
+        solid = walls[1, pl.ds(cell, 8), :] != 0.0
+        for q in range(27):
+            cx, cy, cz = VEL[q]
+            start = cell - PITCH * cz - cy
+            value = full[q, pl.ds(start, 8), :]
+            if cx:
+                value = pltpu.roll(value, cx % 128, 1)
+            if q != 13:
+                blocked = walls[cx + 1, pl.ds(start, 8), :] != 0.0
+                value = jnp.where(blocked, full[26 - q, pl.ds(cell, 8), :], value)
+            f.append(jnp.where(solid, WEIGHT[q], value))
+        done = relaxed(f, sponge, full[AIM, pl.ds(cell, 8), :])
+        for q in range(27):
+            post[q, pl.ds(8 * u, 8), :] = done[q]
+
+    @pl.when(top)
+    def _():
+        for q in range(9):
+            post[q, pl.ds((NZ + 1) * PITCH, PITCH), :] = post[q + 18, pl.ds(NZ * PITCH, PITCH), :]
+
+
+def last_kernel(full, block, columns, x_one, x_two, out, west, east, post, walls, back, done, sems):
     here_x, size_x = lax.axis_index("gx"), lax.axis_size("gx")
     top = lax.axis_index("gz") == lax.axis_size("gz") - 1
     lanes, rows = lane_ids(), row_ids()
 
     def spread(right, left):
-        west[pl.ds(PAD, FLAT), :] = left[...]
-        east[pl.ds(PAD, FLAT), :] = right[...]
+        west[pl.ds(PAD, X_ROWS), :] = left[...]
+        east[pl.ds(PAD, X_ROWS), :] = right[...]
 
     by_parity("gx", x_one, x_two, spread)
 
-    def edged(value, cx, channel, start):
-        if cx == 0:
-            return value
-        if cx > 0:
-            column = pltpu.roll(west[pl.ds(start, 8), :], (128 - 4 * channel - 1) % 128, 1)
-            return jnp.where(lanes == 0, column, pltpu.roll(value, 1, 1))
-        column = pltpu.roll(east[pl.ds(start, 8), :], (127 - 4 * channel - 2) % 128, 1)
-        return jnp.where(lanes == 127, column, pltpu.roll(value, 127, 1))
-
-    for cx in (-1, 0, 1):
-        for t in range(FLAT // 8):
-            start = PAD + 8 * t
-            walls[cx + 1, pl.ds(start, 8), :] = edged(full[WALL, pl.ds(start, 8), :], cx, WALL, start)
-
-    for i, source in enumerate((mine[...], west[pl.ds(PAD, FLAT), :], east[pl.ds(PAD, FLAT), :])):
-        block = jnp.concatenate([source, jnp.zeros((128 - FLAT, 128), F32)], axis=0)
-        turn[i, pl.ds(PAD, 128), :] = block.T
     strip = []
     for c in range(CHANNELS):
-        a = turn[1, pl.ds(PAD + 4 * c, 8), :]
-        b = turn[0, pl.ds(PAD + 4 * c, 8), :]
-        d = turn[0, pl.ds(PAD + 4 * c - 4, 8), :]
-        e = turn[2, pl.ds(PAD + 4 * c - 4, 8), :]
-        strip.append(jnp.where(rows < 2, a, jnp.where(rows < 4, b, jnp.where(rows < 6, d, e))))
+        cx = VEL[c][0] if c < 27 else 0
+        value = jnp.where(
+            rows < 4, columns[pl.ds(PAD + 4 * c, 8), :], columns[pl.ds(PAD + 4 * c - 4, 8), :]
+        )
+        if c <= WALL and cx >= 0:
+            value = jnp.where(rows < 2, west[pl.ds(PAD + 2 * c - (cx == 0), 8), :], value)
+        if c <= WALL and cx <= 0:
+            value = jnp.where(rows >= 6, east[pl.ds(PAD + 2 * c - 6 + (cx == 0), 8), :], value)
+        strip.append(value)
+    strip[WALL] = jnp.where((rows == 0) | (rows == 7), 0.0, strip[WALL])
 
     def shifted(value, q):
         cx, cy, cz = VEL[q]
@@ -303,50 +348,51 @@
     lid = top & (lanes >= (NZ + 2) * PITCH) & (lanes < (NZ + 3) * PITCH)
     for q in range(9):
         sides[q] = jnp.where(lid, pltpu.roll(sides[q + 18], PITCH, 1), sides[q])
-    merged = []
-    for k in range(9):
-        merged.append(jnp.where(rows < 4, sides[3 * k + 2], sides[3 * k]))
-    merged = jnp.concatenate(merged + [jnp.zeros((128 - 72, 128), F32)], axis=0)
-    back[...] = merged.T
-
-    sponge = (here_x * NX + lanes) < SPONGE
+    sides.append(strip[WALL])
+    sides = [
+        jnp.where((rows == 1) | (rows == 5), pltpu.roll(side, 4, 0), side) for side in sides
+    ]
+    sides += [jnp.zeros((8, 128), F32)] * 4
+    for i in range(2):
+        back[i] = jnp.concatenate(sides[16 * i : 16 * i + 16], axis=0).T
+
+    def column_at(c, place, lane, start):
+        value = back[c // 16, pl.ds(start, 8), :]
+        return pltpu.roll(value, (lane - 8 * (c % 16) - place) % 128, 1)
+
+    rim = (lanes == 0) | (lanes == 127)
     for u in range(UNITS):
-        cell = PAD + PITCH + 8 * u
-        f = []
-        solid = walls[1, pl.ds(cell, 8), :] != 0.0
         for q in range(27):
-            cx, cy, cz = VEL[q]
-            start = cell - PITCH * cz - cy
-            value = edged(full[q, pl.ds(start, 8), :], cx, q, start)
-            if q != 13:
-                blocked = walls[cx + 1, pl.ds(start, 8), :] != 0.0
-                value = jnp.where(blocked, full[26 - q, pl.ds(cell, 8), :], value)
-            f.append(jnp.where(solid, WEIGHT[q], value))
-        done = relaxed(f, sponge, full[AIM, pl.ds(cell, 8), :])
-        for q in range(27):
-            post[q, pl.ds(8 * u, 8), :] = done[q]
-
-    @pl.when(top)
-    def _():
-        for q in range(9):
-            post[q, pl.ds((NZ + 1) * PITCH, PITCH), :] = post[q + 18, pl.ds(NZ * PITCH, PITCH), :]
-
+            post[q, pl.ds(8 * u, 8), :] = jnp.where(
+                rim, column_at(q, 2, 0, PITCH + 8 * u), block[q, pl.ds(8 * u, 8), :]
+            )
+        flags = full[WALL, pl.ds(PAD + PITCH + 8 * u, 8), :]
+        walls[1, pl.ds(8 * u, 8), :] = flags
+        for cx, edge, place in ((1, 0, 5), (-1, 127, 6)):
+            walls[cx + 1, pl.ds(8 * u, 8), :] = jnp.where(
+                lanes == edge, column_at(WALL, place, edge, PITCH + 8 * u), pltpu.roll(flags, cx % 128, 1)
+            )
+
+    copies = []
     for z in range(NZ):
         cell = (z + 1) * PITCH + 2
-        solid = walls[1, pl.ds(PAD + PITCH + cell, 8), :] != 0.0
+        solid = walls[1, pl.ds(cell, 8), :] != 0.0
         for q in range(27):
             cx, cy, cz = VEL[q]
             start = cell - PITCH * cz - cy
             value = post[q, pl.ds(start, 8), :]
             if cx:
-                lane = 8 * (q // 3) + (1 if cx > 0 else 6)
-                edge = 0 if cx > 0 else 127
-                side = pltpu.roll(back[pl.ds(PITCH + start, 8), :], (edge - lane) % 128, 1)
+                edge, place = (0, 5) if cx > 0 else (127, 6)
+                side = column_at(q, place, edge, PITCH + start)
                 value = jnp.where(lanes == edge, side, pltpu.roll(value, cx % 128, 1))
             if q != 13:
-                blocked = walls[cx + 1, pl.ds(PAD + PITCH + start, 8), :] != 0.0
+                blocked = walls[cx + 1, pl.ds(start, 8), :] != 0.0
                 value = jnp.where(blocked, post[26 - q, pl.ds(cell, 8), :], value)
-            out[q, z] = jnp.where(solid, WEIGHT[q], value)
+            done[q, z] = jnp.where(solid, WEIGHT[q], value)
+        copies.append(pltpu.make_async_copy(done.at[:, z], out.at[:, z], sems.at[z]))
+        copies[-1].start()
+    for copy in copies:
+        copy.wait()
 
 
 def swap(value, axis, turn, wrap):
@@ -387,32 +433,46 @@
     )(own, y_one, y_two)
     z_two = swap(z_two, "gz", 1, False)
     z_one = swap(z_one, "gz", 0, False)
-    full, mine = pl.pallas_call(
+    full, columns, message = pl.pallas_call(
         third_kernel,
-        out_shape=[shape(CHANNELS, ROWS, 128), shape(FLAT, 128)],
+        out_shape=[shape(CHANNELS, ROWS, 128), shape(PAD + 128 + PAD, 128), shape(X_ROWS, 128)],
         in_specs=[VMEM] * 5,
-        out_specs=[VMEM] * 2,
+        out_specs=[VMEM] * 3,
+        scratch_shapes=[pltpu.VMEM((128, 128), F32)],
         compiler_params=PARAMS,
         name="pack_x",
     )(own, y_one, y_two, z_two, z_one)
-    x_one = swap(mine, "gx", 0, True)
-    x_two = x_one if lax.axis_size("gx") == 2 else swap(mine, "gx", 1, True)
+    x_one = swap(message, "gx", 0, True)
+    x_two = x_one if lax.axis_size("gx") == 2 else swap(message, "gx", 1, True)
+    block = pl.pallas_call(
+        block_kernel,
+        out_shape=shape(27, UNITS * 8, 128),
+        in_specs=[VMEM],
+        out_specs=VMEM,
+        scratch_shapes=[pltpu.VMEM((3, ROWS, 128), F32)],
+        compiler_params=PARAMS,
+        cost_estimate=pl.CostEstimate(
+            flops=27 * 20 * UNITS * 1024, bytes_accessed=2**22, transcendentals=0
+        ),
+        name="block",
+    )(full)
     return pl.pallas_call(
         last_kernel,
         out_shape=shape(27, NZ, NY, NX),
-        in_specs=[VMEM] * 4,
-        out_specs=VMEM,
+        in_specs=[VMEM] * 5,
+        out_specs=HBM,
         scratch_shapes=[
+            pltpu.VMEM((PAD + X_ROWS + PAD, 128), F32),
+            pltpu.VMEM((PAD + X_ROWS + PAD, 128), F32),
             pltpu.VMEM((27, UNITS * 8, 128), F32),
-            pltpu.VMEM((ROWS, 128), F32),
-            pltpu.VMEM((ROWS, 128), F32),
-            pltpu.VMEM((3, PAD + 128 + PAD, 128), F32),
-            pltpu.VMEM((3, ROWS, 128), F32),
-            pltpu.VMEM((128, 128), F32),
+            pltpu.VMEM((3, UNITS * 8, 128), F32),
+            pltpu.VMEM((2, 128, 128), F32),
+            pltpu.VMEM((27, NZ, NY, NX), F32),
+            pltpu.SemaphoreType.DMA((NZ,)),
         ],
         compiler_params=PARAMS,
         name="finish",
-    )(full, mine, x_one, x_two)
+    )(full, block, columns, x_one, x_two)
 
 
 def solution(mesh):

time: 23.6 us -> 23.2 us (0.983)
  waiting for transfers between devices: 8.75 us -> 7.84 us
  Pallas kernels: 3.92 us -> 4.42 us
    ppermute x5, waiting for transfers between devices: 8.75 us -> 7.84 us  [swap(): return lax.ppermute(value, axis, pairs + [(j, i) for i, j in pairs])]
    pallas_call x0 -> x1, Pallas kernels: none -> 0.69 us  [shards(): pl.pallas_call(block_kernel, out_shape=shape(27, UNITS * 8, 128), in_spec...]
    pallas_call x1, Pallas kernels: 1.97 us -> 1.59 us  [shards(): pl.pallas_call(last_kernel, out_shape=shape(27, NZ, NY, NX), in_specs=[VM...]
  transfers between devices with their start and end apart: 5 -> 5, of which waited for: 3 -> 3; matrix products, arithmetic and copies ran while one was open for 0% -> 0% of each run, Pallas kernels for 0% -> 3%
where the time goes in v5:
time: 23.2 us; the launch traced here: 22.7 us
  starting transfers between devices  10.4 us (45%)
  waiting for transfers between devices  7.84 us (34%)
  Pallas kernels  4.42 us (19%)
    ppermute x5, starting transfers between devices, swap(): return lax.ppermute(value, axis, pairs + [(j, i) for i, j in pairs])  10.4 us
    ppermute x5, waiting for transfers between devices, swap(): return lax.ppermute(value, axis, pairs + [(j, i) for i, j in pairs])  7.84 us
    pallas_call x1, Pallas kernels, shards(): pl.pallas_call(last_kernel, out_shape=shape(27, NZ, NY, NX), in_specs=[VM...  1.59 us
    pallas_call x1, Pallas kernels, shards(): pl.pallas_call(first_kernel, out_shape=[shape(CHANNELS * NZ * 8, 128), sh...  1.33 us
    pallas_call x1, Pallas kernels, shards(): pl.pallas_call(third_kernel, out_shape=[shape(CHANNELS, ROWS, 128), shape...  0.77 us
    pallas_call x1, Pallas kernels, shards(): pl.pallas_call(block_kernel, out_shape=shape(27, UNITS * 8, 128), in_spec...  0.69 us
  transfers between devices with their start and end apart: 5, of which 3 were waited for; matrix products, arithmetic and copies ran while one was open for 0% of the time, Pallas kernels for 3%

profile of v5, /device:TPU:1, one launch (start us, length us, event | category | flops | bytes accessed | tf_op | source)
XLA Modules:
  0.0 22.7 jit_solution(16588001695164090857)
XLA Ops:
  0.0 1.3 %collide.1 = (f32[928,128]{1,0:T(8,128)S(1)}, f32[152,128]{1,0:T(8,128)S(1)}, f32[152,128]{1,0:T(8,128)S(1)}) custom-call(f32[27,4,8,128]{3,2,1,0:T(8,128)} %pops_at.1, s32[4,8,128]{2,1,0:T(8,128)} %solid_at.1, f32[4,8]{1,0:T(4,128)} %bitcast.1, s32[8]{0:T(128)} %index_at.1), custom_call_target="tpu_custom_call" | custom-call | tf_op jit(solution)/shard_map/collide/pallas_call | solution.py:409
  1.3 2.2 %collective-permute-start = (f32[152,128]{1,0:T(8,128)S(1)}, f32[152,128]{1,0:T(8,128)S(1)}, u32[]{:S(2)}, u32[]{:S(2)}) collective-permute-start(f32[152,128]{1,0:T(8,128)S(1)} %get-tuple-element.14), channel_id=1, source_target_pairs={{0,4},{8,12},{4,0},{12,8},{1,5},{9,13},{5,1},{13,9},{2,6},{10,14},... | collective-permute-start | bytes 233480 | tf_op jit(solution)/shard_map/ppermute | solution.py:401
  3.5 2.2 %collective-permute-start.1 = (f32[152,128]{1,0:T(8,128)S(1)}, f32[152,128]{1,0:T(8,128)S(1)}, u32[]{:S(2)}, u32[]{:S(2)}) collective-permute-start(f32[152,128]{1,0:T(8,128)S(1)} %get-tuple-element.15), channel_id=1, source_target_pairs={{4,8},{12,0},{8,4},{0,12},{5,9},{13,1},{9,5},{1,13},{6,10},{14,2},... | collective-permute-start | bytes 233480 | tf_op jit(solution)/shard_map/ppermute | solution.py:401
  5.7 0.0 collective-permute-done.y_one
  5.7 3.6 %collective-permute-done.1.y_two = f32[152,128]{1,0:T(8,128)S(1)} collective-permute-done((f32[152,128]{1,0:T(8,128)S(1)}, f32[152,128]{1,0:T(8,128)S(1)}, u32[]{:S(2)}, u32[]{:S(2)}) %collective-permute-start.1) | collective-permute-done | bytes 77856 | tf_op jit(solution)/shard_map/ppermute | solution.py:401
  9.4 4.7 %collective-permute-start.2 = (f32[416,128]{1,0:T(8,128)S(1)}, f32[416,128]{1,0:T(8,128)S(1)}, u32[]{:S(2)}, u32[]{:S(2)}) collective-permute-start(f32[416,128]{1,0:T(8,128)S(1)} %get-tuple-element.16), channel_id=1, source_target_pairs={{1,2},{2,1},{5,6},{6,5},{9,10},{10,9},{13,14},{14,13},{17,18},{18,... | collective-permute-start | bytes 638984 | tf_op jit(solution)/shard_map/ppermute | solution.py:401
  14.1 0.1 collective-permute-start.3
  14.1 3.4 %collective-permute-done.2.z_two = f32[416,128]{1,0:T(8,128)S(1)} collective-permute-done((f32[416,128]{1,0:T(8,128)S(1)}, f32[416,128]{1,0:T(8,128)S(1)}, u32[]{:S(2)}, u32[]{:S(2)}) %collective-permute-start.2) | collective-permute-done | bytes 213024 | tf_op jit(solution)/shard_map/ppermute | solution.py:401
  17.6 0.0 collective-permute-done.3.z_one
  17.6 0.8 %pack_x.1 = (f32[29,112,128]{2,1,0:T(8,128)S(1)}, f32[144,128]{1,0:T(8,128)S(1)}, f32[56,128]{1,0:T(8,128)S(1)}) custom-call(f32[928,128]{1,0:T(8,128)S(1)} %get-tuple-element.13.own, f32[152,128]{1,0:T(8,128)S(1)} %collective-permute-done.y_one, f32[152,128]{1,0:T(8,128)S(1)} %collective-permute-done.1.y_two, f32[416,128]{1,0:T(8,128)S(1)} %collective-permute-done.2.z_two, ...), custom_call_target="tpu_custom_call" | custom-call | tf_op jit(solution)/shard_map/pack_x/pallas_call | solution.py:436
  18.4 1.3 %collective-permute-start.4 = (f32[56,128]{1,0:T(8,128)S(1)}, f32[56,128]{1,0:T(8,128)S(1)}, u32[]{:S(2)}, u32[]{:S(2)}) collective-permute-start(f32[56,128]{1,0:T(8,128)S(1)} %get-tuple-element.20), channel_id=1, source_target_pairs={{0,16},{16,0},{1,17},{17,1},{2,18},{18,2},{3,19},{19,3},{4,20},{20... | collective-permute-start | bytes 86024 | tf_op jit(solution)/shard_map/ppermute | solution.py:401
  19.7 0.7 %block.1 = f32[27,72,128]{2,1,0:T(8,128)S(1)} custom-call(f32[29,112,128]{2,1,0:T(8,128)S(1)} %get-tuple-element.18.full), custom_call_target="tpu_custom_call" | custom-call | flops 4976640 | bytes 4194304 | tf_op jit(solution)/shard_map/block/pallas_call | solution.py:447
  20.4 0.8 %collective-permute-done.4.x_one.x_two = f32[56,128]{1,0:T(8,128)S(1)} collective-permute-done((f32[56,128]{1,0:T(8,128)S(1)}, f32[56,128]{1,0:T(8,128)S(1)}, u32[]{:S(2)}, u32[]{:S(2)}) %collective-permute-start.4) | collective-permute-done | bytes 28704 | tf_op jit(solution)/shard_map/ppermute | solution.py:401
  21.1 1.6 %finish.1 = f32[27,4,8,128]{3,2,1,0:T(8,128)} custom-call(f32[29,112,128]{2,1,0:T(8,128)S(1)} %get-tuple-element.18.full, f32[27,72,128]{2,1,0:T(8,128)S(1)} %block.1, f32[144,128]{1,0:T(8,128)S(1)} %get-tuple-element.19.columns, f32[56,128]{1,0:T(8,128)S(1)} %collective-permute-done.4.x_one.x_two, f32[56,128]{1,0:T(8,128)S(1)} %collective-permute-done.4.x_one.x_two), custom_call_target="tpu_custom_call" | custom-call | tf_op jit(solution)/shard_map/finish/pallas_call | solution.py:459
  (1 shorter events, 0.0 us)
Async XLA Ops:
  1.3 4.4 %collective-permute-start = (f32[152,128]{1,0:T(8,128)S(1)}, f32[152,128]{1,0:T(8,128)S(1)}, u32[]{:S(2)}, u32[]{:S(2)}) collective-permute-start(f32[152,128]{1,0:T(8,128)S(1)} %get-tuple-element.14), channel_id=1, source_target_pairs={{0,4},{8,12},{4,0},{12,8},{1,5},{9,13},{5,1},{13,9},{2,6},{10,14},... | collective-permute-start | bytes 233480 | tf_op jit(solution)/shard_map/ppermute | solution.py:401
  3.5 5.8 %collective-permute-start.1 = (f32[152,128]{1,0:T(8,128)S(1)}, f32[152,128]{1,0:T(8,128)S(1)}, u32[]{:S(2)}, u32[]{:S(2)}) collective-permute-start(f32[152,128]{1,0:T(8,128)S(1)} %get-tuple-element.15), channel_id=1, source_target_pairs={{4,8},{12,0},{8,4},{0,12},{5,9},{13,1},{9,5},{1,13},{6,10},{14,2},... | collective-permute-start | bytes 233480 | tf_op jit(solution)/shard_map/ppermute | solution.py:401
  9.4 8.2 %collective-permute-start.2 = (f32[416,128]{1,0:T(8,128)S(1)}, f32[416,128]{1,0:T(8,128)S(1)}, u32[]{:S(2)}, u32[]{:S(2)}) collective-permute-start(f32[416,128]{1,0:T(8,128)S(1)} %get-tuple-element.16), channel_id=1, source_target_pairs={{1,2},{2,1},{5,6},{6,5},{9,10},{10,9},{13,14},{14,13},{17,18},{18,... | collective-permute-start | bytes 638984 | tf_op jit(solution)/shard_map/ppermute | solution.py:401
  14.1 3.5 %collective-permute-start.3 = (f32[416,128]{1,0:T(8,128)S(1)}, f32[416,128]{1,0:T(8,128)S(1)}, u32[]{:S(2)}, u32[]{:S(2)}) collective-permute-start(f32[416,128]{1,0:T(8,128)S(1)} %get-tuple-element.17), channel_id=1, source_target_pairs={{0,1},{2,3},{1,0},{3,2},{4,5},{6,7},{5,4},{7,6},{8,9},{10,11},{9,8... | collective-permute-start | bytes 638984 | tf_op jit(solution)/shard_map/ppermute | solution.py:401
  18.4 2.8 %collective-permute-start.4 = (f32[56,128]{1,0:T(8,128)S(1)}, f32[56,128]{1,0:T(8,128)S(1)}, u32[]{:S(2)}, u32[]{:S(2)}) collective-permute-start(f32[56,128]{1,0:T(8,128)S(1)} %get-tuple-element.20), channel_id=1, source_target_pairs={{0,16},{16,0},{1,17},{17,1},{2,18},{18,2},{3,19},{19,3},{4,20},{20... | collective-permute-start | bytes 86024 | tf_op jit(solution)/shard_map/ppermute | solution.py:401

commit v6 on v5

--- a/solution.py
+++ b/solution.py
@@ -36,7 +36,8 @@
 Z_FAR = Z_BLOCKS * Z_PITCH
 Z_ROWS = -(-(Z_FAR + 2 * 12) // 8) * 8
 
-X_ROWS = 2 * (WALL + 1)
+OWN = NZ * PITCH
+EDGE = 2 * PITCH
 
 
 def relaxed(f, sponge, aim):
@@ -223,13 +224,27 @@
                 full[WALL, pl.ds(plane_at(z) + row, 1), :] = halo[pl.ds(k * Z_PITCH + first, 1), :]
 
 
-def third_kernel(own, y_one, y_two, z_two, z_one, full, columns, message, pack):
-    last = lax.axis_size("gz") - 1
-    here = lax.axis_index("gz")
+def pack_columns(full, pack, tiles):
+    slot = lane_ids() // 4
+    for source, target in tiles:
+        packed = jnp.zeros((8, 128), F32)
+        for c in range(CHANNELS):
+            moved = pltpu.roll(full[c, pl.ds(PAD + 8 * source, 8), :], (4 * c + 2) % 128, 1)
+            packed = jnp.where(slot == c, moved, packed)
+        pack[pl.ds(8 * target, 8), :] = packed
+
+
+def third_kernel(own, y_one, y_two, full, pack):
     for c in range(CHANNELS):
         for z in range(NZ):
             full[c, pl.ds(plane_at(z) + 2, 8), :] = own[pl.ds((c * NZ + z) * 8, 8), :]
     by_parity("gy", y_one, y_two, functools.partial(add_rows, full))
+    pack_columns(full, pack, [(EDGE // 8 + t, t) for t in range(OWN // 8)])
+
+
+def block_kernel(part, pack, z_two, z_one, full, post, mine, walls):
+    last = lax.axis_size("gz") - 1
+    here = lax.axis_index("gz")
     by_parity("gz", z_one, z_two, functools.partial(add_planes, full))
 
     @pl.when(here == 0)
@@ -240,41 +255,12 @@
     def _():
         for q in range(9):
             full[q, pl.ds(plane_at(NZ), PITCH), :] = full[q + 18, pl.ds(plane_at(NZ - 1), PITCH), :]
-
-    slot = lane_ids() // 4
-    pack[pl.ds(FLAT, 128 - FLAT), :] = jnp.zeros((128 - FLAT, 128), F32)
-    for t in range(FLAT // 8):
-        packed = jnp.zeros((8, 128), F32)
-        for c in range(CHANNELS):
-            moved = pltpu.roll(full[c, pl.ds(PAD + 8 * t, 8), :], (4 * c + 2) % 128, 1)
-            packed = jnp.where(slot == c, moved, packed)
-        pack[pl.ds(8 * t, 8), :] = packed
-    columns[pl.ds(PAD, 128), :] = pack[...].T
-
-    def row(c, i, count):
-        return columns[pl.ds(PAD + 4 * c + i, count), :]
-
-    def returned(q, near, far):
-        cx, cy, cz = VEL[q]
-        step = (-PITCH * cz - cy) % 128
-        value = row(26 - q, near, 8)
-        value = pltpu.roll(value, step, 1) if step else value
-        return jnp.where(row(WALL, far, 8) != 0.0, value, row(q, far, 8))[:1]
-
-    for c in range(WALL + 1):
-        cx = VEL[c][0] if c < 27 else 0
-        if cx == 0:
-            message[pl.ds(2 * c, 2), :] = row(c, 1, 2)
-        elif cx > 0:
-            message[pl.ds(2 * c, 1), :] = returned(c, 1, 0)
-            message[pl.ds(2 * c + 1, 1), :] = row(c, 1, 1)
-        else:
-            message[pl.ds(2 * c, 1), :] = row(c, 2, 1)
-            message[pl.ds(2 * c + 1, 1), :] = returned(c, 2, 3)
-
-
-def block_kernel(full, post, walls):
-    top = lax.axis_index("gz") == lax.axis_size("gz") - 1
+        full[WALL, pl.ds(plane_at(NZ), PITCH), :] = jnp.zeros((PITCH, 128), F32)
+
+    mine[pl.ds(EDGE, OWN), :] = pack[...]
+    rest = [t for t in range(FLAT // 8) if not EDGE <= 8 * t < EDGE + OWN]
+    pack_columns(full, mine, [(t, t) for t in rest])
+
     sponge = (lax.axis_index("gx") * NX + lane_ids()) < SPONGE
     for t in range(ROWS // 8):
         rows = pl.ds(8 * t, 8)
@@ -299,35 +285,58 @@
         for q in range(27):
             post[q, pl.ds(8 * u, 8), :] = done[q]
 
-    @pl.when(top)
+    @pl.when(here == last)
     def _():
         for q in range(9):
             post[q, pl.ds((NZ + 1) * PITCH, PITCH), :] = post[q + 18, pl.ds(NZ * PITCH, PITCH), :]
 
 
-def last_kernel(full, block, columns, x_one, x_two, out, west, east, post, walls, back, done, sems):
+def last_kernel(block, sheet, mine, *refs):
+    turns = 1 if lax.axis_size("gx") == 2 else 2
+    beside, refs = refs[: 3 * turns], refs[3 * turns :]
+    out, west, east, turn, post, walls, back, done, sems = refs
     here_x, size_x = lax.axis_index("gx"), lax.axis_size("gx")
     top = lax.axis_index("gz") == lax.axis_size("gz") - 1
+    bottom = lax.axis_index("gz") == 0
     lanes, rows = lane_ids(), row_ids()
 
-    def spread(right, left):
-        west[pl.ds(PAD, X_ROWS), :] = left[...]
-        east[pl.ds(PAD, X_ROWS), :] = right[...]
-
-    by_parity("gx", x_one, x_two, spread)
+    def gather(target, level, one, two):
+        target[pl.ds(EDGE, OWN), :] = level[...]
+
+        def ends(above, below):
+            target[pl.ds(0, EDGE), :] = below[pl.ds(OWN - EDGE, EDGE), :]
+            target[pl.ds(EDGE + OWN, EDGE), :] = above[pl.ds(0, EDGE), :]
+
+        by_parity("gz", one, two, ends)
+
+    if turns == 1:
+        gather(west, *beside)
+        sources = (mine, west)
+    else:
+
+        def spread(right, left):
+            gather(west, *left)
+            gather(east, *right)
+
+        by_parity("gx", beside[:3], beside[3:], spread)
+        sources = (mine, west, east)
+
+    for i, source in enumerate(sources):
+        square = jnp.concatenate([source[...], jnp.zeros((128 - FLAT, 128), F32)], axis=0)
+        turn[i, pl.ds(PAD, 128), :] = square.T
 
     strip = []
     for c in range(CHANNELS):
-        cx = VEL[c][0] if c < 27 else 0
-        value = jnp.where(
-            rows < 4, columns[pl.ds(PAD + 4 * c, 8), :], columns[pl.ds(PAD + 4 * c - 4, 8), :]
-        )
-        if c <= WALL and cx >= 0:
-            value = jnp.where(rows < 2, west[pl.ds(PAD + 2 * c - (cx == 0), 8), :], value)
-        if c <= WALL and cx <= 0:
-            value = jnp.where(rows >= 6, east[pl.ds(PAD + 2 * c - 6 + (cx == 0), 8), :], value)
-        strip.append(value)
-    strip[WALL] = jnp.where((rows == 0) | (rows == 7), 0.0, strip[WALL])
+        first, second = pl.ds(PAD + 4 * c, 8), pl.ds(PAD + 4 * c - 4, 8)
+        inner = jnp.where(rows < 4, turn[0, first, :], turn[0, second, :])
+        outer = jnp.where(rows < 4, turn[1, first, :], turn[turns, second, :])
+        strip.append(jnp.where((rows >= 2) & (rows < 6), inner, outer))
+
+    ceiling = top & (lanes >= (NZ + 2) * PITCH) & (lanes < (NZ + 3) * PITCH)
+    ground = bottom & (lanes >= PITCH) & (lanes < 2 * PITCH)
+    for q in range(9):
+        strip[q] = jnp.where(ceiling, pltpu.roll(strip[q + 18], PITCH, 1), strip[q])
+    strip[WALL] = jnp.where(ceiling, 0.0, jnp.where(ground, 1.0, strip[WALL]))
 
     def shifted(value, q):
         cx, cy, cz = VEL[q]
@@ -345,9 +354,8 @@
     column = here_x * NX + jnp.where(rows < 4, rows - 2, rows + (NX - 6))
     column = lax.rem(column + size_x * NX, size_x * NX)
     sides = relaxed(moved, column < SPONGE, strip[AIM])
-    lid = top & (lanes >= (NZ + 2) * PITCH) & (lanes < (NZ + 3) * PITCH)
     for q in range(9):
-        sides[q] = jnp.where(lid, pltpu.roll(sides[q + 18], PITCH, 1), sides[q])
+        sides[q] = jnp.where(ceiling, pltpu.roll(sides[q + 18], PITCH, 1), sides[q])
     sides.append(strip[WALL])
     sides = [
         jnp.where((rows == 1) | (rows == 5), pltpu.roll(side, 4, 0), side) for side in sides
@@ -366,11 +374,13 @@
             post[q, pl.ds(8 * u, 8), :] = jnp.where(
                 rim, column_at(q, 2, 0, PITCH + 8 * u), block[q, pl.ds(8 * u, 8), :]
             )
-        flags = full[WALL, pl.ds(PAD + PITCH + 8 * u, 8), :]
+        flags = sheet[1, pl.ds(PAD + PITCH + 8 * u, 8), :]
         walls[1, pl.ds(8 * u, 8), :] = flags
         for cx, edge, place in ((1, 0, 5), (-1, 127, 6)):
             walls[cx + 1, pl.ds(8 * u, 8), :] = jnp.where(
-                lanes == edge, column_at(WALL, place, edge, PITCH + 8 * u), pltpu.roll(flags, cx % 128, 1)
+                lanes == edge,
+                column_at(WALL, place, edge, PITCH + 8 * u),
+                sheet[cx + 1, pl.ds(PAD + PITCH + 8 * u, 8), :],
             )
 
     copies = []
@@ -395,10 +405,27 @@
         copy.wait()
 
 
+def partners(size, turn, wrap):
+    result = list(range(size))
+    for i in range(turn, size if wrap else size - 1, 2):
+        j = (i + 1) % size
+        result[i], result[j] = j, i
+    return result
+
+
 def swap(value, axis, turn, wrap):
-    size = lax.axis_size(axis)
-    pairs = [(i, (i + 1) % size) for i in range(turn, size if wrap else size - 1, 2)]
-    return lax.ppermute(value, axis, pairs + [(j, i) for i, j in pairs])
+    return lax.ppermute(value, axis, list(enumerate(partners(lax.axis_size(axis), turn, wrap))))
+
+
+def swap_across(value, x_turn, z_turn):
+    size = lax.axis_size("gz")
+    over_x = partners(lax.axis_size("gx"), x_turn, True)
+    over_z = partners(size, z_turn, False)
+    pairs = []
+    for i, far_i in enumerate(over_x):
+        for j, far_j in enumerate(over_z):
+            pairs.append((i * size + j, far_i * size + far_j if far_j != j else i * size + j))
+    return lax.ppermute(value, ("gx", "gz"), pairs)
 
 
 def shape(*dims):
@@ -433,37 +460,44 @@
     )(own, y_one, y_two)
     z_two = swap(z_two, "gz", 1, False)
     z_one = swap(z_one, "gz", 0, False)
-    full, columns, message = pl.pallas_call(
+    part, pack = pl.pallas_call(
         third_kernel,
-        out_shape=[shape(CHANNELS, ROWS, 128), shape(PAD + 128 + PAD, 128), shape(X_ROWS, 128)],
-        in_specs=[VMEM] * 5,
-        out_specs=[VMEM] * 3,
-        scratch_shapes=[pltpu.VMEM((128, 128), F32)],
+        out_shape=[shape(CHANNELS, ROWS, 128), shape(OWN, 128)],
+        in_specs=[VMEM] * 3,
+        out_specs=[VMEM] * 2,
         compiler_params=PARAMS,
         name="pack_x",
-    )(own, y_one, y_two, z_two, z_one)
-    x_one = swap(message, "gx", 0, True)
-    x_two = x_one if lax.axis_size("gx") == 2 else swap(message, "gx", 1, True)
-    block = pl.pallas_call(
+    )(own, y_one, y_two)
+    beside = []
+    for turn in range(1 if lax.axis_size("gx") == 2 else 2):
+        beside += [swap(pack, "gx", turn, True)]
+        beside += [swap_across(pack, turn, 0), swap_across(pack, turn, 1)]
+    full, block, mine, sheet = pl.pallas_call(
         block_kernel,
-        out_shape=shape(27, UNITS * 8, 128),
-        in_specs=[VMEM],
-        out_specs=VMEM,
-        scratch_shapes=[pltpu.VMEM((3, ROWS, 128), F32)],
+        out_shape=[
+            shape(CHANNELS, ROWS, 128),
+            shape(27, UNITS * 8, 128),
+            shape(FLAT, 128),
+            shape(3, ROWS, 128),
+        ],
+        in_specs=[VMEM] * 4,
+        out_specs=[VMEM] * 4,
+        input_output_aliases={0: 0},
         compiler_params=PARAMS,
         cost_estimate=pl.CostEstimate(
             flops=27 * 20 * UNITS * 1024, bytes_accessed=2**22, transcendentals=0
         ),
         name="block",
-    )(full)
+    )(part, pack, z_two, z_one)
     return pl.pallas_call(
         last_kernel,
         out_shape=shape(27, NZ, NY, NX),
-        in_specs=[VMEM] * 5,
+        in_specs=[VMEM] * (3 + len(beside)),
         out_specs=HBM,
         scratch_shapes=[
-            pltpu.VMEM((PAD + X_ROWS + PAD, 128), F32),
-            pltpu.VMEM((PAD + X_ROWS + PAD, 128), F32),
+            pltpu.VMEM((FLAT, 128), F32),
+            pltpu.VMEM((FLAT, 128), F32),
+            pltpu.VMEM((3, PAD + 128 + PAD, 128), F32),
             pltpu.VMEM((27, UNITS * 8, 128), F32),
             pltpu.VMEM((3, UNITS * 8, 128), F32),
             pltpu.VMEM((2, 128, 128), F32),
@@ -472,7 +506,7 @@
         ],
         compiler_params=PARAMS,
         name="finish",
-    )(full, block, columns, x_one, x_two)
+    )(block, sheet, mine, *beside)
 
 
 def solution(mesh):

time: 23.2 us -> 24.6 us (1.060); the launches traced: 22.7 us -> 24.4 us
  starting transfers between devices: 10.4 us -> 13.9 us
  waiting for transfers between devices: 7.84 us -> 6.04 us
    ppermute x5 -> x7, starting transfers between devices: 10.4 us -> 13.9 us  [the longest x5 10.4 us: swap(): lax.ppermute(value, axis, list(enumerate(partners(lax.axis_size(axis), tu...]
    ppermute x5 -> x7, waiting for transfers between devices: 7.84 us -> 6.04 us  [the longest x5 3.62 us: swap(): lax.ppermute(value, axis, list(enumerate(partners(lax.axis_size(axis), tu...]
    pallas_call x1, Pallas kernels: 0.77 us -> 0.32 us  [shards(): pl.pallas_call(third_kernel, out_shape=[shape(CHANNELS, ROWS, 128), shape...]
    pallas_call x1, Pallas kernels: 0.69 us -> 0.97 us  [shards(): pl.pallas_call(block_kernel, out_shape=[shape(CHANNELS, ROWS, 128), shape...]
  transfers between devices with their start and end apart: 5 -> 7, of which waited for: 3 -> 2; matrix products, arithmetic and copies ran while one was open for 0% -> 0% of each run, Pallas kernels for 3% -> 5%
where the time goes in v6:
time: 24.6 us; the launch traced here: 24.4 us
  starting transfers between devices  13.9 us (57%)
  waiting for transfers between devices  6.04 us (25%)
  Pallas kernels  4.39 us (18%)
    ppermute x5, starting transfers between devices, swap(): lax.ppermute(value, axis, list(enumerate(partners(lax.axis_size(axis), tu...  10.4 us
    ppermute x5, waiting for transfers between devices, swap(): lax.ppermute(value, axis, list(enumerate(partners(lax.axis_size(axis), tu...  3.62 us
    ppermute x2, starting transfers between devices, swap_across(): return lax.ppermute(value, ('gx', 'gz'), pairs)  3.47 us
    ppermute x2, waiting for transfers between devices, swap_across(): return lax.ppermute(value, ('gx', 'gz'), pairs)  2.42 us
    pallas_call x1, Pallas kernels, shards(): pl.pallas_call(last_kernel, out_shape=shape(27, NZ, NY, NX), in_specs=[VM...  1.72 us
    pallas_call x1, Pallas kernels, shards(): pl.pallas_call(first_kernel, out_shape=[shape(CHANNELS * NZ * 8, 128), sh...  1.33 us
    pallas_call x1, Pallas kernels, shards(): pl.pallas_call(block_kernel, out_shape=[shape(CHANNELS, ROWS, 128), shape...  0.97 us
  transfers between devices with their start and end apart: 7, of which 2 were waited for; matrix products, arithmetic and copies ran while one was open for 0% of the time, Pallas kernels for 5%

profile of v6, /device:TPU:1, one launch (start us, length us, event | category | flops | bytes accessed | tf_op | source)
XLA Modules:
  0.0 24.4 jit_solution(15021469060284343610)
XLA Ops:
  0.0 1.3 %collide.1 = (f32[928,128]{1,0:T(8,128)S(1)}, f32[152,128]{1,0:T(8,128)S(1)}, f32[152,128]{1,0:T(8,128)S(1)}) custom-call(f32[27,4,8,128]{3,2,1,0:T(8,128)} %pops_at.1, s32[4,8,128]{2,1,0:T(8,128)} %solid_at.1, f32[4,8]{1,0:T(4,128)} %bitcast.1, s32[8]{0:T(128)} %index_at.1), custom_call_target="tpu_custom_call" | custom-call | tf_op jit(solution)/shard_map/collide/pallas_call | solution.py:436
  1.3 2.2 %collective-permute-start = (f32[152,128]{1,0:T(8,128)S(1)}, f32[152,128]{1,0:T(8,128)S(1)}, u32[]{:S(2)}, u32[]{:S(2)}) collective-permute-start(f32[152,128]{1,0:T(8,128)S(1)} %get-tuple-element.16), channel_id=1, source_target_pairs={{0,4},{4,0},{8,12},{12,8},{1,5},{5,1},{9,13},{13,9},{2,6},{6,2},{1... | collective-permute-start | bytes 233480 | tf_op jit(solution)/shard_map/ppermute | solution.py:417
  3.5 2.2 %collective-permute-start.1 = (f32[152,128]{1,0:T(8,128)S(1)}, f32[152,128]{1,0:T(8,128)S(1)}, u32[]{:S(2)}, u32[]{:S(2)}) collective-permute-start(f32[152,128]{1,0:T(8,128)S(1)} %get-tuple-element.17), channel_id=1, source_target_pairs={{0,12},{4,8},{8,4},{12,0},{1,13},{5,9},{9,5},{13,1},{2,14},{6,10},... | collective-permute-start | bytes 233480 | tf_op jit(solution)/shard_map/ppermute | solution.py:417
  5.7 0.0 collective-permute-done.y_one
  5.7 3.6 %collective-permute-done.1.y_two = f32[152,128]{1,0:T(8,128)S(1)} collective-permute-done((f32[152,128]{1,0:T(8,128)S(1)}, f32[152,128]{1,0:T(8,128)S(1)}, u32[]{:S(2)}, u32[]{:S(2)}) %collective-permute-start.1) | collective-permute-done | bytes 77856 | tf_op jit(solution)/shard_map/ppermute | solution.py:417
  9.4 4.7 %collective-permute-start.2 = (f32[416,128]{1,0:T(8,128)S(1)}, f32[416,128]{1,0:T(8,128)S(1)}, u32[]{:S(2)}, u32[]{:S(2)}) collective-permute-start(f32[416,128]{1,0:T(8,128)S(1)} %get-tuple-element.20), channel_id=1, source_target_pairs={{0,0},{1,2},{2,1},{3,3},{4,4},{5,6},{6,5},{7,7},{8,8},{9,10},{10,9... | collective-permute-start | bytes 638984 | tf_op jit(solution)/shard_map/ppermute | solution.py:417
  14.1 0.1 collective-permute-start.3
  14.1 0.3 %pack_x.1 = (f32[29,112,128]{2,1,0:T(8,128)S(1)}, f32[48,128]{1,0:T(8,128)S(1)}) custom-call(f32[928,128]{1,0:T(8,128)S(1)} %get-tuple-element.15.own, f32[152,128]{1,0:T(8,128)S(1)} %collective-permute-done.y_one, f32[152,128]{1,0:T(8,128)S(1)} %collective-permute-done.1.y_two), custom_call_target="tpu_custom_call" | custom-call | tf_op jit(solution)/shard_map/pack_x/pallas_call | solution.py:463
  14.5 1.3 %collective-permute-start.4 = (f32[48,128]{1,0:T(8,128)S(1)}, f32[48,128]{1,0:T(8,128)S(1)}, u32[]{:S(2)}, u32[]{:S(2)}) collective-permute-start(f32[48,128]{1,0:T(8,128)S(1)} %get-tuple-element.19.pack), channel_id=1, source_target_pairs={{0,16},{16,0},{1,17},{17,1},{2,18},{18,2},{3,19},{19,3},{4,20},{20... | collective-permute-start | bytes 73736 | tf_op jit(solution)/shard_map/ppermute | solution.py:417
  15.8 0.9 %collective-permute-start.5 = (f32[48,128]{1,0:T(8,128)S(1)}, f32[48,128]{1,0:T(8,128)S(1)}, u32[]{:S(2)}, u32[]{:S(2)}) collective-permute-start(f32[48,128]{1,0:T(8,128)S(1)} %get-tuple-element.19.pack), channel_id=1, source_target_pairs={{0,17},{1,16},{2,19},{3,18},{16,1},{17,0},{18,3},{19,2},{4,21},{5,... | collective-permute-start | bytes 73736 | tf_op jit(solution)/shard_map/ppermute | solution.py:428
  16.7 2.6 %collective-permute-start.6 = (f32[48,128]{1,0:T(8,128)S(1)}, f32[48,128]{1,0:T(8,128)S(1)}, u32[]{:S(2)}, u32[]{:S(2)}) collective-permute-start(f32[48,128]{1,0:T(8,128)S(1)} %get-tuple-element.19.pack), channel_id=1, source_target_pairs={{0,0},{1,18},{2,17},{3,3},{16,16},{17,2},{18,1},{19,19},{4,4},{5,2... | collective-permute-start | bytes 73736 | tf_op jit(solution)/shard_map/ppermute | solution.py:428
  19.2 0.0 collective-permute-done.2.z_two
  19.3 0.0 collective-permute-done.3.z_one
  19.3 1.0 %block.1 = (f32[29,112,128]{2,1,0:T(8,128)S(1)}, f32[27,72,128]{2,1,0:T(8,128)S(1)}, f32[96,128]{1,0:T(8,128)S(1)}, f32[3,112,128]{2,1,0:T(8,128)S(1)}) custom-call(f32[29,112,128]{2,1,0:T(8,128)S(1)} %get-tuple-element.18.part, f32[48,128]{1,0:T(8,128)S(1)} %get-tuple-element.19.pack, ...), custom_call_target="tpu_custom_call", output_to_operand_aliasing={{0}: (0, {})} | custom-call | flops 4976640 | bytes 4194304 | tf_op jit(solution)/shard_map/block/pallas_call | solution.py:475
  20.2 0.0 collective-permute-done.4.refs_0_
  20.3 0.0 collective-permute-done.5.refs_1_
  20.3 2.4 %collective-permute-done.6.refs_2_ = f32[48,128]{1,0:T(8,128)S(1)} collective-permute-done((f32[48,128]{1,0:T(8,128)S(1)}, f32[48,128]{1,0:T(8,128)S(1)}, u32[]{:S(2)}, u32[]{:S(2)}) %collective-permute-start.6) | collective-permute-done | bytes 24608 | tf_op jit(solution)/shard_map/ppermute | solution.py:428
  22.7 1.7 %finish.1 = f32[27,4,8,128]{3,2,1,0:T(8,128)} custom-call(f32[27,72,128]{2,1,0:T(8,128)S(1)} %get-tuple-element.22.block, f32[3,112,128]{2,1,0:T(8,128)S(1)} %get-tuple-element.23.sheet, f32[96,128]{1,0:T(8,128)S(1)} %get-tuple-element.24.mine, f32[48,128]{1,0:T(8,128)S(1)} %collective-permute-done.4.refs_0_, f32[48,128]{1,0:T(8,128)S(1)} %collective-permute-done.5.refs_1_, ...), custom_call_target="tpu_custom_call" | custom-call | tf_op jit(solution)/shard_map/finish/pallas_call | solution.py:492
  (1 shorter events, 0.0 us)
Async XLA Ops:
  1.3 4.4 %collective-permute-start = (f32[152,128]{1,0:T(8,128)S(1)}, f32[152,128]{1,0:T(8,128)S(1)}, u32[]{:S(2)}, u32[]{:S(2)}) collective-permute-start(f32[152,128]{1,0:T(8,128)S(1)} %get-tuple-element.16), channel_id=1, source_target_pairs={{0,4},{4,0},{8,12},{12,8},{1,5},{5,1},{9,13},{13,9},{2,6},{6,2},{1... | collective-permute-start | bytes 233480 | tf_op jit(solution)/shard_map/ppermute | solution.py:417
  3.5 5.8 %collective-permute-start.1 = (f32[152,128]{1,0:T(8,128)S(1)}, f32[152,128]{1,0:T(8,128)S(1)}, u32[]{:S(2)}, u32[]{:S(2)}) collective-permute-start(f32[152,128]{1,0:T(8,128)S(1)} %get-tuple-element.17), channel_id=1, source_target_pairs={{0,12},{4,8},{8,4},{12,0},{1,13},{5,9},{9,5},{13,1},{2,14},{6,10},... | collective-permute-start | bytes 233480 | tf_op jit(solution)/shard_map/ppermute | solution.py:417
  9.4 9.9 %collective-permute-start.2 = (f32[416,128]{1,0:T(8,128)S(1)}, f32[416,128]{1,0:T(8,128)S(1)}, u32[]{:S(2)}, u32[]{:S(2)}) collective-permute-start(f32[416,128]{1,0:T(8,128)S(1)} %get-tuple-element.20), channel_id=1, source_target_pairs={{0,0},{1,2},{2,1},{3,3},{4,4},{5,6},{6,5},{7,7},{8,8},{9,10},{10,9... | collective-permute-start | bytes 638984 | tf_op jit(solution)/shard_map/ppermute | solution.py:417
  14.1 5.2 %collective-permute-start.3 = (f32[416,128]{1,0:T(8,128)S(1)}, f32[416,128]{1,0:T(8,128)S(1)}, u32[]{:S(2)}, u32[]{:S(2)}) collective-permute-start(f32[416,128]{1,0:T(8,128)S(1)} %get-tuple-element.21), channel_id=1, source_target_pairs={{0,1},{1,0},{2,3},{3,2},{4,5},{5,4},{6,7},{7,6},{8,9},{9,8},{10,11... | collective-permute-start | bytes 638984 | tf_op jit(solution)/shard_map/ppermute | solution.py:417
  14.5 5.8 %collective-permute-start.4 = (f32[48,128]{1,0:T(8,128)S(1)}, f32[48,128]{1,0:T(8,128)S(1)}, u32[]{:S(2)}, u32[]{:S(2)}) collective-permute-start(f32[48,128]{1,0:T(8,128)S(1)} %get-tuple-element.19.pack), channel_id=1, source_target_pairs={{0,16},{16,0},{1,17},{17,1},{2,18},{18,2},{3,19},{19,3},{4,20},{20... | collective-permute-start | bytes 73736 | tf_op jit(solution)/shard_map/ppermute | solution.py:417
  15.8 4.5 %collective-permute-start.5 = (f32[48,128]{1,0:T(8,128)S(1)}, f32[48,128]{1,0:T(8,128)S(1)}, u32[]{:S(2)}, u32[]{:S(2)}) collective-permute-start(f32[48,128]{1,0:T(8,128)S(1)} %get-tuple-element.19.pack), channel_id=1, source_target_pairs={{0,17},{1,16},{2,19},{3,18},{16,1},{17,0},{18,3},{19,2},{4,21},{5,... | collective-permute-start | bytes 73736 | tf_op jit(solution)/shard_map/ppermute | solution.py:428
  16.7 6.0 %collective-permute-start.6 = (f32[48,128]{1,0:T(8,128)S(1)}, f32[48,128]{1,0:T(8,128)S(1)}, u32[]{:S(2)}, u32[]{:S(2)}) collective-permute-start(f32[48,128]{1,0:T(8,128)S(1)} %get-tuple-element.19.pack), channel_id=1, source_target_pairs={{0,0},{1,18},{2,17},{3,3},{16,16},{17,2},{18,1},{19,19},{4,4},{5,2... | collective-permute-start | bytes 73736 | tf_op jit(solution)/shard_map/ppermute | solution.py:428

commit v7 on v5

--- a/solution.py
+++ b/solution.py
@@ -223,7 +223,7 @@
                 full[WALL, pl.ds(plane_at(z) + row, 1), :] = halo[pl.ds(k * Z_PITCH + first, 1), :]
 
 
-def third_kernel(own, y_one, y_two, z_two, z_one, full, columns, message, pack):
+def third_kernel(own, y_one, y_two, z_two, z_one, full, columns, messages, pack):
     last = lax.axis_size("gz") - 1
     here = lax.axis_index("gz")
     for c in range(CHANNELS):
@@ -261,6 +261,7 @@
         value = pltpu.roll(value, step, 1) if step else value
         return jnp.where(row(WALL, far, 8) != 0.0, value, row(q, far, 8))[:1]
 
+    message = messages.at[0]
     for c in range(WALL + 1):
         cx = VEL[c][0] if c < 27 else 0
         if cx == 0:
@@ -271,6 +272,7 @@
         else:
             message[pl.ds(2 * c, 1), :] = row(c, 2, 1)
             message[pl.ds(2 * c + 1, 1), :] = returned(c, 2, 3)
+    messages[1] = messages[0]
 
 
 def block_kernel(full, post, walls):
@@ -311,8 +313,9 @@
     lanes, rows = lane_ids(), row_ids()
 
     def spread(right, left):
-        west[pl.ds(PAD, X_ROWS), :] = left[...]
-        east[pl.ds(PAD, X_ROWS), :] = right[...]
+        other = 1 - here_x if size_x == 2 else 0
+        west[pl.ds(PAD, X_ROWS), :] = left[other]
+        east[pl.ds(PAD, X_ROWS), :] = right[other]
 
     by_parity("gx", x_one, x_two, spread)
 
@@ -435,15 +438,17 @@
     z_one = swap(z_one, "gz", 0, False)
     full, columns, message = pl.pallas_call(
         third_kernel,
-        out_shape=[shape(CHANNELS, ROWS, 128), shape(PAD + 128 + PAD, 128), shape(X_ROWS, 128)],
+        out_shape=[shape(CHANNELS, ROWS, 128), shape(PAD + 128 + PAD, 128), shape(2, X_ROWS, 128)],
         in_specs=[VMEM] * 5,
         out_specs=[VMEM] * 3,
         scratch_shapes=[pltpu.VMEM((128, 128), F32)],
         compiler_params=PARAMS,
         name="pack_x",
     )(own, y_one, y_two, z_two, z_one)
-    x_one = swap(message, "gx", 0, True)
-    x_two = x_one if lax.axis_size("gx") == 2 else swap(message, "gx", 1, True)
+    if lax.axis_size("gx") == 2:
+        x_one = x_two = lax.all_to_all(message, "gx", 0, 0)
+    else:
+        x_one, x_two = swap(message, "gx", 0, True), swap(message, "gx", 1, True)
     block = pl.pallas_call(
         block_kernel,
         out_shape=shape(27, UNITS * 8, 128),

time: 23.2 us -> 27.3 us (1.18)
  starting transfers between devices: 10.4 us -> 12.4 us
  waiting for transfers between devices: 7.84 us -> 9.31 us
  Pallas kernels: 4.42 us -> 5.03 us
    all_to_all x0 -> x1, starting transfers between devices: none -> 3.29 us  [shards(): x_one = x_two = lax.all_to_all(message, 'gx', 0, 0)]
    all_to_all x0 -> x1, waiting for transfers between devices: none -> 2.27 us  [shards(): x_one = x_two = lax.all_to_all(message, 'gx', 0, 0)]
    ppermute x5 -> x4, starting transfers between devices: 10.4 us -> 9.12 us  [swap(): return lax.ppermute(value, axis, pairs + [(j, i) for i, j in pairs])]
    ppermute x5 -> x4, waiting for transfers between devices: 7.84 us -> 7.05 us  [swap(): return lax.ppermute(value, axis, pairs + [(j, i) for i, j in pairs])]
    pallas_call x1, Pallas kernels: 0.77 us -> 1.42 us  [shards(): pl.pallas_call(third_kernel, out_shape=[shape(CHANNELS, ROWS, 128), shape...]
  transfers between devices with their start and end apart: 5 -> 5, of which waited for: 3 -> 3; matrix products, arithmetic and copies ran while one was open for 0% -> 0% of each run, Pallas kernels for 3% -> 2%
where the time goes in v7:
time: 27.3 us; the launch traced here: 26.8 us
  starting transfers between devices  12.4 us (45%)
  waiting for transfers between devices  9.31 us (34%)
  Pallas kernels  5.03 us (18%)
    ppermute x4, starting transfers between devices, swap(): return lax.ppermute(value, axis, pairs + [(j, i) for i, j in pairs])  9.12 us
    ppermute x4, waiting for transfers between devices, swap(): return lax.ppermute(value, axis, pairs + [(j, i) for i, j in pairs])  7.05 us
    all_to_all x1, starting transfers between devices, shards(): x_one = x_two = lax.all_to_all(message, 'gx', 0, 0)  3.29 us
    all_to_all x1, waiting for transfers between devices, shards(): x_one = x_two = lax.all_to_all(message, 'gx', 0, 0)  2.27 us
    pallas_call x1, Pallas kernels, shards(): pl.pallas_call(last_kernel, out_shape=shape(27, NZ, NY, NX), in_specs=[VM...  1.6 us
    pallas_call x1, Pallas kernels, shards(): pl.pallas_call(third_kernel, out_shape=[shape(CHANNELS, ROWS, 128), shape...  1.42 us
    pallas_call x1, Pallas kernels, shards(): pl.pallas_call(first_kernel, out_shape=[shape(CHANNELS * NZ * 8, 128), sh...  1.33 us
    pallas_call x1, Pallas kernels, shards(): pl.pallas_call(block_kernel, out_shape=shape(27, UNITS * 8, 128), in_spec...  0.64 us
  transfers between devices with their start and end apart: 5, of which 3 were waited for; matrix products, arithmetic and copies ran while one was open for 0% of the time, Pallas kernels for 2%

profile of v7, /device:TPU:1, one launch (start us, length us, event | category | flops | bytes accessed | tf_op | source)
XLA Modules:
  0.0 26.8 jit_solution(12519836426943608191)
XLA Ops:
  0.0 1.3 %collide.1 = (f32[928,128]{1,0:T(8,128)S(1)}, f32[152,128]{1,0:T(8,128)S(1)}, f32[152,128]{1,0:T(8,128)S(1)}) custom-call(f32[27,4,8,128]{3,2,1,0:T(8,128)} %pops_at.1, s32[4,8,128]{2,1,0:T(8,128)} %solid_at.1, f32[4,8]{1,0:T(4,128)} %bitcast.1, s32[8]{0:T(128)} %index_at.1), custom_call_target="tpu_custom_call" | custom-call | tf_op jit(solution)/shard_map/collide/pallas_call | solution.py:412
  1.3 2.2 %collective-permute-start = (f32[152,128]{1,0:T(8,128)S(1)}, f32[152,128]{1,0:T(8,128)S(1)}, u32[]{:S(2)}, u32[]{:S(2)}) collective-permute-start(f32[152,128]{1,0:T(8,128)S(1)} %get-tuple-element.14), channel_id=1, source_target_pairs={{0,4},{8,12},{4,0},{12,8},{1,5},{9,13},{5,1},{13,9},{2,6},{10,14},... | collective-permute-start | bytes 233480 | tf_op jit(solution)/shard_map/ppermute | solution.py:404
  3.5 2.2 %collective-permute-start.1 = (f32[152,128]{1,0:T(8,128)S(1)}, f32[152,128]{1,0:T(8,128)S(1)}, u32[]{:S(2)}, u32[]{:S(2)}) collective-permute-start(f32[152,128]{1,0:T(8,128)S(1)} %get-tuple-element.15), channel_id=1, source_target_pairs={{4,8},{12,0},{8,4},{0,12},{5,9},{13,1},{9,5},{1,13},{6,10},{14,2},... | collective-permute-start | bytes 233480 | tf_op jit(solution)/shard_map/ppermute | solution.py:404
  5.7 0.0 collective-permute-done.y_one
  5.7 3.6 %collective-permute-done.1.y_two = f32[152,128]{1,0:T(8,128)S(1)} collective-permute-done((f32[152,128]{1,0:T(8,128)S(1)}, f32[152,128]{1,0:T(8,128)S(1)}, u32[]{:S(2)}, u32[]{:S(2)}) %collective-permute-start.1) | collective-permute-done | bytes 77856 | tf_op jit(solution)/shard_map/ppermute | solution.py:404
  9.4 4.7 %collective-permute-start.2 = (f32[416,128]{1,0:T(8,128)S(1)}, f32[416,128]{1,0:T(8,128)S(1)}, u32[]{:S(2)}, u32[]{:S(2)}) collective-permute-start(f32[416,128]{1,0:T(8,128)S(1)} %get-tuple-element.16), channel_id=1, source_target_pairs={{1,2},{2,1},{5,6},{6,5},{9,10},{10,9},{13,14},{14,13},{17,18},{18,... | collective-permute-start | bytes 638984 | tf_op jit(solution)/shard_map/ppermute | solution.py:404
  14.1 0.1 collective-permute-start.3
  14.1 3.4 %collective-permute-done.2.z_two = f32[416,128]{1,0:T(8,128)S(1)} collective-permute-done((f32[416,128]{1,0:T(8,128)S(1)}, f32[416,128]{1,0:T(8,128)S(1)}, u32[]{:S(2)}, u32[]{:S(2)}) %collective-permute-start.2) | collective-permute-done | bytes 213024 | tf_op jit(solution)/shard_map/ppermute | solution.py:404
  17.6 0.0 collective-permute-done.3.z_one
  17.6 1.4 %pack_x.1 = (f32[29,112,128]{2,1,0:T(8,128)S(1)}, f32[144,128]{1,0:T(8,128)S(1)}, f32[2,56,128]{2,1,0:T(8,128)}) custom-call(f32[928,128]{1,0:T(8,128)S(1)} %get-tuple-element.13.own, f32[152,128]{1,0:T(8,128)S(1)} %collective-permute-done.y_one, f32[152,128]{1,0:T(8,128)S(1)} %collective-permute-done.1.y_two, f32[416,128]{1,0:T(8,128)S(1)} %collective-permute-done.2.z_two, ...), custom_call_target="tpu_custom_call" | custom-call | tf_op jit(solution)/shard_map/pack_x/pallas_call | solution.py:439
  19.0 3.3 %all-to-all-start = ((f32[2,56,128]{2,1,0:T(8,128)}), f32[2,56,128]{2,1,0:T(8,128)S(1)}, u32[]{:S(2)}, u32[]{:S(2)}) async-start(f32[2,56,128]{2,1,0:T(8,128)} %get-tuple-element.20), calls=%async_computation | async-start | bytes 114688 | tf_op jit(solution)/shard_map/all_to_all | solution.py:449
  22.3 0.6 %block.1 = f32[27,72,128]{2,1,0:T(8,128)S(1)} custom-call(f32[29,112,128]{2,1,0:T(8,128)S(1)} %get-tuple-element.18.full), custom_call_target="tpu_custom_call" | custom-call | flops 4976640 | bytes 4194304 | tf_op jit(solution)/shard_map/block/pallas_call | solution.py:452
  22.9 2.3 %all-to-all-done.x_one.x_two = f32[2,56,128]{2,1,0:T(8,128)S(1)} async-done(((f32[2,56,128]{2,1,0:T(8,128)}), f32[2,56,128]{2,1,0:T(8,128)S(1)}, u32[]{:S(2)}, u32[]{:S(2)}) %all-to-all-start) | async-done | bytes 57376 | tf_op jit(solution)/shard_map/all_to_all | solution.py:449
  25.2 1.6 %finish.1 = f32[27,4,8,128]{3,2,1,0:T(8,128)} custom-call(f32[29,112,128]{2,1,0:T(8,128)S(1)} %get-tuple-element.18.full, f32[27,72,128]{2,1,0:T(8,128)S(1)} %block.1, f32[144,128]{1,0:T(8,128)S(1)} %get-tuple-element.19.columns, f32[2,56,128]{2,1,0:T(8,128)S(1)} %all-to-all-done.x_one.x_two, f32[2,56,128]{2,1,0:T(8,128)S(1)} %all-to-all-done.x_one.x_two), custom_call_target="tpu_custom_call" | custom-call | tf_op jit(solution)/shard_map/finish/pallas_call | solution.py:464
  (1 shorter events, 0.0 us)
Async XLA Ops:
  1.3 4.4 %collective-permute-start = (f32[152,128]{1,0:T(8,128)S(1)}, f32[152,128]{1,0:T(8,128)S(1)}, u32[]{:S(2)}, u32[]{:S(2)}) collective-permute-start(f32[152,128]{1,0:T(8,128)S(1)} %get-tuple-element.14), channel_id=1, source_target_pairs={{0,4},{8,12},{4,0},{12,8},{1,5},{9,13},{5,1},{13,9},{2,6},{10,14},... | collective-permute-start | bytes 233480 | tf_op jit(solution)/shard_map/ppermute | solution.py:404
  3.5 5.8 %collective-permute-start.1 = (f32[152,128]{1,0:T(8,128)S(1)}, f32[152,128]{1,0:T(8,128)S(1)}, u32[]{:S(2)}, u32[]{:S(2)}) collective-permute-start(f32[152,128]{1,0:T(8,128)S(1)} %get-tuple-element.15), channel_id=1, source_target_pairs={{4,8},{12,0},{8,4},{0,12},{5,9},{13,1},{9,5},{1,13},{6,10},{14,2},... | collective-permute-start | bytes 233480 | tf_op jit(solution)/shard_map/ppermute | solution.py:404
  9.4 8.2 %collective-permute-start.2 = (f32[416,128]{1,0:T(8,128)S(1)}, f32[416,128]{1,0:T(8,128)S(1)}, u32[]{:S(2)}, u32[]{:S(2)}) collective-permute-start(f32[416,128]{1,0:T(8,128)S(1)} %get-tuple-element.16), channel_id=1, source_target_pairs={{1,2},{2,1},{5,6},{6,5},{9,10},{10,9},{13,14},{14,13},{17,18},{18,... | collective-permute-start | bytes 638984 | tf_op jit(solution)/shard_map/ppermute | solution.py:404
  14.1 3.5 %collective-permute-start.3 = (f32[416,128]{1,0:T(8,128)S(1)}, f32[416,128]{1,0:T(8,128)S(1)}, u32[]{:S(2)}, u32[]{:S(2)}) collective-permute-start(f32[416,128]{1,0:T(8,128)S(1)} %get-tuple-element.17), channel_id=1, source_target_pairs={{0,1},{2,3},{1,0},{3,2},{4,5},{6,7},{5,4},{7,6},{8,9},{10,11},{9,8... | collective-permute-start | bytes 638984 | tf_op jit(solution)/shard_map/ppermute | solution.py:404
  19.0 6.2 %all-to-all-start = ((f32[2,56,128]{2,1,0:T(8,128)}), f32[2,56,128]{2,1,0:T(8,128)S(1)}, u32[]{:S(2)}, u32[]{:S(2)}) async-start(f32[2,56,128]{2,1,0:T(8,128)} %get-tuple-element.20), calls=%async_computation | async-start | bytes 114688 | tf_op jit(solution)/shard_map/all_to_all | solution.py:449

commit v8 on v5

--- a/solution.py
+++ b/solution.py
@@ -118,16 +118,16 @@
     pl.when(jnp.logical_not(even))(lambda: body(two, one))
 
 
-def first_kernel(pops_at, solid_at, table_at, index_at, own, one, two, pops, solid, table, index, sems):
+def first_kernel(pops_at, solid_at, table_at, index_at, own, two, one, pops, solid, table, index, sems):
+    small = ((table_at, table), (index_at, index), (solid_at, solid))
+    planes = [(pops_at.at[:, z], pops.at[:, z]) for z in range(NZ)]
     copies = [
         pltpu.make_async_copy(source, target, sems.at[i])
-        for i, (source, target) in enumerate(
-            ((pops_at, pops), (solid_at, solid), (table_at, table), (index_at, index))
-        )
+        for i, (source, target) in enumerate((*small, *planes))
     ]
     for copy in copies:
         copy.start()
-    for copy in copies:
+    for copy in copies[:3]:
         copy.wait()
     lanes, rows = lane_ids(), row_ids()
     sponge = (lax.axis_index("gx") * NX + lanes) < SPONGE
@@ -135,6 +135,7 @@
         aim = jnp.zeros((8, 128), F32)
         for y in range(NY):
             aim = jnp.where(rows == y, table[z, index[y]], aim)
+        copies[3 + z].wait()
         post = relaxed([pops[q, z] for q in range(27)], sponge, aim)
         for q in range(27):
             own[pl.ds((q * NZ + z) * 8, 8), :] = post[q]
@@ -152,7 +153,7 @@
     by_parity("gy", one, two, pack)
 
 
-def second_kernel(own, y_one, y_two, z_two, z_one):
+def second_kernel(own, y_two, y_one, z_two, z_one):
     by_parity(
         "gy",
         y_one,
@@ -223,7 +224,7 @@
                 full[WALL, pl.ds(plane_at(z) + row, 1), :] = halo[pl.ds(k * Z_PITCH + first, 1), :]
 
 
-def third_kernel(own, y_one, y_two, z_two, z_one, full, columns, message, pack):
+def third_kernel(own, y_two, y_one, z_two, z_one, full, columns, message, pack):
     last = lax.axis_size("gz") - 1
     here = lax.axis_index("gz")
     for c in range(CHANNELS):
@@ -406,7 +407,7 @@
 
 
 def shards(pops, solid, profile_table, profile_index):
-    own, y_one, y_two = pl.pallas_call(
+    own, y_two, y_one = pl.pallas_call(
         first_kernel,
         out_shape=[shape(CHANNELS * NZ * 8, 128), shape(Y_ROWS, 128), shape(Y_ROWS, 128)],
         in_specs=[HBM] * 4,
@@ -416,7 +417,7 @@
             pltpu.VMEM(solid.shape, jnp.int32),
             pltpu.SMEM(profile_table.shape[::-1], F32),
             pltpu.SMEM(profile_index.shape, jnp.int32),
-            pltpu.SemaphoreType.DMA((4,)),
+            pltpu.SemaphoreType.DMA((3 + NZ,)),
         ],
         compiler_params=PARAMS,
         name="collide",
@@ -430,7 +431,7 @@
         out_specs=[VMEM] * 2,
         compiler_params=PARAMS,
         name="pack_z",
-    )(own, y_one, y_two)
+    )(own, y_two, y_one)
     z_two = swap(z_two, "gz", 1, False)
     z_one = swap(z_one, "gz", 0, False)
     full, columns, message = pl.pallas_call(
@@ -441,7 +442,7 @@
         scratch_shapes=[pltpu.VMEM((128, 128), F32)],
         compiler_params=PARAMS,
         name="pack_x",
-    )(own, y_one, y_two, z_two, z_one)
+    )(own, y_two, y_one, z_two, z_one)
     x_one = swap(message, "gx", 0, True)
     x_two = x_one if lax.axis_size("gx") == 2 else swap(message, "gx", 1, True)
     block = pl.pallas_call(

time: 23.2 us -> 23.2 us (level)
  transfers between devices with their start and end apart: 5 -> 5, of which waited for: 3 -> 4; matrix products, arithmetic and copies ran while one was open for 0% -> 0% of each run, Pallas kernels for 3% -> 3%
where the time goes in v8:
time: 23.2 us; the launch traced here: 22.7 us
  starting transfers between devices  10.3 us (44%)
  waiting for transfers between devices  7.99 us (34%)
  Pallas kernels  4.43 us (19%)
    ppermute x5, starting transfers between devices, swap(): return lax.ppermute(value, axis, pairs + [(j, i) for i, j in pairs])  10.3 us
    ppermute x5, waiting for transfers between devices, swap(): return lax.ppermute(value, axis, pairs + [(j, i) for i, j in pairs])  7.99 us
    pallas_call x1, Pallas kernels, shards(): pl.pallas_call(last_kernel, out_shape=shape(27, NZ, NY, NX), in_specs=[VM...  1.59 us
    pallas_call x1, Pallas kernels, shards(): pl.pallas_call(first_kernel, out_shape=[shape(CHANNELS * NZ * 8, 128), sh...  1.34 us
    pallas_call x1, Pallas kernels, shards(): pl.pallas_call(third_kernel, out_shape=[shape(CHANNELS, ROWS, 128), shape...  0.77 us
    pallas_call x1, Pallas kernels, shards(): pl.pallas_call(block_kernel, out_shape=shape(27, UNITS * 8, 128), in_spec...  0.69 us
  transfers between devices with their start and end apart: 5, of which 4 were waited for; matrix products, arithmetic and copies ran while one was open for 0% of the time, Pallas kernels for 3%

profile of v8, /device:TPU:1, one launch (start us, length us, event | category | flops | bytes accessed | tf_op | source)
XLA Modules:
  0.0 22.7 jit_solution(14420148134649459293)
XLA Ops:
  0.0 1.3 %collide.1 = (f32[928,128]{1,0:T(8,128)S(1)}, f32[152,128]{1,0:T(8,128)S(1)}, f32[152,128]{1,0:T(8,128)S(1)}) custom-call(f32[27,4,8,128]{3,2,1,0:T(8,128)} %pops_at.1, s32[4,8,128]{2,1,0:T(8,128)} %solid_at.1, f32[4,8]{1,0:T(4,128)} %bitcast.1, s32[8]{0:T(128)} %index_at.1), custom_call_target="tpu_custom_call" | custom-call | tf_op jit(solution)/shard_map/collide/pallas_call | solution.py:410
  1.3 4.2 %collective-permute-start = (f32[152,128]{1,0:T(8,128)S(1)}, f32[152,128]{1,0:T(8,128)S(1)}, u32[]{:S(2)}, u32[]{:S(2)}) collective-permute-start(f32[152,128]{1,0:T(8,128)S(1)} %get-tuple-element.14), channel_id=1, source_target_pairs={{4,8},{12,0},{8,4},{0,12},{5,9},{13,1},{9,5},{1,13},{6,10},{14,2},... | collective-permute-start | bytes 233480 | tf_op jit(solution)/shard_map/ppermute | solution.py:402
  5.6 0.0 collective-permute-start.1
  5.6 1.8 %collective-permute-done.y_two = f32[152,128]{1,0:T(8,128)S(1)} collective-permute-done((f32[152,128]{1,0:T(8,128)S(1)}, f32[152,128]{1,0:T(8,128)S(1)}, u32[]{:S(2)}, u32[]{:S(2)}) %collective-permute-start) | collective-permute-done | bytes 77856 | tf_op jit(solution)/shard_map/ppermute | solution.py:402
  7.4 1.9 %collective-permute-done.1.y_one = f32[152,128]{1,0:T(8,128)S(1)} collective-permute-done((f32[152,128]{1,0:T(8,128)S(1)}, f32[152,128]{1,0:T(8,128)S(1)}, u32[]{:S(2)}, u32[]{:S(2)}) %collective-permute-start.1) | collective-permute-done | bytes 77856 | tf_op jit(solution)/shard_map/ppermute | solution.py:402
  9.4 4.7 %collective-permute-start.2 = (f32[416,128]{1,0:T(8,128)S(1)}, f32[416,128]{1,0:T(8,128)S(1)}, u32[]{:S(2)}, u32[]{:S(2)}) collective-permute-start(f32[416,128]{1,0:T(8,128)S(1)} %get-tuple-element.16), channel_id=1, source_target_pairs={{1,2},{2,1},{5,6},{6,5},{9,10},{10,9},{13,14},{14,13},{17,18},{18,... | collective-permute-start | bytes 638984 | tf_op jit(solution)/shard_map/ppermute | solution.py:402
  14.0 0.1 collective-permute-start.3
  14.1 3.4 %collective-permute-done.2.z_two = f32[416,128]{1,0:T(8,128)S(1)} collective-permute-done((f32[416,128]{1,0:T(8,128)S(1)}, f32[416,128]{1,0:T(8,128)S(1)}, u32[]{:S(2)}, u32[]{:S(2)}) %collective-permute-start.2) | collective-permute-done | bytes 213024 | tf_op jit(solution)/shard_map/ppermute | solution.py:402
  17.6 0.0 collective-permute-done.3.z_one
  17.6 0.8 %pack_x.1 = (f32[29,112,128]{2,1,0:T(8,128)S(1)}, f32[144,128]{1,0:T(8,128)S(1)}, f32[56,128]{1,0:T(8,128)S(1)}) custom-call(f32[928,128]{1,0:T(8,128)S(1)} %get-tuple-element.13.own, f32[152,128]{1,0:T(8,128)S(1)} %collective-permute-done.y_two, f32[152,128]{1,0:T(8,128)S(1)} %collective-permute-done.1.y_one, f32[416,128]{1,0:T(8,128)S(1)} %collective-permute-done.2.z_two, ...), custom_call_target="tpu_custom_call" | custom-call | tf_op jit(solution)/shard_map/pack_x/pallas_call | solution.py:437
  18.3 1.3 %collective-permute-start.4 = (f32[56,128]{1,0:T(8,128)S(1)}, f32[56,128]{1,0:T(8,128)S(1)}, u32[]{:S(2)}, u32[]{:S(2)}) collective-permute-start(f32[56,128]{1,0:T(8,128)S(1)} %get-tuple-element.20), channel_id=1, source_target_pairs={{0,16},{16,0},{1,17},{17,1},{2,18},{18,2},{3,19},{19,3},{4,20},{20... | collective-permute-start | bytes 86024 | tf_op jit(solution)/shard_map/ppermute | solution.py:402
  19.6 0.7 %block.1 = f32[27,72,128]{2,1,0:T(8,128)S(1)} custom-call(f32[29,112,128]{2,1,0:T(8,128)S(1)} %get-tuple-element.18.full), custom_call_target="tpu_custom_call" | custom-call | flops 4976640 | bytes 4194304 | tf_op jit(solution)/shard_map/block/pallas_call | solution.py:448
  20.3 0.8 %collective-permute-done.4.x_one.x_two = f32[56,128]{1,0:T(8,128)S(1)} collective-permute-done((f32[56,128]{1,0:T(8,128)S(1)}, f32[56,128]{1,0:T(8,128)S(1)}, u32[]{:S(2)}, u32[]{:S(2)}) %collective-permute-start.4) | collective-permute-done | bytes 28704 | tf_op jit(solution)/shard_map/ppermute | solution.py:402
  21.1 1.6 %finish.1 = f32[27,4,8,128]{3,2,1,0:T(8,128)} custom-call(f32[29,112,128]{2,1,0:T(8,128)S(1)} %get-tuple-element.18.full, f32[27,72,128]{2,1,0:T(8,128)S(1)} %block.1, f32[144,128]{1,0:T(8,128)S(1)} %get-tuple-element.19.columns, f32[56,128]{1,0:T(8,128)S(1)} %collective-permute-done.4.x_one.x_two, f32[56,128]{1,0:T(8,128)S(1)} %collective-permute-done.4.x_one.x_two), custom_call_target="tpu_custom_call" | custom-call | tf_op jit(solution)/shard_map/finish/pallas_call | solution.py:460
  (1 shorter events, 0.0 us)
Async XLA Ops:
  1.3 6.1 %collective-permute-start = (f32[152,128]{1,0:T(8,128)S(1)}, f32[152,128]{1,0:T(8,128)S(1)}, u32[]{:S(2)}, u32[]{:S(2)}) collective-permute-start(f32[152,128]{1,0:T(8,128)S(1)} %get-tuple-element.14), channel_id=1, source_target_pairs={{4,8},{12,0},{8,4},{0,12},{5,9},{13,1},{9,5},{1,13},{6,10},{14,2},... | collective-permute-start | bytes 233480 | tf_op jit(solution)/shard_map/ppermute | solution.py:402
  5.6 3.8 %collective-permute-start.1 = (f32[152,128]{1,0:T(8,128)S(1)}, f32[152,128]{1,0:T(8,128)S(1)}, u32[]{:S(2)}, u32[]{:S(2)}) collective-permute-start(f32[152,128]{1,0:T(8,128)S(1)} %get-tuple-element.15), channel_id=1, source_target_pairs={{0,4},{8,12},{4,0},{12,8},{1,5},{9,13},{5,1},{13,9},{2,6},{10,14},... | collective-permute-start | bytes 233480 | tf_op jit(solution)/shard_map/ppermute | solution.py:402
  9.4 8.2 %collective-permute-start.2 = (f32[416,128]{1,0:T(8,128)S(1)}, f32[416,128]{1,0:T(8,128)S(1)}, u32[]{:S(2)}, u32[]{:S(2)}) collective-permute-start(f32[416,128]{1,0:T(8,128)S(1)} %get-tuple-element.16), channel_id=1, source_target_pairs={{1,2},{2,1},{5,6},{6,5},{9,10},{10,9},{13,14},{14,13},{17,18},{18,... | collective-permute-start | bytes 638984 | tf_op jit(solution)/shard_map/ppermute | solution.py:402
  14.0 3.5 %collective-permute-start.3 = (f32[416,128]{1,0:T(8,128)S(1)}, f32[416,128]{1,0:T(8,128)S(1)}, u32[]{:S(2)}, u32[]{:S(2)}) collective-permute-start(f32[416,128]{1,0:T(8,128)S(1)} %get-tuple-element.17), channel_id=1, source_target_pairs={{0,1},{2,3},{1,0},{3,2},{4,5},{6,7},{5,4},{7,6},{8,9},{10,11},{9,8... | collective-permute-start | bytes 638984 | tf_op jit(solution)/shard_map/ppermute | solution.py:402
  18.3 2.8 %collective-permute-start.4 = (f32[56,128]{1,0:T(8,128)S(1)}, f32[56,128]{1,0:T(8,128)S(1)}, u32[]{:S(2)}, u32[]{:S(2)}) collective-permute-start(f32[56,128]{1,0:T(8,128)S(1)} %get-tuple-element.20), channel_id=1, source_target_pairs={{0,16},{16,0},{1,17},{17,1},{2,18},{18,2},{3,19},{19,3},{4,20},{20... | collective-permute-start | bytes 86024 | tf_op jit(solution)/shard_map/ppermute | solution.py:402

commit v9 on v8

--- a/solution.py
+++ b/solution.py
@@ -32,8 +32,7 @@
 
 Y_ROWS = (CHANNELS + 9) * NZ
 Z_BLOCKS = CHANNELS + 10
-Z_PITCH = NY + 2
-Z_FAR = Z_BLOCKS * Z_PITCH
+Z_FAR = 2 * Z_BLOCKS
 Z_ROWS = -(-(Z_FAR + 2 * 12) // 8) * 8
 
 X_ROWS = 2 * (WALL + 1)
@@ -118,7 +117,13 @@
     pl.when(jnp.logical_not(even))(lambda: body(two, one))
 
 
-def first_kernel(pops_at, solid_at, table_at, index_at, own, two, one, pops, solid, table, index, sems):
+def z_blocks(near, far, part):
+    blocks = [(c, near) for c in range(CHANNELS)]
+    return blocks + [(9 * part + k, far) for k in range(9)] + [(WALL, far)]
+
+
+def first_kernel(pops_at, solid_at, table_at, index_at, own, two, one, *scratch):
+    pops, solid, table, index, sems = scratch
     small = ((table_at, table), (index_at, index), (solid_at, solid))
     planes = [(pops_at.at[:, z], pops.at[:, z]) for z in range(NZ)]
     copies = [
@@ -153,6 +158,15 @@
     by_parity("gy", one, two, pack)
 
 
+def ahead_kernel(own, two, one):
+    def pack(zup, zdown):
+        for out, first, second, part in ((zup, NZ - 1, NZ - 2, 2), (zdown, 0, 1, 0)):
+            for k, (c, z) in enumerate(z_blocks(first, second, part)):
+                out[pl.ds(8 * k, 8), :] = own[pl.ds((c * NZ + z) * 8, 8), :]
+
+    by_parity("gz", one, two, pack)
+
+
 def second_kernel(own, y_two, y_one, z_two, z_one):
     by_parity(
         "gy",
@@ -166,21 +180,11 @@
 
 def pack_planes(own, below, above, zup, zdown):
     for out, first, second, part in ((zup, NZ - 1, NZ - 2, 2), (zdown, 0, 1, 0)):
-        for k in range(Z_BLOCKS):
-            channel, z = (k, first) if k < CHANNELS else (9 * part + k - CHANNELS, second)
-            if k == Z_BLOCKS - 1:
-                channel = WALL
-            out[pl.ds(k * Z_PITCH + 1, 8), :] = own[pl.ds((channel * NZ + z) * 8, 8), :]
-        for side, (halo, near, group) in enumerate(((below, 0, 2), (above, Z_PITCH - 1, 0))):
-            out[pl.ds(near, CHANNELS, stride=Z_PITCH), :] = halo[
-                pl.ds(first, CHANNELS, stride=NZ), :
-            ]
-            out[pl.ds(CHANNELS * Z_PITCH + near, 9, stride=Z_PITCH), :] = halo[
-                pl.ds(9 * part * NZ + second, 9, stride=NZ), :
-            ]
-            out[pl.ds((Z_BLOCKS - 1) * Z_PITCH + near, 1), :] = halo[
-                pl.ds(WALL * NZ + second, 1), :
-            ]
+        for side, halo in enumerate((below, above)):
+            near = side * Z_BLOCKS
+            out[pl.ds(near, CHANNELS), :] = halo[pl.ds(first, CHANNELS, stride=NZ), :]
+            out[pl.ds(near + CHANNELS, 9), :] = halo[pl.ds(9 * part * NZ + second, 9, stride=NZ), :]
+            out[pl.ds(near + Z_BLOCKS - 1, 1), :] = halo[pl.ds(WALL * NZ + second, 1), :]
             far = Z_FAR + 12 * side
             out[pl.ds(far, 9), :] = halo[pl.ds(CHANNELS * NZ + first, 9, stride=NZ), :]
             out[pl.ds(far + 9, 3), :] = halo[
@@ -205,12 +209,18 @@
         full[WALL, pl.ds(plane_at(0) + far, NZ, stride=PITCH), :] = halo[pl.ds(WALL * NZ, NZ), :]
 
 
+def add_own_planes(full, ceiling, floor):
+    for halo, near, far, part in ((floor, -1, -2, 2), (ceiling, NZ, NZ + 1, 0)):
+        for k, (c, z) in enumerate(z_blocks(near, far, part)):
+            full[c, pl.ds(plane_at(z) + 2, 8), :] = halo[pl.ds(8 * k, 8), :]
+
+
 def add_planes(full, ceiling, floor):
     for halo, near, far, part in ((floor, -1, -2, 2), (ceiling, NZ, NZ + 1, 0)):
-        blocks = [(c, near) for c in range(CHANNELS)]
-        blocks += [(9 * part + k, far) for k in range(9)] + [(WALL, far)]
-        for k, (c, z) in enumerate(blocks):
-            full[c, pl.ds(plane_at(z) + 1, Z_PITCH), :] = halo[pl.ds(k * Z_PITCH, Z_PITCH), :]
+        for k, (c, z) in enumerate(z_blocks(near, far, part)):
+            for side, row in enumerate((1, PITCH - 2)):
+                start = side * Z_BLOCKS + k
+                full[c, pl.ds(plane_at(z) + row, 1), :] = halo[pl.ds(start, 1), :]
         for side, (row, group) in enumerate(((0, 2), (PITCH - 1, 0))):
             start = Z_FAR + 12 * side
             for k in range(9):
@@ -219,18 +229,19 @@
             for k in range(3):
                 q = 9 * part + 3 * group + k
                 full[q, pl.ds(plane_at(far) + row, 1), :] = halo[pl.ds(start + 9 + k, 1), :]
-            first = 0 if side == 0 else Z_PITCH - 1
             for k, z in ((WALL, near), (Z_BLOCKS - 1, far)):
-                full[WALL, pl.ds(plane_at(z) + row, 1), :] = halo[pl.ds(k * Z_PITCH + first, 1), :]
-
-
-def third_kernel(own, y_two, y_one, z_two, z_one, full, columns, message, pack):
+                flag = halo[pl.ds(side * Z_BLOCKS + k, 1), :]
+                full[WALL, pl.ds(plane_at(z) + row, 1), :] = flag
+
+
+def third_kernel(own, y_two, y_one, two, one, z_two, z_one, full, columns, message, pack):
     last = lax.axis_size("gz") - 1
     here = lax.axis_index("gz")
     for c in range(CHANNELS):
         for z in range(NZ):
             full[c, pl.ds(plane_at(z) + 2, 8), :] = own[pl.ds((c * NZ + z) * 8, 8), :]
     by_parity("gy", y_one, y_two, functools.partial(add_rows, full))
+    by_parity("gz", one, two, functools.partial(add_own_planes, full))
     by_parity("gz", z_one, z_two, functools.partial(add_planes, full))
 
     @pl.when(here == 0)
@@ -424,12 +435,23 @@
     )(*(pltpu.with_memory_space_constraint(a, pltpu.HBM) for a in (pops, solid, profile_table.T, profile_index)))
     y_two = swap(y_two, "gy", 1, True)
     y_one = swap(y_one, "gy", 0, True)
+    own_two, own_one = pl.pallas_call(
+        ahead_kernel,
+        out_shape=[shape(Z_BLOCKS * 8, 128)] * 2,
+        in_specs=[VMEM],
+        out_specs=[VMEM] * 2,
+        compiler_params=PARAMS,
+        name="pack_own",
+    )(own)
+    own_two = swap(own_two, "gz", 1, False)
+    own_one = swap(own_one, "gz", 0, False)
     z_two, z_one = pl.pallas_call(
         second_kernel,
         out_shape=[shape(Z_ROWS, 128)] * 2,
         in_specs=[VMEM] * 3,
         out_specs=[VMEM] * 2,
         compiler_params=PARAMS,
+        cost_estimate=pl.CostEstimate(flops=10**9, bytes_accessed=2**20, transcendentals=0),
         name="pack_z",
     )(own, y_two, y_one)
     z_two = swap(z_two, "gz", 1, False)
@@ -437,12 +459,12 @@
     full, columns, message = pl.pallas_call(
         third_kernel,
         out_shape=[shape(CHANNELS, ROWS, 128), shape(PAD + 128 + PAD, 128), shape(X_ROWS, 128)],
-        in_specs=[VMEM] * 5,
+        in_specs=[VMEM] * 7,
         out_specs=[VMEM] * 3,
         scratch_shapes=[pltpu.VMEM((128, 128), F32)],
         compiler_params=PARAMS,
         name="pack_x",
-    )(own, y_two, y_one, z_two, z_one)
+    )(own, y_two, y_one, own_two, own_one, z_two, z_one)
     x_one = swap(message, "gx", 0, True)
     x_two = x_one if lax.axis_size("gx") == 2 else swap(message, "gx", 1, True)
     block = pl.pallas_call(

time: 23.2 us -> 22.2 us (0.957)
  the two profiles are of different devices: /device:TPU:1 before, /device:TPU:0 now
where the time goes in v9:
time: 22.2 us; the launch traced here: 22 us
  starting transfers between devices  13.9 us (63%)
  Pallas kernels  4.47 us (20%)
  waiting for transfers between devices  3.53 us (16%)
    ppermute x7, starting transfers between devices, swap(): return lax.ppermute(value, axis, pairs + [(j, i) for i, j in pairs])  13.9 us
    ppermute x7, waiting for transfers between devices, swap(): return lax.ppermute(value, axis, pairs + [(j, i) for i, j in pairs])  3.53 us
    pallas_call x1, Pallas kernels, shards(): pl.pallas_call(last_kernel, out_shape=shape(27, NZ, NY, NX), in_specs=[VM...  1.59 us
    pallas_call x1, Pallas kernels, shards(): pl.pallas_call(first_kernel, out_shape=[shape(CHANNELS * NZ * 8, 128), sh...  1.34 us
    pallas_call x1, Pallas kernels, shards(): pl.pallas_call(third_kernel, out_shape=[shape(CHANNELS, ROWS, 128), shape...  0.8 us
    pallas_call x1, Pallas kernels, shards(): pl.pallas_call(block_kernel, out_shape=shape(27, UNITS * 8, 128), in_spec...  0.69 us
  transfers between devices with their start and end apart: 7, of which 3 were waited for; matrix products, arithmetic and copies ran while one was open for 0% of the time, Pallas kernels for 3%

profile of v9, /device:TPU:0, one launch (start us, length us, event | category | flops | bytes accessed | tf_op | source)
XLA Modules:
  0.0 22.0 jit_solution(4829548392759208764)
XLA Ops:
  0.0 1.3 %collide.1 = (f32[928,128]{1,0:T(8,128)S(1)}, f32[152,128]{1,0:T(8,128)S(1)}, f32[152,128]{1,0:T(8,128)S(1)}) custom-call(f32[27,4,8,128]{3,2,1,0:T(8,128)} %pops_at.1, s32[4,8,128]{2,1,0:T(8,128)} %solid_at.1, f32[4,8]{1,0:T(4,128)} %bitcast.1, s32[8]{0:T(128)} %index_at.1), custom_call_target="tpu_custom_call" | custom-call | tf_op jit(solution)/shard_map/collide/pallas_call | solution.py:421
  1.3 5.1 %collective-permute-start = (f32[152,128]{1,0:T(8,128)S(1)}, f32[152,128]{1,0:T(8,128)S(1)}, u32[]{:S(2)}, u32[]{:S(2)}) collective-permute-start(f32[152,128]{1,0:T(8,128)S(1)} %get-tuple-element.16), channel_id=1, source_target_pairs={{4,8},{12,0},{8,4},{0,12},{5,9},{13,1},{9,5},{1,13},{6,10},{14,2},... | collective-permute-start | bytes 233480 | tf_op jit(solution)/shard_map/ppermute | solution.py:413
  6.5 0.0 collective-permute-start.1
  6.5 0.7 %collective-permute-start.2 = (f32[312,128]{1,0:T(8,128)S(1)}, f32[312,128]{1,0:T(8,128)S(1)}, u32[]{:S(2)}, u32[]{:S(2)}) collective-permute-start(f32[312,128]{1,0:T(8,128)S(1)} %get-tuple-element.18), channel_id=1, source_target_pairs={{1,2},{2,1},{5,6},{6,5},{9,10},{10,9},{13,14},{14,13},{17,18},{18,... | collective-permute-start | bytes 479240 | tf_op jit(solution)/shard_map/ppermute | solution.py:413
  7.2 2.9 %collective-permute-start.3 = (f32[312,128]{1,0:T(8,128)S(1)}, f32[312,128]{1,0:T(8,128)S(1)}, u32[]{:S(2)}, u32[]{:S(2)}) collective-permute-start(f32[312,128]{1,0:T(8,128)S(1)} %get-tuple-element.19), channel_id=1, source_target_pairs={{0,1},{2,3},{1,0},{3,2},{4,5},{6,7},{5,4},{7,6},{8,9},{10,11},{9,8... | collective-permute-start | bytes 479240 | tf_op jit(solution)/shard_map/ppermute | solution.py:413
  10.1 0.0 collective-permute-done.y_two
  10.1 0.8 %collective-permute-done.1.y_one = f32[152,128]{1,0:T(8,128)S(1)} collective-permute-done((f32[152,128]{1,0:T(8,128)S(1)}, f32[152,128]{1,0:T(8,128)S(1)}, u32[]{:S(2)}, u32[]{:S(2)}) %collective-permute-start.1) | collective-permute-done | bytes 77856 | tf_op jit(solution)/shard_map/ppermute | solution.py:413
  10.9 0.7 %collective-permute-start.4 = (f32[104,128]{1,0:T(8,128)S(1)}, f32[104,128]{1,0:T(8,128)S(1)}, u32[]{:S(2)}, u32[]{:S(2)}) collective-permute-start(f32[104,128]{1,0:T(8,128)S(1)} %get-tuple-element.20), channel_id=1, source_target_pairs={{1,2},{2,1},{5,6},{6,5},{9,10},{10,9},{13,14},{14,13},{17,18},{18,... | collective-permute-start | bytes 159752 | tf_op jit(solution)/shard_map/ppermute | solution.py:413
  11.6 3.0 %collective-permute-start.5 = (f32[104,128]{1,0:T(8,128)S(1)}, f32[104,128]{1,0:T(8,128)S(1)}, u32[]{:S(2)}, u32[]{:S(2)}) collective-permute-start(f32[104,128]{1,0:T(8,128)S(1)} %get-tuple-element.21), channel_id=1, source_target_pairs={{0,1},{2,3},{1,0},{3,2},{4,5},{6,7},{5,4},{7,6},{8,9},{10,11},{9,8... | collective-permute-start | bytes 159752 | tf_op jit(solution)/shard_map/ppermute | solution.py:413
  14.5 0.0 collective-permute-done.4.z_two
  14.5 0.9 %collective-permute-done.5.z_one = f32[104,128]{1,0:T(8,128)S(1)} collective-permute-done((f32[104,128]{1,0:T(8,128)S(1)}, f32[104,128]{1,0:T(8,128)S(1)}, u32[]{:S(2)}, u32[]{:S(2)}) %collective-permute-start.5) | collective-permute-done | bytes 53280 | tf_op jit(solution)/shard_map/ppermute | solution.py:413
  15.4 0.0 collective-permute-done.2.two
  15.4 0.0 collective-permute-done.3.one
  15.4 0.8 %pack_x.1 = (f32[29,112,128]{2,1,0:T(8,128)S(1)}, f32[144,128]{1,0:T(8,128)S(1)}, f32[56,128]{1,0:T(8,128)S(1)}) custom-call(f32[928,128]{1,0:T(8,128)S(1)} %get-tuple-element.15.own, f32[152,128]{1,0:T(8,128)S(1)} %collective-permute-done.y_two, f32[152,128]{1,0:T(8,128)S(1)} %collective-permute-done.1.y_one, f32[312,128]{1,0:T(8,128)S(1)} %collective-permute-done.2.two, ...), custom_call_target="tpu_custom_call" | custom-call | tf_op jit(solution)/shard_map/pack_x/pallas_call | solution.py:459
  16.2 1.6 %collective-permute-start.6 = (f32[56,128]{1,0:T(8,128)S(1)}, f32[56,128]{1,0:T(8,128)S(1)}, u32[]{:S(2)}, u32[]{:S(2)}) collective-permute-start(f32[56,128]{1,0:T(8,128)S(1)} %get-tuple-element.24), channel_id=1, source_target_pairs={{0,16},{16,0},{1,17},{17,1},{2,18},{18,2},{3,19},{19,3},{4,20},{20... | collective-permute-start | bytes 86024 | tf_op jit(solution)/shard_map/ppermute | solution.py:413
  17.8 0.7 %block.1 = f32[27,72,128]{2,1,0:T(8,128)S(1)} custom-call(f32[29,112,128]{2,1,0:T(8,128)S(1)} %get-tuple-element.22.full), custom_call_target="tpu_custom_call" | custom-call | flops 4976640 | bytes 4194304 | tf_op jit(solution)/shard_map/block/pallas_call | solution.py:470
  18.5 1.9 %collective-permute-done.6.x_one.x_two = f32[56,128]{1,0:T(8,128)S(1)} collective-permute-done((f32[56,128]{1,0:T(8,128)S(1)}, f32[56,128]{1,0:T(8,128)S(1)}, u32[]{:S(2)}, u32[]{:S(2)}) %collective-permute-start.6) | collective-permute-done | bytes 28704 | tf_op jit(solution)/shard_map/ppermute | solution.py:413
  20.4 1.6 %finish.1 = f32[27,4,8,128]{3,2,1,0:T(8,128)} custom-call(f32[29,112,128]{2,1,0:T(8,128)S(1)} %get-tuple-element.22.full, f32[27,72,128]{2,1,0:T(8,128)S(1)} %block.1, f32[144,128]{1,0:T(8,128)S(1)} %get-tuple-element.23.columns, f32[56,128]{1,0:T(8,128)S(1)} %collective-permute-done.6.x_one.x_two, f32[56,128]{1,0:T(8,128)S(1)} %collective-permute-done.6.x_one.x_two), custom_call_target="tpu_custom_call" | custom-call | tf_op jit(solution)/shard_map/finish/pallas_call | solution.py:482
  (2 shorter events, 0.0 us)
Async XLA Ops:
  1.3 8.7 %collective-permute-start = (f32[152,128]{1,0:T(8,128)S(1)}, f32[152,128]{1,0:T(8,128)S(1)}, u32[]{:S(2)}, u32[]{:S(2)}) collective-permute-start(f32[152,128]{1,0:T(8,128)S(1)} %get-tuple-element.16), channel_id=1, source_target_pairs={{4,8},{12,0},{8,4},{0,12},{5,9},{13,1},{9,5},{1,13},{6,10},{14,2},... | collective-permute-start | bytes 233480 | tf_op jit(solution)/shard_map/ppermute | solution.py:413
  6.5 4.4 %collective-permute-start.1 = (f32[152,128]{1,0:T(8,128)S(1)}, f32[152,128]{1,0:T(8,128)S(1)}, u32[]{:S(2)}, u32[]{:S(2)}) collective-permute-start(f32[152,128]{1,0:T(8,128)S(1)} %get-tuple-element.17), channel_id=1, source_target_pairs={{0,4},{8,12},{4,0},{12,8},{1,5},{9,13},{5,1},{13,9},{2,6},{10,14},... | collective-permute-start | bytes 233480 | tf_op jit(solution)/shard_map/ppermute | solution.py:413
  6.5 8.9 %collective-permute-start.2 = (f32[312,128]{1,0:T(8,128)S(1)}, f32[312,128]{1,0:T(8,128)S(1)}, u32[]{:S(2)}, u32[]{:S(2)}) collective-permute-start(f32[312,128]{1,0:T(8,128)S(1)} %get-tuple-element.18), channel_id=1, source_target_pairs={{1,2},{2,1},{5,6},{6,5},{9,10},{10,9},{13,14},{14,13},{17,18},{18,... | collective-permute-start | bytes 479240 | tf_op jit(solution)/shard_map/ppermute | solution.py:413
  7.2 8.3 %collective-permute-start.3 = (f32[312,128]{1,0:T(8,128)S(1)}, f32[312,128]{1,0:T(8,128)S(1)}, u32[]{:S(2)}, u32[]{:S(2)}) collective-permute-start(f32[312,128]{1,0:T(8,128)S(1)} %get-tuple-element.19), channel_id=1, source_target_pairs={{0,1},{2,3},{1,0},{3,2},{4,5},{6,7},{5,4},{7,6},{8,9},{10,11},{9,8... | collective-permute-start | bytes 479240 | tf_op jit(solution)/shard_map/ppermute | solution.py:413
  10.9 3.7 %collective-permute-start.4 = (f32[104,128]{1,0:T(8,128)S(1)}, f32[104,128]{1,0:T(8,128)S(1)}, u32[]{:S(2)}, u32[]{:S(2)}) collective-permute-start(f32[104,128]{1,0:T(8,128)S(1)} %get-tuple-element.20), channel_id=1, source_target_pairs={{1,2},{2,1},{5,6},{6,5},{9,10},{10,9},{13,14},{14,13},{17,18},{18,... | collective-permute-start | bytes 159752 | tf_op jit(solution)/shard_map/ppermute | solution.py:413
  11.6 3.9 %collective-permute-start.5 = (f32[104,128]{1,0:T(8,128)S(1)}, f32[104,128]{1,0:T(8,128)S(1)}, u32[]{:S(2)}, u32[]{:S(2)}) collective-permute-start(f32[104,128]{1,0:T(8,128)S(1)} %get-tuple-element.21), channel_id=1, source_target_pairs={{0,1},{2,3},{1,0},{3,2},{4,5},{6,7},{5,4},{7,6},{8,9},{10,11},{9,8... | collective-permute-start | bytes 159752 | tf_op jit(solution)/shard_map/ppermute | solution.py:413
  16.2 4.1 %collective-permute-start.6 = (f32[56,128]{1,0:T(8,128)S(1)}, f32[56,128]{1,0:T(8,128)S(1)}, u32[]{:S(2)}, u32[]{:S(2)}) collective-permute-start(f32[56,128]{1,0:T(8,128)S(1)} %get-tuple-element.24), channel_id=1, source_target_pairs={{0,16},{16,0},{1,17},{17,1},{2,18},{18,2},{3,19},{19,3},{4,20},{20... | collective-permute-start | bytes 86024 | tf_op jit(solution)/shard_map/ppermute | solution.py:413

commit v10 on v9

--- a/solution.py
+++ b/solution.py
@@ -234,14 +234,32 @@
                 full[WALL, pl.ds(plane_at(z) + row, 1), :] = flag
 
 
-def third_kernel(own, y_two, y_one, two, one, z_two, z_one, full, columns, message, pack):
-    last = lax.axis_size("gz") - 1
-    here = lax.axis_index("gz")
+def pack_columns(full, pack, tiles):
+    slot = lane_ids() // 4
+    for t in tiles:
+        packed = jnp.zeros((8, 128), F32)
+        for c in range(CHANNELS):
+            moved = pltpu.roll(full[c, pl.ds(PAD + 8 * t, 8), :], (4 * c + 2) % 128, 1)
+            packed = jnp.where(slot == c, moved, packed)
+        pack[pl.ds(8 * t, 8), :] = packed
+
+
+OWN_TILES = range(2 * PITCH // 8, (NZ + 2) * PITCH // 8)
+
+
+def fill_kernel(own, y_two, y_one, two, one, full, pack):
     for c in range(CHANNELS):
         for z in range(NZ):
             full[c, pl.ds(plane_at(z) + 2, 8), :] = own[pl.ds((c * NZ + z) * 8, 8), :]
     by_parity("gy", y_one, y_two, functools.partial(add_rows, full))
     by_parity("gz", one, two, functools.partial(add_own_planes, full))
+    pack_columns(full, pack, OWN_TILES)
+    pack[pl.ds(FLAT, 128 - FLAT), :] = jnp.zeros((128 - FLAT, 128), F32)
+
+
+def third_kernel(part, packed, z_two, z_one, full, pack, columns, message):
+    last = lax.axis_size("gz") - 1
+    here = lax.axis_index("gz")
     by_parity("gz", z_one, z_two, functools.partial(add_planes, full))
 
     @pl.when(here == 0)
@@ -253,14 +271,7 @@
         for q in range(9):
             full[q, pl.ds(plane_at(NZ), PITCH), :] = full[q + 18, pl.ds(plane_at(NZ - 1), PITCH), :]
 
-    slot = lane_ids() // 4
-    pack[pl.ds(FLAT, 128 - FLAT), :] = jnp.zeros((128 - FLAT, 128), F32)
-    for t in range(FLAT // 8):
-        packed = jnp.zeros((8, 128), F32)
-        for c in range(CHANNELS):
-            moved = pltpu.roll(full[c, pl.ds(PAD + 8 * t, 8), :], (4 * c + 2) % 128, 1)
-            packed = jnp.where(slot == c, moved, packed)
-        pack[pl.ds(8 * t, 8), :] = packed
+    pack_columns(full, pack, [t for t in range(FLAT // 8) if t not in OWN_TILES])
     columns[pl.ds(PAD, 128), :] = pack[...].T
 
     def row(c, i, count):
@@ -317,7 +328,7 @@
             post[q, pl.ds((NZ + 1) * PITCH, PITCH), :] = post[q + 18, pl.ds(NZ * PITCH, PITCH), :]
 
 
-def last_kernel(full, block, columns, x_one, x_two, out, west, east, post, walls, back, done, sems):
+def last_kernel(full, block, columns, x_one, x_two, out, west, east, walls, back, done, sems):
     here_x, size_x = lax.axis_index("gx"), lax.axis_size("gx")
     top = lax.axis_index("gz") == lax.axis_size("gz") - 1
     lanes, rows = lane_ids(), row_ids()
@@ -360,29 +371,29 @@
     lid = top & (lanes >= (NZ + 2) * PITCH) & (lanes < (NZ + 3) * PITCH)
     for q in range(9):
         sides[q] = jnp.where(lid, pltpu.roll(sides[q + 18], PITCH, 1), sides[q])
-    sides.append(strip[WALL])
-    sides = [
-        jnp.where((rows == 1) | (rows == 5), pltpu.roll(side, 4, 0), side) for side in sides
-    ]
-    sides += [jnp.zeros((8, 128), F32)] * 4
+    ends = [jnp.where(rows == 1, pltpu.roll(side, 4, 0), side) for side in sides]
+    ends += [jnp.zeros((8, 128), F32)] * 5
     for i in range(2):
-        back[i] = jnp.concatenate(sides[16 * i : 16 * i + 16], axis=0).T
-
-    def column_at(c, place, lane, start):
-        value = back[c // 16, pl.ds(start, 8), :]
-        return pltpu.roll(value, (lane - 8 * (c % 16) - place) % 128, 1)
+        back[i] = jnp.concatenate(ends[16 * i : 16 * i + 16], axis=0).T
+    pairs = [jnp.where(rows < 4, sides[3 * k + 2], sides[3 * k]) for k in range(9)]
+    pairs += [strip[WALL]] + [jnp.zeros((8, 128), F32)] * 6
+    back[2] = jnp.concatenate(pairs, axis=0).T
+
+    def column_at(i, place, lane, start):
+        return pltpu.roll(back[i, pl.ds(start, 8), :], (lane - place) % 128, 1)
 
     rim = (lanes == 0) | (lanes == 127)
+
+    def rimmed(q, start):
+        ends = column_at(q // 16, 8 * (q % 16) + 2, 0, PITCH + start)
+        return jnp.where(rim, ends, block[q, pl.ds(start, 8), :])
+
     for u in range(UNITS):
-        for q in range(27):
-            post[q, pl.ds(8 * u, 8), :] = jnp.where(
-                rim, column_at(q, 2, 0, PITCH + 8 * u), block[q, pl.ds(8 * u, 8), :]
-            )
         flags = full[WALL, pl.ds(PAD + PITCH + 8 * u, 8), :]
         walls[1, pl.ds(8 * u, 8), :] = flags
-        for cx, edge, place in ((1, 0, 5), (-1, 127, 6)):
+        for cx, edge, place in ((1, 0, 73), (-1, 127, 78)):
             walls[cx + 1, pl.ds(8 * u, 8), :] = jnp.where(
-                lanes == edge, column_at(WALL, place, edge, PITCH + 8 * u), pltpu.roll(flags, cx % 128, 1)
+                lanes == edge, column_at(2, place, edge, PITCH + 8 * u), pltpu.roll(flags, cx % 128, 1)
             )
 
     copies = []
@@ -392,14 +403,17 @@
         for q in range(27):
             cx, cy, cz = VEL[q]
             start = cell - PITCH * cz - cy
-            value = post[q, pl.ds(start, 8), :]
-            if cx:
-                edge, place = (0, 5) if cx > 0 else (127, 6)
-                side = column_at(q, place, edge, PITCH + start)
-                value = jnp.where(lanes == edge, side, pltpu.roll(value, cx % 128, 1))
+            if cx > 0:
+                side = column_at(2, 8 * (q // 3) + 1, 0, PITCH + start)
+                value = jnp.where(lanes < 2, side, pltpu.roll(block[q, pl.ds(start, 8), :], 1, 1))
+            elif cx < 0:
+                side = column_at(2, 8 * (q // 3) + 5, 126, PITCH + start)
+                value = jnp.where(lanes > 125, side, pltpu.roll(block[q, pl.ds(start, 8), :], 127, 1))
+            else:
+                value = rimmed(q, start)
             if q != 13:
                 blocked = walls[cx + 1, pl.ds(start, 8), :] != 0.0
-                value = jnp.where(blocked, post[26 - q, pl.ds(cell, 8), :], value)
+                value = jnp.where(blocked, rimmed(26 - q, cell), value)
             done[q, z] = jnp.where(solid, WEIGHT[q], value)
         copies.append(pltpu.make_async_copy(done.at[:, z], out.at[:, z], sems.at[z]))
         copies[-1].start()
@@ -456,15 +470,29 @@
     )(own, y_two, y_one)
     z_two = swap(z_two, "gz", 1, False)
     z_one = swap(z_one, "gz", 0, False)
-    full, columns, message = pl.pallas_call(
+    part, packed = pl.pallas_call(
+        fill_kernel,
+        out_shape=[shape(CHANNELS, ROWS, 128), shape(128, 128)],
+        in_specs=[VMEM] * 5,
+        out_specs=[VMEM] * 2,
+        compiler_params=PARAMS,
+        cost_estimate=pl.CostEstimate(flops=10**6, bytes_accessed=2**22, transcendentals=0),
+        name="fill",
+    )(own, y_two, y_one, own_two, own_one)
+    full, packed, columns, message = pl.pallas_call(
         third_kernel,
-        out_shape=[shape(CHANNELS, ROWS, 128), shape(PAD + 128 + PAD, 128), shape(X_ROWS, 128)],
-        in_specs=[VMEM] * 7,
-        out_specs=[VMEM] * 3,
-        scratch_shapes=[pltpu.VMEM((128, 128), F32)],
+        out_shape=[
+            shape(CHANNELS, ROWS, 128),
+            shape(128, 128),
+            shape(PAD + 128 + PAD, 128),
+            shape(X_ROWS, 128),
+        ],
+        in_specs=[VMEM] * 4,
+        out_specs=[VMEM] * 4,
+        input_output_aliases={0: 0, 1: 1},
         compiler_params=PARAMS,
         name="pack_x",
-    )(own, y_two, y_one, own_two, own_one, z_two, z_one)
+    )(part, packed, z_two, z_one)
     x_one = swap(message, "gx", 0, True)
     x_two = x_one if lax.axis_size("gx") == 2 else swap(message, "gx", 1, True)
     block = pl.pallas_call(
@@ -487,9 +515,8 @@
         scratch_shapes=[
             pltpu.VMEM((PAD + X_ROWS + PAD, 128), F32),
             pltpu.VMEM((PAD + X_ROWS + PAD, 128), F32),
-            pltpu.VMEM((27, UNITS * 8, 128), F32),
             pltpu.VMEM((3, UNITS * 8, 128), F32),
-            pltpu.VMEM((2, 128, 128), F32),
+            pltpu.VMEM((3, 128, 128), F32),
             pltpu.VMEM((27, NZ, NY, NX), F32),
             pltpu.SemaphoreType.DMA((NZ,)),
         ],

time: 22.2 us -> 21.7 us (0.977)
  waiting for transfers between devices: 3.53 us -> 3.12 us
    ppermute x7, waiting for transfers between devices: 3.53 us -> 3.12 us  [swap(): return lax.ppermute(value, axis, pairs + [(j, i) for i, j in pairs])]
    pallas_call x0 -> x1, Pallas kernels: none -> 0.35 us  [shards(): pl.pallas_call(fill_kernel, out_shape=[shape(CHANNELS, ROWS, 128), shape(...]
    pallas_call x1, Pallas kernels: 0.8 us -> 0.51 us  [shards(): pl.pallas_call(third_kernel, out_shape=[shape(CHANNELS, ROWS, 128), shape...]
  transfers between devices with their start and end apart: 7 -> 7, of which waited for: 3 -> 3; matrix products, arithmetic and copies ran while one was open for 0% -> 0% of each run, Pallas kernels for 3% -> 5%
where the time goes in v10:
time: 21.7 us; the launch traced here: 21.5 us
  starting transfers between devices  13.9 us (64%)
  Pallas kernels  4.4 us (20%)
  waiting for transfers between devices  3.12 us (14%)
    ppermute x7, starting transfers between devices, swap(): return lax.ppermute(value, axis, pairs + [(j, i) for i, j in pairs])  13.9 us
    ppermute x7, waiting for transfers between devices, swap(): return lax.ppermute(value, axis, pairs + [(j, i) for i, j in pairs])  3.12 us
    pallas_call x1, Pallas kernels, shards(): pl.pallas_call(last_kernel, out_shape=shape(27, NZ, NY, NX), in_specs=[VM...  1.44 us
    pallas_call x1, Pallas kernels, shards(): pl.pallas_call(first_kernel, out_shape=[shape(CHANNELS * NZ * 8, 128), sh...  1.34 us
    pallas_call x1, Pallas kernels, shards(): pl.pallas_call(block_kernel, out_shape=shape(27, UNITS * 8, 128), in_spec...  0.72 us
    pallas_call x1, Pallas kernels, shards(): pl.pallas_call(third_kernel, out_shape=[shape(CHANNELS, ROWS, 128), shape...  0.51 us
  transfers between devices with their start and end apart: 7, of which 3 were waited for; matrix products, arithmetic and copies ran while one was open for 0% of the time, Pallas kernels for 5%

profile of v10, /device:TPU:0, one launch (start us, length us, event | category | flops | bytes accessed | tf_op | source)
XLA Modules:
  0.0 21.5 jit_solution(9130037050287190502)
XLA Ops:
  0.0 1.3 %collide.1 = (f32[928,128]{1,0:T(8,128)S(1)}, f32[152,128]{1,0:T(8,128)S(1)}, f32[152,128]{1,0:T(8,128)S(1)}) custom-call(f32[27,4,8,128]{3,2,1,0:T(8,128)} %pops_at.1, s32[4,8,128]{2,1,0:T(8,128)} %solid_at.1, f32[4,8]{1,0:T(4,128)} %bitcast.1, s32[8]{0:T(128)} %index_at.1), custom_call_target="tpu_custom_call" | custom-call | tf_op jit(solution)/shard_map/collide/pallas_call | solution.py:435
  1.3 5.1 %collective-permute-start = (f32[152,128]{1,0:T(8,128)S(1)}, f32[152,128]{1,0:T(8,128)S(1)}, u32[]{:S(2)}, u32[]{:S(2)}) collective-permute-start(f32[152,128]{1,0:T(8,128)S(1)} %get-tuple-element.18), channel_id=1, source_target_pairs={{4,8},{12,0},{8,4},{0,12},{5,9},{13,1},{9,5},{1,13},{6,10},{14,2},... | collective-permute-start | bytes 233480 | tf_op jit(solution)/shard_map/ppermute | solution.py:427
  6.5 0.0 collective-permute-start.1
  6.5 0.7 %collective-permute-start.2 = (f32[312,128]{1,0:T(8,128)S(1)}, f32[312,128]{1,0:T(8,128)S(1)}, u32[]{:S(2)}, u32[]{:S(2)}) collective-permute-start(f32[312,128]{1,0:T(8,128)S(1)} %get-tuple-element.20), channel_id=1, source_target_pairs={{1,2},{2,1},{5,6},{6,5},{9,10},{10,9},{13,14},{14,13},{17,18},{18,... | collective-permute-start | bytes 479240 | tf_op jit(solution)/shard_map/ppermute | solution.py:427
  7.2 2.9 %collective-permute-start.3 = (f32[312,128]{1,0:T(8,128)S(1)}, f32[312,128]{1,0:T(8,128)S(1)}, u32[]{:S(2)}, u32[]{:S(2)}) collective-permute-start(f32[312,128]{1,0:T(8,128)S(1)} %get-tuple-element.21), channel_id=1, source_target_pairs={{0,1},{2,3},{1,0},{3,2},{4,5},{6,7},{5,4},{7,6},{8,9},{10,11},{9,8... | collective-permute-start | bytes 479240 | tf_op jit(solution)/shard_map/ppermute | solution.py:427
  10.1 0.0 collective-permute-done.y_two
  10.1 0.8 %collective-permute-done.1.y_one = f32[152,128]{1,0:T(8,128)S(1)} collective-permute-done((f32[152,128]{1,0:T(8,128)S(1)}, f32[152,128]{1,0:T(8,128)S(1)}, u32[]{:S(2)}, u32[]{:S(2)}) %collective-permute-start.1) | collective-permute-done | bytes 77856 | tf_op jit(solution)/shard_map/ppermute | solution.py:427
  10.9 0.7 %collective-permute-start.4 = (f32[104,128]{1,0:T(8,128)S(1)}, f32[104,128]{1,0:T(8,128)S(1)}, u32[]{:S(2)}, u32[]{:S(2)}) collective-permute-start(f32[104,128]{1,0:T(8,128)S(1)} %get-tuple-element.24), channel_id=1, source_target_pairs={{1,2},{2,1},{5,6},{6,5},{9,10},{10,9},{13,14},{14,13},{17,18},{18,... | collective-permute-start | bytes 159752 | tf_op jit(solution)/shard_map/ppermute | solution.py:427
  11.6 3.0 %collective-permute-start.5 = (f32[104,128]{1,0:T(8,128)S(1)}, f32[104,128]{1,0:T(8,128)S(1)}, u32[]{:S(2)}, u32[]{:S(2)}) collective-permute-start(f32[104,128]{1,0:T(8,128)S(1)} %get-tuple-element.25), channel_id=1, source_target_pairs={{0,1},{2,3},{1,0},{3,2},{4,5},{6,7},{5,4},{7,6},{8,9},{10,11},{9,8... | collective-permute-start | bytes 159752 | tf_op jit(solution)/shard_map/ppermute | solution.py:427
  14.5 0.0 collective-permute-done.2.two
  14.5 0.0 collective-permute-done.3.one
  14.5 0.3 %fill.1 = (f32[29,112,128]{2,1,0:T(8,128)S(1)}, f32[128,128]{1,0:T(8,128)S(1)}) custom-call(f32[928,128]{1,0:T(8,128)S(1)} %get-tuple-element.17.own, f32[152,128]{1,0:T(8,128)S(1)} %collective-permute-done.y_two, f32[152,128]{1,0:T(8,128)S(1)} %collective-permute-done.1.y_one, f32[312,128]{1,0:T(8,128)S(1)} %collective-permute-done.2.two, ...), custom_call_target="tpu_custom_call" | custom-call | flops 1000000 | bytes 4194304 | tf_op jit(solution)/shard_map/fill/pallas_call | solution.py:473
  14.9 0.0 collective-permute-done.4.z_two
  14.9 0.5 %collective-permute-done.5.z_one = f32[104,128]{1,0:T(8,128)S(1)} collective-permute-done((f32[104,128]{1,0:T(8,128)S(1)}, f32[104,128]{1,0:T(8,128)S(1)}, u32[]{:S(2)}, u32[]{:S(2)}) %collective-permute-start.5) | collective-permute-done | bytes 53280 | tf_op jit(solution)/shard_map/ppermute | solution.py:427
  15.4 0.5 %pack_x.1 = (f32[29,112,128]{2,1,0:T(8,128)S(1)}, f32[128,128]{1,0:T(8,128)S(1)}, f32[144,128]{1,0:T(8,128)S(1)}, f32[56,128]{1,0:T(8,128)S(1)}) custom-call(f32[29,112,128]{2,1,0:T(8,128)S(1)} %get-tuple-element.22.part, f32[128,128]{1,0:T(8,128)S(1)} %get-tuple-element.23.packed, ...), custom_call_target="tpu_custom_call", output_to_operand_aliasing={{0}: (0, {}), {1}: (1, {})} | custom-call | tf_op jit(solution)/shard_map/pack_x/pallas_call | solution.py:482
  15.9 1.6 %collective-permute-start.6 = (f32[56,128]{1,0:T(8,128)S(1)}, f32[56,128]{1,0:T(8,128)S(1)}, u32[]{:S(2)}, u32[]{:S(2)}) collective-permute-start(f32[56,128]{1,0:T(8,128)S(1)} %get-tuple-element.28), channel_id=1, source_target_pairs={{0,16},{16,0},{1,17},{17,1},{2,18},{18,2},{3,19},{19,3},{4,20},{20... | collective-permute-start | bytes 86024 | tf_op jit(solution)/shard_map/ppermute | solution.py:427
  17.5 0.7 %block.1 = f32[27,72,128]{2,1,0:T(8,128)S(1)} custom-call(f32[29,112,128]{2,1,0:T(8,128)S(1)} %get-tuple-element.26.full), custom_call_target="tpu_custom_call" | custom-call | flops 4976640 | bytes 4194304 | tf_op jit(solution)/shard_map/block/pallas_call | solution.py:498
  18.3 1.8 %collective-permute-done.6.x_one.x_two = f32[56,128]{1,0:T(8,128)S(1)} collective-permute-done((f32[56,128]{1,0:T(8,128)S(1)}, f32[56,128]{1,0:T(8,128)S(1)}, u32[]{:S(2)}, u32[]{:S(2)}) %collective-permute-start.6) | collective-permute-done | bytes 28704 | tf_op jit(solution)/shard_map/ppermute | solution.py:427
  20.1 1.4 %finish.1 = f32[27,4,8,128]{3,2,1,0:T(8,128)} custom-call(f32[29,112,128]{2,1,0:T(8,128)S(1)} %get-tuple-element.26.full, f32[27,72,128]{2,1,0:T(8,128)S(1)} %block.1, f32[144,128]{1,0:T(8,128)S(1)} %get-tuple-element.27.columns, f32[56,128]{1,0:T(8,128)S(1)} %collective-permute-done.6.x_one.x_two, f32[56,128]{1,0:T(8,128)S(1)} %collective-permute-done.6.x_one.x_two), custom_call_target="tpu_custom_call" | custom-call | tf_op jit(solution)/shard_map/finish/pallas_call | solution.py:510
  (2 shorter events, 0.0 us)
Async XLA Ops:
  1.3 8.7 %collective-permute-start = (f32[152,128]{1,0:T(8,128)S(1)}, f32[152,128]{1,0:T(8,128)S(1)}, u32[]{:S(2)}, u32[]{:S(2)}) collective-permute-start(f32[152,128]{1,0:T(8,128)S(1)} %get-tuple-element.18), channel_id=1, source_target_pairs={{4,8},{12,0},{8,4},{0,12},{5,9},{13,1},{9,5},{1,13},{6,10},{14,2},... | collective-permute-start | bytes 233480 | tf_op jit(solution)/shard_map/ppermute | solution.py:427
  6.5 4.4 %collective-permute-start.1 = (f32[152,128]{1,0:T(8,128)S(1)}, f32[152,128]{1,0:T(8,128)S(1)}, u32[]{:S(2)}, u32[]{:S(2)}) collective-permute-start(f32[152,128]{1,0:T(8,128)S(1)} %get-tuple-element.19), channel_id=1, source_target_pairs={{0,4},{8,12},{4,0},{12,8},{1,5},{9,13},{5,1},{13,9},{2,6},{10,14},... | collective-permute-start | bytes 233480 | tf_op jit(solution)/shard_map/ppermute | solution.py:427
  6.5 8.0 %collective-permute-start.2 = (f32[312,128]{1,0:T(8,128)S(1)}, f32[312,128]{1,0:T(8,128)S(1)}, u32[]{:S(2)}, u32[]{:S(2)}) collective-permute-start(f32[312,128]{1,0:T(8,128)S(1)} %get-tuple-element.20), channel_id=1, source_target_pairs={{1,2},{2,1},{5,6},{6,5},{9,10},{10,9},{13,14},{14,13},{17,18},{18,... | collective-permute-start | bytes 479240 | tf_op jit(solution)/shard_map/ppermute | solution.py:427
  7.2 7.4 %collective-permute-start.3 = (f32[312,128]{1,0:T(8,128)S(1)}, f32[312,128]{1,0:T(8,128)S(1)}, u32[]{:S(2)}, u32[]{:S(2)}) collective-permute-start(f32[312,128]{1,0:T(8,128)S(1)} %get-tuple-element.21), channel_id=1, source_target_pairs={{0,1},{2,3},{1,0},{3,2},{4,5},{6,7},{5,4},{7,6},{8,9},{10,11},{9,8... | collective-permute-start | bytes 479240 | tf_op jit(solution)/shard_map/ppermute | solution.py:427
  10.9 4.0 %collective-permute-start.4 = (f32[104,128]{1,0:T(8,128)S(1)}, f32[104,128]{1,0:T(8,128)S(1)}, u32[]{:S(2)}, u32[]{:S(2)}) collective-permute-start(f32[104,128]{1,0:T(8,128)S(1)} %get-tuple-element.24), channel_id=1, source_target_pairs={{1,2},{2,1},{5,6},{6,5},{9,10},{10,9},{13,14},{14,13},{17,18},{18,... | collective-permute-start | bytes 159752 | tf_op jit(solution)/shard_map/ppermute | solution.py:427
  11.6 3.9 %collective-permute-start.5 = (f32[104,128]{1,0:T(8,128)S(1)}, f32[104,128]{1,0:T(8,128)S(1)}, u32[]{:S(2)}, u32[]{:S(2)}) collective-permute-start(f32[104,128]{1,0:T(8,128)S(1)} %get-tuple-element.25), channel_id=1, source_target_pairs={{0,1},{2,3},{1,0},{3,2},{4,5},{6,7},{5,4},{7,6},{8,9},{10,11},{9,8... | collective-permute-start | bytes 159752 | tf_op jit(solution)/shard_map/ppermute | solution.py:427
  15.9 4.1 %collective-permute-start.6 = (f32[56,128]{1,0:T(8,128)S(1)}, f32[56,128]{1,0:T(8,128)S(1)}, u32[]{:S(2)}, u32[]{:S(2)}) collective-permute-start(f32[56,128]{1,0:T(8,128)S(1)} %get-tuple-element.28), channel_id=1, source_target_pairs={{0,16},{16,0},{1,17},{17,1},{2,18},{18,2},{3,19},{19,3},{4,20},{20... | collective-permute-start | bytes 86024 | tf_op jit(solution)/shard_map/ppermute | solution.py:427

commit v11 on v10

--- a/solution.py
+++ b/solution.py
@@ -33,9 +33,10 @@
 Y_ROWS = (CHANNELS + 9) * NZ
 Z_BLOCKS = CHANNELS + 10
 Z_FAR = 2 * Z_BLOCKS
-Z_ROWS = -(-(Z_FAR + 2 * 12) // 8) * 8
-
-X_ROWS = 2 * (WALL + 1)
+Z_ROWS = -(-(Z_FAR + 2 * 12) // 8) * 8 + 2 * PITCH
+
+OWN = NZ * PITCH
+EDGE = 2 * PITCH
 
 
 def relaxed(f, sponge, aim):
@@ -158,7 +159,15 @@
     by_parity("gy", one, two, pack)
 
 
-def ahead_kernel(own, two, one):
+def ahead_kernel(own, columns, two, one):
+    slot = lane_ids() // 4
+    for z in range(NZ):
+        packed = jnp.zeros((8, 128), F32)
+        for c in range(CHANNELS):
+            moved = pltpu.roll(own[pl.ds((c * NZ + z) * 8, 8), :], (4 * c + 2) % 128, 1)
+            packed = jnp.where(slot == c, moved, packed)
+        columns[pl.ds(8 * z, 8), :] = packed
+
     def pack(zup, zdown):
         for out, first, second, part in ((zup, NZ - 1, NZ - 2, 2), (zdown, 0, 1, 0)):
             for k, (c, z) in enumerate(z_blocks(first, second, part)):
@@ -167,19 +176,54 @@
     by_parity("gz", one, two, pack)
 
 
-def second_kernel(own, y_two, y_one, z_two, z_one):
+def second_kernel(y_two, y_one, *refs):
+    turns = 1 if lax.axis_size("gx") == 2 else 2
+    level, refs = refs[: 3 * turns], refs[3 * turns :]
+    z_two, z_one, beside = refs
+
+    def gather(straight, two, one, lanes):
+        def put(target, count, source, start):
+            value = source[pl.ds(start, count), :]
+            if lanes is not None:
+                value = jnp.where(lanes[:count], value, beside[pl.ds(target, count), :])
+            beside[pl.ds(target, count), :] = value
+
+        def rows(above, below):
+            for z in range(NZ):
+                put(z * PITCH, 2, below, z * NY + NY - 2)
+                put(z * PITCH + 2, NY, straight, z * NY)
+                put(z * PITCH + 2 + NY, 2, above, z * NY)
+
+        by_parity("gy", one, two, rows)
+
+    if turns == 1:
+        gather(*level, None)
+    else:
+        right_lanes = lax.rem(lane_ids(), 4) >= 2
+
+        def sides(right, left):
+            gather(*left, None)
+            gather(*right, right_lanes)
+
+        by_parity("gx", level[:3], level[3:], sides)
+
     by_parity(
         "gy",
         y_one,
         y_two,
         lambda above, below: by_parity(
-            "gz", z_one, z_two, lambda zup, zdown: pack_planes(own, below, above, zup, zdown)
+            "gz",
+            z_one,
+            z_two,
+            lambda zup, zdown: pack_planes(below, above, beside, zup, zdown),
         ),
     )
 
 
-def pack_planes(own, below, above, zup, zdown):
+def pack_planes(below, above, beside, zup, zdown):
     for out, first, second, part in ((zup, NZ - 1, NZ - 2, 2), (zdown, 0, 1, 0)):
+        start = min(first, second) * PITCH
+        out[pl.ds(Z_ROWS - EDGE, EDGE), :] = beside[pl.ds(start, EDGE), :]
         for side, halo in enumerate((below, above)):
             near = side * Z_BLOCKS
             out[pl.ds(near, CHANNELS), :] = halo[pl.ds(first, CHANNELS, stride=NZ), :]
@@ -244,67 +288,20 @@
         pack[pl.ds(8 * t, 8), :] = packed
 
 
-OWN_TILES = range(2 * PITCH // 8, (NZ + 2) * PITCH // 8)
-
-
-def fill_kernel(own, y_two, y_one, two, one, full, pack):
-    for c in range(CHANNELS):
-        for z in range(NZ):
-            full[c, pl.ds(plane_at(z) + 2, 8), :] = own[pl.ds((c * NZ + z) * 8, 8), :]
-    by_parity("gy", y_one, y_two, functools.partial(add_rows, full))
-    by_parity("gz", one, two, functools.partial(add_own_planes, full))
-    pack_columns(full, pack, OWN_TILES)
-    pack[pl.ds(FLAT, 128 - FLAT), :] = jnp.zeros((128 - FLAT, 128), F32)
-
-
-def third_kernel(part, packed, z_two, z_one, full, pack, columns, message):
-    last = lax.axis_size("gz") - 1
-    here = lax.axis_index("gz")
-    by_parity("gz", z_one, z_two, functools.partial(add_planes, full))
-
-    @pl.when(here == 0)
-    def _():
-        full[WALL, pl.ds(plane_at(-1), PITCH), :] = jnp.ones((PITCH, 128), F32)
-
-    @pl.when(here == last)
-    def _():
-        for q in range(9):
-            full[q, pl.ds(plane_at(NZ), PITCH), :] = full[q + 18, pl.ds(plane_at(NZ - 1), PITCH), :]
-
-    pack_columns(full, pack, [t for t in range(FLAT // 8) if t not in OWN_TILES])
-    columns[pl.ds(PAD, 128), :] = pack[...].T
-
-    def row(c, i, count):
-        return columns[pl.ds(PAD + 4 * c + i, count), :]
-
-    def returned(q, near, far):
-        cx, cy, cz = VEL[q]
-        step = (-PITCH * cz - cy) % 128
-        value = row(26 - q, near, 8)
-        value = pltpu.roll(value, step, 1) if step else value
-        return jnp.where(row(WALL, far, 8) != 0.0, value, row(q, far, 8))[:1]
-
-    for c in range(WALL + 1):
-        cx = VEL[c][0] if c < 27 else 0
-        if cx == 0:
-            message[pl.ds(2 * c, 2), :] = row(c, 1, 2)
-        elif cx > 0:
-            message[pl.ds(2 * c, 1), :] = returned(c, 1, 0)
-            message[pl.ds(2 * c + 1, 1), :] = row(c, 1, 1)
-        else:
-            message[pl.ds(2 * c, 1), :] = row(c, 2, 1)
-            message[pl.ds(2 * c + 1, 1), :] = returned(c, 2, 3)
-
-
-def block_kernel(full, post, walls):
-    top = lax.axis_index("gz") == lax.axis_size("gz") - 1
-    sponge = (lax.axis_index("gx") * NX + lane_ids()) < SPONGE
-    for t in range(ROWS // 8):
+OWN_TILES = range(EDGE // 8, (EDGE + OWN) // 8)
+INNER = range(2 * PITCH // 8, NZ * PITCH // 8)
+
+
+def roll_walls(full, walls, tiles):
+    for t in tiles:
         rows = pl.ds(8 * t, 8)
         flags = full[WALL, rows, :]
         for cx in (-1, 0, 1):
             walls[cx + 1, rows, :] = pltpu.roll(flags, cx % 128, 1) if cx else flags
-    for u in range(UNITS):
+
+
+def step_rows(full, walls, post, sponge, units):
+    for u in units:
         cell = PAD + PITCH + 8 * u
         f = []
         solid = walls[1, pl.ds(cell, 8), :] != 0.0
@@ -322,35 +319,63 @@
         for q in range(27):
             post[q, pl.ds(8 * u, 8), :] = done[q]
 
+
+def fill_kernel(own, y_two, y_one, two, one, full, mine, post, walls):
+    for c in range(CHANNELS):
+        for z in range(NZ):
+            full[c, pl.ds(plane_at(z) + 2, 8), :] = own[pl.ds((c * NZ + z) * 8, 8), :]
+    by_parity("gy", y_one, y_two, functools.partial(add_rows, full))
+    by_parity("gz", one, two, functools.partial(add_own_planes, full))
+    pack_columns(full, mine, OWN_TILES)
+    sponge = (lax.axis_index("gx") * NX + lane_ids()) < SPONGE
+    roll_walls(full, walls, range(ROWS // 8))
+    step_rows(full, walls, post, sponge, INNER)
+
+
+def last_kernel(
+    part, packed, inner, beside, z_two, z_one, out, full, mine, post, walls, near, turn, sheet, back,
+    done, sems
+):
+    here_x, size_x = lax.axis_index("gx"), lax.axis_size("gx")
+    here, last = lax.axis_index("gz"), lax.axis_size("gz") - 1
+    top, bottom = here == last, here == 0
+    lanes, rows = lane_ids(), row_ids()
+
+    def add_halo(ceiling, floor):
+        add_planes(full, ceiling, floor)
+        near[pl.ds(0, EDGE), :] = floor[pl.ds(Z_ROWS - EDGE, EDGE), :]
+        near[pl.ds(EDGE + OWN, EDGE), :] = ceiling[pl.ds(Z_ROWS - EDGE, EDGE), :]
+
+    by_parity("gz", z_one, z_two, add_halo)
+
+    @pl.when(bottom)
+    def _():
+        full[WALL, pl.ds(plane_at(-1), PITCH), :] = jnp.ones((PITCH, 128), F32)
+
     @pl.when(top)
     def _():
         for q in range(9):
-            post[q, pl.ds((NZ + 1) * PITCH, PITCH), :] = post[q + 18, pl.ds(NZ * PITCH, PITCH), :]
-
-
-def last_kernel(full, block, columns, x_one, x_two, out, west, east, walls, back, done, sems):
-    here_x, size_x = lax.axis_index("gx"), lax.axis_size("gx")
-    top = lax.axis_index("gz") == lax.axis_size("gz") - 1
-    lanes, rows = lane_ids(), row_ids()
-
-    def spread(right, left):
-        west[pl.ds(PAD, X_ROWS), :] = left[...]
-        east[pl.ds(PAD, X_ROWS), :] = right[...]
-
-    by_parity("gx", x_one, x_two, spread)
+            full[q, pl.ds(plane_at(NZ), PITCH), :] = full[q + 18, pl.ds(plane_at(NZ - 1), PITCH), :]
+
+    near[pl.ds(EDGE, OWN), :] = beside[...]
+    pack_columns(full, mine, [t for t in range(FLAT // 8) if t not in OWN_TILES])
+
+    for i, source in enumerate((mine, near)):
+        square = jnp.concatenate([source[...], jnp.zeros((128 - FLAT, 128), F32)], axis=0)
+        turn[i, pl.ds(PAD, 128), :] = square.T
 
     strip = []
     for c in range(CHANNELS):
-        cx = VEL[c][0] if c < 27 else 0
-        value = jnp.where(
-            rows < 4, columns[pl.ds(PAD + 4 * c, 8), :], columns[pl.ds(PAD + 4 * c - 4, 8), :]
-        )
-        if c <= WALL and cx >= 0:
-            value = jnp.where(rows < 2, west[pl.ds(PAD + 2 * c - (cx == 0), 8), :], value)
-        if c <= WALL and cx <= 0:
-            value = jnp.where(rows >= 6, east[pl.ds(PAD + 2 * c - 6 + (cx == 0), 8), :], value)
-        strip.append(value)
-    strip[WALL] = jnp.where((rows == 0) | (rows == 7), 0.0, strip[WALL])
+        first, second = pl.ds(PAD + 4 * c, 8), pl.ds(PAD + 4 * c - 4, 8)
+        own = jnp.where(rows < 4, turn[0, first, :], turn[0, second, :])
+        other = jnp.where(rows < 4, turn[1, first, :], turn[1, second, :])
+        strip.append(jnp.where((rows >= 2) & (rows < 6), own, other))
+
+    ceiling = top & (lanes >= (NZ + 2) * PITCH) & (lanes < (NZ + 3) * PITCH)
+    ground = bottom & (lanes >= PITCH) & (lanes < 2 * PITCH)
+    for q in range(9):
+        strip[q] = jnp.where(ceiling, pltpu.roll(strip[q + 18], PITCH, 1), strip[q])
+    strip[WALL] = jnp.where(ceiling, 0.0, jnp.where(ground, 1.0, strip[WALL]))
 
     def shifted(value, q):
         cx, cy, cz = VEL[q]
@@ -368,9 +393,8 @@
     column = here_x * NX + jnp.where(rows < 4, rows - 2, rows + (NX - 6))
     column = lax.rem(column + size_x * NX, size_x * NX)
     sides = relaxed(moved, column < SPONGE, strip[AIM])
-    lid = top & (lanes >= (NZ + 2) * PITCH) & (lanes < (NZ + 3) * PITCH)
     for q in range(9):
-        sides[q] = jnp.where(lid, pltpu.roll(sides[q + 18], PITCH, 1), sides[q])
+        sides[q] = jnp.where(ceiling, pltpu.roll(sides[q + 18], PITCH, 1), sides[q])
     ends = [jnp.where(rows == 1, pltpu.roll(side, 4, 0), side) for side in sides]
     ends += [jnp.zeros((8, 128), F32)] * 5
     for i in range(2):
@@ -379,41 +403,50 @@
     pairs += [strip[WALL]] + [jnp.zeros((8, 128), F32)] * 6
     back[2] = jnp.concatenate(pairs, axis=0).T
 
+    sponge = (here_x * NX + lanes) < SPONGE
+    roll_walls(full, walls, [t for t in range(ROWS // 8)])
+    step_rows(full, walls, post, sponge, [u for u in range(UNITS) if u not in INNER])
+
     def column_at(i, place, lane, start):
         return pltpu.roll(back[i, pl.ds(start, 8), :], (lane - place) % 128, 1)
 
+    for u in range(UNITS):
+        cell = pl.ds(PAD + PITCH + 8 * u, 8)
+        sheet[1, pl.ds(8 * u, 8), :] = walls[1, cell, :]
+        for cx, edge, place in ((1, 0, 73), (-1, 127, 78)):
+            side = column_at(2, place, edge, PITCH + 8 * u)
+            sheet[cx + 1, pl.ds(8 * u, 8), :] = jnp.where(lanes == edge, side, walls[cx + 1, cell, :])
+
     rim = (lanes == 0) | (lanes == 127)
 
-    def rimmed(q, start):
-        ends = column_at(q // 16, 8 * (q % 16) + 2, 0, PITCH + start)
-        return jnp.where(rim, ends, block[q, pl.ds(start, 8), :])
-
-    for u in range(UNITS):
-        flags = full[WALL, pl.ds(PAD + PITCH + 8 * u, 8), :]
-        walls[1, pl.ds(8 * u, 8), :] = flags
-        for cx, edge, place in ((1, 0, 73), (-1, 127, 78)):
-            walls[cx + 1, pl.ds(8 * u, 8), :] = jnp.where(
-                lanes == edge, column_at(2, place, edge, PITCH + 8 * u), pltpu.roll(flags, cx % 128, 1)
-            )
+    def block(q, z, start):
+        value = post[q, pl.ds(start, 8), :]
+        if z == NZ - 1 and VEL[q][2] < 0:
+            value = jnp.where(top, post[q + 18, pl.ds(start - PITCH, 8), :], value)
+        return value
+
+    def rimmed(value, q, start):
+        return jnp.where(rim, column_at(q // 16, 8 * (q % 16) + 2, 0, PITCH + start), value)
 
     copies = []
     for z in range(NZ):
         cell = (z + 1) * PITCH + 2
-        solid = walls[1, pl.ds(cell, 8), :] != 0.0
+        solid = sheet[1, pl.ds(cell, 8), :] != 0.0
         for q in range(27):
             cx, cy, cz = VEL[q]
             start = cell - PITCH * cz - cy
+            value = block(q, z, start)
             if cx > 0:
                 side = column_at(2, 8 * (q // 3) + 1, 0, PITCH + start)
-                value = jnp.where(lanes < 2, side, pltpu.roll(block[q, pl.ds(start, 8), :], 1, 1))
+                value = jnp.where(lanes < 2, side, pltpu.roll(value, 1, 1))
             elif cx < 0:
                 side = column_at(2, 8 * (q // 3) + 5, 126, PITCH + start)
-                value = jnp.where(lanes > 125, side, pltpu.roll(block[q, pl.ds(start, 8), :], 127, 1))
+                value = jnp.where(lanes > 125, side, pltpu.roll(value, 127, 1))
             else:
-                value = rimmed(q, start)
+                value = rimmed(value, q, start)
             if q != 13:
-                blocked = walls[cx + 1, pl.ds(start, 8), :] != 0.0
-                value = jnp.where(blocked, rimmed(26 - q, cell), value)
+                blocked = sheet[cx + 1, pl.ds(start, 8), :] != 0.0
+                value = jnp.where(blocked, rimmed(post[26 - q, pl.ds(cell, 8), :], 26 - q, cell), value)
             done[q, z] = jnp.where(solid, WEIGHT[q], value)
         copies.append(pltpu.make_async_copy(done.at[:, z], out.at[:, z], sems.at[z]))
         copies[-1].start()
@@ -421,10 +454,21 @@
         copy.wait()
 
 
+def pairs(size, turn, wrap):
+    ahead = [(i, (i + 1) % size) for i in range(turn, size if wrap else size - 1, 2)]
+    return ahead + [(j, i) for i, j in ahead]
+
+
 def swap(value, axis, turn, wrap):
-    size = lax.axis_size(axis)
-    pairs = [(i, (i + 1) % size) for i in range(turn, size if wrap else size - 1, 2)]
-    return lax.ppermute(value, axis, pairs + [(j, i) for i, j in pairs])
+    return lax.ppermute(value, axis, pairs(lax.axis_size(axis), turn, wrap))
+
+
+def swap_across(value, x_turn, y_turn):
+    size = lax.axis_size("gy")
+    over_x = pairs(lax.axis_size("gx"), x_turn, True)
+    over_y = pairs(size, y_turn, True)
+    both = [(i * size + j, far_i * size + far_j) for i, far_i in over_x for j, far_j in over_y]
+    return lax.ppermute(value, ("gx", "gy"), both)
 
 
 def shape(*dims):
@@ -449,72 +493,56 @@
     )(*(pltpu.with_memory_space_constraint(a, pltpu.HBM) for a in (pops, solid, profile_table.T, profile_index)))
     y_two = swap(y_two, "gy", 1, True)
     y_one = swap(y_one, "gy", 0, True)
-    own_two, own_one = pl.pallas_call(
+    columns, own_two, own_one = pl.pallas_call(
         ahead_kernel,
-        out_shape=[shape(Z_BLOCKS * 8, 128)] * 2,
+        out_shape=[shape(NZ * NY, 128), *[shape(Z_BLOCKS * 8, 128)] * 2],
         in_specs=[VMEM],
-        out_specs=[VMEM] * 2,
+        out_specs=[VMEM] * 3,
         compiler_params=PARAMS,
         name="pack_own",
     )(own)
+    level = []
+    for turn in range(1 if lax.axis_size("gx") == 2 else 2):
+        level += [swap(columns, "gx", turn, True)]
+        level += [swap_across(columns, turn, 1), swap_across(columns, turn, 0)]
     own_two = swap(own_two, "gz", 1, False)
     own_one = swap(own_one, "gz", 0, False)
-    z_two, z_one = pl.pallas_call(
+    z_two, z_one, beside = pl.pallas_call(
         second_kernel,
-        out_shape=[shape(Z_ROWS, 128)] * 2,
-        in_specs=[VMEM] * 3,
-        out_specs=[VMEM] * 2,
+        out_shape=[*[shape(Z_ROWS, 128)] * 2, shape(OWN, 128)],
+        in_specs=[VMEM] * (2 + len(level)),
+        out_specs=[VMEM] * 3,
         compiler_params=PARAMS,
         cost_estimate=pl.CostEstimate(flops=10**9, bytes_accessed=2**20, transcendentals=0),
         name="pack_z",
-    )(own, y_two, y_one)
+    )(y_two, y_one, *level)
     z_two = swap(z_two, "gz", 1, False)
     z_one = swap(z_one, "gz", 0, False)
-    part, packed = pl.pallas_call(
+    part, packed, inner = pl.pallas_call(
         fill_kernel,
-        out_shape=[shape(CHANNELS, ROWS, 128), shape(128, 128)],
+        out_shape=[shape(CHANNELS, ROWS, 128), shape(FLAT, 128), shape(27, UNITS * 8, 128)],
         in_specs=[VMEM] * 5,
-        out_specs=[VMEM] * 2,
+        out_specs=[VMEM] * 3,
+        scratch_shapes=[pltpu.VMEM((3, ROWS, 128), F32)],
         compiler_params=PARAMS,
         cost_estimate=pl.CostEstimate(flops=10**6, bytes_accessed=2**22, transcendentals=0),
         name="fill",
     )(own, y_two, y_one, own_two, own_one)
-    full, packed, columns, message = pl.pallas_call(
-        third_kernel,
-        out_shape=[
-            shape(CHANNELS, ROWS, 128),
-            shape(128, 128),
-            shape(PAD + 128 + PAD, 128),
-            shape(X_ROWS, 128),
-        ],
-        in_specs=[VMEM] * 4,
-        out_specs=[VMEM] * 4,
-        input_output_aliases={0: 0, 1: 1},
-        compiler_params=PARAMS,
-        name="pack_x",
-    )(part, packed, z_two, z_one)
-    x_one = swap(message, "gx", 0, True)
-    x_two = x_one if lax.axis_size("gx") == 2 else swap(message, "gx", 1, True)
-    block = pl.pallas_call(
-        block_kernel,
-        out_shape=shape(27, UNITS * 8, 128),
-        in_specs=[VMEM],
-        out_specs=VMEM,
-        scratch_shapes=[pltpu.VMEM((3, ROWS, 128), F32)],
-        compiler_params=PARAMS,
-        cost_estimate=pl.CostEstimate(
-            flops=27 * 20 * UNITS * 1024, bytes_accessed=2**22, transcendentals=0
-        ),
-        name="block",
-    )(full)
     return pl.pallas_call(
         last_kernel,
-        out_shape=shape(27, NZ, NY, NX),
-        in_specs=[VMEM] * 5,
-        out_specs=HBM,
+        out_shape=[
+            shape(27, NZ, NY, NX),
+            shape(CHANNELS, ROWS, 128),
+            shape(FLAT, 128),
+            shape(27, UNITS * 8, 128),
+        ],
+        in_specs=[VMEM] * 6,
+        out_specs=[HBM] + [VMEM] * 3,
+        input_output_aliases={0: 1, 1: 2, 2: 3},
         scratch_shapes=[
-            pltpu.VMEM((PAD + X_ROWS + PAD, 128), F32),
-            pltpu.VMEM((PAD + X_ROWS + PAD, 128), F32),
+            pltpu.VMEM((3, ROWS, 128), F32),
+            pltpu.VMEM((FLAT, 128), F32),
+            pltpu.VMEM((2, PAD + 128 + PAD, 128), F32),
             pltpu.VMEM((3, UNITS * 8, 128), F32),
             pltpu.VMEM((3, 128, 128), F32),
             pltpu.VMEM((27, NZ, NY, NX), F32),
@@ -522,7 +550,7 @@
         ],
         compiler_params=PARAMS,
         name="finish",
-    )(full, block, columns, x_one, x_two)
+    )(part, packed, inner, beside, z_two, z_one)[0]
 
 
 def solution(mesh):

time: 21.7 us -> 24.2 us (1.12)
  the two profiles are of different devices: /device:TPU:0 before, /device:TPU:1 now
where the time goes in v11:
time: 24.2 us; the launch traced here: 24 us
  starting transfers between devices  16.5 us (68%)
  Pallas kernels  4.32 us (18%)
  waiting for transfers between devices  3.15 us (13%)
    ppermute x7, starting transfers between devices, swap(): return lax.ppermute(value, axis, pairs(lax.axis_size(axis), turn, wrap))  14 us
    ppermute x2, starting transfers between devices, swap_across(): return lax.ppermute(value, ('gx', 'gy'), both)  2.51 us
    pallas_call x1, Pallas kernels, shards(): pl.pallas_call(last_kernel, out_shape=[shape(27, NZ, NY, NX), shape(CHANN...  2.15 us
    ppermute x7, waiting for transfers between devices, swap(): return lax.ppermute(value, axis, pairs(lax.axis_size(axis), turn, wrap))  1.9 us
    pallas_call x1, Pallas kernels, shards(): pl.pallas_call(first_kernel, out_shape=[shape(CHANNELS * NZ * 8, 128), sh...  1.34 us
    ppermute x2, waiting for transfers between devices, swap_across(): return lax.ppermute(value, ('gx', 'gy'), both)  1.24 us
    pallas_call x1, Pallas kernels, shards(): pl.pallas_call(fill_kernel, out_shape=[shape(CHANNELS, ROWS, 128), shape(...  0.57 us
  transfers between devices with their start and end apart: 9, of which 2 were waited for; matrix products, arithmetic and copies ran while one was open for 0% of the time, Pallas kernels for 3%

profile of v11, /device:TPU:1, one launch (start us, length us, event | category | flops | bytes accessed | tf_op | source)
XLA Modules:
  0.0 24.0 jit_solution(153131121981423427)
XLA Ops:
  0.0 1.3 %collide.1 = (f32[928,128]{1,0:T(8,128)S(1)}, f32[152,128]{1,0:T(8,128)S(1)}, f32[152,128]{1,0:T(8,128)S(1)}) custom-call(f32[27,4,8,128]{3,2,1,0:T(8,128)} %pops_at.1, s32[4,8,128]{2,1,0:T(8,128)} %solid_at.1, f32[4,8]{1,0:T(4,128)} %bitcast.1, s32[8]{0:T(128)} %index_at.1), custom_call_target="tpu_custom_call" | custom-call | tf_op jit(solution)/shard_map/collide/pallas_call | solution.py:479
  1.3 4.2 %collective-permute-start = (f32[152,128]{1,0:T(8,128)S(1)}, f32[152,128]{1,0:T(8,128)S(1)}, u32[]{:S(2)}, u32[]{:S(2)}) collective-permute-start(f32[152,128]{1,0:T(8,128)S(1)} %get-tuple-element.19), channel_id=1, source_target_pairs={{4,8},{12,0},{8,4},{0,12},{5,9},{13,1},{9,5},{1,13},{6,10},{14,2},... | collective-permute-start | bytes 233480 | tf_op jit(solution)/shard_map/ppermute | solution.py:463
  5.6 0.0 collective-permute-start.1
  5.6 0.2 pack_own.1
  5.8 2.5 %collective-permute-start.6 = (f32[32,128]{1,0:T(8,128)S(1)}, f32[32,128]{1,0:T(8,128)S(1)}, u32[]{:S(2)}, u32[]{:S(2)}) collective-permute-start(f32[32,128]{1,0:T(8,128)S(1)} %get-tuple-element.26), channel_id=1, source_target_pairs={{0,20},{8,28},{4,16},{12,24},{16,4},{24,12},{20,0},{28,8},{1,21},{... | collective-permute-start | bytes 49160 | tf_op jit(solution)/shard_map/ppermute | solution.py:471
  8.3 0.0 collective-permute-start.5
  8.3 1.2 %collective-permute-start.4 = (f32[32,128]{1,0:T(8,128)S(1)}, f32[32,128]{1,0:T(8,128)S(1)}, u32[]{:S(2)}, u32[]{:S(2)}) collective-permute-start(f32[32,128]{1,0:T(8,128)S(1)} %get-tuple-element.26), channel_id=1, source_target_pairs={{0,16},{16,0},{1,17},{17,1},{2,18},{18,2},{3,19},{19,3},{4,20},{20... | collective-permute-start | bytes 49160 | tf_op jit(solution)/shard_map/ppermute | solution.py:463
  9.5 1.2 %collective-permute-done.6.refs_2_ = f32[32,128]{1,0:T(8,128)S(1)} collective-permute-done((f32[32,128]{1,0:T(8,128)S(1)}, f32[32,128]{1,0:T(8,128)S(1)}, u32[]{:S(2)}, u32[]{:S(2)}) %collective-permute-start.6) | collective-permute-done | bytes 16416 | tf_op jit(solution)/shard_map/ppermute | solution.py:471
  10.8 4.5 %collective-permute-start.2 = (f32[312,128]{1,0:T(8,128)S(1)}, f32[312,128]{1,0:T(8,128)S(1)}, u32[]{:S(2)}, u32[]{:S(2)}) collective-permute-start(f32[312,128]{1,0:T(8,128)S(1)} %get-tuple-element.21), channel_id=1, source_target_pairs={{1,2},{2,1},{5,6},{6,5},{9,10},{10,9},{13,14},{14,13},{17,18},{18,... | collective-permute-start | bytes 479240 | tf_op jit(solution)/shard_map/ppermute | solution.py:463
  15.3 0.0 collective-permute-done.5.refs_1_
  15.3 0.9 %collective-permute-start.3 = (f32[312,128]{1,0:T(8,128)S(1)}, f32[312,128]{1,0:T(8,128)S(1)}, u32[]{:S(2)}, u32[]{:S(2)}) collective-permute-start(f32[312,128]{1,0:T(8,128)S(1)} %get-tuple-element.22), channel_id=1, source_target_pairs={{0,1},{2,3},{1,0},{3,2},{4,5},{6,7},{5,4},{7,6},{8,9},{10,11},{9,8... | collective-permute-start | bytes 479240 | tf_op jit(solution)/shard_map/ppermute | solution.py:463
  16.2 0.0 collective-permute-done.4.refs_0_
  16.2 0.0 collective-permute-done.y_two
  16.2 0.0 collective-permute-done.1.y_one
  16.2 0.1 pack_z.1
  16.3 3.0 %collective-permute-start.7 = (f32[128,128]{1,0:T(8,128)S(1)}, f32[128,128]{1,0:T(8,128)S(1)}, u32[]{:S(2)}, u32[]{:S(2)}) collective-permute-start(f32[128,128]{1,0:T(8,128)S(1)} %get-tuple-element.28), channel_id=1, source_target_pairs={{1,2},{2,1},{5,6},{6,5},{9,10},{10,9},{13,14},{14,13},{17,18},{18,... | collective-permute-start | bytes 196616 | tf_op jit(solution)/shard_map/ppermute | solution.py:463
  19.3 0.1 collective-permute-start.8
  19.4 0.0 collective-permute-done.2.two
  19.4 0.0 collective-permute-done.3.one
  19.4 0.6 %fill.1 = (f32[29,112,128]{2,1,0:T(8,128)S(1)}, f32[96,128]{1,0:T(8,128)S(1)}, f32[27,72,128]{2,1,0:T(8,128)S(1)}) custom-call(f32[928,128]{1,0:T(8,128)S(1)} %get-tuple-element.18.own, f32[152,128]{1,0:T(8,128)S(1)} %collective-permute-done.y_two, f32[152,128]{1,0:T(8,128)S(1)} %collective-permute-done.1.y_one, f32[312,128]{1,0:T(8,128)S(1)} %collective-permute-done.2.two, ...), custom_call_target="tpu_custom_call" | custom-call | flops 1000000 | bytes 4194304 | tf_op jit(solution)/shard_map/fill/pallas_call | solution.py:521
  20.0 1.9 %collective-permute-done.7.z_two = f32[128,128]{1,0:T(8,128)S(1)} collective-permute-done((f32[128,128]{1,0:T(8,128)S(1)}, f32[128,128]{1,0:T(8,128)S(1)}, u32[]{:S(2)}, u32[]{:S(2)}) %collective-permute-start.7) | collective-permute-done | bytes 65568 | tf_op jit(solution)/shard_map/ppermute | solution.py:463
  21.9 0.0 collective-permute-done.8.z_one
  21.9 2.1 %finish.1 = (f32[27,4,8,128]{3,2,1,0:T(8,128)}, f32[29,112,128]{2,1,0:T(8,128)S(1)}, f32[96,128]{1,0:T(8,128)S(1)}, f32[27,72,128]{2,1,0:T(8,128)S(1)}) custom-call(f32[29,112,128]{2,1,0:T(8,128)S(1)} %get-tuple-element.23.part, f32[96,128]{1,0:T(8,128)S(1)} %get-tuple-element.24.packed, ...), custom_call_target="tpu_custom_call", output_to_operand_aliasing={{1}: (0, {}), {2}: (1, {}), {3}: (2, {})} | custom-call | tf_op jit(solution)/shard_map/finish/pallas_call | solution.py:531
Async XLA Ops:
  1.3 14.9 %collective-permute-start = (f32[152,128]{1,0:T(8,128)S(1)}, f32[152,128]{1,0:T(8,128)S(1)}, u32[]{:S(2)}, u32[]{:S(2)}) collective-permute-start(f32[152,128]{1,0:T(8,128)S(1)} %get-tuple-element.19), channel_id=1, source_target_pairs={{4,8},{12,0},{8,4},{0,12},{5,9},{13,1},{9,5},{1,13},{6,10},{14,2},... | collective-permute-start | bytes 233480 | tf_op jit(solution)/shard_map/ppermute | solution.py:463
  5.6 10.7 %collective-permute-start.1 = (f32[152,128]{1,0:T(8,128)S(1)}, f32[152,128]{1,0:T(8,128)S(1)}, u32[]{:S(2)}, u32[]{:S(2)}) collective-permute-start(f32[152,128]{1,0:T(8,128)S(1)} %get-tuple-element.20), channel_id=1, source_target_pairs={{0,4},{8,12},{4,0},{12,8},{1,5},{9,13},{5,1},{13,9},{2,6},{10,14},... | collective-permute-start | bytes 233480 | tf_op jit(solution)/shard_map/ppermute | solution.py:463
  5.8 5.0 %collective-permute-start.6 = (f32[32,128]{1,0:T(8,128)S(1)}, f32[32,128]{1,0:T(8,128)S(1)}, u32[]{:S(2)}, u32[]{:S(2)}) collective-permute-start(f32[32,128]{1,0:T(8,128)S(1)} %get-tuple-element.26), channel_id=1, source_target_pairs={{0,20},{8,28},{4,16},{12,24},{16,4},{24,12},{20,0},{28,8},{1,21},{... | collective-permute-start | bytes 49160 | tf_op jit(solution)/shard_map/ppermute | solution.py:471
  8.3 7.0 %collective-permute-start.5 = (f32[32,128]{1,0:T(8,128)S(1)}, f32[32,128]{1,0:T(8,128)S(1)}, u32[]{:S(2)}, u32[]{:S(2)}) collective-permute-start(f32[32,128]{1,0:T(8,128)S(1)} %get-tuple-element.26), channel_id=1, source_target_pairs={{4,24},{12,16},{8,20},{0,28},{20,8},{28,0},{24,4},{16,12},{5,25},{... | collective-permute-start | bytes 49160 | tf_op jit(solution)/shard_map/ppermute | solution.py:471
  8.3 7.9 %collective-permute-start.4 = (f32[32,128]{1,0:T(8,128)S(1)}, f32[32,128]{1,0:T(8,128)S(1)}, u32[]{:S(2)}, u32[]{:S(2)}) collective-permute-start(f32[32,128]{1,0:T(8,128)S(1)} %get-tuple-element.26), channel_id=1, source_target_pairs={{0,16},{16,0},{1,17},{17,1},{2,18},{18,2},{3,19},{19,3},{4,20},{20... | collective-permute-start | bytes 49160 | tf_op jit(solution)/shard_map/ppermute | solution.py:463
  10.8 8.6 %collective-permute-start.2 = (f32[312,128]{1,0:T(8,128)S(1)}, f32[312,128]{1,0:T(8,128)S(1)}, u32[]{:S(2)}, u32[]{:S(2)}) collective-permute-start(f32[312,128]{1,0:T(8,128)S(1)} %get-tuple-element.21), channel_id=1, source_target_pairs={{1,2},{2,1},{5,6},{6,5},{9,10},{10,9},{13,14},{14,13},{17,18},{18,... | collective-permute-start | bytes 479240 | tf_op jit(solution)/shard_map/ppermute | solution.py:463
  15.3 4.1 %collective-permute-start.3 = (f32[312,128]{1,0:T(8,128)S(1)}, f32[312,128]{1,0:T(8,128)S(1)}, u32[]{:S(2)}, u32[]{:S(2)}) collective-permute-start(f32[312,128]{1,0:T(8,128)S(1)} %get-tuple-element.22), channel_id=1, source_target_pairs={{0,1},{2,3},{1,0},{3,2},{4,5},{6,7},{5,4},{7,6},{8,9},{10,11},{9,8... | collective-permute-start | bytes 479240 | tf_op jit(solution)/shard_map/ppermute | solution.py:463
  16.3 5.6 %collective-permute-start.7 = (f32[128,128]{1,0:T(8,128)S(1)}, f32[128,128]{1,0:T(8,128)S(1)}, u32[]{:S(2)}, u32[]{:S(2)}) collective-permute-start(f32[128,128]{1,0:T(8,128)S(1)} %get-tuple-element.28), channel_id=1, source_target_pairs={{1,2},{2,1},{5,6},{6,5},{9,10},{10,9},{13,14},{14,13},{17,18},{18,... | collective-permute-start | bytes 196616 | tf_op jit(solution)/shard_map/ppermute | solution.py:463
  19.3 2.6 %collective-permute-start.8 = (f32[128,128]{1,0:T(8,128)S(1)}, f32[128,128]{1,0:T(8,128)S(1)}, u32[]{:S(2)}, u32[]{:S(2)}) collective-permute-start(f32[128,128]{1,0:T(8,128)S(1)} %get-tuple-element.29), channel_id=1, source_target_pairs={{0,1},{2,3},{1,0},{3,2},{4,5},{6,7},{5,4},{7,6},{8,9},{10,11},{9,8... | collective-permute-start | bytes 196616 | tf_op jit(solution)/shard_map/ppermute | solution.py:463

commit v12 on v10

--- a/solution.py
+++ b/solution.py
@@ -125,7 +125,8 @@
 def first_kernel(pops_at, solid_at, table_at, index_at, own, two, one, *scratch):
     pops, solid, table, index, sems = scratch
     small = ((table_at, table), (index_at, index), (solid_at, solid))
-    planes = [(pops_at.at[:, z], pops.at[:, z]) for z in range(NZ)]
+    parts = [(pl.ds(q, 9), z) for z in range(NZ) for q in (0, 9, 18)]
+    planes = [(pops_at.at[part], pops.at[part]) for part in parts]
     copies = [
         pltpu.make_async_copy(source, target, sems.at[i])
         for i, (source, target) in enumerate((*small, *planes))
@@ -140,7 +141,8 @@
         aim = jnp.zeros((8, 128), F32)
         for y in range(NY):
             aim = jnp.where(rows == y, table[z, index[y]], aim)
-        copies[3 + z].wait()
+        for copy in copies[3 * z + 3 : 3 * z + 6]:
+            copy.wait()
         post = relaxed([pops[q, z] for q in range(27)], sponge, aim)
         for q in range(27):
             own[pl.ds((q * NZ + z) * 8, 8), :] = post[q]
@@ -199,39 +201,40 @@
 def add_rows(full, above, below):
     for c in range(CHANNELS):
         for halo, near in ((below, 1), (above, PITCH - 2)):
-            full[c, pl.ds(plane_at(0) + near, NZ, stride=PITCH), :] = halo[pl.ds(c * NZ, NZ), :]
+            full[pl.ds(c * ROWS + plane_at(0) + near, NZ, stride=PITCH), :] = halo[pl.ds(c * NZ, NZ), :]
     for halo, far, group in ((below, 0, 6), (above, PITCH - 1, 0)):
         for k in range(9):
             q = 9 * (k // 3) + group + k % 3
-            full[q, pl.ds(plane_at(0) + far, NZ, stride=PITCH), :] = halo[
+            full[pl.ds(q * ROWS + plane_at(0) + far, NZ, stride=PITCH), :] = halo[
                 pl.ds((CHANNELS + k) * NZ, NZ), :
             ]
-        full[WALL, pl.ds(plane_at(0) + far, NZ, stride=PITCH), :] = halo[pl.ds(WALL * NZ, NZ), :]
+        full[pl.ds(WALL * ROWS + plane_at(0) + far, NZ, stride=PITCH), :] = halo[pl.ds(WALL * NZ, NZ), :]
 
 
 def add_own_planes(full, ceiling, floor):
     for halo, near, far, part in ((floor, -1, -2, 2), (ceiling, NZ, NZ + 1, 0)):
         for k, (c, z) in enumerate(z_blocks(near, far, part)):
-            full[c, pl.ds(plane_at(z) + 2, 8), :] = halo[pl.ds(8 * k, 8), :]
+            full[pl.ds(c * ROWS + plane_at(z) + 2, 8), :] = halo[pl.ds(8 * k, 8), :]
 
 
 def add_planes(full, ceiling, floor):
+    def put(count, channel, z, row, source):
+        start = channel * ROWS + plane_at(z) + row
+        full[pl.ds(start, count, stride=ROWS), :] = source
+
     for halo, near, far, part in ((floor, -1, -2, 2), (ceiling, NZ, NZ + 1, 0)):
-        for k, (c, z) in enumerate(z_blocks(near, far, part)):
-            for side, row in enumerate((1, PITCH - 2)):
-                start = side * Z_BLOCKS + k
-                full[c, pl.ds(plane_at(z) + row, 1), :] = halo[pl.ds(start, 1), :]
-        for side, (row, group) in enumerate(((0, 2), (PITCH - 1, 0))):
+        for side, (row, beyond, group) in enumerate(((1, 0, 2), (PITCH - 2, PITCH - 1, 0))):
+            start = side * Z_BLOCKS
+            put(CHANNELS, 0, near, row, halo[pl.ds(start, CHANNELS), :])
+            put(9, 9 * part, far, row, halo[pl.ds(start + CHANNELS, 9), :])
+            first, second = (halo[pl.ds(start + k, 1), :] for k in (WALL, Z_BLOCKS - 1))
+            put(1, WALL, far, row, second)
             start = Z_FAR + 12 * side
-            for k in range(9):
-                q = 9 * (k // 3) + 3 * group + k % 3
-                full[q, pl.ds(plane_at(near) + row, 1), :] = halo[pl.ds(start + k, 1), :]
             for k in range(3):
-                q = 9 * part + 3 * group + k
-                full[q, pl.ds(plane_at(far) + row, 1), :] = halo[pl.ds(start + 9 + k, 1), :]
-            for k, z in ((WALL, near), (Z_BLOCKS - 1, far)):
-                flag = halo[pl.ds(side * Z_BLOCKS + k, 1), :]
-                full[WALL, pl.ds(plane_at(z) + row, 1), :] = flag
+                put(3, 9 * k + 3 * group, near, beyond, halo[pl.ds(start + 3 * k, 3), :])
+            put(3, 9 * part + 3 * group, far, beyond, halo[pl.ds(start + 9, 3), :])
+            put(1, WALL, near, beyond, first)
+            put(1, WALL, far, beyond, second)
 
 
 def pack_columns(full, pack, tiles):
@@ -239,7 +242,7 @@
     for t in tiles:
         packed = jnp.zeros((8, 128), F32)
         for c in range(CHANNELS):
-            moved = pltpu.roll(full[c, pl.ds(PAD + 8 * t, 8), :], (4 * c + 2) % 128, 1)
+            moved = pltpu.roll(full[pl.ds(c * ROWS + PAD + 8 * t, 8), :], (4 * c + 2) % 128, 1)
             packed = jnp.where(slot == c, moved, packed)
         pack[pl.ds(8 * t, 8), :] = packed
 
@@ -250,7 +253,7 @@
 def fill_kernel(own, y_two, y_one, two, one, full, pack):
     for c in range(CHANNELS):
         for z in range(NZ):
-            full[c, pl.ds(plane_at(z) + 2, 8), :] = own[pl.ds((c * NZ + z) * 8, 8), :]
+            full[pl.ds(c * ROWS + plane_at(z) + 2, 8), :] = own[pl.ds((c * NZ + z) * 8, 8), :]
     by_parity("gy", y_one, y_two, functools.partial(add_rows, full))
     by_parity("gz", one, two, functools.partial(add_own_planes, full))
     pack_columns(full, pack, OWN_TILES)
@@ -264,12 +267,12 @@
 
     @pl.when(here == 0)
     def _():
-        full[WALL, pl.ds(plane_at(-1), PITCH), :] = jnp.ones((PITCH, 128), F32)
+        full[pl.ds(WALL * ROWS + plane_at(-1), PITCH), :] = jnp.ones((PITCH, 128), F32)
 
     @pl.when(here == last)
     def _():
         for q in range(9):
-            full[q, pl.ds(plane_at(NZ), PITCH), :] = full[q + 18, pl.ds(plane_at(NZ - 1), PITCH), :]
+            full[pl.ds(q * ROWS + plane_at(NZ), PITCH), :] = full[pl.ds((q + 18) * ROWS + plane_at(NZ - 1), PITCH), :]
 
     pack_columns(full, pack, [t for t in range(FLAT // 8) if t not in OWN_TILES])
     columns[pl.ds(PAD, 128), :] = pack[...].T
@@ -301,7 +304,7 @@
     sponge = (lax.axis_index("gx") * NX + lane_ids()) < SPONGE
     for t in range(ROWS // 8):
         rows = pl.ds(8 * t, 8)
-        flags = full[WALL, rows, :]
+        flags = full[pl.ds(WALL * ROWS + 8 * t, 8), :]
         for cx in (-1, 0, 1):
             walls[cx + 1, rows, :] = pltpu.roll(flags, cx % 128, 1) if cx else flags
     for u in range(UNITS):
@@ -311,14 +314,14 @@
         for q in range(27):
             cx, cy, cz = VEL[q]
             start = cell - PITCH * cz - cy
-            value = full[q, pl.ds(start, 8), :]
+            value = full[pl.ds(q * ROWS + start, 8), :]
             if cx:
                 value = pltpu.roll(value, cx % 128, 1)
             if q != 13:
                 blocked = walls[cx + 1, pl.ds(start, 8), :] != 0.0
-                value = jnp.where(blocked, full[26 - q, pl.ds(cell, 8), :], value)
+                value = jnp.where(blocked, full[pl.ds((26 - q) * ROWS + cell, 8), :], value)
             f.append(jnp.where(solid, WEIGHT[q], value))
-        done = relaxed(f, sponge, full[AIM, pl.ds(cell, 8), :])
+        done = relaxed(f, sponge, full[pl.ds(AIM * ROWS + cell, 8), :])
         for q in range(27):
             post[q, pl.ds(8 * u, 8), :] = done[q]
 
@@ -328,7 +331,7 @@
             post[q, pl.ds((NZ + 1) * PITCH, PITCH), :] = post[q + 18, pl.ds(NZ * PITCH, PITCH), :]
 
 
-def last_kernel(full, block, columns, x_one, x_two, out, west, east, walls, back, done, sems):
+def last_kernel(full, block, columns, x_one, x_two, out, west, east, column, walls, back, done, sems):
     here_x, size_x = lax.axis_index("gx"), lax.axis_size("gx")
     top = lax.axis_index("gz") == lax.axis_size("gz") - 1
     lanes, rows = lane_ids(), row_ids()
@@ -365,35 +368,49 @@
         if q != 13:
             value = jnp.where(shifted(strip[WALL], q) != 0.0, strip[26 - q], value)
         moved.append(jnp.where(strip[WALL] != 0.0, WEIGHT[q], value))
-    column = here_x * NX + jnp.where(rows < 4, rows - 2, rows + (NX - 6))
-    column = lax.rem(column + size_x * NX, size_x * NX)
-    sides = relaxed(moved, column < SPONGE, strip[AIM])
+    place = here_x * NX + jnp.where(rows < 4, rows - 2, rows + (NX - 6))
+    place = lax.rem(place + size_x * NX, size_x * NX)
+    sides = relaxed(moved, place < SPONGE, strip[AIM])
     lid = top & (lanes >= (NZ + 2) * PITCH) & (lanes < (NZ + 3) * PITCH)
     for q in range(9):
         sides[q] = jnp.where(lid, pltpu.roll(sides[q + 18], PITCH, 1), sides[q])
-    ends = [jnp.where(rows == 1, pltpu.roll(side, 4, 0), side) for side in sides]
-    ends += [jnp.zeros((8, 128), F32)] * 5
-    for i in range(2):
-        back[i] = jnp.concatenate(ends[16 * i : 16 * i + 16], axis=0).T
-    pairs = [jnp.where(rows < 4, sides[3 * k + 2], sides[3 * k]) for k in range(9)]
-    pairs += [strip[WALL]] + [jnp.zeros((8, 128), F32)] * 6
-    back[2] = jnp.concatenate(pairs, axis=0).T
-
-    def column_at(i, place, lane, start):
-        return pltpu.roll(back[i, pl.ds(start, 8), :], (lane - place) % 128, 1)
+    for q, side in enumerate(sides + [strip[WALL]]):
+        column[pl.ds(PAD + 8 * q, 8), :] = side
+
+    def picked(wanted):
+        value = None
+        for sublane, (q, row) in enumerate(wanted):
+            moved = column[pl.ds(PAD + 8 * q + row - sublane, 8), :]
+            value = moved if value is None else jnp.where(rows == sublane, moved, value)
+        return value
+
+    packed = []
+    for k in range(9):
+        a, b = 3 * k + 2, 3 * k
+        packed.append(
+            picked([(a, 5), (a, 2), (a, 1), (a, 2), (b, 5), (b, 2), (b, 5), (b, 6)])
+        )
+    rest = [(3 * k + 1, row) for k in range(9) for row in (5, 2)] + [(27, 1), (27, 6)]
+    packed += [picked(rest[i : i + 8]) for i in range(0, len(rest), 8)]
+    packed += [jnp.zeros((8, 128), F32)] * (16 - len(packed))
+    back[...] = jnp.concatenate(packed, axis=0).T
+
+    def column_at(place, lane, start):
+        return pltpu.roll(back[pl.ds(start, 8), :], (lane - place) % 128, 1)
 
     rim = (lanes == 0) | (lanes == 127)
 
     def rimmed(q, start):
-        ends = column_at(q // 16, 8 * (q % 16) + 2, 0, PITCH + start)
+        k = q // 3
+        ends = column_at((8 * k + 5, 73 + 2 * k, 8 * k + 1)[q % 3], 0, PITCH + start)
         return jnp.where(rim, ends, block[q, pl.ds(start, 8), :])
 
     for u in range(UNITS):
-        flags = full[WALL, pl.ds(PAD + PITCH + 8 * u, 8), :]
+        flags = full[pl.ds(WALL * ROWS + PAD + PITCH + 8 * u, 8), :]
         walls[1, pl.ds(8 * u, 8), :] = flags
-        for cx, edge, place in ((1, 0, 73), (-1, 127, 78)):
+        for cx, edge, place in ((1, 0, 90), (-1, 127, 91)):
             walls[cx + 1, pl.ds(8 * u, 8), :] = jnp.where(
-                lanes == edge, column_at(2, place, edge, PITCH + 8 * u), pltpu.roll(flags, cx % 128, 1)
+                lanes == edge, column_at(place, edge, PITCH + 8 * u), pltpu.roll(flags, cx % 128, 1)
             )
 
     copies = []
@@ -404,10 +421,10 @@
             cx, cy, cz = VEL[q]
             start = cell - PITCH * cz - cy
             if cx > 0:
-                side = column_at(2, 8 * (q // 3) + 1, 0, PITCH + start)
+                side = column_at(8 * (q // 3) + 2, 0, PITCH + start)
                 value = jnp.where(lanes < 2, side, pltpu.roll(block[q, pl.ds(start, 8), :], 1, 1))
             elif cx < 0:
-                side = column_at(2, 8 * (q // 3) + 5, 126, PITCH + start)
+                side = column_at(8 * (q // 3) + 6, 126, PITCH + start)
                 value = jnp.where(lanes > 125, side, pltpu.roll(block[q, pl.ds(start, 8), :], 127, 1))
             else:
                 value = rimmed(q, start)
@@ -442,7 +459,7 @@
             pltpu.VMEM(solid.shape, jnp.int32),
             pltpu.SMEM(profile_table.shape[::-1], F32),
             pltpu.SMEM(profile_index.shape, jnp.int32),
-            pltpu.SemaphoreType.DMA((3 + NZ,)),
+            pltpu.SemaphoreType.DMA((3 + 3 * NZ,)),
         ],
         compiler_params=PARAMS,
         name="collide",
@@ -472,7 +489,7 @@
     z_one = swap(z_one, "gz", 0, False)
     part, packed = pl.pallas_call(
         fill_kernel,
-        out_shape=[shape(CHANNELS, ROWS, 128), shape(128, 128)],
+        out_shape=[shape(CHANNELS * ROWS, 128), shape(128, 128)],
         in_specs=[VMEM] * 5,
         out_specs=[VMEM] * 2,
         compiler_params=PARAMS,
@@ -482,7 +499,7 @@
     full, packed, columns, message = pl.pallas_call(
         third_kernel,
         out_shape=[
-            shape(CHANNELS, ROWS, 128),
+            shape(CHANNELS * ROWS, 128),
             shape(128, 128),
             shape(PAD + 128 + PAD, 128),
             shape(X_ROWS, 128),
@@ -515,8 +532,9 @@
         scratch_shapes=[
             pltpu.VMEM((PAD + X_ROWS + PAD, 128), F32),
             pltpu.VMEM((PAD + X_ROWS + PAD, 128), F32),
+            pltpu.VMEM((PAD + 28 * 8 + PAD, 128), F32),
             pltpu.VMEM((3, UNITS * 8, 128), F32),
-            pltpu.VMEM((3, 128, 128), F32),
+            pltpu.VMEM((128, 128), F32),
             pltpu.VMEM((27, NZ, NY, NX), F32),
             pltpu.SemaphoreType.DMA((NZ,)),
         ],

time: 21.7 us -> 21.7 us (level)
  no operation moved by 1% of the time
where the time goes in v12:
time: 21.7 us; the launch traced here: 21.5 us
  starting transfers between devices  13.9 us (64%)
  Pallas kernels  4.34 us (20%)
  waiting for transfers between devices  3.12 us (14%)
    ppermute x7, starting transfers between devices, swap(): return lax.ppermute(value, axis, pairs + [(j, i) for i, j in pairs])  13.9 us
    ppermute x7, waiting for transfers between devices, swap(): return lax.ppermute(value, axis, pairs + [(j, i) for i, j in pairs])  3.12 us
    pallas_call x1, Pallas kernels, shards(): pl.pallas_call(last_kernel, out_shape=shape(27, NZ, NY, NX), in_specs=[VM...  1.42 us
    pallas_call x1, Pallas kernels, shards(): pl.pallas_call(first_kernel, out_shape=[shape(CHANNELS * NZ * 8, 128), sh...  1.33 us
    pallas_call x1, Pallas kernels, shards(): pl.pallas_call(block_kernel, out_shape=shape(27, UNITS * 8, 128), in_spec...  0.72 us
    pallas_call x1, Pallas kernels, shards(): pl.pallas_call(third_kernel, out_shape=[shape(CHANNELS * ROWS, 128), shap...  0.49 us
  transfers between devices with their start and end apart: 7, of which 3 were waited for; matrix products, arithmetic and copies ran while one was open for 0% of the time, Pallas kernels for 5%

profile of v12, /device:TPU:0, one launch (start us, length us, event | category | flops | bytes accessed | tf_op | source)
XLA Modules:
  0.0 21.5 jit_solution(11449509875472346522)
XLA Ops:
  0.0 1.3 %collide.1 = (f32[928,128]{1,0:T(8,128)S(1)}, f32[152,128]{1,0:T(8,128)S(1)}, f32[152,128]{1,0:T(8,128)S(1)}) custom-call(f32[27,4,8,128]{3,2,1,0:T(8,128)} %pops_at.1, s32[4,8,128]{2,1,0:T(8,128)} %solid_at.1, f32[4,8]{1,0:T(4,128)} %bitcast.1, s32[8]{0:T(128)} %index_at.1), custom_call_target="tpu_custom_call" | custom-call | tf_op jit(solution)/shard_map/collide/pallas_call | solution.py:452
  1.3 5.1 %collective-permute-start = (f32[152,128]{1,0:T(8,128)S(1)}, f32[152,128]{1,0:T(8,128)S(1)}, u32[]{:S(2)}, u32[]{:S(2)}) collective-permute-start(f32[152,128]{1,0:T(8,128)S(1)} %get-tuple-element.18), channel_id=1, source_target_pairs={{4,8},{12,0},{8,4},{0,12},{5,9},{13,1},{9,5},{1,13},{6,10},{14,2},... | collective-permute-start | bytes 233480 | tf_op jit(solution)/shard_map/ppermute | solution.py:444
  6.5 0.0 collective-permute-start.1
  6.5 0.7 %collective-permute-start.2 = (f32[312,128]{1,0:T(8,128)S(1)}, f32[312,128]{1,0:T(8,128)S(1)}, u32[]{:S(2)}, u32[]{:S(2)}) collective-permute-start(f32[312,128]{1,0:T(8,128)S(1)} %get-tuple-element.20), channel_id=1, source_target_pairs={{1,2},{2,1},{5,6},{6,5},{9,10},{10,9},{13,14},{14,13},{17,18},{18,... | collective-permute-start | bytes 479240 | tf_op jit(solution)/shard_map/ppermute | solution.py:444
  7.2 2.9 %collective-permute-start.3 = (f32[312,128]{1,0:T(8,128)S(1)}, f32[312,128]{1,0:T(8,128)S(1)}, u32[]{:S(2)}, u32[]{:S(2)}) collective-permute-start(f32[312,128]{1,0:T(8,128)S(1)} %get-tuple-element.21), channel_id=1, source_target_pairs={{0,1},{2,3},{1,0},{3,2},{4,5},{6,7},{5,4},{7,6},{8,9},{10,11},{9,8... | collective-permute-start | bytes 479240 | tf_op jit(solution)/shard_map/ppermute | solution.py:444
  10.1 0.0 collective-permute-done.y_two
  10.1 0.8 %collective-permute-done.1.y_one = f32[152,128]{1,0:T(8,128)S(1)} collective-permute-done((f32[152,128]{1,0:T(8,128)S(1)}, f32[152,128]{1,0:T(8,128)S(1)}, u32[]{:S(2)}, u32[]{:S(2)}) %collective-permute-start.1) | collective-permute-done | bytes 77856 | tf_op jit(solution)/shard_map/ppermute | solution.py:444
  10.9 0.7 %collective-permute-start.4 = (f32[104,128]{1,0:T(8,128)S(1)}, f32[104,128]{1,0:T(8,128)S(1)}, u32[]{:S(2)}, u32[]{:S(2)}) collective-permute-start(f32[104,128]{1,0:T(8,128)S(1)} %get-tuple-element.24), channel_id=1, source_target_pairs={{1,2},{2,1},{5,6},{6,5},{9,10},{10,9},{13,14},{14,13},{17,18},{18,... | collective-permute-start | bytes 159752 | tf_op jit(solution)/shard_map/ppermute | solution.py:444
  11.6 3.0 %collective-permute-start.5 = (f32[104,128]{1,0:T(8,128)S(1)}, f32[104,128]{1,0:T(8,128)S(1)}, u32[]{:S(2)}, u32[]{:S(2)}) collective-permute-start(f32[104,128]{1,0:T(8,128)S(1)} %get-tuple-element.25), channel_id=1, source_target_pairs={{0,1},{2,3},{1,0},{3,2},{4,5},{6,7},{5,4},{7,6},{8,9},{10,11},{9,8... | collective-permute-start | bytes 159752 | tf_op jit(solution)/shard_map/ppermute | solution.py:444
  14.5 0.0 collective-permute-done.2.two
  14.5 0.0 collective-permute-done.3.one
  14.5 0.3 %fill.1 = (f32[3248,128]{1,0:T(8,128)S(1)}, f32[128,128]{1,0:T(8,128)S(1)}) custom-call(f32[928,128]{1,0:T(8,128)S(1)} %get-tuple-element.17.own, f32[152,128]{1,0:T(8,128)S(1)} %collective-permute-done.y_two, f32[152,128]{1,0:T(8,128)S(1)} %collective-permute-done.1.y_one, f32[312,128]{1,0:T(8,128)S(1)} %collective-permute-done.2.two, ...), custom_call_target="tpu_custom_call" | custom-call | flops 1000000 | bytes 4194304 | tf_op jit(solution)/shard_map/fill/pallas_call | solution.py:490
  14.9 0.0 collective-permute-done.4.z_two
  14.9 0.5 %collective-permute-done.5.z_one = f32[104,128]{1,0:T(8,128)S(1)} collective-permute-done((f32[104,128]{1,0:T(8,128)S(1)}, f32[104,128]{1,0:T(8,128)S(1)}, u32[]{:S(2)}, u32[]{:S(2)}) %collective-permute-start.5) | collective-permute-done | bytes 53280 | tf_op jit(solution)/shard_map/ppermute | solution.py:444
  15.4 0.5 %pack_x.1 = (f32[3248,128]{1,0:T(8,128)S(1)}, f32[128,128]{1,0:T(8,128)S(1)}, f32[144,128]{1,0:T(8,128)S(1)}, f32[56,128]{1,0:T(8,128)S(1)}) custom-call(f32[3248,128]{1,0:T(8,128)S(1)} %get-tuple-element.22.part, f32[128,128]{1,0:T(8,128)S(1)} %get-tuple-element.23.packed, ...), custom_call_target="tpu_custom_call", output_to_operand_aliasing={{0}: (0, {}), {1}: (1, {})} | custom-call | tf_op jit(solution)/shard_map/pack_x/pallas_call | solution.py:499
  15.9 1.6 %collective-permute-start.6 = (f32[56,128]{1,0:T(8,128)S(1)}, f32[56,128]{1,0:T(8,128)S(1)}, u32[]{:S(2)}, u32[]{:S(2)}) collective-permute-start(f32[56,128]{1,0:T(8,128)S(1)} %get-tuple-element.28), channel_id=1, source_target_pairs={{0,16},{16,0},{1,17},{17,1},{2,18},{18,2},{3,19},{19,3},{4,20},{20... | collective-permute-start | bytes 86024 | tf_op jit(solution)/shard_map/ppermute | solution.py:444
  17.5 0.7 %block.1 = f32[27,72,128]{2,1,0:T(8,128)S(1)} custom-call(f32[3248,128]{1,0:T(8,128)S(1)} %get-tuple-element.26.full), custom_call_target="tpu_custom_call" | custom-call | flops 4976640 | bytes 4194304 | tf_op jit(solution)/shard_map/block/pallas_call | solution.py:515
  18.2 1.8 %collective-permute-done.6.x_one.x_two = f32[56,128]{1,0:T(8,128)S(1)} collective-permute-done((f32[56,128]{1,0:T(8,128)S(1)}, f32[56,128]{1,0:T(8,128)S(1)}, u32[]{:S(2)}, u32[]{:S(2)}) %collective-permute-start.6) | collective-permute-done | bytes 28704 | tf_op jit(solution)/shard_map/ppermute | solution.py:444
  20.0 1.4 %finish.1 = f32[27,4,8,128]{3,2,1,0:T(8,128)} custom-call(f32[3248,128]{1,0:T(8,128)S(1)} %get-tuple-element.26.full, f32[27,72,128]{2,1,0:T(8,128)S(1)} %block.1, f32[144,128]{1,0:T(8,128)S(1)} %get-tuple-element.27.columns, f32[56,128]{1,0:T(8,128)S(1)} %collective-permute-done.6.x_one.x_two, f32[56,128]{1,0:T(8,128)S(1)} %collective-permute-done.6.x_one.x_two), custom_call_target="tpu_custom_call" | custom-call | tf_op jit(solution)/shard_map/finish/pallas_call | solution.py:527
  (2 shorter events, 0.0 us)
Async XLA Ops:
  1.3 8.7 %collective-permute-start = (f32[152,128]{1,0:T(8,128)S(1)}, f32[152,128]{1,0:T(8,128)S(1)}, u32[]{:S(2)}, u32[]{:S(2)}) collective-permute-start(f32[152,128]{1,0:T(8,128)S(1)} %get-tuple-element.18), channel_id=1, source_target_pairs={{4,8},{12,0},{8,4},{0,12},{5,9},{13,1},{9,5},{1,13},{6,10},{14,2},... | collective-permute-start | bytes 233480 | tf_op jit(solution)/shard_map/ppermute | solution.py:444
  6.5 4.4 %collective-permute-start.1 = (f32[152,128]{1,0:T(8,128)S(1)}, f32[152,128]{1,0:T(8,128)S(1)}, u32[]{:S(2)}, u32[]{:S(2)}) collective-permute-start(f32[152,128]{1,0:T(8,128)S(1)} %get-tuple-element.19), channel_id=1, source_target_pairs={{0,4},{8,12},{4,0},{12,8},{1,5},{9,13},{5,1},{13,9},{2,6},{10,14},... | collective-permute-start | bytes 233480 | tf_op jit(solution)/shard_map/ppermute | solution.py:444
  6.5 8.0 %collective-permute-start.2 = (f32[312,128]{1,0:T(8,128)S(1)}, f32[312,128]{1,0:T(8,128)S(1)}, u32[]{:S(2)}, u32[]{:S(2)}) collective-permute-start(f32[312,128]{1,0:T(8,128)S(1)} %get-tuple-element.20), channel_id=1, source_target_pairs={{1,2},{2,1},{5,6},{6,5},{9,10},{10,9},{13,14},{14,13},{17,18},{18,... | collective-permute-start | bytes 479240 | tf_op jit(solution)/shard_map/ppermute | solution.py:444
  7.2 7.4 %collective-permute-start.3 = (f32[312,128]{1,0:T(8,128)S(1)}, f32[312,128]{1,0:T(8,128)S(1)}, u32[]{:S(2)}, u32[]{:S(2)}) collective-permute-start(f32[312,128]{1,0:T(8,128)S(1)} %get-tuple-element.21), channel_id=1, source_target_pairs={{0,1},{2,3},{1,0},{3,2},{4,5},{6,7},{5,4},{7,6},{8,9},{10,11},{9,8... | collective-permute-start | bytes 479240 | tf_op jit(solution)/shard_map/ppermute | solution.py:444
  10.9 4.0 %collective-permute-start.4 = (f32[104,128]{1,0:T(8,128)S(1)}, f32[104,128]{1,0:T(8,128)S(1)}, u32[]{:S(2)}, u32[]{:S(2)}) collective-permute-start(f32[104,128]{1,0:T(8,128)S(1)} %get-tuple-element.24), channel_id=1, source_target_pairs={{1,2},{2,1},{5,6},{6,5},{9,10},{10,9},{13,14},{14,13},{17,18},{18,... | collective-permute-start | bytes 159752 | tf_op jit(solution)/shard_map/ppermute | solution.py:444
  11.6 3.9 %collective-permute-start.5 = (f32[104,128]{1,0:T(8,128)S(1)}, f32[104,128]{1,0:T(8,128)S(1)}, u32[]{:S(2)}, u32[]{:S(2)}) collective-permute-start(f32[104,128]{1,0:T(8,128)S(1)} %get-tuple-element.25), channel_id=1, source_target_pairs={{0,1},{2,3},{1,0},{3,2},{4,5},{6,7},{5,4},{7,6},{8,9},{10,11},{9,8... | collective-permute-start | bytes 159752 | tf_op jit(solution)/shard_map/ppermute | solution.py:444
  15.9 4.1 %collective-permute-start.6 = (f32[56,128]{1,0:T(8,128)S(1)}, f32[56,128]{1,0:T(8,128)S(1)}, u32[]{:S(2)}, u32[]{:S(2)}) collective-permute-start(f32[56,128]{1,0:T(8,128)S(1)} %get-tuple-element.28), channel_id=1, source_target_pairs={{0,16},{16,0},{1,17},{17,1},{2,18},{18,2},{3,19},{19,3},{4,20},{20... | collective-permute-start | bytes 86024 | tf_op jit(solution)/shard_map/ppermute | solution.py:444

commit v13 on v12

--- a/solution.py
+++ b/solution.py
@@ -30,7 +30,8 @@
 HBM = pl.BlockSpec(memory_space=pltpu.HBM)
 F32 = jnp.float32
 
-Y_ROWS = (CHANNELS + 9) * NZ
+MIXED = 24
+Y_ROWS = (MIXED + 1 + 9) * NZ
 Z_BLOCKS = CHANNELS + 10
 Z_FAR = 2 * Z_BLOCKS
 Z_ROWS = -(-(Z_FAR + 2 * 12) // 8) * 8
@@ -150,10 +151,22 @@
         own[pl.ds((AIM * NZ + z) * 8, 8), :] = aim
 
     def pack(yup, ydown):
+        inside = lax.rem(lanes, 4)
         for out, edge, second, part in ((yup, 7, 6, 6), (ydown, 0, 1, 0)):
-            out[pl.ds(0, CHANNELS * NZ), :] = own[pl.ds(edge, CHANNELS * NZ, stride=8), :]
+            back = 15 - part
+            for first, count, place in ((0, back, 0), (back + 3, 24 - back, back)):
+                out[pl.ds(place * NZ, count * NZ), :] = own[
+                    pl.ds(first * NZ * 8 + edge, count * NZ, stride=8), :
+                ]
+            for z in range(NZ):
+                west, east, aim, flag = (
+                    own[pl.ds((c * NZ + z) * 8, 8), :] for c in (back, back + 2, AIM, WALL)
+                )
+                mixed = jnp.where(inside < 2, jnp.where(inside == 0, west, aim), flag)
+                mixed = jnp.where(inside == 3, east, mixed)
+                out[pl.ds(MIXED * NZ + z, 1), :] = mixed[edge : edge + 1]
             for a in range(3):
-                out[pl.ds((CHANNELS + 3 * a) * NZ, 3 * NZ), :] = own[
+                out[pl.ds((MIXED + 1 + 3 * a) * NZ, 3 * NZ), :] = own[
                     pl.ds((9 * a + part) * NZ * 8 + second, 3 * NZ, stride=8), :
                 ]
 
@@ -169,46 +182,88 @@
     by_parity("gz", one, two, pack)
 
 
-def second_kernel(own, y_two, y_one, z_two, z_one):
-    by_parity(
-        "gy",
-        y_one,
-        y_two,
-        lambda above, below: by_parity(
-            "gz", z_one, z_two, lambda zup, zdown: pack_planes(own, below, above, zup, zdown)
-        ),
-    )
-
-
-def pack_planes(own, below, above, zup, zdown):
+def y_runs(part):
+    back = 15 - part
+    return (0, back, 0), (back, 3, None), (back + 3, 24 - back, back)
+
+
+def spread_mixed(below, above, flags, aims):
+    flags[pl.ds(0, NZ), :] = below[pl.ds(MIXED * NZ, NZ), :]
+    flags[pl.ds(NZ, NZ), :] = above[pl.ds(MIXED * NZ, NZ), :]
+    mixed = flags[...]
+    inside = lax.rem(lane_ids(), 4)
+    moved = {k: pltpu.roll(mixed, k % 128, 1) if k else mixed for k in (-2, -1, 0, 1, 2)}
+
+    def from_lane(source):
+        value = moved[0]
+        for lane in range(4):
+            if lane != source:
+                value = jnp.where(inside == lane, moved[lane - source], value)
+        return value
+
+    aims[...] = from_lane(1)
+    flags[...] = from_lane(2)
+
+
+def second_kernel(y_two, y_one, z_two, z_one, flags, aims):
+    def pack(above, below):
+        spread_mixed(below, above, flags, aims)
+        by_parity(
+            "gz",
+            z_one,
+            z_two,
+            lambda zup, zdown: pack_planes(below, above, flags, aims, zup, zdown),
+        )
+
+    by_parity("gy", y_one, y_two, pack)
+
+
+def pack_planes(below, above, flags, aims, zup, zdown):
     for out, first, second, part in ((zup, NZ - 1, NZ - 2, 2), (zdown, 0, 1, 0)):
-        for side, halo in enumerate((below, above)):
+        for side, (halo, inward) in enumerate(((below, 6), (above, 0))):
             near = side * Z_BLOCKS
-            out[pl.ds(near, CHANNELS), :] = halo[pl.ds(first, CHANNELS, stride=NZ), :]
-            out[pl.ds(near + CHANNELS, 9), :] = halo[pl.ds(9 * part * NZ + second, 9, stride=NZ), :]
-            out[pl.ds(near + Z_BLOCKS - 1, 1), :] = halo[pl.ds(WALL * NZ + second, 1), :]
+            for channel, count, place in y_runs(inward):
+                if place is None:
+                    row = halo[pl.ds(MIXED * NZ + first, 1), :]
+                    out[pl.ds(near + channel, 3), :] = jnp.broadcast_to(row, (3, 128))
+                else:
+                    out[pl.ds(near + channel, count), :] = halo[
+                        pl.ds(place * NZ + first, count, stride=NZ), :
+                    ]
+            out[pl.ds(near + WALL, 1), :] = flags[pl.ds(side * NZ + first, 1), :]
+            out[pl.ds(near + AIM, 1), :] = aims[pl.ds(side * NZ + first, 1), :]
+            place = 15 if part else 0
+            out[pl.ds(near + CHANNELS, 9), :] = halo[pl.ds(place * NZ + second, 9, stride=NZ), :]
+            out[pl.ds(near + Z_BLOCKS - 1, 1), :] = flags[pl.ds(side * NZ + second, 1), :]
             far = Z_FAR + 12 * side
-            out[pl.ds(far, 9), :] = halo[pl.ds(CHANNELS * NZ + first, 9, stride=NZ), :]
-            out[pl.ds(far + 9, 3), :] = halo[
-                pl.ds((CHANNELS + 3 * part) * NZ + second, 3, stride=NZ), :
-            ]
+            start = (MIXED + 1) * NZ
+            out[pl.ds(far, 9), :] = halo[pl.ds(start + first, 9, stride=NZ), :]
+            out[pl.ds(far + 9, 3), :] = halo[pl.ds(start + 3 * part * NZ + second, 3, stride=NZ), :]
 
 
 def plane_at(z):
     return PAD + (z + 2) * PITCH
 
 
-def add_rows(full, above, below):
-    for c in range(CHANNELS):
-        for halo, near in ((below, 1), (above, PITCH - 2)):
-            full[pl.ds(c * ROWS + plane_at(0) + near, NZ, stride=PITCH), :] = halo[pl.ds(c * NZ, NZ), :]
-    for halo, far, group in ((below, 0, 6), (above, PITCH - 1, 0)):
+def add_rows(full, flags, aims, above, below):
+    spread_mixed(below, above, flags, aims)
+
+    def put(channel, row, source):
+        full[pl.ds(channel * ROWS + plane_at(0) + row, NZ, stride=PITCH), :] = source
+
+    sides = ((below, 1, 0, 6), (above, PITCH - 2, PITCH - 1, 0))
+    for side, (halo, near, far, inward) in enumerate(sides):
+        for first, count, place in y_runs(inward):
+            for k in range(count):
+                row = MIXED if place is None else place + k
+                put(first + k, near, halo[pl.ds(row * NZ, NZ), :])
+        flag = flags[pl.ds(side * NZ, NZ), :]
+        put(WALL, near, flag)
+        put(WALL, far, flag)
+        put(AIM, near, aims[pl.ds(side * NZ, NZ), :])
         for k in range(9):
-            q = 9 * (k // 3) + group + k % 3
-            full[pl.ds(q * ROWS + plane_at(0) + far, NZ, stride=PITCH), :] = halo[
-                pl.ds((CHANNELS + k) * NZ, NZ), :
-            ]
-        full[pl.ds(WALL * ROWS + plane_at(0) + far, NZ, stride=PITCH), :] = halo[pl.ds(WALL * NZ, NZ), :]
+            q = 9 * (k // 3) + inward + k % 3
+            put(q, far, halo[pl.ds((MIXED + 1 + k) * NZ, NZ), :])
 
 
 def add_own_planes(full, ceiling, floor):
@@ -250,11 +305,11 @@
 OWN_TILES = range(2 * PITCH // 8, (NZ + 2) * PITCH // 8)
 
 
-def fill_kernel(own, y_two, y_one, two, one, full, pack):
+def fill_kernel(own, y_two, y_one, two, one, full, pack, flags, aims):
     for c in range(CHANNELS):
         for z in range(NZ):
             full[pl.ds(c * ROWS + plane_at(z) + 2, 8), :] = own[pl.ds((c * NZ + z) * 8, 8), :]
-    by_parity("gy", y_one, y_two, functools.partial(add_rows, full))
+    by_parity("gy", y_one, y_two, functools.partial(add_rows, full, flags, aims))
     by_parity("gz", one, two, functools.partial(add_own_planes, full))
     pack_columns(full, pack, OWN_TILES)
     pack[pl.ds(FLAT, 128 - FLAT), :] = jnp.zeros((128 - FLAT, 128), F32)
@@ -479,12 +534,13 @@
     z_two, z_one = pl.pallas_call(
         second_kernel,
         out_shape=[shape(Z_ROWS, 128)] * 2,
-        in_specs=[VMEM] * 3,
+        in_specs=[VMEM] * 2,
         out_specs=[VMEM] * 2,
+        scratch_shapes=[pltpu.VMEM((2 * NZ, 128), F32)] * 2,
         compiler_params=PARAMS,
         cost_estimate=pl.CostEstimate(flops=10**9, bytes_accessed=2**20, transcendentals=0),
         name="pack_z",
-    )(own, y_two, y_one)
+    )(y_two, y_one)
     z_two = swap(z_two, "gz", 1, False)
     z_one = swap(z_one, "gz", 0, False)
     part, packed = pl.pallas_call(
@@ -492,6 +548,7 @@
         out_shape=[shape(CHANNELS * ROWS, 128), shape(128, 128)],
         in_specs=[VMEM] * 5,
         out_specs=[VMEM] * 2,
+        scratch_shapes=[pltpu.VMEM((2 * NZ, 128), F32)] * 2,
         compiler_params=PARAMS,
         cost_estimate=pl.CostEstimate(flops=10**6, bytes_accessed=2**22, transcendentals=0),
         name="fill",

time: 21.7 us -> 21.6 us (level)
  transfers between devices with their start and end apart: 7 -> 7, of which waited for: 3 -> 3; matrix products, arithmetic and copies ran while one was open for 0% -> 0% of each run, Pallas kernels for 5% -> 6%
where the time goes in v13:
time: 21.6 us; the launch traced here: 21.4 us
  starting transfers between devices  13.9 us (64%)
  Pallas kernels  4.45 us (21%)
  waiting for transfers between devices  2.99 us (14%)
    ppermute x7, starting transfers between devices, swap(): return lax.ppermute(value, axis, pairs + [(j, i) for i, j in pairs])  13.9 us
    ppermute x7, waiting for transfers between devices, swap(): return lax.ppermute(value, axis, pairs + [(j, i) for i, j in pairs])  2.99 us
    pallas_call x1, Pallas kernels, shards(): pl.pallas_call(last_kernel, out_shape=shape(27, NZ, NY, NX), in_specs=[VM...  1.42 us
    pallas_call x1, Pallas kernels, shards(): pl.pallas_call(first_kernel, out_shape=[shape(CHANNELS * NZ * 8, 128), sh...  1.33 us
    pallas_call x1, Pallas kernels, shards(): pl.pallas_call(block_kernel, out_shape=shape(27, UNITS * 8, 128), in_spec...  0.72 us
    pallas_call x1, Pallas kernels, shards(): pl.pallas_call(third_kernel, out_shape=[shape(CHANNELS * ROWS, 128), shap...  0.49 us
  transfers between devices with their start and end apart: 7, of which 3 were waited for; matrix products, arithmetic and copies ran while one was open for 0% of the time, Pallas kernels for 6%

profile of v13, /device:TPU:0, one launch (start us, length us, event | category | flops | bytes accessed | tf_op | source)
XLA Modules:
  0.0 21.4 jit_solution(14908307936518681135)
XLA Ops:
  0.0 1.3 %collide.1 = (f32[928,128]{1,0:T(8,128)S(1)}, f32[136,128]{1,0:T(8,128)S(1)}, f32[136,128]{1,0:T(8,128)S(1)}) custom-call(f32[27,4,8,128]{3,2,1,0:T(8,128)} %pops_at.1, s32[4,8,128]{2,1,0:T(8,128)} %solid_at.1, f32[4,8]{1,0:T(4,128)} %bitcast.1, s32[8]{0:T(128)} %index_at.1), custom_call_target="tpu_custom_call" | custom-call | tf_op jit(solution)/shard_map/collide/pallas_call | solution.py:507
  1.3 5.1 %collective-permute-start = (f32[136,128]{1,0:T(8,128)S(1)}, f32[136,128]{1,0:T(8,128)S(1)}, u32[]{:S(2)}, u32[]{:S(2)}) collective-permute-start(f32[136,128]{1,0:T(8,128)S(1)} %get-tuple-element.18), channel_id=1, source_target_pairs={{4,8},{12,0},{8,4},{0,12},{5,9},{13,1},{9,5},{1,13},{6,10},{14,2},... | collective-permute-start | bytes 208904 | tf_op jit(solution)/shard_map/ppermute | solution.py:499
  6.5 0.0 collective-permute-start.1
  6.5 0.7 %collective-permute-start.2 = (f32[312,128]{1,0:T(8,128)S(1)}, f32[312,128]{1,0:T(8,128)S(1)}, u32[]{:S(2)}, u32[]{:S(2)}) collective-permute-start(f32[312,128]{1,0:T(8,128)S(1)} %get-tuple-element.20), channel_id=1, source_target_pairs={{1,2},{2,1},{5,6},{6,5},{9,10},{10,9},{13,14},{14,13},{17,18},{18,... | collective-permute-start | bytes 479240 | tf_op jit(solution)/shard_map/ppermute | solution.py:499
  7.2 2.9 %collective-permute-start.3 = (f32[312,128]{1,0:T(8,128)S(1)}, f32[312,128]{1,0:T(8,128)S(1)}, u32[]{:S(2)}, u32[]{:S(2)}) collective-permute-start(f32[312,128]{1,0:T(8,128)S(1)} %get-tuple-element.21), channel_id=1, source_target_pairs={{0,1},{2,3},{1,0},{3,2},{4,5},{6,7},{5,4},{7,6},{8,9},{10,11},{9,8... | collective-permute-start | bytes 479240 | tf_op jit(solution)/shard_map/ppermute | solution.py:499
  10.1 0.0 collective-permute-done.y_two
  10.1 0.7 %collective-permute-done.1.y_one = f32[136,128]{1,0:T(8,128)S(1)} collective-permute-done((f32[136,128]{1,0:T(8,128)S(1)}, f32[136,128]{1,0:T(8,128)S(1)}, u32[]{:S(2)}, u32[]{:S(2)}) %collective-permute-start.1) | collective-permute-done | bytes 69664 | tf_op jit(solution)/shard_map/ppermute | solution.py:499
  10.8 0.1 pack_z.1
  10.9 0.7 %collective-permute-start.4 = (f32[104,128]{1,0:T(8,128)S(1)}, f32[104,128]{1,0:T(8,128)S(1)}, u32[]{:S(2)}, u32[]{:S(2)}) collective-permute-start(f32[104,128]{1,0:T(8,128)S(1)} %get-tuple-element.24), channel_id=1, source_target_pairs={{1,2},{2,1},{5,6},{6,5},{9,10},{10,9},{13,14},{14,13},{17,18},{18,... | collective-permute-start | bytes 159752 | tf_op jit(solution)/shard_map/ppermute | solution.py:499
  11.5 2.9 %collective-permute-start.5 = (f32[104,128]{1,0:T(8,128)S(1)}, f32[104,128]{1,0:T(8,128)S(1)}, u32[]{:S(2)}, u32[]{:S(2)}) collective-permute-start(f32[104,128]{1,0:T(8,128)S(1)} %get-tuple-element.25), channel_id=1, source_target_pairs={{0,1},{2,3},{1,0},{3,2},{4,5},{6,7},{5,4},{7,6},{8,9},{10,11},{9,8... | collective-permute-start | bytes 159752 | tf_op jit(solution)/shard_map/ppermute | solution.py:499
  14.4 0.0 collective-permute-done.2.two
  14.4 0.0 collective-permute-done.3.one
  14.4 0.4 %fill.1 = (f32[3248,128]{1,0:T(8,128)S(1)}, f32[128,128]{1,0:T(8,128)S(1)}) custom-call(f32[928,128]{1,0:T(8,128)S(1)} %get-tuple-element.17.own, f32[136,128]{1,0:T(8,128)S(1)} %collective-permute-done.y_two, f32[136,128]{1,0:T(8,128)S(1)} %collective-permute-done.1.y_one, f32[312,128]{1,0:T(8,128)S(1)} %collective-permute-done.2.two, ...), custom_call_target="tpu_custom_call" | custom-call | flops 1000000 | bytes 4194304 | tf_op jit(solution)/shard_map/fill/pallas_call | solution.py:546
  14.8 0.0 collective-permute-done.4.z_two
  14.8 0.5 %collective-permute-done.5.z_one = f32[104,128]{1,0:T(8,128)S(1)} collective-permute-done((f32[104,128]{1,0:T(8,128)S(1)}, f32[104,128]{1,0:T(8,128)S(1)}, u32[]{:S(2)}, u32[]{:S(2)}) %collective-permute-start.5) | collective-permute-done | bytes 53280 | tf_op jit(solution)/shard_map/ppermute | solution.py:499
  15.3 0.5 %pack_x.1 = (f32[3248,128]{1,0:T(8,128)S(1)}, f32[128,128]{1,0:T(8,128)S(1)}, f32[144,128]{1,0:T(8,128)S(1)}, f32[56,128]{1,0:T(8,128)S(1)}) custom-call(f32[3248,128]{1,0:T(8,128)S(1)} %get-tuple-element.22.part, f32[128,128]{1,0:T(8,128)S(1)} %get-tuple-element.23.packed, ...), custom_call_target="tpu_custom_call", output_to_operand_aliasing={{0}: (0, {}), {1}: (1, {})} | custom-call | tf_op jit(solution)/shard_map/pack_x/pallas_call | solution.py:556
  15.8 1.6 %collective-permute-start.6 = (f32[56,128]{1,0:T(8,128)S(1)}, f32[56,128]{1,0:T(8,128)S(1)}, u32[]{:S(2)}, u32[]{:S(2)}) collective-permute-start(f32[56,128]{1,0:T(8,128)S(1)} %get-tuple-element.28), channel_id=1, source_target_pairs={{0,16},{16,0},{1,17},{17,1},{2,18},{18,2},{3,19},{19,3},{4,20},{20... | collective-permute-start | bytes 86024 | tf_op jit(solution)/shard_map/ppermute | solution.py:499
  17.4 0.7 %block.1 = f32[27,72,128]{2,1,0:T(8,128)S(1)} custom-call(f32[3248,128]{1,0:T(8,128)S(1)} %get-tuple-element.26.full), custom_call_target="tpu_custom_call" | custom-call | flops 4976640 | bytes 4194304 | tf_op jit(solution)/shard_map/block/pallas_call | solution.py:572
  18.1 1.8 %collective-permute-done.6.x_one.x_two = f32[56,128]{1,0:T(8,128)S(1)} collective-permute-done((f32[56,128]{1,0:T(8,128)S(1)}, f32[56,128]{1,0:T(8,128)S(1)}, u32[]{:S(2)}, u32[]{:S(2)}) %collective-permute-start.6) | collective-permute-done | bytes 28704 | tf_op jit(solution)/shard_map/ppermute | solution.py:499
  19.9 1.4 %finish.1 = f32[27,4,8,128]{3,2,1,0:T(8,128)} custom-call(f32[3248,128]{1,0:T(8,128)S(1)} %get-tuple-element.26.full, f32[27,72,128]{2,1,0:T(8,128)S(1)} %block.1, f32[144,128]{1,0:T(8,128)S(1)} %get-tuple-element.27.columns, f32[56,128]{1,0:T(8,128)S(1)} %collective-permute-done.6.x_one.x_two, f32[56,128]{1,0:T(8,128)S(1)} %collective-permute-done.6.x_one.x_two), custom_call_target="tpu_custom_call" | custom-call | tf_op jit(solution)/shard_map/finish/pallas_call | solution.py:584
  (1 shorter events, 0.0 us)
Async XLA Ops:
  1.3 8.7 %collective-permute-start = (f32[136,128]{1,0:T(8,128)S(1)}, f32[136,128]{1,0:T(8,128)S(1)}, u32[]{:S(2)}, u32[]{:S(2)}) collective-permute-start(f32[136,128]{1,0:T(8,128)S(1)} %get-tuple-element.18), channel_id=1, source_target_pairs={{4,8},{12,0},{8,4},{0,12},{5,9},{13,1},{9,5},{1,13},{6,10},{14,2},... | collective-permute-start | bytes 208904 | tf_op jit(solution)/shard_map/ppermute | solution.py:499
  6.5 4.3 %collective-permute-start.1 = (f32[136,128]{1,0:T(8,128)S(1)}, f32[136,128]{1,0:T(8,128)S(1)}, u32[]{:S(2)}, u32[]{:S(2)}) collective-permute-start(f32[136,128]{1,0:T(8,128)S(1)} %get-tuple-element.19), channel_id=1, source_target_pairs={{0,4},{8,12},{4,0},{12,8},{1,5},{9,13},{5,1},{13,9},{2,6},{10,14},... | collective-permute-start | bytes 208904 | tf_op jit(solution)/shard_map/ppermute | solution.py:499
  6.5 7.9 %collective-permute-start.2 = (f32[312,128]{1,0:T(8,128)S(1)}, f32[312,128]{1,0:T(8,128)S(1)}, u32[]{:S(2)}, u32[]{:S(2)}) collective-permute-start(f32[312,128]{1,0:T(8,128)S(1)} %get-tuple-element.20), channel_id=1, source_target_pairs={{1,2},{2,1},{5,6},{6,5},{9,10},{10,9},{13,14},{14,13},{17,18},{18,... | collective-permute-start | bytes 479240 | tf_op jit(solution)/shard_map/ppermute | solution.py:499
  7.2 7.3 %collective-permute-start.3 = (f32[312,128]{1,0:T(8,128)S(1)}, f32[312,128]{1,0:T(8,128)S(1)}, u32[]{:S(2)}, u32[]{:S(2)}) collective-permute-start(f32[312,128]{1,0:T(8,128)S(1)} %get-tuple-element.21), channel_id=1, source_target_pairs={{0,1},{2,3},{1,0},{3,2},{4,5},{6,7},{5,4},{7,6},{8,9},{10,11},{9,8... | collective-permute-start | bytes 479240 | tf_op jit(solution)/shard_map/ppermute | solution.py:499
  10.9 4.0 %collective-permute-start.4 = (f32[104,128]{1,0:T(8,128)S(1)}, f32[104,128]{1,0:T(8,128)S(1)}, u32[]{:S(2)}, u32[]{:S(2)}) collective-permute-start(f32[104,128]{1,0:T(8,128)S(1)} %get-tuple-element.24), channel_id=1, source_target_pairs={{1,2},{2,1},{5,6},{6,5},{9,10},{10,9},{13,14},{14,13},{17,18},{18,... | collective-permute-start | bytes 159752 | tf_op jit(solution)/shard_map/ppermute | solution.py:499
  11.5 3.8 %collective-permute-start.5 = (f32[104,128]{1,0:T(8,128)S(1)}, f32[104,128]{1,0:T(8,128)S(1)}, u32[]{:S(2)}, u32[]{:S(2)}) collective-permute-start(f32[104,128]{1,0:T(8,128)S(1)} %get-tuple-element.25), channel_id=1, source_target_pairs={{0,1},{2,3},{1,0},{3,2},{4,5},{6,7},{5,4},{7,6},{8,9},{10,11},{9,8... | collective-permute-start | bytes 159752 | tf_op jit(solution)/shard_map/ppermute | solution.py:499
  15.8 4.1 %collective-permute-start.6 = (f32[56,128]{1,0:T(8,128)S(1)}, f32[56,128]{1,0:T(8,128)S(1)}, u32[]{:S(2)}, u32[]{:S(2)}) collective-permute-start(f32[56,128]{1,0:T(8,128)S(1)} %get-tuple-element.28), channel_id=1, source_target_pairs={{0,16},{16,0},{1,17},{17,1},{2,18},{18,2},{3,19},{19,3},{4,20},{20... | collective-permute-start | bytes 86024 | tf_op jit(solution)/shard_map/ppermute | solution.py:499

commit v14 on v13

--- a/solution.py
+++ b/solution.py
@@ -125,30 +125,36 @@
 
 def first_kernel(pops_at, solid_at, table_at, index_at, own, two, one, *scratch):
     pops, solid, table, index, sems = scratch
-    small = ((table_at, table), (index_at, index), (solid_at, solid))
     parts = [(pl.ds(q, 9), z) for z in range(NZ) for q in (0, 9, 18)]
     planes = [(pops_at.at[part], pops.at[part]) for part in parts]
+    small = [(table_at, table), (index_at, index)]
     copies = [
         pltpu.make_async_copy(source, target, sems.at[i])
-        for i, (source, target) in enumerate((*small, *planes))
+        for i, (source, target) in enumerate([*small, *planes, (solid_at, solid)])
     ]
     for copy in copies:
         copy.start()
-    for copy in copies[:3]:
+    for copy in copies[:2]:
         copy.wait()
     lanes, rows = lane_ids(), row_ids()
     sponge = (lax.axis_index("gx") * NX + lanes) < SPONGE
+    profiles = [index[y] for y in range(NY)]
+    aims = []
     for z in range(NZ):
         aim = jnp.zeros((8, 128), F32)
-        for y in range(NY):
-            aim = jnp.where(rows == y, table[z, index[y]], aim)
-        for copy in copies[3 * z + 3 : 3 * z + 6]:
+        for y, profile in enumerate(profiles):
+            aim = jnp.where(rows == y, table[z, profile], aim)
+        aims.append(aim)
+    for z, aim in enumerate(aims):
+        for copy in copies[3 * z + 2 : 3 * z + 5]:
             copy.wait()
         post = relaxed([pops[q, z] for q in range(27)], sponge, aim)
         for q in range(27):
             own[pl.ds((q * NZ + z) * 8, 8), :] = post[q]
+        own[pl.ds((AIM * NZ + z) * 8, 8), :] = aim
+    copies[-1].wait()
+    for z in range(NZ):
         own[pl.ds((WALL * NZ + z) * 8, 8), :] = solid[z].astype(F32)
-        own[pl.ds((AIM * NZ + z) * 8, 8), :] = aim
 
     def pack(yup, ydown):
         inside = lax.rem(lanes, 4)
@@ -391,11 +397,23 @@
     top = lax.axis_index("gz") == lax.axis_size("gz") - 1
     lanes, rows = lane_ids(), row_ids()
 
-    def spread(right, left):
-        west[pl.ds(PAD, X_ROWS), :] = left[...]
-        east[pl.ds(PAD, X_ROWS), :] = right[...]
-
-    by_parity("gx", x_one, x_two, spread)
+    if size_x == 2:
+
+        def beside(side, start):
+            first = min(max(start, 0), X_ROWS - 8)
+            value = x_one[pl.ds(first, 8), :]
+            return pltpu.roll(value, (first - start) % 8, 0) if first != start else value
+
+    else:
+
+        def spread(right, left):
+            west[pl.ds(PAD, X_ROWS), :] = left[...]
+            east[pl.ds(PAD, X_ROWS), :] = right[...]
+
+        by_parity("gx", x_one, x_two, spread)
+
+        def beside(side, start):
+            return (west if side < 0 else east)[pl.ds(PAD + start, 8), :]
 
     strip = []
     for c in range(CHANNELS):
@@ -404,9 +422,9 @@
             rows < 4, columns[pl.ds(PAD + 4 * c, 8), :], columns[pl.ds(PAD + 4 * c - 4, 8), :]
         )
         if c <= WALL and cx >= 0:
-            value = jnp.where(rows < 2, west[pl.ds(PAD + 2 * c - (cx == 0), 8), :], value)
+            value = jnp.where(rows < 2, beside(-1, 2 * c - (cx == 0)), value)
         if c <= WALL and cx <= 0:
-            value = jnp.where(rows >= 6, east[pl.ds(PAD + 2 * c - 6 + (cx == 0), 8), :], value)
+            value = jnp.where(rows >= 6, beside(1, 2 * c - 6 + (cx == 0)), value)
         strip.append(value)
     strip[WALL] = jnp.where((rows == 0) | (rows == 7), 0.0, strip[WALL])
 

time: 21.6 us -> 21.5 us (level)
  no operation moved by 1% of the time
where the time goes in v14:
time: 21.5 us; the launch traced here: 21.3 us
  starting transfers between devices  13.9 us (65%)
  Pallas kernels  4.44 us (21%)
  waiting for transfers between devices  2.99 us (14%)
    ppermute x7, starting transfers between devices, swap(): return lax.ppermute(value, axis, pairs + [(j, i) for i, j in pairs])  13.9 us
    ppermute x7, waiting for transfers between devices, swap(): return lax.ppermute(value, axis, pairs + [(j, i) for i, j in pairs])  2.99 us
    pallas_call x1, Pallas kernels, shards(): pl.pallas_call(last_kernel, out_shape=shape(27, NZ, NY, NX), in_specs=[VM...  1.41 us
    pallas_call x1, Pallas kernels, shards(): pl.pallas_call(first_kernel, out_shape=[shape(CHANNELS * NZ * 8, 128), sh...  1.33 us
    pallas_call x1, Pallas kernels, shards(): pl.pallas_call(block_kernel, out_shape=shape(27, UNITS * 8, 128), in_spec...  0.72 us
    pallas_call x1, Pallas kernels, shards(): pl.pallas_call(third_kernel, out_shape=[shape(CHANNELS * ROWS, 128), shap...  0.49 us
  transfers between devices with their start and end apart: 7, of which 3 were waited for; matrix products, arithmetic and copies ran while one was open for 0% of the time, Pallas kernels for 6%

profile of v14, /device:TPU:0, one launch (start us, length us, event | category | flops | bytes accessed | tf_op | source)
XLA Modules:
  0.0 21.3 jit_solution(8953649548235644568)
XLA Ops:
  0.0 1.3 %collide.1 = (f32[928,128]{1,0:T(8,128)S(1)}, f32[136,128]{1,0:T(8,128)S(1)}, f32[136,128]{1,0:T(8,128)S(1)}) custom-call(f32[27,4,8,128]{3,2,1,0:T(8,128)} %pops_at.1, s32[4,8,128]{2,1,0:T(8,128)} %solid_at.1, f32[4,8]{1,0:T(4,128)} %bitcast.1, s32[8]{0:T(128)} %index_at.1), custom_call_target="tpu_custom_call" | custom-call | tf_op jit(solution)/shard_map/collide/pallas_call | solution.py:525
  1.3 5.1 %collective-permute-start = (f32[136,128]{1,0:T(8,128)S(1)}, f32[136,128]{1,0:T(8,128)S(1)}, u32[]{:S(2)}, u32[]{:S(2)}) collective-permute-start(f32[136,128]{1,0:T(8,128)S(1)} %get-tuple-element.18), channel_id=1, source_target_pairs={{4,8},{12,0},{8,4},{0,12},{5,9},{13,1},{9,5},{1,13},{6,10},{14,2},... | collective-permute-start | bytes 208904 | tf_op jit(solution)/shard_map/ppermute | solution.py:517
  6.5 0.0 collective-permute-start.1
  6.5 0.7 %collective-permute-start.2 = (f32[312,128]{1,0:T(8,128)S(1)}, f32[312,128]{1,0:T(8,128)S(1)}, u32[]{:S(2)}, u32[]{:S(2)}) collective-permute-start(f32[312,128]{1,0:T(8,128)S(1)} %get-tuple-element.20), channel_id=1, source_target_pairs={{1,2},{2,1},{5,6},{6,5},{9,10},{10,9},{13,14},{14,13},{17,18},{18,... | collective-permute-start | bytes 479240 | tf_op jit(solution)/shard_map/ppermute | solution.py:517
  7.2 2.9 %collective-permute-start.3 = (f32[312,128]{1,0:T(8,128)S(1)}, f32[312,128]{1,0:T(8,128)S(1)}, u32[]{:S(2)}, u32[]{:S(2)}) collective-permute-start(f32[312,128]{1,0:T(8,128)S(1)} %get-tuple-element.21), channel_id=1, source_target_pairs={{0,1},{2,3},{1,0},{3,2},{4,5},{6,7},{5,4},{7,6},{8,9},{10,11},{9,8... | collective-permute-start | bytes 479240 | tf_op jit(solution)/shard_map/ppermute | solution.py:517
  10.1 0.0 collective-permute-done.y_two
  10.1 0.7 %collective-permute-done.1.y_one = f32[136,128]{1,0:T(8,128)S(1)} collective-permute-done((f32[136,128]{1,0:T(8,128)S(1)}, f32[136,128]{1,0:T(8,128)S(1)}, u32[]{:S(2)}, u32[]{:S(2)}) %collective-permute-start.1) | collective-permute-done | bytes 69664 | tf_op jit(solution)/shard_map/ppermute | solution.py:517
  10.8 0.1 pack_z.1
  10.8 0.7 %collective-permute-start.4 = (f32[104,128]{1,0:T(8,128)S(1)}, f32[104,128]{1,0:T(8,128)S(1)}, u32[]{:S(2)}, u32[]{:S(2)}) collective-permute-start(f32[104,128]{1,0:T(8,128)S(1)} %get-tuple-element.24), channel_id=1, source_target_pairs={{1,2},{2,1},{5,6},{6,5},{9,10},{10,9},{13,14},{14,13},{17,18},{18,... | collective-permute-start | bytes 159752 | tf_op jit(solution)/shard_map/ppermute | solution.py:517
  11.5 2.9 %collective-permute-start.5 = (f32[104,128]{1,0:T(8,128)S(1)}, f32[104,128]{1,0:T(8,128)S(1)}, u32[]{:S(2)}, u32[]{:S(2)}) collective-permute-start(f32[104,128]{1,0:T(8,128)S(1)} %get-tuple-element.25), channel_id=1, source_target_pairs={{0,1},{2,3},{1,0},{3,2},{4,5},{6,7},{5,4},{7,6},{8,9},{10,11},{9,8... | collective-permute-start | bytes 159752 | tf_op jit(solution)/shard_map/ppermute | solution.py:517
  14.4 0.0 collective-permute-done.2.two
  14.4 0.0 collective-permute-done.3.one
  14.4 0.4 %fill.1 = (f32[3248,128]{1,0:T(8,128)S(1)}, f32[128,128]{1,0:T(8,128)S(1)}) custom-call(f32[928,128]{1,0:T(8,128)S(1)} %get-tuple-element.17.own, f32[136,128]{1,0:T(8,128)S(1)} %collective-permute-done.y_two, f32[136,128]{1,0:T(8,128)S(1)} %collective-permute-done.1.y_one, f32[312,128]{1,0:T(8,128)S(1)} %collective-permute-done.2.two, ...), custom_call_target="tpu_custom_call" | custom-call | flops 1000000 | bytes 4194304 | tf_op jit(solution)/shard_map/fill/pallas_call | solution.py:564
  14.8 0.0 collective-permute-done.4.z_two
  14.8 0.5 %collective-permute-done.5.z_one = f32[104,128]{1,0:T(8,128)S(1)} collective-permute-done((f32[104,128]{1,0:T(8,128)S(1)}, f32[104,128]{1,0:T(8,128)S(1)}, u32[]{:S(2)}, u32[]{:S(2)}) %collective-permute-start.5) | collective-permute-done | bytes 53280 | tf_op jit(solution)/shard_map/ppermute | solution.py:517
  15.3 0.5 %pack_x.1 = (f32[3248,128]{1,0:T(8,128)S(1)}, f32[128,128]{1,0:T(8,128)S(1)}, f32[144,128]{1,0:T(8,128)S(1)}, f32[56,128]{1,0:T(8,128)S(1)}) custom-call(f32[3248,128]{1,0:T(8,128)S(1)} %get-tuple-element.22.part, f32[128,128]{1,0:T(8,128)S(1)} %get-tuple-element.23.packed, ...), custom_call_target="tpu_custom_call", output_to_operand_aliasing={{0}: (0, {}), {1}: (1, {})} | custom-call | tf_op jit(solution)/shard_map/pack_x/pallas_call | solution.py:574
  15.8 1.6 %collective-permute-start.6 = (f32[56,128]{1,0:T(8,128)S(1)}, f32[56,128]{1,0:T(8,128)S(1)}, u32[]{:S(2)}, u32[]{:S(2)}) collective-permute-start(f32[56,128]{1,0:T(8,128)S(1)} %get-tuple-element.28), channel_id=1, source_target_pairs={{0,16},{16,0},{1,17},{17,1},{2,18},{18,2},{3,19},{19,3},{4,20},{20... | collective-permute-start | bytes 86024 | tf_op jit(solution)/shard_map/ppermute | solution.py:517
  17.4 0.7 %block.1 = f32[27,72,128]{2,1,0:T(8,128)S(1)} custom-call(f32[3248,128]{1,0:T(8,128)S(1)} %get-tuple-element.26.full), custom_call_target="tpu_custom_call" | custom-call | flops 4976640 | bytes 4194304 | tf_op jit(solution)/shard_map/block/pallas_call | solution.py:590
  18.1 1.8 %collective-permute-done.6.x_one.x_two = f32[56,128]{1,0:T(8,128)S(1)} collective-permute-done((f32[56,128]{1,0:T(8,128)S(1)}, f32[56,128]{1,0:T(8,128)S(1)}, u32[]{:S(2)}, u32[]{:S(2)}) %collective-permute-start.6) | collective-permute-done | bytes 28704 | tf_op jit(solution)/shard_map/ppermute | solution.py:517
  19.9 1.4 %finish.1 = f32[27,4,8,128]{3,2,1,0:T(8,128)} custom-call(f32[3248,128]{1,0:T(8,128)S(1)} %get-tuple-element.26.full, f32[27,72,128]{2,1,0:T(8,128)S(1)} %block.1, f32[144,128]{1,0:T(8,128)S(1)} %get-tuple-element.27.columns, f32[56,128]{1,0:T(8,128)S(1)} %collective-permute-done.6.x_one.x_two, f32[56,128]{1,0:T(8,128)S(1)} %collective-permute-done.6.x_one.x_two), custom_call_target="tpu_custom_call" | custom-call | tf_op jit(solution)/shard_map/finish/pallas_call | solution.py:602
  (1 shorter events, 0.0 us)
Async XLA Ops:
  1.3 8.7 %collective-permute-start = (f32[136,128]{1,0:T(8,128)S(1)}, f32[136,128]{1,0:T(8,128)S(1)}, u32[]{:S(2)}, u32[]{:S(2)}) collective-permute-start(f32[136,128]{1,0:T(8,128)S(1)} %get-tuple-element.18), channel_id=1, source_target_pairs={{4,8},{12,0},{8,4},{0,12},{5,9},{13,1},{9,5},{1,13},{6,10},{14,2},... | collective-permute-start | bytes 208904 | tf_op jit(solution)/shard_map/ppermute | solution.py:517
  6.5 4.3 %collective-permute-start.1 = (f32[136,128]{1,0:T(8,128)S(1)}, f32[136,128]{1,0:T(8,128)S(1)}, u32[]{:S(2)}, u32[]{:S(2)}) collective-permute-start(f32[136,128]{1,0:T(8,128)S(1)} %get-tuple-element.19), channel_id=1, source_target_pairs={{0,4},{8,12},{4,0},{12,8},{1,5},{9,13},{5,1},{13,9},{2,6},{10,14},... | collective-permute-start | bytes 208904 | tf_op jit(solution)/shard_map/ppermute | solution.py:517
  6.5 7.9 %collective-permute-start.2 = (f32[312,128]{1,0:T(8,128)S(1)}, f32[312,128]{1,0:T(8,128)S(1)}, u32[]{:S(2)}, u32[]{:S(2)}) collective-permute-start(f32[312,128]{1,0:T(8,128)S(1)} %get-tuple-element.20), channel_id=1, source_target_pairs={{1,2},{2,1},{5,6},{6,5},{9,10},{10,9},{13,14},{14,13},{17,18},{18,... | collective-permute-start | bytes 479240 | tf_op jit(solution)/shard_map/ppermute | solution.py:517
  7.2 7.3 %collective-permute-start.3 = (f32[312,128]{1,0:T(8,128)S(1)}, f32[312,128]{1,0:T(8,128)S(1)}, u32[]{:S(2)}, u32[]{:S(2)}) collective-permute-start(f32[312,128]{1,0:T(8,128)S(1)} %get-tuple-element.21), channel_id=1, source_target_pairs={{0,1},{2,3},{1,0},{3,2},{4,5},{6,7},{5,4},{7,6},{8,9},{10,11},{9,8... | collective-permute-start | bytes 479240 | tf_op jit(solution)/shard_map/ppermute | solution.py:517
  10.8 4.0 %collective-permute-start.4 = (f32[104,128]{1,0:T(8,128)S(1)}, f32[104,128]{1,0:T(8,128)S(1)}, u32[]{:S(2)}, u32[]{:S(2)}) collective-permute-start(f32[104,128]{1,0:T(8,128)S(1)} %get-tuple-element.24), channel_id=1, source_target_pairs={{1,2},{2,1},{5,6},{6,5},{9,10},{10,9},{13,14},{14,13},{17,18},{18,... | collective-permute-start | bytes 159752 | tf_op jit(solution)/shard_map/ppermute | solution.py:517
  11.5 3.8 %collective-permute-start.5 = (f32[104,128]{1,0:T(8,128)S(1)}, f32[104,128]{1,0:T(8,128)S(1)}, u32[]{:S(2)}, u32[]{:S(2)}) collective-permute-start(f32[104,128]{1,0:T(8,128)S(1)} %get-tuple-element.25), channel_id=1, source_target_pairs={{0,1},{2,3},{1,0},{3,2},{4,5},{6,7},{5,4},{7,6},{8,9},{10,11},{9,8... | collective-permute-start | bytes 159752 | tf_op jit(solution)/shard_map/ppermute | solution.py:517
  15.8 4.1 %collective-permute-start.6 = (f32[56,128]{1,0:T(8,128)S(1)}, f32[56,128]{1,0:T(8,128)S(1)}, u32[]{:S(2)}, u32[]{:S(2)}) collective-permute-start(f32[56,128]{1,0:T(8,128)S(1)} %get-tuple-element.28), channel_id=1, source_target_pairs={{0,16},{16,0},{1,17},{17,1},{2,18},{18,2},{3,19},{19,3},{4,20},{20... | collective-permute-start | bytes 86024 | tf_op jit(solution)/shard_map/ppermute | solution.py:517

commit v15 on v14

--- a/solution.py
+++ b/solution.py
@@ -23,6 +23,7 @@
 FLAT = (NZ + 4) * PITCH
 PAD = 8
 ROWS = PAD + FLAT + PAD
+SLABS = CHANNELS + 6
 UNITS = (NZ + 2) * PITCH // 8
 
 PARAMS = pltpu.CompilerParams(vmem_limit_bytes=12 * 2**20)
@@ -196,7 +197,7 @@
 def spread_mixed(below, above, flags, aims):
     flags[pl.ds(0, NZ), :] = below[pl.ds(MIXED * NZ, NZ), :]
     flags[pl.ds(NZ, NZ), :] = above[pl.ds(MIXED * NZ, NZ), :]
-    mixed = flags[...]
+    mixed = flags[pl.ds(0, 2 * NZ), :]
     inside = lax.rem(lane_ids(), 4)
     moved = {k: pltpu.roll(mixed, k % 128, 1) if k else mixed for k in (-2, -1, 0, 1, 2)}
 
@@ -207,8 +208,8 @@
                 value = jnp.where(inside == lane, moved[lane - source], value)
         return value
 
-    aims[...] = from_lane(1)
-    flags[...] = from_lane(2)
+    aims[pl.ds(0, 2 * NZ), :] = from_lane(1)
+    flags[pl.ds(0, 2 * NZ), :] = from_lane(2)
 
 
 def second_kernel(y_two, y_one, z_two, z_one, flags, aims):
@@ -239,12 +240,18 @@
             out[pl.ds(near + WALL, 1), :] = flags[pl.ds(side * NZ + first, 1), :]
             out[pl.ds(near + AIM, 1), :] = aims[pl.ds(side * NZ + first, 1), :]
             place = 15 if part else 0
-            out[pl.ds(near + CHANNELS, 9), :] = halo[pl.ds(place * NZ + second, 9, stride=NZ), :]
+            for k, count in ((0, 8), (8, 1)):
+                out[pl.ds(near + CHANNELS + k, count), :] = halo[
+                    pl.ds((place + k) * NZ + second, count, stride=NZ if count > 1 else 1), :
+                ]
             out[pl.ds(near + Z_BLOCKS - 1, 1), :] = flags[pl.ds(side * NZ + second, 1), :]
             far = Z_FAR + 12 * side
             start = (MIXED + 1) * NZ
-            out[pl.ds(far, 9), :] = halo[pl.ds(start + first, 9, stride=NZ), :]
-            out[pl.ds(far + 9, 3), :] = halo[pl.ds(start + 3 * part * NZ + second, 3, stride=NZ), :]
+            out[pl.ds(far, 8), :] = halo[pl.ds(start + first, 8, stride=NZ), :]
+            out[pl.ds(far + 8, 1), :] = halo[pl.ds(start + 8 * NZ + first, 1), :]
+            for k in range(3):
+                row = halo[pl.ds(start + (3 * part + k) * NZ + second, 1), :]
+                out[pl.ds(far + 9 + k, 1), :] = row
 
 
 def plane_at(z):
@@ -415,31 +422,33 @@
         def beside(side, start):
             return (west if side < 0 else east)[pl.ds(PAD + start, 8), :]
 
-    strip = []
-    for c in range(CHANNELS):
+    def strip_at(c, shift):
         cx = VEL[c][0] if c < 27 else 0
-        value = jnp.where(
-            rows < 4, columns[pl.ds(PAD + 4 * c, 8), :], columns[pl.ds(PAD + 4 * c - 4, 8), :]
-        )
+        at = rows - shift
+        first = PAD + 4 * c - shift
+        value = jnp.where(at < 4, columns[pl.ds(first, 8), :], columns[pl.ds(first - 4, 8), :])
         if c <= WALL and cx >= 0:
-            value = jnp.where(rows < 2, beside(-1, 2 * c - (cx == 0)), value)
+            value = jnp.where(at < 2, beside(-1, 2 * c - (cx == 0) - shift), value)
         if c <= WALL and cx <= 0:
-            value = jnp.where(rows >= 6, beside(1, 2 * c - 6 + (cx == 0)), value)
-        strip.append(value)
-    strip[WALL] = jnp.where((rows == 0) | (rows == 7), 0.0, strip[WALL])
-
-    def shifted(value, q):
+            value = jnp.where(at >= 6, beside(1, 2 * c - 6 + (cx == 0) - shift), value)
+        if c == WALL:
+            value = jnp.where((at == 0) | (at == 7), 0.0, value)
+        return value
+
+    strip = [strip_at(c, 0) for c in range(CHANNELS)]
+    flags_at = {cx: strip_at(WALL, cx) if cx else strip[WALL] for cx in (-1, 0, 1)}
+
+    def moved_along(value, q):
         cx, cy, cz = VEL[q]
-        if cx:
-            value = pltpu.roll(value, cx % 8, 0)
         step = (PITCH * cz + cy) % 128
         return pltpu.roll(value, step, 1) if step else value
 
     moved = []
     for q in range(27):
-        value = shifted(strip[q], q)
+        cx = VEL[q][0]
+        value = moved_along(strip_at(q, cx) if cx else strip[q], q)
         if q != 13:
-            value = jnp.where(shifted(strip[WALL], q) != 0.0, strip[26 - q], value)
+            value = jnp.where(moved_along(flags_at[cx], q) != 0.0, strip[26 - q], value)
         moved.append(jnp.where(strip[WALL] != 0.0, WEIGHT[q], value))
     place = here_x * NX + jnp.where(rows < 4, rows - 2, rows + (NX - 6))
     place = lax.rem(place + size_x * NX, size_x * NX)
@@ -554,7 +563,7 @@
         out_shape=[shape(Z_ROWS, 128)] * 2,
         in_specs=[VMEM] * 2,
         out_specs=[VMEM] * 2,
-        scratch_shapes=[pltpu.VMEM((2 * NZ, 128), F32)] * 2,
+        scratch_shapes=[pltpu.VMEM((4 * NZ, 128), F32)] * 2,
         compiler_params=PARAMS,
         cost_estimate=pl.CostEstimate(flops=10**9, bytes_accessed=2**20, transcendentals=0),
         name="pack_z",
@@ -563,10 +572,10 @@
     z_one = swap(z_one, "gz", 0, False)
     part, packed = pl.pallas_call(
         fill_kernel,
-        out_shape=[shape(CHANNELS * ROWS, 128), shape(128, 128)],
+        out_shape=[shape(SLABS * ROWS, 128), shape(128, 128)],
         in_specs=[VMEM] * 5,
         out_specs=[VMEM] * 2,
-        scratch_shapes=[pltpu.VMEM((2 * NZ, 128), F32)] * 2,
+        scratch_shapes=[pltpu.VMEM((4 * NZ, 128), F32)] * 2,
         compiler_params=PARAMS,
         cost_estimate=pl.CostEstimate(flops=10**6, bytes_accessed=2**22, transcendentals=0),
         name="fill",
@@ -574,7 +583,7 @@
     full, packed, columns, message = pl.pallas_call(
         third_kernel,
         out_shape=[
-            shape(CHANNELS * ROWS, 128),
+            shape(SLABS * ROWS, 128),
             shape(128, 128),
             shape(PAD + 128 + PAD, 128),
             shape(X_ROWS, 128),

time: 21.5 us -> 21.5 us (level)
  no operation moved by 1% of the time
where the time goes in v15:
time: 21.5 us; the launch traced here: 21.3 us
  starting transfers between devices  13.9 us (65%)
  Pallas kernels  4.44 us (21%)
  waiting for transfers between devices  2.99 us (14%)
    ppermute x7, starting transfers between devices, swap(): return lax.ppermute(value, axis, pairs + [(j, i) for i, j in pairs])  13.9 us
    ppermute x7, waiting for transfers between devices, swap(): return lax.ppermute(value, axis, pairs + [(j, i) for i, j in pairs])  2.99 us
    pallas_call x1, Pallas kernels, shards(): pl.pallas_call(last_kernel, out_shape=shape(27, NZ, NY, NX), in_specs=[VM...  1.41 us
    pallas_call x1, Pallas kernels, shards(): pl.pallas_call(first_kernel, out_shape=[shape(CHANNELS * NZ * 8, 128), sh...  1.33 us
    pallas_call x1, Pallas kernels, shards(): pl.pallas_call(block_kernel, out_shape=shape(27, UNITS * 8, 128), in_spec...  0.72 us
    pallas_call x1, Pallas kernels, shards(): pl.pallas_call(third_kernel, out_shape=[shape(SLABS * ROWS, 128), shape(1...  0.49 us
  transfers between devices with their start and end apart: 7, of which 3 were waited for; matrix products, arithmetic and copies ran while one was open for 0% of the time, Pallas kernels for 6%

profile of v15, /device:TPU:0, one launch (start us, length us, event | category | flops | bytes accessed | tf_op | source)
XLA Modules:
  0.0 21.3 jit_solution(12267524370052472699)
XLA Ops:
  0.0 1.3 %collide.1 = (f32[928,128]{1,0:T(8,128)S(1)}, f32[136,128]{1,0:T(8,128)S(1)}, f32[136,128]{1,0:T(8,128)S(1)}) custom-call(f32[27,4,8,128]{3,2,1,0:T(8,128)} %pops_at.1, s32[4,8,128]{2,1,0:T(8,128)} %solid_at.1, f32[4,8]{1,0:T(4,128)} %bitcast.1, s32[8]{0:T(128)} %index_at.1), custom_call_target="tpu_custom_call" | custom-call | tf_op jit(solution)/shard_map/collide/pallas_call | solution.py:534
  1.3 5.1 %collective-permute-start = (f32[136,128]{1,0:T(8,128)S(1)}, f32[136,128]{1,0:T(8,128)S(1)}, u32[]{:S(2)}, u32[]{:S(2)}) collective-permute-start(f32[136,128]{1,0:T(8,128)S(1)} %get-tuple-element.18), channel_id=1, source_target_pairs={{4,8},{12,0},{8,4},{0,12},{5,9},{13,1},{9,5},{1,13},{6,10},{14,2},... | collective-permute-start | bytes 208904 | tf_op jit(solution)/shard_map/ppermute | solution.py:526
  6.5 0.0 collective-permute-start.1
  6.5 0.7 %collective-permute-start.2 = (f32[312,128]{1,0:T(8,128)S(1)}, f32[312,128]{1,0:T(8,128)S(1)}, u32[]{:S(2)}, u32[]{:S(2)}) collective-permute-start(f32[312,128]{1,0:T(8,128)S(1)} %get-tuple-element.20), channel_id=1, source_target_pairs={{1,2},{2,1},{5,6},{6,5},{9,10},{10,9},{13,14},{14,13},{17,18},{18,... | collective-permute-start | bytes 479240 | tf_op jit(solution)/shard_map/ppermute | solution.py:526
  7.2 2.9 %collective-permute-start.3 = (f32[312,128]{1,0:T(8,128)S(1)}, f32[312,128]{1,0:T(8,128)S(1)}, u32[]{:S(2)}, u32[]{:S(2)}) collective-permute-start(f32[312,128]{1,0:T(8,128)S(1)} %get-tuple-element.21), channel_id=1, source_target_pairs={{0,1},{2,3},{1,0},{3,2},{4,5},{6,7},{5,4},{7,6},{8,9},{10,11},{9,8... | collective-permute-start | bytes 479240 | tf_op jit(solution)/shard_map/ppermute | solution.py:526
  10.1 0.0 collective-permute-done.y_two
  10.1 0.7 %collective-permute-done.1.y_one = f32[136,128]{1,0:T(8,128)S(1)} collective-permute-done((f32[136,128]{1,0:T(8,128)S(1)}, f32[136,128]{1,0:T(8,128)S(1)}, u32[]{:S(2)}, u32[]{:S(2)}) %collective-permute-start.1) | collective-permute-done | bytes 69664 | tf_op jit(solution)/shard_map/ppermute | solution.py:526
  10.8 0.1 pack_z.1
  10.8 0.7 %collective-permute-start.4 = (f32[104,128]{1,0:T(8,128)S(1)}, f32[104,128]{1,0:T(8,128)S(1)}, u32[]{:S(2)}, u32[]{:S(2)}) collective-permute-start(f32[104,128]{1,0:T(8,128)S(1)} %get-tuple-element.24), channel_id=1, source_target_pairs={{1,2},{2,1},{5,6},{6,5},{9,10},{10,9},{13,14},{14,13},{17,18},{18,... | collective-permute-start | bytes 159752 | tf_op jit(solution)/shard_map/ppermute | solution.py:526
  11.5 2.9 %collective-permute-start.5 = (f32[104,128]{1,0:T(8,128)S(1)}, f32[104,128]{1,0:T(8,128)S(1)}, u32[]{:S(2)}, u32[]{:S(2)}) collective-permute-start(f32[104,128]{1,0:T(8,128)S(1)} %get-tuple-element.25), channel_id=1, source_target_pairs={{0,1},{2,3},{1,0},{3,2},{4,5},{6,7},{5,4},{7,6},{8,9},{10,11},{9,8... | collective-permute-start | bytes 159752 | tf_op jit(solution)/shard_map/ppermute | solution.py:526
  14.4 0.0 collective-permute-done.2.two
  14.4 0.0 collective-permute-done.3.one
  14.4 0.4 %fill.1 = (f32[3920,128]{1,0:T(8,128)S(1)}, f32[128,128]{1,0:T(8,128)S(1)}) custom-call(f32[928,128]{1,0:T(8,128)S(1)} %get-tuple-element.17.own, f32[136,128]{1,0:T(8,128)S(1)} %collective-permute-done.y_two, f32[136,128]{1,0:T(8,128)S(1)} %collective-permute-done.1.y_one, f32[312,128]{1,0:T(8,128)S(1)} %collective-permute-done.2.two, ...), custom_call_target="tpu_custom_call" | custom-call | flops 1000000 | bytes 4194304 | tf_op jit(solution)/shard_map/fill/pallas_call | solution.py:573
  14.8 0.0 collective-permute-done.4.z_two
  14.8 0.5 %collective-permute-done.5.z_one = f32[104,128]{1,0:T(8,128)S(1)} collective-permute-done((f32[104,128]{1,0:T(8,128)S(1)}, f32[104,128]{1,0:T(8,128)S(1)}, u32[]{:S(2)}, u32[]{:S(2)}) %collective-permute-start.5) | collective-permute-done | bytes 53280 | tf_op jit(solution)/shard_map/ppermute | solution.py:526
  15.3 0.5 %pack_x.1 = (f32[3920,128]{1,0:T(8,128)S(1)}, f32[128,128]{1,0:T(8,128)S(1)}, f32[144,128]{1,0:T(8,128)S(1)}, f32[56,128]{1,0:T(8,128)S(1)}) custom-call(f32[3920,128]{1,0:T(8,128)S(1)} %get-tuple-element.22.part, f32[128,128]{1,0:T(8,128)S(1)} %get-tuple-element.23.packed, ...), custom_call_target="tpu_custom_call", output_to_operand_aliasing={{0}: (0, {}), {1}: (1, {})} | custom-call | tf_op jit(solution)/shard_map/pack_x/pallas_call | solution.py:583
  15.8 1.6 %collective-permute-start.6 = (f32[56,128]{1,0:T(8,128)S(1)}, f32[56,128]{1,0:T(8,128)S(1)}, u32[]{:S(2)}, u32[]{:S(2)}) collective-permute-start(f32[56,128]{1,0:T(8,128)S(1)} %get-tuple-element.28), channel_id=1, source_target_pairs={{0,16},{16,0},{1,17},{17,1},{2,18},{18,2},{3,19},{19,3},{4,20},{20... | collective-permute-start | bytes 86024 | tf_op jit(solution)/shard_map/ppermute | solution.py:526
  17.4 0.7 %block.1 = f32[27,72,128]{2,1,0:T(8,128)S(1)} custom-call(f32[3920,128]{1,0:T(8,128)S(1)} %get-tuple-element.26.full), custom_call_target="tpu_custom_call" | custom-call | flops 4976640 | bytes 4194304 | tf_op jit(solution)/shard_map/block/pallas_call | solution.py:599
  18.1 1.8 %collective-permute-done.6.x_one.x_two = f32[56,128]{1,0:T(8,128)S(1)} collective-permute-done((f32[56,128]{1,0:T(8,128)S(1)}, f32[56,128]{1,0:T(8,128)S(1)}, u32[]{:S(2)}, u32[]{:S(2)}) %collective-permute-start.6) | collective-permute-done | bytes 28704 | tf_op jit(solution)/shard_map/ppermute | solution.py:526
  19.9 1.4 %finish.1 = f32[27,4,8,128]{3,2,1,0:T(8,128)} custom-call(f32[3920,128]{1,0:T(8,128)S(1)} %get-tuple-element.26.full, f32[27,72,128]{2,1,0:T(8,128)S(1)} %block.1, f32[144,128]{1,0:T(8,128)S(1)} %get-tuple-element.27.columns, f32[56,128]{1,0:T(8,128)S(1)} %collective-permute-done.6.x_one.x_two, f32[56,128]{1,0:T(8,128)S(1)} %collective-permute-done.6.x_one.x_two), custom_call_target="tpu_custom_call" | custom-call | tf_op jit(solution)/shard_map/finish/pallas_call | solution.py:611
  (1 shorter events, 0.0 us)
Async XLA Ops:
  1.3 8.7 %collective-permute-start = (f32[136,128]{1,0:T(8,128)S(1)}, f32[136,128]{1,0:T(8,128)S(1)}, u32[]{:S(2)}, u32[]{:S(2)}) collective-permute-start(f32[136,128]{1,0:T(8,128)S(1)} %get-tuple-element.18), channel_id=1, source_target_pairs={{4,8},{12,0},{8,4},{0,12},{5,9},{13,1},{9,5},{1,13},{6,10},{14,2},... | collective-permute-start | bytes 208904 | tf_op jit(solution)/shard_map/ppermute | solution.py:526
  6.5 4.3 %collective-permute-start.1 = (f32[136,128]{1,0:T(8,128)S(1)}, f32[136,128]{1,0:T(8,128)S(1)}, u32[]{:S(2)}, u32[]{:S(2)}) collective-permute-start(f32[136,128]{1,0:T(8,128)S(1)} %get-tuple-element.19), channel_id=1, source_target_pairs={{0,4},{8,12},{4,0},{12,8},{1,5},{9,13},{5,1},{13,9},{2,6},{10,14},... | collective-permute-start | bytes 208904 | tf_op jit(solution)/shard_map/ppermute | solution.py:526
  6.5 7.9 %collective-permute-start.2 = (f32[312,128]{1,0:T(8,128)S(1)}, f32[312,128]{1,0:T(8,128)S(1)}, u32[]{:S(2)}, u32[]{:S(2)}) collective-permute-start(f32[312,128]{1,0:T(8,128)S(1)} %get-tuple-element.20), channel_id=1, source_target_pairs={{1,2},{2,1},{5,6},{6,5},{9,10},{10,9},{13,14},{14,13},{17,18},{18,... | collective-permute-start | bytes 479240 | tf_op jit(solution)/shard_map/ppermute | solution.py:526
  7.2 7.3 %collective-permute-start.3 = (f32[312,128]{1,0:T(8,128)S(1)}, f32[312,128]{1,0:T(8,128)S(1)}, u32[]{:S(2)}, u32[]{:S(2)}) collective-permute-start(f32[312,128]{1,0:T(8,128)S(1)} %get-tuple-element.21), channel_id=1, source_target_pairs={{0,1},{2,3},{1,0},{3,2},{4,5},{6,7},{5,4},{7,6},{8,9},{10,11},{9,8... | collective-permute-start | bytes 479240 | tf_op jit(solution)/shard_map/ppermute | solution.py:526
  10.8 4.0 %collective-permute-start.4 = (f32[104,128]{1,0:T(8,128)S(1)}, f32[104,128]{1,0:T(8,128)S(1)}, u32[]{:S(2)}, u32[]{:S(2)}) collective-permute-start(f32[104,128]{1,0:T(8,128)S(1)} %get-tuple-element.24), channel_id=1, source_target_pairs={{1,2},{2,1},{5,6},{6,5},{9,10},{10,9},{13,14},{14,13},{17,18},{18,... | collective-permute-start | bytes 159752 | tf_op jit(solution)/shard_map/ppermute | solution.py:526
  11.5 3.8 %collective-permute-start.5 = (f32[104,128]{1,0:T(8,128)S(1)}, f32[104,128]{1,0:T(8,128)S(1)}, u32[]{:S(2)}, u32[]{:S(2)}) collective-permute-start(f32[104,128]{1,0:T(8,128)S(1)} %get-tuple-element.25), channel_id=1, source_target_pairs={{0,1},{2,3},{1,0},{3,2},{4,5},{6,7},{5,4},{7,6},{8,9},{10,11},{9,8... | collective-permute-start | bytes 159752 | tf_op jit(solution)/shard_map/ppermute | solution.py:526
  15.8 4.1 %collective-permute-start.6 = (f32[56,128]{1,0:T(8,128)S(1)}, f32[56,128]{1,0:T(8,128)S(1)}, u32[]{:S(2)}, u32[]{:S(2)}) collective-permute-start(f32[56,128]{1,0:T(8,128)S(1)} %get-tuple-element.28), channel_id=1, source_target_pairs={{0,16},{16,0},{1,17},{17,1},{2,18},{18,2},{3,19},{19,3},{4,20},{20... | collective-permute-start | bytes 86024 | tf_op jit(solution)/shard_map/ppermute | solution.py:526

commit v16 on v15

--- a/solution.py
+++ b/solution.py
@@ -126,12 +126,11 @@
 
 def first_kernel(pops_at, solid_at, table_at, index_at, own, two, one, *scratch):
     pops, solid, table, index, sems = scratch
-    parts = [(pl.ds(q, 9), z) for z in range(NZ) for q in (0, 9, 18)]
-    planes = [(pops_at.at[part], pops.at[part]) for part in parts]
+    groups = [(pops_at.at[pl.ds(q, 9)], pops.at[pl.ds(q, 9)]) for q in (0, 9, 18)]
     small = [(table_at, table), (index_at, index)]
     copies = [
         pltpu.make_async_copy(source, target, sems.at[i])
-        for i, (source, target) in enumerate([*small, *planes, (solid_at, solid)])
+        for i, (source, target) in enumerate([*small, *groups, (solid_at, solid)])
     ]
     for copy in copies:
         copy.start()
@@ -146,9 +145,9 @@
         for y, profile in enumerate(profiles):
             aim = jnp.where(rows == y, table[z, profile], aim)
         aims.append(aim)
+    for copy in copies[2:-1]:
+        copy.wait()
     for z, aim in enumerate(aims):
-        for copy in copies[3 * z + 2 : 3 * z + 5]:
-            copy.wait()
         post = relaxed([pops[q, z] for q in range(27)], sponge, aim)
         for q in range(27):
             own[pl.ds((q * NZ + z) * 8, 8), :] = post[q]
@@ -495,26 +494,33 @@
                 lanes == edge, column_at(place, edge, PITCH + 8 * u), pltpu.roll(flags, cx % 128, 1)
             )
 
+    cells = [(z + 1) * PITCH + 2 for z in range(NZ)]
+    solids = [walls[1, pl.ds(cell, 8), :] != 0.0 for cell in cells]
+
+    def streamed(q, z):
+        cx, cy, cz = VEL[q]
+        cell = cells[z]
+        start = cell - PITCH * cz - cy
+        if cx > 0:
+            side = column_at(8 * (q // 3) + 2, 0, PITCH + start)
+            value = jnp.where(lanes < 2, side, pltpu.roll(block[q, pl.ds(start, 8), :], 1, 1))
+        elif cx < 0:
+            side = column_at(8 * (q // 3) + 6, 126, PITCH + start)
+            value = jnp.where(lanes > 125, side, pltpu.roll(block[q, pl.ds(start, 8), :], 127, 1))
+        else:
+            value = rimmed(q, start)
+        if q != 13:
+            blocked = walls[cx + 1, pl.ds(start, 8), :] != 0.0
+            value = jnp.where(blocked, rimmed(26 - q, cell), value)
+        return jnp.where(solids[z], WEIGHT[q], value)
+
     copies = []
-    for z in range(NZ):
-        cell = (z + 1) * PITCH + 2
-        solid = walls[1, pl.ds(cell, 8), :] != 0.0
-        for q in range(27):
-            cx, cy, cz = VEL[q]
-            start = cell - PITCH * cz - cy
-            if cx > 0:
-                side = column_at(8 * (q // 3) + 2, 0, PITCH + start)
-                value = jnp.where(lanes < 2, side, pltpu.roll(block[q, pl.ds(start, 8), :], 1, 1))
-            elif cx < 0:
-                side = column_at(8 * (q // 3) + 6, 126, PITCH + start)
-                value = jnp.where(lanes > 125, side, pltpu.roll(block[q, pl.ds(start, 8), :], 127, 1))
-            else:
-                value = rimmed(q, start)
-            if q != 13:
-                blocked = walls[cx + 1, pl.ds(start, 8), :] != 0.0
-                value = jnp.where(blocked, rimmed(26 - q, cell), value)
-            done[q, z] = jnp.where(solid, WEIGHT[q], value)
-        copies.append(pltpu.make_async_copy(done.at[:, z], out.at[:, z], sems.at[z]))
+    for first, count in ((0, 9), (9, 8), (17, 6), (23, 4)):
+        for q in range(first, first + count):
+            for z in range(NZ):
+                done[q, z] = streamed(q, z)
+        part = pl.ds(first, count)
+        copies.append(pltpu.make_async_copy(done.at[part], out.at[part], sems.at[len(copies)]))
         copies[-1].start()
     for copy in copies:
         copy.wait()
@@ -541,7 +547,7 @@
             pltpu.VMEM(solid.shape, jnp.int32),
             pltpu.SMEM(profile_table.shape[::-1], F32),
             pltpu.SMEM(profile_index.shape, jnp.int32),
-            pltpu.SemaphoreType.DMA((3 + 3 * NZ,)),
+            pltpu.SemaphoreType.DMA((6,)),
         ],
         compiler_params=PARAMS,
         name="collide",

time: 21.5 us -> 21.5 us (level)
  no operation moved by 1% of the time
where the time goes in v16:
time: 21.5 us; the launch traced here: 21.4 us
  starting transfers between devices  13.9 us (65%)
  Pallas kernels  4.46 us (21%)
  waiting for transfers between devices  2.99 us (14%)
    ppermute x7, starting transfers between devices, swap(): return lax.ppermute(value, axis, pairs + [(j, i) for i, j in pairs])  13.9 us
    ppermute x7, waiting for transfers between devices, swap(): return lax.ppermute(value, axis, pairs + [(j, i) for i, j in pairs])  2.99 us
    pallas_call x1, Pallas kernels, shards(): pl.pallas_call(last_kernel, out_shape=shape(27, NZ, NY, NX), in_specs=[VM...  1.4 us
    pallas_call x1, Pallas kernels, shards(): pl.pallas_call(first_kernel, out_shape=[shape(CHANNELS * NZ * 8, 128), sh...  1.36 us
    pallas_call x1, Pallas kernels, shards(): pl.pallas_call(block_kernel, out_shape=shape(27, UNITS * 8, 128), in_spec...  0.72 us
    pallas_call x1, Pallas kernels, shards(): pl.pallas_call(third_kernel, out_shape=[shape(SLABS * ROWS, 128), shape(1...  0.49 us
  transfers between devices with their start and end apart: 7, of which 3 were waited for; matrix products, arithmetic and copies ran while one was open for 0% of the time, Pallas kernels for 6%

profile of v16, /device:TPU:0, one launch (start us, length us, event | category | flops | bytes accessed | tf_op | source)
XLA Modules:
  0.0 21.4 jit_solution(14019091663019090562)
XLA Ops:
  0.0 1.4 %collide.1 = (f32[928,128]{1,0:T(8,128)S(1)}, f32[136,128]{1,0:T(8,128)S(1)}, f32[136,128]{1,0:T(8,128)S(1)}) custom-call(f32[27,4,8,128]{3,2,1,0:T(8,128)} %pops_at.1, s32[4,8,128]{2,1,0:T(8,128)} %solid_at.1, f32[4,8]{1,0:T(4,128)} %bitcast.1, s32[8]{0:T(128)} %index_at.1), custom_call_target="tpu_custom_call" | custom-call | tf_op jit(solution)/shard_map/collide/pallas_call | solution.py:540
  1.4 5.1 %collective-permute-start = (f32[136,128]{1,0:T(8,128)S(1)}, f32[136,128]{1,0:T(8,128)S(1)}, u32[]{:S(2)}, u32[]{:S(2)}) collective-permute-start(f32[136,128]{1,0:T(8,128)S(1)} %get-tuple-element.18), channel_id=1, source_target_pairs={{4,8},{12,0},{8,4},{0,12},{5,9},{13,1},{9,5},{1,13},{6,10},{14,2},... | collective-permute-start | bytes 208904 | tf_op jit(solution)/shard_map/ppermute | solution.py:532
  6.5 0.0 collective-permute-start.1
  6.5 0.7 %collective-permute-start.2 = (f32[312,128]{1,0:T(8,128)S(1)}, f32[312,128]{1,0:T(8,128)S(1)}, u32[]{:S(2)}, u32[]{:S(2)}) collective-permute-start(f32[312,128]{1,0:T(8,128)S(1)} %get-tuple-element.20), channel_id=1, source_target_pairs={{1,2},{2,1},{5,6},{6,5},{9,10},{10,9},{13,14},{14,13},{17,18},{18,... | collective-permute-start | bytes 479240 | tf_op jit(solution)/shard_map/ppermute | solution.py:532
  7.2 2.9 %collective-permute-start.3 = (f32[312,128]{1,0:T(8,128)S(1)}, f32[312,128]{1,0:T(8,128)S(1)}, u32[]{:S(2)}, u32[]{:S(2)}) collective-permute-start(f32[312,128]{1,0:T(8,128)S(1)} %get-tuple-element.21), channel_id=1, source_target_pairs={{0,1},{2,3},{1,0},{3,2},{4,5},{6,7},{5,4},{7,6},{8,9},{10,11},{9,8... | collective-permute-start | bytes 479240 | tf_op jit(solution)/shard_map/ppermute | solution.py:532
  10.1 0.0 collective-permute-done.y_two
  10.1 0.7 %collective-permute-done.1.y_one = f32[136,128]{1,0:T(8,128)S(1)} collective-permute-done((f32[136,128]{1,0:T(8,128)S(1)}, f32[136,128]{1,0:T(8,128)S(1)}, u32[]{:S(2)}, u32[]{:S(2)}) %collective-permute-start.1) | collective-permute-done | bytes 69664 | tf_op jit(solution)/shard_map/ppermute | solution.py:532
  10.8 0.1 pack_z.1
  10.9 0.7 %collective-permute-start.4 = (f32[104,128]{1,0:T(8,128)S(1)}, f32[104,128]{1,0:T(8,128)S(1)}, u32[]{:S(2)}, u32[]{:S(2)}) collective-permute-start(f32[104,128]{1,0:T(8,128)S(1)} %get-tuple-element.24), channel_id=1, source_target_pairs={{1,2},{2,1},{5,6},{6,5},{9,10},{10,9},{13,14},{14,13},{17,18},{18,... | collective-permute-start | bytes 159752 | tf_op jit(solution)/shard_map/ppermute | solution.py:532
  11.5 2.9 %collective-permute-start.5 = (f32[104,128]{1,0:T(8,128)S(1)}, f32[104,128]{1,0:T(8,128)S(1)}, u32[]{:S(2)}, u32[]{:S(2)}) collective-permute-start(f32[104,128]{1,0:T(8,128)S(1)} %get-tuple-element.25), channel_id=1, source_target_pairs={{0,1},{2,3},{1,0},{3,2},{4,5},{6,7},{5,4},{7,6},{8,9},{10,11},{9,8... | collective-permute-start | bytes 159752 | tf_op jit(solution)/shard_map/ppermute | solution.py:532
  14.5 0.0 collective-permute-done.2.two
  14.5 0.0 collective-permute-done.3.one
  14.5 0.4 %fill.1 = (f32[3920,128]{1,0:T(8,128)S(1)}, f32[128,128]{1,0:T(8,128)S(1)}) custom-call(f32[928,128]{1,0:T(8,128)S(1)} %get-tuple-element.17.own, f32[136,128]{1,0:T(8,128)S(1)} %collective-permute-done.y_two, f32[136,128]{1,0:T(8,128)S(1)} %collective-permute-done.1.y_one, f32[312,128]{1,0:T(8,128)S(1)} %collective-permute-done.2.two, ...), custom_call_target="tpu_custom_call" | custom-call | flops 1000000 | bytes 4194304 | tf_op jit(solution)/shard_map/fill/pallas_call | solution.py:579
  14.9 0.0 collective-permute-done.4.z_two
  14.9 0.5 %collective-permute-done.5.z_one = f32[104,128]{1,0:T(8,128)S(1)} collective-permute-done((f32[104,128]{1,0:T(8,128)S(1)}, f32[104,128]{1,0:T(8,128)S(1)}, u32[]{:S(2)}, u32[]{:S(2)}) %collective-permute-start.5) | collective-permute-done | bytes 53280 | tf_op jit(solution)/shard_map/ppermute | solution.py:532
  15.3 0.5 %pack_x.1 = (f32[3920,128]{1,0:T(8,128)S(1)}, f32[128,128]{1,0:T(8,128)S(1)}, f32[144,128]{1,0:T(8,128)S(1)}, f32[56,128]{1,0:T(8,128)S(1)}) custom-call(f32[3920,128]{1,0:T(8,128)S(1)} %get-tuple-element.22.part, f32[128,128]{1,0:T(8,128)S(1)} %get-tuple-element.23.packed, ...), custom_call_target="tpu_custom_call", output_to_operand_aliasing={{0}: (0, {}), {1}: (1, {})} | custom-call | tf_op jit(solution)/shard_map/pack_x/pallas_call | solution.py:589
  15.8 1.6 %collective-permute-start.6 = (f32[56,128]{1,0:T(8,128)S(1)}, f32[56,128]{1,0:T(8,128)S(1)}, u32[]{:S(2)}, u32[]{:S(2)}) collective-permute-start(f32[56,128]{1,0:T(8,128)S(1)} %get-tuple-element.28), channel_id=1, source_target_pairs={{0,16},{16,0},{1,17},{17,1},{2,18},{18,2},{3,19},{19,3},{4,20},{20... | collective-permute-start | bytes 86024 | tf_op jit(solution)/shard_map/ppermute | solution.py:532
  17.4 0.7 %block.1 = f32[27,72,128]{2,1,0:T(8,128)S(1)} custom-call(f32[3920,128]{1,0:T(8,128)S(1)} %get-tuple-element.26.full), custom_call_target="tpu_custom_call" | custom-call | flops 4976640 | bytes 4194304 | tf_op jit(solution)/shard_map/block/pallas_call | solution.py:605
  18.2 1.8 %collective-permute-done.6.x_one.x_two = f32[56,128]{1,0:T(8,128)S(1)} collective-permute-done((f32[56,128]{1,0:T(8,128)S(1)}, f32[56,128]{1,0:T(8,128)S(1)}, u32[]{:S(2)}, u32[]{:S(2)}) %collective-permute-start.6) | collective-permute-done | bytes 28704 | tf_op jit(solution)/shard_map/ppermute | solution.py:532
  20.0 1.4 %finish.1 = f32[27,4,8,128]{3,2,1,0:T(8,128)} custom-call(f32[3920,128]{1,0:T(8,128)S(1)} %get-tuple-element.26.full, f32[27,72,128]{2,1,0:T(8,128)S(1)} %block.1, f32[144,128]{1,0:T(8,128)S(1)} %get-tuple-element.27.columns, f32[56,128]{1,0:T(8,128)S(1)} %collective-permute-done.6.x_one.x_two, f32[56,128]{1,0:T(8,128)S(1)} %collective-permute-done.6.x_one.x_two), custom_call_target="tpu_custom_call" | custom-call | tf_op jit(solution)/shard_map/finish/pallas_call | solution.py:617
  (1 shorter events, 0.0 us)
Async XLA Ops:
  1.4 8.7 %collective-permute-start = (f32[136,128]{1,0:T(8,128)S(1)}, f32[136,128]{1,0:T(8,128)S(1)}, u32[]{:S(2)}, u32[]{:S(2)}) collective-permute-start(f32[136,128]{1,0:T(8,128)S(1)} %get-tuple-element.18), channel_id=1, source_target_pairs={{4,8},{12,0},{8,4},{0,12},{5,9},{13,1},{9,5},{1,13},{6,10},{14,2},... | collective-permute-start | bytes 208904 | tf_op jit(solution)/shard_map/ppermute | solution.py:532
  6.5 4.3 %collective-permute-start.1 = (f32[136,128]{1,0:T(8,128)S(1)}, f32[136,128]{1,0:T(8,128)S(1)}, u32[]{:S(2)}, u32[]{:S(2)}) collective-permute-start(f32[136,128]{1,0:T(8,128)S(1)} %get-tuple-element.19), channel_id=1, source_target_pairs={{0,4},{8,12},{4,0},{12,8},{1,5},{9,13},{5,1},{13,9},{2,6},{10,14},... | collective-permute-start | bytes 208904 | tf_op jit(solution)/shard_map/ppermute | solution.py:532
  6.5 7.9 %collective-permute-start.2 = (f32[312,128]{1,0:T(8,128)S(1)}, f32[312,128]{1,0:T(8,128)S(1)}, u32[]{:S(2)}, u32[]{:S(2)}) collective-permute-start(f32[312,128]{1,0:T(8,128)S(1)} %get-tuple-element.20), channel_id=1, source_target_pairs={{1,2},{2,1},{5,6},{6,5},{9,10},{10,9},{13,14},{14,13},{17,18},{18,... | collective-permute-start | bytes 479240 | tf_op jit(solution)/shard_map/ppermute | solution.py:532
  7.2 7.3 %collective-permute-start.3 = (f32[312,128]{1,0:T(8,128)S(1)}, f32[312,128]{1,0:T(8,128)S(1)}, u32[]{:S(2)}, u32[]{:S(2)}) collective-permute-start(f32[312,128]{1,0:T(8,128)S(1)} %get-tuple-element.21), channel_id=1, source_target_pairs={{0,1},{2,3},{1,0},{3,2},{4,5},{6,7},{5,4},{7,6},{8,9},{10,11},{9,8... | collective-permute-start | bytes 479240 | tf_op jit(solution)/shard_map/ppermute | solution.py:532
  10.9 4.0 %collective-permute-start.4 = (f32[104,128]{1,0:T(8,128)S(1)}, f32[104,128]{1,0:T(8,128)S(1)}, u32[]{:S(2)}, u32[]{:S(2)}) collective-permute-start(f32[104,128]{1,0:T(8,128)S(1)} %get-tuple-element.24), channel_id=1, source_target_pairs={{1,2},{2,1},{5,6},{6,5},{9,10},{10,9},{13,14},{14,13},{17,18},{18,... | collective-permute-start | bytes 159752 | tf_op jit(solution)/shard_map/ppermute | solution.py:532
  11.5 3.8 %collective-permute-start.5 = (f32[104,128]{1,0:T(8,128)S(1)}, f32[104,128]{1,0:T(8,128)S(1)}, u32[]{:S(2)}, u32[]{:S(2)}) collective-permute-start(f32[104,128]{1,0:T(8,128)S(1)} %get-tuple-element.25), channel_id=1, source_target_pairs={{0,1},{2,3},{1,0},{3,2},{4,5},{6,7},{5,4},{7,6},{8,9},{10,11},{9,8... | collective-permute-start | bytes 159752 | tf_op jit(solution)/shard_map/ppermute | solution.py:532
  15.8 4.1 %collective-permute-start.6 = (f32[56,128]{1,0:T(8,128)S(1)}, f32[56,128]{1,0:T(8,128)S(1)}, u32[]{:S(2)}, u32[]{:S(2)}) collective-permute-start(f32[56,128]{1,0:T(8,128)S(1)} %get-tuple-element.28), channel_id=1, source_target_pairs={{0,16},{16,0},{1,17},{17,1},{2,18},{18,2},{3,19},{19,3},{4,20},{20... | collective-permute-start | bytes 86024 | tf_op jit(solution)/shard_map/ppermute | solution.py:532

commit v17 on v16

--- a/solution.py
+++ b/solution.py
@@ -139,19 +139,24 @@
     lanes, rows = lane_ids(), row_ids()
     sponge = (lax.axis_index("gx") * NX + lanes) < SPONGE
     profiles = [index[y] for y in range(NY)]
-    aims = []
     for z in range(NZ):
         aim = jnp.zeros((8, 128), F32)
         for y, profile in enumerate(profiles):
             aim = jnp.where(rows == y, table[z, profile], aim)
-        aims.append(aim)
+        own[pl.ds((AIM * NZ + z) * 8, 8), :] = aim
     for copy in copies[2:-1]:
         copy.wait()
-    for z, aim in enumerate(aims):
-        post = relaxed([pops[q, z] for q in range(27)], sponge, aim)
+
+    def plane(z, carry):
+        def at(c):
+            return pl.ds(pl.multiple_of((c * NZ + z) * 8, 8), 8)
+
+        post = relaxed([pops[q, z] for q in range(27)], sponge, own[at(AIM), :])
         for q in range(27):
-            own[pl.ds((q * NZ + z) * 8, 8), :] = post[q]
-        own[pl.ds((AIM * NZ + z) * 8, 8), :] = aim
+            own[at(q), :] = post[q]
+        return carry
+
+    lax.fori_loop(0, NZ, plane, 0)
     copies[-1].wait()
     for z in range(NZ):
         own[pl.ds((WALL * NZ + z) * 8, 8), :] = solid[z].astype(F32)

time: 21.5 us -> 21.7 us (level)
  no operation moved by 1% of the time
where the time goes in v17:
time: 21.7 us; the launch traced here: 21.5 us
  starting transfers between devices  13.9 us (64%)
  Pallas kernels  4.58 us (21%)
  waiting for transfers between devices  2.99 us (14%)
    ppermute x7, starting transfers between devices, swap(): return lax.ppermute(value, axis, pairs + [(j, i) for i, j in pairs])  13.9 us
    ppermute x7, waiting for transfers between devices, swap(): return lax.ppermute(value, axis, pairs + [(j, i) for i, j in pairs])  2.99 us
    pallas_call x1, Pallas kernels, shards(): pl.pallas_call(first_kernel, out_shape=[shape(CHANNELS * NZ * 8, 128), sh...  1.48 us
    pallas_call x1, Pallas kernels, shards(): pl.pallas_call(last_kernel, out_shape=shape(27, NZ, NY, NX), in_specs=[VM...  1.4 us
    pallas_call x1, Pallas kernels, shards(): pl.pallas_call(block_kernel, out_shape=shape(27, UNITS * 8, 128), in_spec...  0.72 us
    pallas_call x1, Pallas kernels, shards(): pl.pallas_call(third_kernel, out_shape=[shape(SLABS * ROWS, 128), shape(1...  0.49 us
  transfers between devices with their start and end apart: 7, of which 3 were waited for; matrix products, arithmetic and copies ran while one was open for 0% of the time, Pallas kernels for 6%

profile of v17, /device:TPU:0, one launch (start us, length us, event | category | flops | bytes accessed | tf_op | source)
XLA Modules:
  0.0 21.5 jit_solution(3727407200880987702)
XLA Ops:
  0.0 1.5 %collide.1 = (f32[928,128]{1,0:T(8,128)S(1)}, f32[136,128]{1,0:T(8,128)S(1)}, f32[136,128]{1,0:T(8,128)S(1)}) custom-call(f32[27,4,8,128]{3,2,1,0:T(8,128)} %pops_at.1, s32[4,8,128]{2,1,0:T(8,128)} %solid_at.1, f32[4,8]{1,0:T(4,128)} %bitcast.1, s32[8]{0:T(128)} %index_at.1), custom_call_target="tpu_custom_call" | custom-call | tf_op jit(solution)/shard_map/collide/pallas_call | solution.py:545
  1.5 5.1 %collective-permute-start = (f32[136,128]{1,0:T(8,128)S(1)}, f32[136,128]{1,0:T(8,128)S(1)}, u32[]{:S(2)}, u32[]{:S(2)}) collective-permute-start(f32[136,128]{1,0:T(8,128)S(1)} %get-tuple-element.18), channel_id=1, source_target_pairs={{4,8},{12,0},{8,4},{0,12},{5,9},{13,1},{9,5},{1,13},{6,10},{14,2},... | collective-permute-start | bytes 208904 | tf_op jit(solution)/shard_map/ppermute | solution.py:537
  6.6 0.0 collective-permute-start.1
  6.6 0.7 %collective-permute-start.2 = (f32[312,128]{1,0:T(8,128)S(1)}, f32[312,128]{1,0:T(8,128)S(1)}, u32[]{:S(2)}, u32[]{:S(2)}) collective-permute-start(f32[312,128]{1,0:T(8,128)S(1)} %get-tuple-element.20), channel_id=1, source_target_pairs={{1,2},{2,1},{5,6},{6,5},{9,10},{10,9},{13,14},{14,13},{17,18},{18,... | collective-permute-start | bytes 479240 | tf_op jit(solution)/shard_map/ppermute | solution.py:537
  7.3 2.9 %collective-permute-start.3 = (f32[312,128]{1,0:T(8,128)S(1)}, f32[312,128]{1,0:T(8,128)S(1)}, u32[]{:S(2)}, u32[]{:S(2)}) collective-permute-start(f32[312,128]{1,0:T(8,128)S(1)} %get-tuple-element.21), channel_id=1, source_target_pairs={{0,1},{2,3},{1,0},{3,2},{4,5},{6,7},{5,4},{7,6},{8,9},{10,11},{9,8... | collective-permute-start | bytes 479240 | tf_op jit(solution)/shard_map/ppermute | solution.py:537
  10.2 0.0 collective-permute-done.y_two
  10.2 0.7 %collective-permute-done.1.y_one = f32[136,128]{1,0:T(8,128)S(1)} collective-permute-done((f32[136,128]{1,0:T(8,128)S(1)}, f32[136,128]{1,0:T(8,128)S(1)}, u32[]{:S(2)}, u32[]{:S(2)}) %collective-permute-start.1) | collective-permute-done | bytes 69664 | tf_op jit(solution)/shard_map/ppermute | solution.py:537
  10.9 0.1 pack_z.1
  11.0 0.7 %collective-permute-start.4 = (f32[104,128]{1,0:T(8,128)S(1)}, f32[104,128]{1,0:T(8,128)S(1)}, u32[]{:S(2)}, u32[]{:S(2)}) collective-permute-start(f32[104,128]{1,0:T(8,128)S(1)} %get-tuple-element.24), channel_id=1, source_target_pairs={{1,2},{2,1},{5,6},{6,5},{9,10},{10,9},{13,14},{14,13},{17,18},{18,... | collective-permute-start | bytes 159752 | tf_op jit(solution)/shard_map/ppermute | solution.py:537
  11.7 2.9 %collective-permute-start.5 = (f32[104,128]{1,0:T(8,128)S(1)}, f32[104,128]{1,0:T(8,128)S(1)}, u32[]{:S(2)}, u32[]{:S(2)}) collective-permute-start(f32[104,128]{1,0:T(8,128)S(1)} %get-tuple-element.25), channel_id=1, source_target_pairs={{0,1},{2,3},{1,0},{3,2},{4,5},{6,7},{5,4},{7,6},{8,9},{10,11},{9,8... | collective-permute-start | bytes 159752 | tf_op jit(solution)/shard_map/ppermute | solution.py:537
  14.6 0.0 collective-permute-done.2.two
  14.6 0.0 collective-permute-done.3.one
  14.6 0.4 %fill.1 = (f32[3920,128]{1,0:T(8,128)S(1)}, f32[128,128]{1,0:T(8,128)S(1)}) custom-call(f32[928,128]{1,0:T(8,128)S(1)} %get-tuple-element.17.own, f32[136,128]{1,0:T(8,128)S(1)} %collective-permute-done.y_two, f32[136,128]{1,0:T(8,128)S(1)} %collective-permute-done.1.y_one, f32[312,128]{1,0:T(8,128)S(1)} %collective-permute-done.2.two, ...), custom_call_target="tpu_custom_call" | custom-call | flops 1000000 | bytes 4194304 | tf_op jit(solution)/shard_map/fill/pallas_call | solution.py:584
  15.0 0.0 collective-permute-done.4.z_two
  15.0 0.5 %collective-permute-done.5.z_one = f32[104,128]{1,0:T(8,128)S(1)} collective-permute-done((f32[104,128]{1,0:T(8,128)S(1)}, f32[104,128]{1,0:T(8,128)S(1)}, u32[]{:S(2)}, u32[]{:S(2)}) %collective-permute-start.5) | collective-permute-done | bytes 53280 | tf_op jit(solution)/shard_map/ppermute | solution.py:537
  15.5 0.5 %pack_x.1 = (f32[3920,128]{1,0:T(8,128)S(1)}, f32[128,128]{1,0:T(8,128)S(1)}, f32[144,128]{1,0:T(8,128)S(1)}, f32[56,128]{1,0:T(8,128)S(1)}) custom-call(f32[3920,128]{1,0:T(8,128)S(1)} %get-tuple-element.22.part, f32[128,128]{1,0:T(8,128)S(1)} %get-tuple-element.23.packed, ...), custom_call_target="tpu_custom_call", output_to_operand_aliasing={{0}: (0, {}), {1}: (1, {})} | custom-call | tf_op jit(solution)/shard_map/pack_x/pallas_call | solution.py:594
  16.0 1.6 %collective-permute-start.6 = (f32[56,128]{1,0:T(8,128)S(1)}, f32[56,128]{1,0:T(8,128)S(1)}, u32[]{:S(2)}, u32[]{:S(2)}) collective-permute-start(f32[56,128]{1,0:T(8,128)S(1)} %get-tuple-element.28), channel_id=1, source_target_pairs={{0,16},{16,0},{1,17},{17,1},{2,18},{18,2},{3,19},{19,3},{4,20},{20... | collective-permute-start | bytes 86024 | tf_op jit(solution)/shard_map/ppermute | solution.py:537
  17.5 0.7 %block.1 = f32[27,72,128]{2,1,0:T(8,128)S(1)} custom-call(f32[3920,128]{1,0:T(8,128)S(1)} %get-tuple-element.26.full), custom_call_target="tpu_custom_call" | custom-call | flops 4976640 | bytes 4194304 | tf_op jit(solution)/shard_map/block/pallas_call | solution.py:610
  18.3 1.8 %collective-permute-done.6.x_one.x_two = f32[56,128]{1,0:T(8,128)S(1)} collective-permute-done((f32[56,128]{1,0:T(8,128)S(1)}, f32[56,128]{1,0:T(8,128)S(1)}, u32[]{:S(2)}, u32[]{:S(2)}) %collective-permute-start.6) | collective-permute-done | bytes 28704 | tf_op jit(solution)/shard_map/ppermute | solution.py:537
  20.1 1.4 %finish.1 = f32[27,4,8,128]{3,2,1,0:T(8,128)} custom-call(f32[3920,128]{1,0:T(8,128)S(1)} %get-tuple-element.26.full, f32[27,72,128]{2,1,0:T(8,128)S(1)} %block.1, f32[144,128]{1,0:T(8,128)S(1)} %get-tuple-element.27.columns, f32[56,128]{1,0:T(8,128)S(1)} %collective-permute-done.6.x_one.x_two, f32[56,128]{1,0:T(8,128)S(1)} %collective-permute-done.6.x_one.x_two), custom_call_target="tpu_custom_call" | custom-call | tf_op jit(solution)/shard_map/finish/pallas_call | solution.py:622
  (1 shorter events, 0.0 us)
Async XLA Ops:
  1.5 8.7 %collective-permute-start = (f32[136,128]{1,0:T(8,128)S(1)}, f32[136,128]{1,0:T(8,128)S(1)}, u32[]{:S(2)}, u32[]{:S(2)}) collective-permute-start(f32[136,128]{1,0:T(8,128)S(1)} %get-tuple-element.18), channel_id=1, source_target_pairs={{4,8},{12,0},{8,4},{0,12},{5,9},{13,1},{9,5},{1,13},{6,10},{14,2},... | collective-permute-start | bytes 208904 | tf_op jit(solution)/shard_map/ppermute | solution.py:537
  6.6 4.3 %collective-permute-start.1 = (f32[136,128]{1,0:T(8,128)S(1)}, f32[136,128]{1,0:T(8,128)S(1)}, u32[]{:S(2)}, u32[]{:S(2)}) collective-permute-start(f32[136,128]{1,0:T(8,128)S(1)} %get-tuple-element.19), channel_id=1, source_target_pairs={{0,4},{8,12},{4,0},{12,8},{1,5},{9,13},{5,1},{13,9},{2,6},{10,14},... | collective-permute-start | bytes 208904 | tf_op jit(solution)/shard_map/ppermute | solution.py:537
  6.6 7.9 %collective-permute-start.2 = (f32[312,128]{1,0:T(8,128)S(1)}, f32[312,128]{1,0:T(8,128)S(1)}, u32[]{:S(2)}, u32[]{:S(2)}) collective-permute-start(f32[312,128]{1,0:T(8,128)S(1)} %get-tuple-element.20), channel_id=1, source_target_pairs={{1,2},{2,1},{5,6},{6,5},{9,10},{10,9},{13,14},{14,13},{17,18},{18,... | collective-permute-start | bytes 479240 | tf_op jit(solution)/shard_map/ppermute | solution.py:537
  7.3 7.3 %collective-permute-start.3 = (f32[312,128]{1,0:T(8,128)S(1)}, f32[312,128]{1,0:T(8,128)S(1)}, u32[]{:S(2)}, u32[]{:S(2)}) collective-permute-start(f32[312,128]{1,0:T(8,128)S(1)} %get-tuple-element.21), channel_id=1, source_target_pairs={{0,1},{2,3},{1,0},{3,2},{4,5},{6,7},{5,4},{7,6},{8,9},{10,11},{9,8... | collective-permute-start | bytes 479240 | tf_op jit(solution)/shard_map/ppermute | solution.py:537
  11.0 4.0 %collective-permute-start.4 = (f32[104,128]{1,0:T(8,128)S(1)}, f32[104,128]{1,0:T(8,128)S(1)}, u32[]{:S(2)}, u32[]{:S(2)}) collective-permute-start(f32[104,128]{1,0:T(8,128)S(1)} %get-tuple-element.24), channel_id=1, source_target_pairs={{1,2},{2,1},{5,6},{6,5},{9,10},{10,9},{13,14},{14,13},{17,18},{18,... | collective-permute-start | bytes 159752 | tf_op jit(solution)/shard_map/ppermute | solution.py:537
  11.7 3.8 %collective-permute-start.5 = (f32[104,128]{1,0:T(8,128)S(1)}, f32[104,128]{1,0:T(8,128)S(1)}, u32[]{:S(2)}, u32[]{:S(2)}) collective-permute-start(f32[104,128]{1,0:T(8,128)S(1)} %get-tuple-element.25), channel_id=1, source_target_pairs={{0,1},{2,3},{1,0},{3,2},{4,5},{6,7},{5,4},{7,6},{8,9},{10,11},{9,8... | collective-permute-start | bytes 159752 | tf_op jit(solution)/shard_map/ppermute | solution.py:537
  16.0 4.1 %collective-permute-start.6 = (f32[56,128]{1,0:T(8,128)S(1)}, f32[56,128]{1,0:T(8,128)S(1)}, u32[]{:S(2)}, u32[]{:S(2)}) collective-permute-start(f32[56,128]{1,0:T(8,128)S(1)} %get-tuple-element.28), channel_id=1, source_target_pairs={{0,16},{16,0},{1,17},{17,1},{2,18},{18,2},{3,19},{19,3},{4,20},{20... | collective-permute-start | bytes 86024 | tf_op jit(solution)/shard_map/ppermute | solution.py:537

commit v18 on v16

--- a/solution.py
+++ b/solution.py
@@ -211,7 +211,7 @@
     flags[pl.ds(0, 2 * NZ), :] = from_lane(2)
 
 
-def second_kernel(y_two, y_one, z_two, z_one, flags, aims):
+def second_kernel(y_two, y_one, z_one, z_two, flags, aims):
     def pack(above, below):
         spread_mixed(below, above, flags, aims)
         by_parity(
@@ -327,7 +327,7 @@
     pack[pl.ds(FLAT, 128 - FLAT), :] = jnp.zeros((128 - FLAT, 128), F32)
 
 
-def third_kernel(part, packed, z_two, z_one, full, pack, columns, message):
+def third_kernel(part, packed, z_one, z_two, full, pack, columns, message):
     last = lax.axis_size("gz") - 1
     here = lax.axis_index("gz")
     by_parity("gz", z_one, z_two, functools.partial(add_planes, full))
@@ -564,7 +564,7 @@
     )(own)
     own_two = swap(own_two, "gz", 1, False)
     own_one = swap(own_one, "gz", 0, False)
-    z_two, z_one = pl.pallas_call(
+    z_one, z_two = pl.pallas_call(
         second_kernel,
         out_shape=[shape(Z_ROWS, 128)] * 2,
         in_specs=[VMEM] * 2,
@@ -574,8 +574,8 @@
         cost_estimate=pl.CostEstimate(flops=10**9, bytes_accessed=2**20, transcendentals=0),
         name="pack_z",
     )(y_two, y_one)
+    z_one = swap(z_one, "gz", 0, False)
     z_two = swap(z_two, "gz", 1, False)
-    z_one = swap(z_one, "gz", 0, False)
     part, packed = pl.pallas_call(
         fill_kernel,
         out_shape=[shape(SLABS * ROWS, 128), shape(128, 128)],
@@ -599,7 +599,7 @@
         input_output_aliases={0: 0, 1: 1},
         compiler_params=PARAMS,
         name="pack_x",
-    )(part, packed, z_two, z_one)
+    )(part, packed, z_one, z_two)
     x_one = swap(message, "gx", 0, True)
     x_two = x_one if lax.axis_size("gx") == 2 else swap(message, "gx", 1, True)
     block = pl.pallas_call(

time: 21.5 us -> 21.3 us (level)
  the two profiles are of different devices: /device:TPU:0 before, /device:TPU:1 now
where the time goes in v18:
time: 21.3 us; the launch traced here: 21.1 us
  starting transfers between devices  13.8 us (65%)
  Pallas kernels  4.49 us (21%)
  waiting for transfers between devices  2.76 us (13%)
    ppermute x7, starting transfers between devices, swap(): return lax.ppermute(value, axis, pairs + [(j, i) for i, j in pairs])  13.8 us
    ppermute x7, waiting for transfers between devices, swap(): return lax.ppermute(value, axis, pairs + [(j, i) for i, j in pairs])  2.76 us
    pallas_call x1, Pallas kernels, shards(): pl.pallas_call(last_kernel, out_shape=shape(27, NZ, NY, NX), in_specs=[VM...  1.4 us
    pallas_call x1, Pallas kernels, shards(): pl.pallas_call(first_kernel, out_shape=[shape(CHANNELS * NZ * 8, 128), sh...  1.36 us
    pallas_call x1, Pallas kernels, shards(): pl.pallas_call(block_kernel, out_shape=shape(27, UNITS * 8, 128), in_spec...  0.72 us
    pallas_call x1, Pallas kernels, shards(): pl.pallas_call(third_kernel, out_shape=[shape(SLABS * ROWS, 128), shape(1...  0.48 us
  transfers between devices with their start and end apart: 7, of which 2 were waited for; matrix products, arithmetic and copies ran while one was open for 0% of the time, Pallas kernels for 6%

profile of v18, /device:TPU:1, one launch (start us, length us, event | category | flops | bytes accessed | tf_op | source)
XLA Modules:
  0.0 21.1 jit_solution(13015864644288415466)
XLA Ops:
  0.0 1.4 %collide.1 = (f32[928,128]{1,0:T(8,128)S(1)}, f32[136,128]{1,0:T(8,128)S(1)}, f32[136,128]{1,0:T(8,128)S(1)}) custom-call(f32[27,4,8,128]{3,2,1,0:T(8,128)} %pops_at.1, s32[4,8,128]{2,1,0:T(8,128)} %solid_at.1, f32[4,8]{1,0:T(4,128)} %bitcast.1, s32[8]{0:T(128)} %index_at.1), custom_call_target="tpu_custom_call" | custom-call | tf_op jit(solution)/shard_map/collide/pallas_call | solution.py:540
  1.4 4.2 %collective-permute-start = (f32[136,128]{1,0:T(8,128)S(1)}, f32[136,128]{1,0:T(8,128)S(1)}, u32[]{:S(2)}, u32[]{:S(2)}) collective-permute-start(f32[136,128]{1,0:T(8,128)S(1)} %get-tuple-element.18), channel_id=1, source_target_pairs={{4,8},{12,0},{8,4},{0,12},{5,9},{13,1},{9,5},{1,13},{6,10},{14,2},... | collective-permute-start | bytes 208904 | tf_op jit(solution)/shard_map/ppermute | solution.py:532
  5.6 0.0 collective-permute-start.1
  5.6 4.0 %collective-permute-start.2 = (f32[312,128]{1,0:T(8,128)S(1)}, f32[312,128]{1,0:T(8,128)S(1)}, u32[]{:S(2)}, u32[]{:S(2)}) collective-permute-start(f32[312,128]{1,0:T(8,128)S(1)} %get-tuple-element.20), channel_id=1, source_target_pairs={{1,2},{2,1},{5,6},{6,5},{9,10},{10,9},{13,14},{14,13},{17,18},{18,... | collective-permute-start | bytes 479240 | tf_op jit(solution)/shard_map/ppermute | solution.py:532
  9.6 0.1 collective-permute-start.3
  9.7 0.0 collective-permute-done.y_two
  9.7 0.0 collective-permute-done.1.y_one
  9.7 0.1 pack_z.1
  9.8 1.2 %collective-permute-start.4 = (f32[104,128]{1,0:T(8,128)S(1)}, f32[104,128]{1,0:T(8,128)S(1)}, u32[]{:S(2)}, u32[]{:S(2)}) collective-permute-start(f32[104,128]{1,0:T(8,128)S(1)} %get-tuple-element.24), channel_id=1, source_target_pairs={{0,1},{2,3},{1,0},{3,2},{4,5},{6,7},{5,4},{7,6},{8,9},{10,11},{9,8... | collective-permute-start | bytes 159752 | tf_op jit(solution)/shard_map/ppermute | solution.py:532
  11.0 3.0 %collective-permute-start.5 = (f32[104,128]{1,0:T(8,128)S(1)}, f32[104,128]{1,0:T(8,128)S(1)}, u32[]{:S(2)}, u32[]{:S(2)}) collective-permute-start(f32[104,128]{1,0:T(8,128)S(1)} %get-tuple-element.25), channel_id=1, source_target_pairs={{1,2},{2,1},{5,6},{6,5},{9,10},{10,9},{13,14},{14,13},{17,18},{18,... | collective-permute-start | bytes 159752 | tf_op jit(solution)/shard_map/ppermute | solution.py:532
  14.0 0.0 collective-permute-done.2.two
  14.0 0.0 collective-permute-done.3.one
  14.0 0.4 %fill.1 = (f32[3920,128]{1,0:T(8,128)S(1)}, f32[128,128]{1,0:T(8,128)S(1)}) custom-call(f32[928,128]{1,0:T(8,128)S(1)} %get-tuple-element.17.own, f32[136,128]{1,0:T(8,128)S(1)} %collective-permute-done.y_two, f32[136,128]{1,0:T(8,128)S(1)} %collective-permute-done.1.y_one, f32[312,128]{1,0:T(8,128)S(1)} %collective-permute-done.2.two, ...), custom_call_target="tpu_custom_call" | custom-call | flops 1000000 | bytes 4194304 | tf_op jit(solution)/shard_map/fill/pallas_call | solution.py:579
  14.4 0.0 collective-permute-done.4.z_one
  14.4 2.0 %collective-permute-done.5.z_two = f32[104,128]{1,0:T(8,128)S(1)} collective-permute-done((f32[104,128]{1,0:T(8,128)S(1)}, f32[104,128]{1,0:T(8,128)S(1)}, u32[]{:S(2)}, u32[]{:S(2)}) %collective-permute-start.5) | collective-permute-done | bytes 53280 | tf_op jit(solution)/shard_map/ppermute | solution.py:532
  16.4 0.5 %pack_x.1 = (f32[3920,128]{1,0:T(8,128)S(1)}, f32[128,128]{1,0:T(8,128)S(1)}, f32[144,128]{1,0:T(8,128)S(1)}, f32[56,128]{1,0:T(8,128)S(1)}) custom-call(f32[3920,128]{1,0:T(8,128)S(1)} %get-tuple-element.22.part, f32[128,128]{1,0:T(8,128)S(1)} %get-tuple-element.23.packed, ...), custom_call_target="tpu_custom_call", output_to_operand_aliasing={{0}: (0, {}), {1}: (1, {})} | custom-call | tf_op jit(solution)/shard_map/pack_x/pallas_call | solution.py:589
  16.9 1.3 %collective-permute-start.6 = (f32[56,128]{1,0:T(8,128)S(1)}, f32[56,128]{1,0:T(8,128)S(1)}, u32[]{:S(2)}, u32[]{:S(2)}) collective-permute-start(f32[56,128]{1,0:T(8,128)S(1)} %get-tuple-element.28), channel_id=1, source_target_pairs={{0,16},{16,0},{1,17},{17,1},{2,18},{18,2},{3,19},{19,3},{4,20},{20... | collective-permute-start | bytes 86024 | tf_op jit(solution)/shard_map/ppermute | solution.py:532
  18.2 0.7 %block.1 = f32[27,72,128]{2,1,0:T(8,128)S(1)} custom-call(f32[3920,128]{1,0:T(8,128)S(1)} %get-tuple-element.26.full), custom_call_target="tpu_custom_call" | custom-call | flops 4976640 | bytes 4194304 | tf_op jit(solution)/shard_map/block/pallas_call | solution.py:605
  19.0 0.8 %collective-permute-done.6.x_one.x_two = f32[56,128]{1,0:T(8,128)S(1)} collective-permute-done((f32[56,128]{1,0:T(8,128)S(1)}, f32[56,128]{1,0:T(8,128)S(1)}, u32[]{:S(2)}, u32[]{:S(2)}) %collective-permute-start.6) | collective-permute-done | bytes 28704 | tf_op jit(solution)/shard_map/ppermute | solution.py:532
  19.7 1.4 %finish.1 = f32[27,4,8,128]{3,2,1,0:T(8,128)} custom-call(f32[3920,128]{1,0:T(8,128)S(1)} %get-tuple-element.26.full, f32[27,72,128]{2,1,0:T(8,128)S(1)} %block.1, f32[144,128]{1,0:T(8,128)S(1)} %get-tuple-element.27.columns, f32[56,128]{1,0:T(8,128)S(1)} %collective-permute-done.6.x_one.x_two, f32[56,128]{1,0:T(8,128)S(1)} %collective-permute-done.6.x_one.x_two), custom_call_target="tpu_custom_call" | custom-call | tf_op jit(solution)/shard_map/finish/pallas_call | solution.py:617
  (1 shorter events, 0.0 us)
Async XLA Ops:
  1.4 8.3 %collective-permute-start = (f32[136,128]{1,0:T(8,128)S(1)}, f32[136,128]{1,0:T(8,128)S(1)}, u32[]{:S(2)}, u32[]{:S(2)}) collective-permute-start(f32[136,128]{1,0:T(8,128)S(1)} %get-tuple-element.18), channel_id=1, source_target_pairs={{4,8},{12,0},{8,4},{0,12},{5,9},{13,1},{9,5},{1,13},{6,10},{14,2},... | collective-permute-start | bytes 208904 | tf_op jit(solution)/shard_map/ppermute | solution.py:532
  5.6 4.1 %collective-permute-start.1 = (f32[136,128]{1,0:T(8,128)S(1)}, f32[136,128]{1,0:T(8,128)S(1)}, u32[]{:S(2)}, u32[]{:S(2)}) collective-permute-start(f32[136,128]{1,0:T(8,128)S(1)} %get-tuple-element.19), channel_id=1, source_target_pairs={{0,4},{8,12},{4,0},{12,8},{1,5},{9,13},{5,1},{13,9},{2,6},{10,14},... | collective-permute-start | bytes 208904 | tf_op jit(solution)/shard_map/ppermute | solution.py:532
  5.6 8.4 %collective-permute-start.2 = (f32[312,128]{1,0:T(8,128)S(1)}, f32[312,128]{1,0:T(8,128)S(1)}, u32[]{:S(2)}, u32[]{:S(2)}) collective-permute-start(f32[312,128]{1,0:T(8,128)S(1)} %get-tuple-element.20), channel_id=1, source_target_pairs={{1,2},{2,1},{5,6},{6,5},{9,10},{10,9},{13,14},{14,13},{17,18},{18,... | collective-permute-start | bytes 479240 | tf_op jit(solution)/shard_map/ppermute | solution.py:532
  9.6 4.4 %collective-permute-start.3 = (f32[312,128]{1,0:T(8,128)S(1)}, f32[312,128]{1,0:T(8,128)S(1)}, u32[]{:S(2)}, u32[]{:S(2)}) collective-permute-start(f32[312,128]{1,0:T(8,128)S(1)} %get-tuple-element.21), channel_id=1, source_target_pairs={{0,1},{2,3},{1,0},{3,2},{4,5},{6,7},{5,4},{7,6},{8,9},{10,11},{9,8... | collective-permute-start | bytes 479240 | tf_op jit(solution)/shard_map/ppermute | solution.py:532
  9.8 4.6 %collective-permute-start.4 = (f32[104,128]{1,0:T(8,128)S(1)}, f32[104,128]{1,0:T(8,128)S(1)}, u32[]{:S(2)}, u32[]{:S(2)}) collective-permute-start(f32[104,128]{1,0:T(8,128)S(1)} %get-tuple-element.24), channel_id=1, source_target_pairs={{0,1},{2,3},{1,0},{3,2},{4,5},{6,7},{5,4},{7,6},{8,9},{10,11},{9,8... | collective-permute-start | bytes 159752 | tf_op jit(solution)/shard_map/ppermute | solution.py:532
  11.0 5.4 %collective-permute-start.5 = (f32[104,128]{1,0:T(8,128)S(1)}, f32[104,128]{1,0:T(8,128)S(1)}, u32[]{:S(2)}, u32[]{:S(2)}) collective-permute-start(f32[104,128]{1,0:T(8,128)S(1)} %get-tuple-element.25), channel_id=1, source_target_pairs={{1,2},{2,1},{5,6},{6,5},{9,10},{10,9},{13,14},{14,13},{17,18},{18,... | collective-permute-start | bytes 159752 | tf_op jit(solution)/shard_map/ppermute | solution.py:532
  16.9 2.8 %collective-permute-start.6 = (f32[56,128]{1,0:T(8,128)S(1)}, f32[56,128]{1,0:T(8,128)S(1)}, u32[]{:S(2)}, u32[]{:S(2)}) collective-permute-start(f32[56,128]{1,0:T(8,128)S(1)} %get-tuple-element.28), channel_id=1, source_target_pairs={{0,16},{16,0},{1,17},{17,1},{2,18},{18,2},{3,19},{19,3},{4,20},{20... | collective-permute-start | bytes 86024 | tf_op jit(solution)/shard_map/ppermute | solution.py:532

commit v19 on v18

--- a/solution.py
+++ b/solution.py
@@ -119,12 +119,18 @@
     pl.when(jnp.logical_not(even))(lambda: body(two, one))
 
 
+def by_roles(first, second, body):
+    even = lax.rem(lax.axis_index("gz"), 2) == 0
+    pl.when(even)(lambda: by_parity("gy", second, first, body))
+    pl.when(jnp.logical_not(even))(lambda: by_parity("gy", first, second, body))
+
+
 def z_blocks(near, far, part):
     blocks = [(c, near) for c in range(CHANNELS)]
     return blocks + [(9 * part + k, far) for k in range(9)] + [(WALL, far)]
 
 
-def first_kernel(pops_at, solid_at, table_at, index_at, own, two, one, *scratch):
+def first_kernel(pops_at, solid_at, table_at, index_at, own, first_out, second_out, *scratch):
     pops, solid, table, index, sems = scratch
     groups = [(pops_at.at[pl.ds(q, 9)], pops.at[pl.ds(q, 9)]) for q in (0, 9, 18)]
     small = [(table_at, table), (index_at, index)]
@@ -176,7 +182,7 @@
                     pl.ds((9 * a + part) * NZ * 8 + second, 3 * NZ, stride=8), :
                 ]
 
-    by_parity("gy", one, two, pack)
+    by_roles(first_out, second_out, pack)
 
 
 def ahead_kernel(own, two, one):
@@ -211,17 +217,17 @@
     flags[pl.ds(0, 2 * NZ), :] = from_lane(2)
 
 
-def second_kernel(y_two, y_one, z_one, z_two, flags, aims):
-    def pack(above, below):
+def second_kernel(y_first, y_second, z_one, z_two, flags, aims):
+    def pack(zup, zdown, above, below):
         spread_mixed(below, above, flags, aims)
-        by_parity(
-            "gz",
-            z_one,
-            z_two,
-            lambda zup, zdown: pack_planes(below, above, flags, aims, zup, zdown),
+        pack_planes(below, above, flags, aims, zup, zdown)
+
+    even = lax.rem(lax.axis_index("gz"), 2) == 0
+    ways = ((even, y_second, y_first, z_one, z_two), (~even, y_first, y_second, z_two, z_one))
+    for here, one, two, zup, zdown in ways:
+        pl.when(here)(
+            functools.partial(by_parity, "gy", one, two, functools.partial(pack, zup, zdown))
         )
-
-    by_parity("gy", y_one, y_two, pack)
 
 
 def pack_planes(below, above, flags, aims, zup, zdown):
@@ -317,11 +323,11 @@
 OWN_TILES = range(2 * PITCH // 8, (NZ + 2) * PITCH // 8)
 
 
-def fill_kernel(own, y_two, y_one, two, one, full, pack, flags, aims):
+def fill_kernel(own, y_first, y_second, two, one, full, pack, flags, aims):
     for c in range(CHANNELS):
         for z in range(NZ):
             full[pl.ds(c * ROWS + plane_at(z) + 2, 8), :] = own[pl.ds((c * NZ + z) * 8, 8), :]
-    by_parity("gy", y_one, y_two, functools.partial(add_rows, full, flags, aims))
+    by_roles(y_first, y_second, functools.partial(add_rows, full, flags, aims))
     by_parity("gz", one, two, functools.partial(add_own_planes, full))
     pack_columns(full, pack, OWN_TILES)
     pack[pl.ds(FLAT, 128 - FLAT), :] = jnp.zeros((128 - FLAT, 128), F32)
@@ -526,10 +532,23 @@
         copy.wait()
 
 
+def pairs(size, turn, wrap):
+    ahead = [(i, (i + 1) % size) for i in range(turn, size if wrap else size - 1, 2)]
+    return ahead + [(j, i) for i, j in ahead]
+
+
 def swap(value, axis, turn, wrap):
-    size = lax.axis_size(axis)
-    pairs = [(i, (i + 1) % size) for i in range(turn, size if wrap else size - 1, 2)]
-    return lax.ppermute(value, axis, pairs + [(j, i) for i, j in pairs])
+    return lax.ppermute(value, axis, pairs(lax.axis_size(axis), turn, wrap))
+
+
+def swap_mixed(value, turn):
+    size, planes = lax.axis_size("gy"), lax.axis_size("gz")
+    moves = []
+    for k in range(planes):
+        moves += [
+            (i * planes + k, j * planes + k) for i, j in pairs(size, (turn + k) % 2, True)
+        ]
+    return lax.ppermute(value, ("gy", "gz"), moves)
 
 
 def shape(*dims):
@@ -537,7 +556,7 @@
 
 
 def shards(pops, solid, profile_table, profile_index):
-    own, y_two, y_one = pl.pallas_call(
+    own, y_first, y_second = pl.pallas_call(
         first_kernel,
         out_shape=[shape(CHANNELS * NZ * 8, 128), shape(Y_ROWS, 128), shape(Y_ROWS, 128)],
         in_specs=[HBM] * 4,
@@ -552,8 +571,8 @@
         compiler_params=PARAMS,
         name="collide",
     )(*(pltpu.with_memory_space_constraint(a, pltpu.HBM) for a in (pops, solid, profile_table.T, profile_index)))
-    y_two = swap(y_two, "gy", 1, True)
-    y_one = swap(y_one, "gy", 0, True)
+    y_first = swap_mixed(y_first, 1)
+    y_second = swap_mixed(y_second, 0)
     own_two, own_one = pl.pallas_call(
         ahead_kernel,
         out_shape=[shape(Z_BLOCKS * 8, 128)] * 2,
@@ -573,7 +592,7 @@
         compiler_params=PARAMS,
         cost_estimate=pl.CostEstimate(flops=10**9, bytes_accessed=2**20, transcendentals=0),
         name="pack_z",
-    )(y_two, y_one)
+    )(y_first, y_second)
     z_one = swap(z_one, "gz", 0, False)
     z_two = swap(z_two, "gz", 1, False)
     part, packed = pl.pallas_call(
@@ -585,7 +604,7 @@
         compiler_params=PARAMS,
         cost_estimate=pl.CostEstimate(flops=10**6, bytes_accessed=2**22, transcendentals=0),
         name="fill",
-    )(own, y_two, y_one, own_two, own_one)
+    )(own, y_first, y_second, own_two, own_one)
     full, packed, columns, message = pl.pallas_call(
         third_kernel,
         out_shape=[

time: 21.3 us -> 21.3 us (level)
  no operation moved by 1% of the time
where the time goes in v19:
time: 21.3 us; the launch traced here: 21.1 us
  starting transfers between devices  13.8 us (65%)
  Pallas kernels  4.51 us (21%)
  waiting for transfers between devices  2.75 us (13%)
    ppermute x5, starting transfers between devices, swap(): return lax.ppermute(value, axis, pairs(lax.axis_size(axis), turn, wrap))  9.37 us
    ppermute x2, starting transfers between devices, swap_mixed(): return lax.ppermute(value, ('gy', 'gz'), moves)  4.39 us
    ppermute x5, waiting for transfers between devices, swap(): return lax.ppermute(value, axis, pairs(lax.axis_size(axis), turn, wrap))  2.74 us
    pallas_call x1, Pallas kernels, shards(): pl.pallas_call(last_kernel, out_shape=shape(27, NZ, NY, NX), in_specs=[VM...  1.4 us
    pallas_call x1, Pallas kernels, shards(): pl.pallas_call(first_kernel, out_shape=[shape(CHANNELS * NZ * 8, 128), sh...  1.38 us
    pallas_call x1, Pallas kernels, shards(): pl.pallas_call(block_kernel, out_shape=shape(27, UNITS * 8, 128), in_spec...  0.72 us
    pallas_call x1, Pallas kernels, shards(): pl.pallas_call(third_kernel, out_shape=[shape(SLABS * ROWS, 128), shape(1...  0.48 us
  transfers between devices with their start and end apart: 7, of which 2 were waited for; matrix products, arithmetic and copies ran while one was open for 0% of the time, Pallas kernels for 6%

profile of v19, /device:TPU:1, one launch (start us, length us, event | category | flops | bytes accessed | tf_op | source)
XLA Modules:
  0.0 21.1 jit_solution(13563039533268706079)
XLA Ops:
  0.0 1.4 %collide.1 = (f32[928,128]{1,0:T(8,128)S(1)}, f32[136,128]{1,0:T(8,128)S(1)}, f32[136,128]{1,0:T(8,128)S(1)}) custom-call(f32[27,4,8,128]{3,2,1,0:T(8,128)} %pops_at.1, s32[4,8,128]{2,1,0:T(8,128)} %solid_at.1, f32[4,8]{1,0:T(4,128)} %bitcast.1, s32[8]{0:T(128)} %index_at.1), custom_call_target="tpu_custom_call" | custom-call | tf_op jit(solution)/shard_map/collide/pallas_call | solution.py:559
  1.4 2.2 %collective-permute-start = (f32[136,128]{1,0:T(8,128)S(1)}, f32[136,128]{1,0:T(8,128)S(1)}, u32[]{:S(2)}, u32[]{:S(2)}) collective-permute-start(f32[136,128]{1,0:T(8,128)S(1)} %get-tuple-element.18), channel_id=1, source_target_pairs={{4,8},{12,0},{8,4},{0,12},{1,5},{9,13},{5,1},{13,9},{6,10},{14,2},... | collective-permute-start | bytes 208904 | tf_op jit(solution)/shard_map/ppermute | solution.py:551
  3.6 2.2 %collective-permute-start.1 = (f32[136,128]{1,0:T(8,128)S(1)}, f32[136,128]{1,0:T(8,128)S(1)}, u32[]{:S(2)}, u32[]{:S(2)}) collective-permute-start(f32[136,128]{1,0:T(8,128)S(1)} %get-tuple-element.19), channel_id=1, source_target_pairs={{0,4},{8,12},{4,0},{12,8},{5,9},{13,1},{9,5},{1,13},{2,6},{10,14},... | collective-permute-start | bytes 208904 | tf_op jit(solution)/shard_map/ppermute | solution.py:551
  5.8 3.8 %collective-permute-start.2 = (f32[312,128]{1,0:T(8,128)S(1)}, f32[312,128]{1,0:T(8,128)S(1)}, u32[]{:S(2)}, u32[]{:S(2)}) collective-permute-start(f32[312,128]{1,0:T(8,128)S(1)} %get-tuple-element.20), channel_id=1, source_target_pairs={{1,2},{2,1},{5,6},{6,5},{9,10},{10,9},{13,14},{14,13},{17,18},{18,... | collective-permute-start | bytes 479240 | tf_op jit(solution)/shard_map/ppermute | solution.py:541
  9.6 0.1 collective-permute-start.3
  9.7 0.0 collective-permute-done.y_first
  9.7 0.0 collective-permute-done.1.y_second
  9.7 0.1 pack_z.1
  9.8 1.2 %collective-permute-start.4 = (f32[104,128]{1,0:T(8,128)S(1)}, f32[104,128]{1,0:T(8,128)S(1)}, u32[]{:S(2)}, u32[]{:S(2)}) collective-permute-start(f32[104,128]{1,0:T(8,128)S(1)} %get-tuple-element.24), channel_id=1, source_target_pairs={{0,1},{2,3},{1,0},{3,2},{4,5},{6,7},{5,4},{7,6},{8,9},{10,11},{9,8... | collective-permute-start | bytes 159752 | tf_op jit(solution)/shard_map/ppermute | solution.py:541
  11.0 3.0 %collective-permute-start.5 = (f32[104,128]{1,0:T(8,128)S(1)}, f32[104,128]{1,0:T(8,128)S(1)}, u32[]{:S(2)}, u32[]{:S(2)}) collective-permute-start(f32[104,128]{1,0:T(8,128)S(1)} %get-tuple-element.25), channel_id=1, source_target_pairs={{1,2},{2,1},{5,6},{6,5},{9,10},{10,9},{13,14},{14,13},{17,18},{18,... | collective-permute-start | bytes 159752 | tf_op jit(solution)/shard_map/ppermute | solution.py:541
  14.0 0.0 collective-permute-done.2.two
  14.0 0.0 collective-permute-done.3.one
  14.0 0.4 %fill.1 = (f32[3920,128]{1,0:T(8,128)S(1)}, f32[128,128]{1,0:T(8,128)S(1)}) custom-call(f32[928,128]{1,0:T(8,128)S(1)} %get-tuple-element.17.own, f32[136,128]{1,0:T(8,128)S(1)} %collective-permute-done.y_first, f32[136,128]{1,0:T(8,128)S(1)} %collective-permute-done.1.y_second, f32[312,128]{1,0:T(8,128)S(1)} %collective-permute-done.2.two, ...), custom_call_target="tpu_custom_call" | custom-call | flops 1000000 | bytes 4194304 | tf_op jit(solution)/shard_map/fill/pallas_call | solution.py:598
  14.4 0.0 collective-permute-done.4.z_one
  14.5 2.0 %collective-permute-done.5.z_two = f32[104,128]{1,0:T(8,128)S(1)} collective-permute-done((f32[104,128]{1,0:T(8,128)S(1)}, f32[104,128]{1,0:T(8,128)S(1)}, u32[]{:S(2)}, u32[]{:S(2)}) %collective-permute-start.5) | collective-permute-done | bytes 53280 | tf_op jit(solution)/shard_map/ppermute | solution.py:541
  16.4 0.5 %pack_x.1 = (f32[3920,128]{1,0:T(8,128)S(1)}, f32[128,128]{1,0:T(8,128)S(1)}, f32[144,128]{1,0:T(8,128)S(1)}, f32[56,128]{1,0:T(8,128)S(1)}) custom-call(f32[3920,128]{1,0:T(8,128)S(1)} %get-tuple-element.22.part, f32[128,128]{1,0:T(8,128)S(1)} %get-tuple-element.23.packed, ...), custom_call_target="tpu_custom_call", output_to_operand_aliasing={{0}: (0, {}), {1}: (1, {})} | custom-call | tf_op jit(solution)/shard_map/pack_x/pallas_call | solution.py:608
  16.9 1.3 %collective-permute-start.6 = (f32[56,128]{1,0:T(8,128)S(1)}, f32[56,128]{1,0:T(8,128)S(1)}, u32[]{:S(2)}, u32[]{:S(2)}) collective-permute-start(f32[56,128]{1,0:T(8,128)S(1)} %get-tuple-element.28), channel_id=1, source_target_pairs={{0,16},{16,0},{1,17},{17,1},{2,18},{18,2},{3,19},{19,3},{4,20},{20... | collective-permute-start | bytes 86024 | tf_op jit(solution)/shard_map/ppermute | solution.py:541
  18.2 0.7 %block.1 = f32[27,72,128]{2,1,0:T(8,128)S(1)} custom-call(f32[3920,128]{1,0:T(8,128)S(1)} %get-tuple-element.26.full), custom_call_target="tpu_custom_call" | custom-call | flops 4976640 | bytes 4194304 | tf_op jit(solution)/shard_map/block/pallas_call | solution.py:624
  19.0 0.8 %collective-permute-done.6.x_one.x_two = f32[56,128]{1,0:T(8,128)S(1)} collective-permute-done((f32[56,128]{1,0:T(8,128)S(1)}, f32[56,128]{1,0:T(8,128)S(1)}, u32[]{:S(2)}, u32[]{:S(2)}) %collective-permute-start.6) | collective-permute-done | bytes 28704 | tf_op jit(solution)/shard_map/ppermute | solution.py:541
  19.7 1.4 %finish.1 = f32[27,4,8,128]{3,2,1,0:T(8,128)} custom-call(f32[3920,128]{1,0:T(8,128)S(1)} %get-tuple-element.26.full, f32[27,72,128]{2,1,0:T(8,128)S(1)} %block.1, f32[144,128]{1,0:T(8,128)S(1)} %get-tuple-element.27.columns, f32[56,128]{1,0:T(8,128)S(1)} %collective-permute-done.6.x_one.x_two, f32[56,128]{1,0:T(8,128)S(1)} %collective-permute-done.6.x_one.x_two), custom_call_target="tpu_custom_call" | custom-call | tf_op jit(solution)/shard_map/finish/pallas_call | solution.py:636
  (1 shorter events, 0.0 us)
Async XLA Ops:
  1.4 8.3 %collective-permute-start = (f32[136,128]{1,0:T(8,128)S(1)}, f32[136,128]{1,0:T(8,128)S(1)}, u32[]{:S(2)}, u32[]{:S(2)}) collective-permute-start(f32[136,128]{1,0:T(8,128)S(1)} %get-tuple-element.18), channel_id=1, source_target_pairs={{4,8},{12,0},{8,4},{0,12},{1,5},{9,13},{5,1},{13,9},{6,10},{14,2},... | collective-permute-start | bytes 208904 | tf_op jit(solution)/shard_map/ppermute | solution.py:551
  3.6 6.1 %collective-permute-start.1 = (f32[136,128]{1,0:T(8,128)S(1)}, f32[136,128]{1,0:T(8,128)S(1)}, u32[]{:S(2)}, u32[]{:S(2)}) collective-permute-start(f32[136,128]{1,0:T(8,128)S(1)} %get-tuple-element.19), channel_id=1, source_target_pairs={{0,4},{8,12},{4,0},{12,8},{5,9},{13,1},{9,5},{1,13},{2,6},{10,14},... | collective-permute-start | bytes 208904 | tf_op jit(solution)/shard_map/ppermute | solution.py:551
  5.8 8.2 %collective-permute-start.2 = (f32[312,128]{1,0:T(8,128)S(1)}, f32[312,128]{1,0:T(8,128)S(1)}, u32[]{:S(2)}, u32[]{:S(2)}) collective-permute-start(f32[312,128]{1,0:T(8,128)S(1)} %get-tuple-element.20), channel_id=1, source_target_pairs={{1,2},{2,1},{5,6},{6,5},{9,10},{10,9},{13,14},{14,13},{17,18},{18,... | collective-permute-start | bytes 479240 | tf_op jit(solution)/shard_map/ppermute | solution.py:541
  9.6 4.4 %collective-permute-start.3 = (f32[312,128]{1,0:T(8,128)S(1)}, f32[312,128]{1,0:T(8,128)S(1)}, u32[]{:S(2)}, u32[]{:S(2)}) collective-permute-start(f32[312,128]{1,0:T(8,128)S(1)} %get-tuple-element.21), channel_id=1, source_target_pairs={{0,1},{2,3},{1,0},{3,2},{4,5},{6,7},{5,4},{7,6},{8,9},{10,11},{9,8... | collective-permute-start | bytes 479240 | tf_op jit(solution)/shard_map/ppermute | solution.py:541
  9.8 4.6 %collective-permute-start.4 = (f32[104,128]{1,0:T(8,128)S(1)}, f32[104,128]{1,0:T(8,128)S(1)}, u32[]{:S(2)}, u32[]{:S(2)}) collective-permute-start(f32[104,128]{1,0:T(8,128)S(1)} %get-tuple-element.24), channel_id=1, source_target_pairs={{0,1},{2,3},{1,0},{3,2},{4,5},{6,7},{5,4},{7,6},{8,9},{10,11},{9,8... | collective-permute-start | bytes 159752 | tf_op jit(solution)/shard_map/ppermute | solution.py:541
  11.0 5.4 %collective-permute-start.5 = (f32[104,128]{1,0:T(8,128)S(1)}, f32[104,128]{1,0:T(8,128)S(1)}, u32[]{:S(2)}, u32[]{:S(2)}) collective-permute-start(f32[104,128]{1,0:T(8,128)S(1)} %get-tuple-element.25), channel_id=1, source_target_pairs={{1,2},{2,1},{5,6},{6,5},{9,10},{10,9},{13,14},{14,13},{17,18},{18,... | collective-permute-start | bytes 159752 | tf_op jit(solution)/shard_map/ppermute | solution.py:541
  16.9 2.8 %collective-permute-start.6 = (f32[56,128]{1,0:T(8,128)S(1)}, f32[56,128]{1,0:T(8,128)S(1)}, u32[]{:S(2)}, u32[]{:S(2)}) collective-permute-start(f32[56,128]{1,0:T(8,128)S(1)} %get-tuple-element.28), channel_id=1, source_target_pairs={{0,16},{16,0},{1,17},{17,1},{2,18},{18,2},{3,19},{19,3},{4,20},{20... | collective-permute-start | bytes 86024 | tf_op jit(solution)/shard_map/ppermute | solution.py:541

commit v20 on v19

--- a/solution.py
+++ b/solution.py
@@ -121,8 +121,8 @@
 
 def by_roles(first, second, body):
     even = lax.rem(lax.axis_index("gz"), 2) == 0
-    pl.when(even)(lambda: by_parity("gy", second, first, body))
-    pl.when(jnp.logical_not(even))(lambda: by_parity("gy", first, second, body))
+    pl.when(even)(lambda: by_parity("gy", first, second, body))
+    pl.when(jnp.logical_not(even))(lambda: by_parity("gy", second, first, body))
 
 
 def z_blocks(near, far, part):
@@ -223,7 +223,7 @@
         pack_planes(below, above, flags, aims, zup, zdown)
 
     even = lax.rem(lax.axis_index("gz"), 2) == 0
-    ways = ((even, y_second, y_first, z_one, z_two), (~even, y_first, y_second, z_two, z_one))
+    ways = ((even, y_first, y_second, z_one, z_two), (~even, y_second, y_first, z_two, z_one))
     for here, one, two, zup, zdown in ways:
         pl.when(here)(
             functools.partial(by_parity, "gy", one, two, functools.partial(pack, zup, zdown))
@@ -571,8 +571,8 @@
         compiler_params=PARAMS,
         name="collide",
     )(*(pltpu.with_memory_space_constraint(a, pltpu.HBM) for a in (pops, solid, profile_table.T, profile_index)))
-    y_first = swap_mixed(y_first, 1)
-    y_second = swap_mixed(y_second, 0)
+    y_first = swap_mixed(y_first, 0)
+    y_second = swap_mixed(y_second, 1)
     own_two, own_one = pl.pallas_call(
         ahead_kernel,
         out_shape=[shape(Z_BLOCKS * 8, 128)] * 2,

time: 21.3 us -> 21.1 us (level)
  starting transfers between devices: 13.8 us -> 13.5 us
where the time goes in v20:
time: 21.1 us; the launch traced here: 20.9 us
  starting transfers between devices  13.5 us (64%)
  Pallas kernels  4.51 us (21%)
  waiting for transfers between devices  2.75 us (13%)
    ppermute x5, starting transfers between devices, swap(): return lax.ppermute(value, axis, pairs(lax.axis_size(axis), turn, wrap))  9.31 us
    ppermute x2, starting transfers between devices, swap_mixed(): return lax.ppermute(value, ('gy', 'gz'), moves)  4.22 us
    ppermute x5, waiting for transfers between devices, swap(): return lax.ppermute(value, axis, pairs(lax.axis_size(axis), turn, wrap))  2.74 us
    pallas_call x1, Pallas kernels, shards(): pl.pallas_call(last_kernel, out_shape=shape(27, NZ, NY, NX), in_specs=[VM...  1.4 us
    pallas_call x1, Pallas kernels, shards(): pl.pallas_call(first_kernel, out_shape=[shape(CHANNELS * NZ * 8, 128), sh...  1.38 us
    pallas_call x1, Pallas kernels, shards(): pl.pallas_call(block_kernel, out_shape=shape(27, UNITS * 8, 128), in_spec...  0.72 us
    pallas_call x1, Pallas kernels, shards(): pl.pallas_call(third_kernel, out_shape=[shape(SLABS * ROWS, 128), shape(1...  0.48 us
  transfers between devices with their start and end apart: 7, of which 2 were waited for; matrix products, arithmetic and copies ran while one was open for 0% of the time, Pallas kernels for 6%

profile of v20, /device:TPU:1, one launch (start us, length us, event | category | flops | bytes accessed | tf_op | source)
XLA Modules:
  0.0 20.9 jit_solution(3223272003639981531)
XLA Ops:
  0.0 1.4 %collide.1 = (f32[928,128]{1,0:T(8,128)S(1)}, f32[136,128]{1,0:T(8,128)S(1)}, f32[136,128]{1,0:T(8,128)S(1)}) custom-call(f32[27,4,8,128]{3,2,1,0:T(8,128)} %pops_at.1, s32[4,8,128]{2,1,0:T(8,128)} %solid_at.1, f32[4,8]{1,0:T(4,128)} %bitcast.1, s32[8]{0:T(128)} %index_at.1), custom_call_target="tpu_custom_call" | custom-call | tf_op jit(solution)/shard_map/collide/pallas_call | solution.py:559
  1.4 4.2 %collective-permute-start = (f32[136,128]{1,0:T(8,128)S(1)}, f32[136,128]{1,0:T(8,128)S(1)}, u32[]{:S(2)}, u32[]{:S(2)}) collective-permute-start(f32[136,128]{1,0:T(8,128)S(1)} %get-tuple-element.18), channel_id=1, source_target_pairs={{0,4},{8,12},{4,0},{12,8},{5,9},{13,1},{9,5},{1,13},{2,6},{10,14},... | collective-permute-start | bytes 208904 | tf_op jit(solution)/shard_map/ppermute | solution.py:551
  5.6 0.0 collective-permute-start.1
  5.6 4.4 %collective-permute-start.2 = (f32[312,128]{1,0:T(8,128)S(1)}, f32[312,128]{1,0:T(8,128)S(1)}, u32[]{:S(2)}, u32[]{:S(2)}) collective-permute-start(f32[312,128]{1,0:T(8,128)S(1)} %get-tuple-element.20), channel_id=1, source_target_pairs={{1,2},{2,1},{5,6},{6,5},{9,10},{10,9},{13,14},{14,13},{17,18},{18,... | collective-permute-start | bytes 479240 | tf_op jit(solution)/shard_map/ppermute | solution.py:541
  10.1 0.1 collective-permute-start.3
  10.1 0.0 collective-permute-done.y_first
  10.1 0.0 collective-permute-done.1.y_second
  10.2 0.1 pack_z.1
  10.3 0.5 %collective-permute-start.4 = (f32[104,128]{1,0:T(8,128)S(1)}, f32[104,128]{1,0:T(8,128)S(1)}, u32[]{:S(2)}, u32[]{:S(2)}) collective-permute-start(f32[104,128]{1,0:T(8,128)S(1)} %get-tuple-element.24), channel_id=1, source_target_pairs={{0,1},{2,3},{1,0},{3,2},{4,5},{6,7},{5,4},{7,6},{8,9},{10,11},{9,8... | collective-permute-start | bytes 159752 | tf_op jit(solution)/shard_map/ppermute | solution.py:541
  10.8 3.0 %collective-permute-start.5 = (f32[104,128]{1,0:T(8,128)S(1)}, f32[104,128]{1,0:T(8,128)S(1)}, u32[]{:S(2)}, u32[]{:S(2)}) collective-permute-start(f32[104,128]{1,0:T(8,128)S(1)} %get-tuple-element.25), channel_id=1, source_target_pairs={{1,2},{2,1},{5,6},{6,5},{9,10},{10,9},{13,14},{14,13},{17,18},{18,... | collective-permute-start | bytes 159752 | tf_op jit(solution)/shard_map/ppermute | solution.py:541
  13.8 0.0 collective-permute-done.2.two
  13.8 0.0 collective-permute-done.3.one
  13.8 0.4 %fill.1 = (f32[3920,128]{1,0:T(8,128)S(1)}, f32[128,128]{1,0:T(8,128)S(1)}) custom-call(f32[928,128]{1,0:T(8,128)S(1)} %get-tuple-element.17.own, f32[136,128]{1,0:T(8,128)S(1)} %collective-permute-done.y_first, f32[136,128]{1,0:T(8,128)S(1)} %collective-permute-done.1.y_second, f32[312,128]{1,0:T(8,128)S(1)} %collective-permute-done.2.two, ...), custom_call_target="tpu_custom_call" | custom-call | flops 1000000 | bytes 4194304 | tf_op jit(solution)/shard_map/fill/pallas_call | solution.py:598
  14.2 0.0 collective-permute-done.4.z_one
  14.2 2.0 %collective-permute-done.5.z_two = f32[104,128]{1,0:T(8,128)S(1)} collective-permute-done((f32[104,128]{1,0:T(8,128)S(1)}, f32[104,128]{1,0:T(8,128)S(1)}, u32[]{:S(2)}, u32[]{:S(2)}) %collective-permute-start.5) | collective-permute-done | bytes 53280 | tf_op jit(solution)/shard_map/ppermute | solution.py:541
  16.2 0.5 %pack_x.1 = (f32[3920,128]{1,0:T(8,128)S(1)}, f32[128,128]{1,0:T(8,128)S(1)}, f32[144,128]{1,0:T(8,128)S(1)}, f32[56,128]{1,0:T(8,128)S(1)}) custom-call(f32[3920,128]{1,0:T(8,128)S(1)} %get-tuple-element.22.part, f32[128,128]{1,0:T(8,128)S(1)} %get-tuple-element.23.packed, ...), custom_call_target="tpu_custom_call", output_to_operand_aliasing={{0}: (0, {}), {1}: (1, {})} | custom-call | tf_op jit(solution)/shard_map/pack_x/pallas_call | solution.py:608
  16.7 1.3 %collective-permute-start.6 = (f32[56,128]{1,0:T(8,128)S(1)}, f32[56,128]{1,0:T(8,128)S(1)}, u32[]{:S(2)}, u32[]{:S(2)}) collective-permute-start(f32[56,128]{1,0:T(8,128)S(1)} %get-tuple-element.28), channel_id=1, source_target_pairs={{0,16},{16,0},{1,17},{17,1},{2,18},{18,2},{3,19},{19,3},{4,20},{20... | collective-permute-start | bytes 86024 | tf_op jit(solution)/shard_map/ppermute | solution.py:541
  18.0 0.7 %block.1 = f32[27,72,128]{2,1,0:T(8,128)S(1)} custom-call(f32[3920,128]{1,0:T(8,128)S(1)} %get-tuple-element.26.full), custom_call_target="tpu_custom_call" | custom-call | flops 4976640 | bytes 4194304 | tf_op jit(solution)/shard_map/block/pallas_call | solution.py:624
  18.7 0.8 %collective-permute-done.6.x_one.x_two = f32[56,128]{1,0:T(8,128)S(1)} collective-permute-done((f32[56,128]{1,0:T(8,128)S(1)}, f32[56,128]{1,0:T(8,128)S(1)}, u32[]{:S(2)}, u32[]{:S(2)}) %collective-permute-start.6) | collective-permute-done | bytes 28704 | tf_op jit(solution)/shard_map/ppermute | solution.py:541
  19.5 1.4 %finish.1 = f32[27,4,8,128]{3,2,1,0:T(8,128)} custom-call(f32[3920,128]{1,0:T(8,128)S(1)} %get-tuple-element.26.full, f32[27,72,128]{2,1,0:T(8,128)S(1)} %block.1, f32[144,128]{1,0:T(8,128)S(1)} %get-tuple-element.27.columns, f32[56,128]{1,0:T(8,128)S(1)} %collective-permute-done.6.x_one.x_two, f32[56,128]{1,0:T(8,128)S(1)} %collective-permute-done.6.x_one.x_two), custom_call_target="tpu_custom_call" | custom-call | tf_op jit(solution)/shard_map/finish/pallas_call | solution.py:636
  (1 shorter events, 0.0 us)
Async XLA Ops:
  1.4 8.7 %collective-permute-start = (f32[136,128]{1,0:T(8,128)S(1)}, f32[136,128]{1,0:T(8,128)S(1)}, u32[]{:S(2)}, u32[]{:S(2)}) collective-permute-start(f32[136,128]{1,0:T(8,128)S(1)} %get-tuple-element.18), channel_id=1, source_target_pairs={{0,4},{8,12},{4,0},{12,8},{5,9},{13,1},{9,5},{1,13},{2,6},{10,14},... | collective-permute-start | bytes 208904 | tf_op jit(solution)/shard_map/ppermute | solution.py:551
  5.6 4.5 %collective-permute-start.1 = (f32[136,128]{1,0:T(8,128)S(1)}, f32[136,128]{1,0:T(8,128)S(1)}, u32[]{:S(2)}, u32[]{:S(2)}) collective-permute-start(f32[136,128]{1,0:T(8,128)S(1)} %get-tuple-element.19), channel_id=1, source_target_pairs={{4,8},{12,0},{8,4},{0,12},{1,5},{9,13},{5,1},{13,9},{6,10},{14,2},... | collective-permute-start | bytes 208904 | tf_op jit(solution)/shard_map/ppermute | solution.py:551
  5.6 8.2 %collective-permute-start.2 = (f32[312,128]{1,0:T(8,128)S(1)}, f32[312,128]{1,0:T(8,128)S(1)}, u32[]{:S(2)}, u32[]{:S(2)}) collective-permute-start(f32[312,128]{1,0:T(8,128)S(1)} %get-tuple-element.20), channel_id=1, source_target_pairs={{1,2},{2,1},{5,6},{6,5},{9,10},{10,9},{13,14},{14,13},{17,18},{18,... | collective-permute-start | bytes 479240 | tf_op jit(solution)/shard_map/ppermute | solution.py:541
  10.1 3.8 %collective-permute-start.3 = (f32[312,128]{1,0:T(8,128)S(1)}, f32[312,128]{1,0:T(8,128)S(1)}, u32[]{:S(2)}, u32[]{:S(2)}) collective-permute-start(f32[312,128]{1,0:T(8,128)S(1)} %get-tuple-element.21), channel_id=1, source_target_pairs={{0,1},{2,3},{1,0},{3,2},{4,5},{6,7},{5,4},{7,6},{8,9},{10,11},{9,8... | collective-permute-start | bytes 479240 | tf_op jit(solution)/shard_map/ppermute | solution.py:541
  10.3 4.0 %collective-permute-start.4 = (f32[104,128]{1,0:T(8,128)S(1)}, f32[104,128]{1,0:T(8,128)S(1)}, u32[]{:S(2)}, u32[]{:S(2)}) collective-permute-start(f32[104,128]{1,0:T(8,128)S(1)} %get-tuple-element.24), channel_id=1, source_target_pairs={{0,1},{2,3},{1,0},{3,2},{4,5},{6,7},{5,4},{7,6},{8,9},{10,11},{9,8... | collective-permute-start | bytes 159752 | tf_op jit(solution)/shard_map/ppermute | solution.py:541
  10.8 5.4 %collective-permute-start.5 = (f32[104,128]{1,0:T(8,128)S(1)}, f32[104,128]{1,0:T(8,128)S(1)}, u32[]{:S(2)}, u32[]{:S(2)}) collective-permute-start(f32[104,128]{1,0:T(8,128)S(1)} %get-tuple-element.25), channel_id=1, source_target_pairs={{1,2},{2,1},{5,6},{6,5},{9,10},{10,9},{13,14},{14,13},{17,18},{18,... | collective-permute-start | bytes 159752 | tf_op jit(solution)/shard_map/ppermute | solution.py:541
  16.7 2.8 %collective-permute-start.6 = (f32[56,128]{1,0:T(8,128)S(1)}, f32[56,128]{1,0:T(8,128)S(1)}, u32[]{:S(2)}, u32[]{:S(2)}) collective-permute-start(f32[56,128]{1,0:T(8,128)S(1)} %get-tuple-element.28), channel_id=1, source_target_pairs={{0,16},{16,0},{1,17},{17,1},{2,18},{18,2},{3,19},{19,3},{4,20},{20... | collective-permute-start | bytes 86024 | tf_op jit(solution)/shard_map/ppermute | solution.py:541

commit v21 on v20

--- a/solution.py
+++ b/solution.py
@@ -120,9 +120,9 @@
 
 
 def by_roles(first, second, body):
-    even = lax.rem(lax.axis_index("gz"), 2) == 0
-    pl.when(even)(lambda: by_parity("gy", first, second, body))
-    pl.when(jnp.logical_not(even))(lambda: by_parity("gy", second, first, body))
+    inner = lax.rem((lax.axis_index("gz") + 1) // 2, 2) == 1
+    pl.when(inner)(lambda: by_parity("gy", first, second, body))
+    pl.when(jnp.logical_not(inner))(lambda: by_parity("gy", second, first, body))
 
 
 def z_blocks(near, far, part):
@@ -218,16 +218,16 @@
 
 
 def second_kernel(y_first, y_second, z_one, z_two, flags, aims):
-    def pack(zup, zdown, above, below):
+    def pack(above, below):
         spread_mixed(below, above, flags, aims)
-        pack_planes(below, above, flags, aims, zup, zdown)
-
-    even = lax.rem(lax.axis_index("gz"), 2) == 0
-    ways = ((even, y_first, y_second, z_one, z_two), (~even, y_second, y_first, z_two, z_one))
-    for here, one, two, zup, zdown in ways:
-        pl.when(here)(
-            functools.partial(by_parity, "gy", one, two, functools.partial(pack, zup, zdown))
+        by_parity(
+            "gz",
+            z_one,
+            z_two,
+            lambda zup, zdown: pack_planes(below, above, flags, aims, zup, zdown),
         )
+
+    by_roles(y_first, y_second, pack)
 
 
 def pack_planes(below, above, flags, aims, zup, zdown):
@@ -546,7 +546,8 @@
     moves = []
     for k in range(planes):
         moves += [
-            (i * planes + k, j * planes + k) for i, j in pairs(size, (turn + k) % 2, True)
+            (i * planes + k, j * planes + k)
+            for i, j in pairs(size, (turn + (k + 1) // 2 + 1) % 2, True)
         ]
     return lax.ppermute(value, ("gy", "gz"), moves)
 

time: 21.1 us -> 21.3 us (level)
  waiting for transfers between devices: 2.75 us -> 2.98 us
    ppermute x5, waiting for transfers between devices: 2.74 us -> 2.97 us  [swap(): return lax.ppermute(value, axis, pairs(lax.axis_size(axis), turn, wrap))]
where the time goes in v21:
time: 21.3 us; the launch traced here: 21.1 us
  starting transfers between devices  13.5 us (63%)
  Pallas kernels  4.54 us (21%)
  waiting for transfers between devices  2.98 us (14%)
    ppermute x5, starting transfers between devices, swap(): return lax.ppermute(value, axis, pairs(lax.axis_size(axis), turn, wrap))  9.12 us
    ppermute x2, starting transfers between devices, swap_mixed(): return lax.ppermute(value, ('gy', 'gz'), moves)  4.39 us
    ppermute x5, waiting for transfers between devices, swap(): return lax.ppermute(value, axis, pairs(lax.axis_size(axis), turn, wrap))  2.97 us
    pallas_call x1, Pallas kernels, shards(): pl.pallas_call(last_kernel, out_shape=shape(27, NZ, NY, NX), in_specs=[VM...  1.4 us
    pallas_call x1, Pallas kernels, shards(): pl.pallas_call(first_kernel, out_shape=[shape(CHANNELS * NZ * 8, 128), sh...  1.38 us
    pallas_call x1, Pallas kernels, shards(): pl.pallas_call(block_kernel, out_shape=shape(27, UNITS * 8, 128), in_spec...  0.72 us
    pallas_call x1, Pallas kernels, shards(): pl.pallas_call(third_kernel, out_shape=[shape(SLABS * ROWS, 128), shape(1...  0.48 us
  transfers between devices with their start and end apart: 7, of which 2 were waited for; matrix products, arithmetic and copies ran while one was open for 0% of the time, Pallas kernels for 6%

profile of v21, /device:TPU:1, one launch (start us, length us, event | category | flops | bytes accessed | tf_op | source)
XLA Modules:
  0.0 21.1 jit_solution(17527920471746110704)
XLA Ops:
  0.0 1.4 %collide.1 = (f32[928,128]{1,0:T(8,128)S(1)}, f32[136,128]{1,0:T(8,128)S(1)}, f32[136,128]{1,0:T(8,128)S(1)}) custom-call(f32[27,4,8,128]{3,2,1,0:T(8,128)} %pops_at.1, s32[4,8,128]{2,1,0:T(8,128)} %solid_at.1, f32[4,8]{1,0:T(4,128)} %bitcast.1, s32[8]{0:T(128)} %index_at.1), custom_call_target="tpu_custom_call" | custom-call | tf_op jit(solution)/shard_map/collide/pallas_call | solution.py:560
  1.4 2.2 %collective-permute-start = (f32[136,128]{1,0:T(8,128)S(1)}, f32[136,128]{1,0:T(8,128)S(1)}, u32[]{:S(2)}, u32[]{:S(2)}) collective-permute-start(f32[136,128]{1,0:T(8,128)S(1)} %get-tuple-element.18), channel_id=1, source_target_pairs={{4,8},{12,0},{8,4},{0,12},{1,5},{9,13},{5,1},{13,9},{2,6},{10,14},... | collective-permute-start | bytes 208904 | tf_op jit(solution)/shard_map/ppermute | solution.py:552
  3.6 2.2 %collective-permute-start.1 = (f32[136,128]{1,0:T(8,128)S(1)}, f32[136,128]{1,0:T(8,128)S(1)}, u32[]{:S(2)}, u32[]{:S(2)}) collective-permute-start(f32[136,128]{1,0:T(8,128)S(1)} %get-tuple-element.19), channel_id=1, source_target_pairs={{0,4},{8,12},{4,0},{12,8},{5,9},{13,1},{9,5},{1,13},{6,10},{14,2},... | collective-permute-start | bytes 208904 | tf_op jit(solution)/shard_map/ppermute | solution.py:552
  5.8 4.2 %collective-permute-start.2 = (f32[312,128]{1,0:T(8,128)S(1)}, f32[312,128]{1,0:T(8,128)S(1)}, u32[]{:S(2)}, u32[]{:S(2)}) collective-permute-start(f32[312,128]{1,0:T(8,128)S(1)} %get-tuple-element.20), channel_id=1, source_target_pairs={{1,2},{2,1},{5,6},{6,5},{9,10},{10,9},{13,14},{14,13},{17,18},{18,... | collective-permute-start | bytes 479240 | tf_op jit(solution)/shard_map/ppermute | solution.py:541
  10.1 0.1 collective-permute-start.3
  10.1 0.0 collective-permute-done.y_first
  10.1 0.0 collective-permute-done.1.y_second
  10.2 0.1 pack_z.1
  10.3 0.7 %collective-permute-start.4 = (f32[104,128]{1,0:T(8,128)S(1)}, f32[104,128]{1,0:T(8,128)S(1)}, u32[]{:S(2)}, u32[]{:S(2)}) collective-permute-start(f32[104,128]{1,0:T(8,128)S(1)} %get-tuple-element.24), channel_id=1, source_target_pairs={{0,1},{2,3},{1,0},{3,2},{4,5},{6,7},{5,4},{7,6},{8,9},{10,11},{9,8... | collective-permute-start | bytes 159752 | tf_op jit(solution)/shard_map/ppermute | solution.py:541
  11.0 2.8 %collective-permute-start.5 = (f32[104,128]{1,0:T(8,128)S(1)}, f32[104,128]{1,0:T(8,128)S(1)}, u32[]{:S(2)}, u32[]{:S(2)}) collective-permute-start(f32[104,128]{1,0:T(8,128)S(1)} %get-tuple-element.25), channel_id=1, source_target_pairs={{1,2},{2,1},{5,6},{6,5},{9,10},{10,9},{13,14},{14,13},{17,18},{18,... | collective-permute-start | bytes 159752 | tf_op jit(solution)/shard_map/ppermute | solution.py:541
  13.8 0.0 collective-permute-done.2.two
  13.8 0.0 collective-permute-done.3.one
  13.8 0.4 %fill.1 = (f32[3920,128]{1,0:T(8,128)S(1)}, f32[128,128]{1,0:T(8,128)S(1)}) custom-call(f32[928,128]{1,0:T(8,128)S(1)} %get-tuple-element.17.own, f32[136,128]{1,0:T(8,128)S(1)} %collective-permute-done.y_first, f32[136,128]{1,0:T(8,128)S(1)} %collective-permute-done.1.y_second, f32[312,128]{1,0:T(8,128)S(1)} %collective-permute-done.2.two, ...), custom_call_target="tpu_custom_call" | custom-call | flops 1000000 | bytes 4194304 | tf_op jit(solution)/shard_map/fill/pallas_call | solution.py:599
  14.2 0.0 collective-permute-done.4.z_one
  14.2 2.2 %collective-permute-done.5.z_two = f32[104,128]{1,0:T(8,128)S(1)} collective-permute-done((f32[104,128]{1,0:T(8,128)S(1)}, f32[104,128]{1,0:T(8,128)S(1)}, u32[]{:S(2)}, u32[]{:S(2)}) %collective-permute-start.5) | collective-permute-done | bytes 53280 | tf_op jit(solution)/shard_map/ppermute | solution.py:541
  16.5 0.5 %pack_x.1 = (f32[3920,128]{1,0:T(8,128)S(1)}, f32[128,128]{1,0:T(8,128)S(1)}, f32[144,128]{1,0:T(8,128)S(1)}, f32[56,128]{1,0:T(8,128)S(1)}) custom-call(f32[3920,128]{1,0:T(8,128)S(1)} %get-tuple-element.22.part, f32[128,128]{1,0:T(8,128)S(1)} %get-tuple-element.23.packed, ...), custom_call_target="tpu_custom_call", output_to_operand_aliasing={{0}: (0, {}), {1}: (1, {})} | custom-call | tf_op jit(solution)/shard_map/pack_x/pallas_call | solution.py:609
  16.9 1.3 %collective-permute-start.6 = (f32[56,128]{1,0:T(8,128)S(1)}, f32[56,128]{1,0:T(8,128)S(1)}, u32[]{:S(2)}, u32[]{:S(2)}) collective-permute-start(f32[56,128]{1,0:T(8,128)S(1)} %get-tuple-element.28), channel_id=1, source_target_pairs={{0,16},{16,0},{1,17},{17,1},{2,18},{18,2},{3,19},{19,3},{4,20},{20... | collective-permute-start | bytes 86024 | tf_op jit(solution)/shard_map/ppermute | solution.py:541
  18.2 0.7 %block.1 = f32[27,72,128]{2,1,0:T(8,128)S(1)} custom-call(f32[3920,128]{1,0:T(8,128)S(1)} %get-tuple-element.26.full), custom_call_target="tpu_custom_call" | custom-call | flops 4976640 | bytes 4194304 | tf_op jit(solution)/shard_map/block/pallas_call | solution.py:625
  19.0 0.8 %collective-permute-done.6.x_one.x_two = f32[56,128]{1,0:T(8,128)S(1)} collective-permute-done((f32[56,128]{1,0:T(8,128)S(1)}, f32[56,128]{1,0:T(8,128)S(1)}, u32[]{:S(2)}, u32[]{:S(2)}) %collective-permute-start.6) | collective-permute-done | bytes 28704 | tf_op jit(solution)/shard_map/ppermute | solution.py:541
  19.7 1.4 %finish.1 = f32[27,4,8,128]{3,2,1,0:T(8,128)} custom-call(f32[3920,128]{1,0:T(8,128)S(1)} %get-tuple-element.26.full, f32[27,72,128]{2,1,0:T(8,128)S(1)} %block.1, f32[144,128]{1,0:T(8,128)S(1)} %get-tuple-element.27.columns, f32[56,128]{1,0:T(8,128)S(1)} %collective-permute-done.6.x_one.x_two, f32[56,128]{1,0:T(8,128)S(1)} %collective-permute-done.6.x_one.x_two), custom_call_target="tpu_custom_call" | custom-call | tf_op jit(solution)/shard_map/finish/pallas_call | solution.py:637
  (1 shorter events, 0.0 us)
Async XLA Ops:
  1.4 8.7 %collective-permute-start = (f32[136,128]{1,0:T(8,128)S(1)}, f32[136,128]{1,0:T(8,128)S(1)}, u32[]{:S(2)}, u32[]{:S(2)}) collective-permute-start(f32[136,128]{1,0:T(8,128)S(1)} %get-tuple-element.18), channel_id=1, source_target_pairs={{4,8},{12,0},{8,4},{0,12},{1,5},{9,13},{5,1},{13,9},{2,6},{10,14},... | collective-permute-start | bytes 208904 | tf_op jit(solution)/shard_map/ppermute | solution.py:552
  3.6 6.6 %collective-permute-start.1 = (f32[136,128]{1,0:T(8,128)S(1)}, f32[136,128]{1,0:T(8,128)S(1)}, u32[]{:S(2)}, u32[]{:S(2)}) collective-permute-start(f32[136,128]{1,0:T(8,128)S(1)} %get-tuple-element.19), channel_id=1, source_target_pairs={{0,4},{8,12},{4,0},{12,8},{5,9},{13,1},{9,5},{1,13},{6,10},{14,2},... | collective-permute-start | bytes 208904 | tf_op jit(solution)/shard_map/ppermute | solution.py:552
  5.8 8.0 %collective-permute-start.2 = (f32[312,128]{1,0:T(8,128)S(1)}, f32[312,128]{1,0:T(8,128)S(1)}, u32[]{:S(2)}, u32[]{:S(2)}) collective-permute-start(f32[312,128]{1,0:T(8,128)S(1)} %get-tuple-element.20), channel_id=1, source_target_pairs={{1,2},{2,1},{5,6},{6,5},{9,10},{10,9},{13,14},{14,13},{17,18},{18,... | collective-permute-start | bytes 479240 | tf_op jit(solution)/shard_map/ppermute | solution.py:541
  10.1 3.8 %collective-permute-start.3 = (f32[312,128]{1,0:T(8,128)S(1)}, f32[312,128]{1,0:T(8,128)S(1)}, u32[]{:S(2)}, u32[]{:S(2)}) collective-permute-start(f32[312,128]{1,0:T(8,128)S(1)} %get-tuple-element.21), channel_id=1, source_target_pairs={{0,1},{2,3},{1,0},{3,2},{4,5},{6,7},{5,4},{7,6},{8,9},{10,11},{9,8... | collective-permute-start | bytes 479240 | tf_op jit(solution)/shard_map/ppermute | solution.py:541
  10.3 3.9 %collective-permute-start.4 = (f32[104,128]{1,0:T(8,128)S(1)}, f32[104,128]{1,0:T(8,128)S(1)}, u32[]{:S(2)}, u32[]{:S(2)}) collective-permute-start(f32[104,128]{1,0:T(8,128)S(1)} %get-tuple-element.24), channel_id=1, source_target_pairs={{0,1},{2,3},{1,0},{3,2},{4,5},{6,7},{5,4},{7,6},{8,9},{10,11},{9,8... | collective-permute-start | bytes 159752 | tf_op jit(solution)/shard_map/ppermute | solution.py:541
  11.0 5.4 %collective-permute-start.5 = (f32[104,128]{1,0:T(8,128)S(1)}, f32[104,128]{1,0:T(8,128)S(1)}, u32[]{:S(2)}, u32[]{:S(2)}) collective-permute-start(f32[104,128]{1,0:T(8,128)S(1)} %get-tuple-element.25), channel_id=1, source_target_pairs={{1,2},{2,1},{5,6},{6,5},{9,10},{10,9},{13,14},{14,13},{17,18},{18,... | collective-permute-start | bytes 159752 | tf_op jit(solution)/shard_map/ppermute | solution.py:541
  16.9 2.8 %collective-permute-start.6 = (f32[56,128]{1,0:T(8,128)S(1)}, f32[56,128]{1,0:T(8,128)S(1)}, u32[]{:S(2)}, u32[]{:S(2)}) collective-permute-start(f32[56,128]{1,0:T(8,128)S(1)} %get-tuple-element.28), channel_id=1, source_target_pairs={{0,16},{16,0},{1,17},{17,1},{2,18},{18,2},{3,19},{19,3},{4,20},{20... | collective-permute-start | bytes 86024 | tf_op jit(solution)/shard_map/ppermute | solution.py:541

commit v22 on v20

--- a/solution.py
+++ b/solution.py
@@ -119,10 +119,14 @@
     pl.when(jnp.logical_not(even))(lambda: body(two, one))
 
 
+def way(*axes):
+    return lax.rem(sum(lax.axis_index(axis) for axis in axes), 2)
+
+
 def by_roles(first, second, body):
-    even = lax.rem(lax.axis_index("gz"), 2) == 0
-    pl.when(even)(lambda: by_parity("gy", first, second, body))
-    pl.when(jnp.logical_not(even))(lambda: by_parity("gy", second, first, body))
+    ahead = way("gz", "gy") == 0
+    pl.when(ahead)(lambda: body(first, second))
+    pl.when(jnp.logical_not(ahead))(lambda: body(second, first))
 
 
 def z_blocks(near, far, part):
@@ -131,7 +135,7 @@
 
 
 def first_kernel(pops_at, solid_at, table_at, index_at, own, first_out, second_out, *scratch):
-    pops, solid, table, index, sems = scratch
+    pops, solid, table, index, messages, sems = scratch
     groups = [(pops_at.at[pl.ds(q, 9)], pops.at[pl.ds(q, 9)]) for q in (0, 9, 18)]
     small = [(table_at, table), (index_at, index)]
     copies = [
@@ -162,27 +166,28 @@
     for z in range(NZ):
         own[pl.ds((WALL * NZ + z) * 8, 8), :] = solid[z].astype(F32)
 
-    def pack(yup, ydown):
-        inside = lax.rem(lanes, 4)
-        for out, edge, second, part in ((yup, 7, 6, 6), (ydown, 0, 1, 0)):
-            back = 15 - part
-            for first, count, place in ((0, back, 0), (back + 3, 24 - back, back)):
-                out[pl.ds(place * NZ, count * NZ), :] = own[
-                    pl.ds(first * NZ * 8 + edge, count * NZ, stride=8), :
-                ]
-            for z in range(NZ):
-                west, east, aim, flag = (
-                    own[pl.ds((c * NZ + z) * 8, 8), :] for c in (back, back + 2, AIM, WALL)
-                )
-                mixed = jnp.where(inside < 2, jnp.where(inside == 0, west, aim), flag)
-                mixed = jnp.where(inside == 3, east, mixed)
-                out[pl.ds(MIXED * NZ + z, 1), :] = mixed[edge : edge + 1]
-            for a in range(3):
-                out[pl.ds((MIXED + 1 + 3 * a) * NZ, 3 * NZ), :] = own[
-                    pl.ds((9 * a + part) * NZ * 8 + second, 3 * NZ, stride=8), :
-                ]
-
-    by_roles(first_out, second_out, pack)
+    inside = lax.rem(lanes, 4)
+    for out, edge, second, part in ((messages.at[0], 7, 6, 6), (messages.at[1], 0, 1, 0)):
+        back = 15 - part
+        for first, count, place in ((0, back, 0), (back + 3, 24 - back, back)):
+            out[pl.ds(place * NZ, count * NZ), :] = own[
+                pl.ds(first * NZ * 8 + edge, count * NZ, stride=8), :
+            ]
+        for z in range(NZ):
+            west, east, aim, flag = (
+                own[pl.ds((c * NZ + z) * 8, 8), :] for c in (back, back + 2, AIM, WALL)
+            )
+            mixed = jnp.where(inside < 2, jnp.where(inside == 0, west, aim), flag)
+            mixed = jnp.where(inside == 3, east, mixed)
+            out[pl.ds(MIXED * NZ + z, 1), :] = mixed[edge : edge + 1]
+        for a in range(3):
+            out[pl.ds((MIXED + 1 + 3 * a) * NZ, 3 * NZ), :] = own[
+                pl.ds((9 * a + part) * NZ * 8 + second, 3 * NZ, stride=8), :
+            ]
+
+    ahead = way("gz", "gy")
+    first_out[...] = messages[ahead]
+    second_out[...] = messages[1 - ahead]
 
 
 def ahead_kernel(own, two, one):
@@ -217,17 +222,16 @@
     flags[pl.ds(0, 2 * NZ), :] = from_lane(2)
 
 
-def second_kernel(y_first, y_second, z_one, z_two, flags, aims):
-    def pack(zup, zdown, above, below):
-        spread_mixed(below, above, flags, aims)
-        pack_planes(below, above, flags, aims, zup, zdown)
-
-    even = lax.rem(lax.axis_index("gz"), 2) == 0
-    ways = ((even, y_first, y_second, z_one, z_two), (~even, y_second, y_first, z_two, z_one))
-    for here, one, two, zup, zdown in ways:
-        pl.when(here)(
-            functools.partial(by_parity, "gy", one, two, functools.partial(pack, zup, zdown))
-        )
+def second_kernel(y_first, y_second, z_one, z_two, flags, aims, halos, messages):
+    ahead = way("gz", "gy")
+    halos[ahead] = y_first[...]
+    halos[1 - ahead] = y_second[...]
+    above, below = halos.at[0], halos.at[1]
+    spread_mixed(below, above, flags, aims)
+    pack_planes(below, above, flags, aims, messages.at[0], messages.at[1])
+    ahead = way("gz")
+    z_one[...] = messages[ahead]
+    z_two[...] = messages[1 - ahead]
 
 
 def pack_planes(below, above, flags, aims, zup, zdown):
@@ -333,19 +337,19 @@
     pack[pl.ds(FLAT, 128 - FLAT), :] = jnp.zeros((128 - FLAT, 128), F32)
 
 
-def third_kernel(part, packed, z_one, z_two, full, pack, columns, message):
-    last = lax.axis_size("gz") - 1
-    here = lax.axis_index("gz")
-    by_parity("gz", z_one, z_two, functools.partial(add_planes, full))
-
-    @pl.when(here == 0)
-    def _():
-        full[pl.ds(WALL * ROWS + plane_at(-1), PITCH), :] = jnp.ones((PITCH, 128), F32)
-
-    @pl.when(here == last)
-    def _():
-        for q in range(9):
-            full[pl.ds(q * ROWS + plane_at(NZ), PITCH), :] = full[pl.ds((q + 18) * ROWS + plane_at(NZ - 1), PITCH), :]
+def third_kernel(part, packed, z_one, z_two, full, pack, columns, message, halos):
+    here, last = lax.axis_index("gz"), lax.axis_size("gz") - 1
+    ahead = way("gz")
+    halos[ahead] = z_one[...]
+    halos[1 - ahead] = z_two[...]
+    add_planes(full, halos.at[0], halos.at[1])
+
+    ground = pl.ds(WALL * ROWS + plane_at(-1), PITCH)
+    full[ground, :] = jnp.where(here == 0, 1.0, full[ground, :])
+    for q in range(9):
+        above = pl.ds(q * ROWS + plane_at(NZ), PITCH)
+        mirrored = full[pl.ds((q + 18) * ROWS + plane_at(NZ - 1), PITCH), :]
+        full[above, :] = jnp.where(here == last, mirrored, full[above, :])
 
     pack_columns(full, pack, [t for t in range(FLAT // 8) if t not in OWN_TILES])
     columns[pl.ds(PAD, 128), :] = pack[...].T
@@ -566,6 +570,7 @@
             pltpu.VMEM(solid.shape, jnp.int32),
             pltpu.SMEM(profile_table.shape[::-1], F32),
             pltpu.SMEM(profile_index.shape, jnp.int32),
+            pltpu.VMEM((2, Y_ROWS, 128), F32),
             pltpu.SemaphoreType.DMA((6,)),
         ],
         compiler_params=PARAMS,
@@ -588,7 +593,11 @@
         out_shape=[shape(Z_ROWS, 128)] * 2,
         in_specs=[VMEM] * 2,
         out_specs=[VMEM] * 2,
-        scratch_shapes=[pltpu.VMEM((4 * NZ, 128), F32)] * 2,
+        scratch_shapes=[
+            *[pltpu.VMEM((4 * NZ, 128), F32)] * 2,
+            pltpu.VMEM((2, Y_ROWS, 128), F32),
+            pltpu.VMEM((2, Z_ROWS, 128), F32),
+        ],
         compiler_params=PARAMS,
         cost_estimate=pl.CostEstimate(flops=10**9, bytes_accessed=2**20, transcendentals=0),
         name="pack_z",
@@ -615,6 +624,7 @@
         ],
         in_specs=[VMEM] * 4,
         out_specs=[VMEM] * 4,
+        scratch_shapes=[pltpu.VMEM((2, Z_ROWS, 128), F32)],
         input_output_aliases={0: 0, 1: 1},
         compiler_params=PARAMS,
         name="pack_x",

time: 21.1 us -> 21.1 us (level)
  no operation moved by 1% of the time
where the time goes in v22:
time: 21.1 us; the launch traced here: 20.9 us
  starting transfers between devices  13.6 us (64%)
  Pallas kernels  4.45 us (21%)
  waiting for transfers between devices  2.76 us (13%)
    ppermute x5, starting transfers between devices, swap(): return lax.ppermute(value, axis, pairs(lax.axis_size(axis), turn, wrap))  9.35 us
    ppermute x2, starting transfers between devices, swap_mixed(): return lax.ppermute(value, ('gy', 'gz'), moves)  4.22 us
    ppermute x5, waiting for transfers between devices, swap(): return lax.ppermute(value, axis, pairs(lax.axis_size(axis), turn, wrap))  2.75 us
    pallas_call x1, Pallas kernels, shards(): pl.pallas_call(last_kernel, out_shape=shape(27, NZ, NY, NX), in_specs=[VM...  1.4 us
    pallas_call x1, Pallas kernels, shards(): pl.pallas_call(first_kernel, out_shape=[shape(CHANNELS * NZ * 8, 128), sh...  1.37 us
    pallas_call x1, Pallas kernels, shards(): pl.pallas_call(block_kernel, out_shape=shape(27, UNITS * 8, 128), in_spec...  0.72 us
    pallas_call x1, Pallas kernels, shards(): pl.pallas_call(third_kernel, out_shape=[shape(SLABS * ROWS, 128), shape(1...  0.44 us
  transfers between devices with their start and end apart: 7, of which 2 were waited for; matrix products, arithmetic and copies ran while one was open for 0% of the time, Pallas kernels for 6%

profile of v22, /device:TPU:1, one launch (start us, length us, event | category | flops | bytes accessed | tf_op | source)
XLA Modules:
  0.0 20.9 jit_solution(11670990102396004018)
XLA Ops:
  0.0 1.4 %collide.1 = (f32[928,128]{1,0:T(8,128)S(1)}, f32[136,128]{1,0:T(8,128)S(1)}, f32[136,128]{1,0:T(8,128)S(1)}) custom-call(f32[27,4,8,128]{3,2,1,0:T(8,128)} %pops_at.1, s32[4,8,128]{2,1,0:T(8,128)} %solid_at.1, f32[4,8]{1,0:T(4,128)} %bitcast.1, s32[8]{0:T(128)} %index_at.1), custom_call_target="tpu_custom_call" | custom-call | tf_op jit(solution)/shard_map/collide/pallas_call | solution.py:563
  1.4 4.2 %collective-permute-start = (f32[136,128]{1,0:T(8,128)S(1)}, f32[136,128]{1,0:T(8,128)S(1)}, u32[]{:S(2)}, u32[]{:S(2)}) collective-permute-start(f32[136,128]{1,0:T(8,128)S(1)} %get-tuple-element.18), channel_id=1, source_target_pairs={{0,4},{8,12},{4,0},{12,8},{5,9},{13,1},{9,5},{1,13},{2,6},{10,14},... | collective-permute-start | bytes 208904 | tf_op jit(solution)/shard_map/ppermute | solution.py:555
  5.6 0.0 collective-permute-start.1
  5.6 4.4 %collective-permute-start.2 = (f32[312,128]{1,0:T(8,128)S(1)}, f32[312,128]{1,0:T(8,128)S(1)}, u32[]{:S(2)}, u32[]{:S(2)}) collective-permute-start(f32[312,128]{1,0:T(8,128)S(1)} %get-tuple-element.20), channel_id=1, source_target_pairs={{1,2},{2,1},{5,6},{6,5},{9,10},{10,9},{13,14},{14,13},{17,18},{18,... | collective-permute-start | bytes 479240 | tf_op jit(solution)/shard_map/ppermute | solution.py:545
  10.0 0.1 collective-permute-start.3
  10.1 0.0 collective-permute-done.y_first
  10.1 0.0 collective-permute-done.1.y_second
  10.1 0.1 pack_z.1
  10.3 0.5 %collective-permute-start.4 = (f32[104,128]{1,0:T(8,128)S(1)}, f32[104,128]{1,0:T(8,128)S(1)}, u32[]{:S(2)}, u32[]{:S(2)}) collective-permute-start(f32[104,128]{1,0:T(8,128)S(1)} %get-tuple-element.24), channel_id=1, source_target_pairs={{0,1},{2,3},{1,0},{3,2},{4,5},{6,7},{5,4},{7,6},{8,9},{10,11},{9,8... | collective-permute-start | bytes 159752 | tf_op jit(solution)/shard_map/ppermute | solution.py:545
  10.8 3.0 %collective-permute-start.5 = (f32[104,128]{1,0:T(8,128)S(1)}, f32[104,128]{1,0:T(8,128)S(1)}, u32[]{:S(2)}, u32[]{:S(2)}) collective-permute-start(f32[104,128]{1,0:T(8,128)S(1)} %get-tuple-element.25), channel_id=1, source_target_pairs={{1,2},{2,1},{5,6},{6,5},{9,10},{10,9},{13,14},{14,13},{17,18},{18,... | collective-permute-start | bytes 159752 | tf_op jit(solution)/shard_map/ppermute | solution.py:545
  13.8 0.0 collective-permute-done.2.two
  13.8 0.0 collective-permute-done.3.one
  13.8 0.4 %fill.1 = (f32[3920,128]{1,0:T(8,128)S(1)}, f32[128,128]{1,0:T(8,128)S(1)}) custom-call(f32[928,128]{1,0:T(8,128)S(1)} %get-tuple-element.17.own, f32[136,128]{1,0:T(8,128)S(1)} %collective-permute-done.y_first, f32[136,128]{1,0:T(8,128)S(1)} %collective-permute-done.1.y_second, f32[312,128]{1,0:T(8,128)S(1)} %collective-permute-done.2.two, ...), custom_call_target="tpu_custom_call" | custom-call | flops 1000000 | bytes 4194304 | tf_op jit(solution)/shard_map/fill/pallas_call | solution.py:607
  14.2 0.0 collective-permute-done.4.z_one
  14.3 2.0 %collective-permute-done.5.z_two = f32[104,128]{1,0:T(8,128)S(1)} collective-permute-done((f32[104,128]{1,0:T(8,128)S(1)}, f32[104,128]{1,0:T(8,128)S(1)}, u32[]{:S(2)}, u32[]{:S(2)}) %collective-permute-start.5) | collective-permute-done | bytes 53280 | tf_op jit(solution)/shard_map/ppermute | solution.py:545
  16.2 0.4 %pack_x.1 = (f32[3920,128]{1,0:T(8,128)S(1)}, f32[128,128]{1,0:T(8,128)S(1)}, f32[144,128]{1,0:T(8,128)S(1)}, f32[56,128]{1,0:T(8,128)S(1)}) custom-call(f32[3920,128]{1,0:T(8,128)S(1)} %get-tuple-element.22.part, f32[128,128]{1,0:T(8,128)S(1)} %get-tuple-element.23.packed, ...), custom_call_target="tpu_custom_call", output_to_operand_aliasing={{0}: (0, {}), {1}: (1, {})} | custom-call | tf_op jit(solution)/shard_map/pack_x/pallas_call | solution.py:617
  16.7 1.3 %collective-permute-start.6 = (f32[56,128]{1,0:T(8,128)S(1)}, f32[56,128]{1,0:T(8,128)S(1)}, u32[]{:S(2)}, u32[]{:S(2)}) collective-permute-start(f32[56,128]{1,0:T(8,128)S(1)} %get-tuple-element.28), channel_id=1, source_target_pairs={{0,16},{16,0},{1,17},{17,1},{2,18},{18,2},{3,19},{19,3},{4,20},{20... | collective-permute-start | bytes 86024 | tf_op jit(solution)/shard_map/ppermute | solution.py:545
  18.0 0.7 %block.1 = f32[27,72,128]{2,1,0:T(8,128)S(1)} custom-call(f32[3920,128]{1,0:T(8,128)S(1)} %get-tuple-element.26.full), custom_call_target="tpu_custom_call" | custom-call | flops 4976640 | bytes 4194304 | tf_op jit(solution)/shard_map/block/pallas_call | solution.py:634
  18.7 0.8 %collective-permute-done.6.x_one.x_two = f32[56,128]{1,0:T(8,128)S(1)} collective-permute-done((f32[56,128]{1,0:T(8,128)S(1)}, f32[56,128]{1,0:T(8,128)S(1)}, u32[]{:S(2)}, u32[]{:S(2)}) %collective-permute-start.6) | collective-permute-done | bytes 28704 | tf_op jit(solution)/shard_map/ppermute | solution.py:545
  19.5 1.4 %finish.1 = f32[27,4,8,128]{3,2,1,0:T(8,128)} custom-call(f32[3920,128]{1,0:T(8,128)S(1)} %get-tuple-element.26.full, f32[27,72,128]{2,1,0:T(8,128)S(1)} %block.1, f32[144,128]{1,0:T(8,128)S(1)} %get-tuple-element.27.columns, f32[56,128]{1,0:T(8,128)S(1)} %collective-permute-done.6.x_one.x_two, f32[56,128]{1,0:T(8,128)S(1)} %collective-permute-done.6.x_one.x_two), custom_call_target="tpu_custom_call" | custom-call | tf_op jit(solution)/shard_map/finish/pallas_call | solution.py:646
  (1 shorter events, 0.0 us)
Async XLA Ops:
  1.4 8.7 %collective-permute-start = (f32[136,128]{1,0:T(8,128)S(1)}, f32[136,128]{1,0:T(8,128)S(1)}, u32[]{:S(2)}, u32[]{:S(2)}) collective-permute-start(f32[136,128]{1,0:T(8,128)S(1)} %get-tuple-element.18), channel_id=1, source_target_pairs={{0,4},{8,12},{4,0},{12,8},{5,9},{13,1},{9,5},{1,13},{2,6},{10,14},... | collective-permute-start | bytes 208904 | tf_op jit(solution)/shard_map/ppermute | solution.py:555
  5.6 4.5 %collective-permute-start.1 = (f32[136,128]{1,0:T(8,128)S(1)}, f32[136,128]{1,0:T(8,128)S(1)}, u32[]{:S(2)}, u32[]{:S(2)}) collective-permute-start(f32[136,128]{1,0:T(8,128)S(1)} %get-tuple-element.19), channel_id=1, source_target_pairs={{4,8},{12,0},{8,4},{0,12},{1,5},{9,13},{5,1},{13,9},{6,10},{14,2},... | collective-permute-start | bytes 208904 | tf_op jit(solution)/shard_map/ppermute | solution.py:555
  5.6 8.2 %collective-permute-start.2 = (f32[312,128]{1,0:T(8,128)S(1)}, f32[312,128]{1,0:T(8,128)S(1)}, u32[]{:S(2)}, u32[]{:S(2)}) collective-permute-start(f32[312,128]{1,0:T(8,128)S(1)} %get-tuple-element.20), channel_id=1, source_target_pairs={{1,2},{2,1},{5,6},{6,5},{9,10},{10,9},{13,14},{14,13},{17,18},{18,... | collective-permute-start | bytes 479240 | tf_op jit(solution)/shard_map/ppermute | solution.py:545
  10.0 3.8 %collective-permute-start.3 = (f32[312,128]{1,0:T(8,128)S(1)}, f32[312,128]{1,0:T(8,128)S(1)}, u32[]{:S(2)}, u32[]{:S(2)}) collective-permute-start(f32[312,128]{1,0:T(8,128)S(1)} %get-tuple-element.21), channel_id=1, source_target_pairs={{0,1},{2,3},{1,0},{3,2},{4,5},{6,7},{5,4},{7,6},{8,9},{10,11},{9,8... | collective-permute-start | bytes 479240 | tf_op jit(solution)/shard_map/ppermute | solution.py:545
  10.3 4.0 %collective-permute-start.4 = (f32[104,128]{1,0:T(8,128)S(1)}, f32[104,128]{1,0:T(8,128)S(1)}, u32[]{:S(2)}, u32[]{:S(2)}) collective-permute-start(f32[104,128]{1,0:T(8,128)S(1)} %get-tuple-element.24), channel_id=1, source_target_pairs={{0,1},{2,3},{1,0},{3,2},{4,5},{6,7},{5,4},{7,6},{8,9},{10,11},{9,8... | collective-permute-start | bytes 159752 | tf_op jit(solution)/shard_map/ppermute | solution.py:545
  10.8 5.4 %collective-permute-start.5 = (f32[104,128]{1,0:T(8,128)S(1)}, f32[104,128]{1,0:T(8,128)S(1)}, u32[]{:S(2)}, u32[]{:S(2)}) collective-permute-start(f32[104,128]{1,0:T(8,128)S(1)} %get-tuple-element.25), channel_id=1, source_target_pairs={{1,2},{2,1},{5,6},{6,5},{9,10},{10,9},{13,14},{14,13},{17,18},{18,... | collective-permute-start | bytes 159752 | tf_op jit(solution)/shard_map/ppermute | solution.py:545
  16.7 2.8 %collective-permute-start.6 = (f32[56,128]{1,0:T(8,128)S(1)}, f32[56,128]{1,0:T(8,128)S(1)}, u32[]{:S(2)}, u32[]{:S(2)}) collective-permute-start(f32[56,128]{1,0:T(8,128)S(1)} %get-tuple-element.28), channel_id=1, source_target_pairs={{0,16},{16,0},{1,17},{17,1},{2,18},{18,2},{3,19},{19,3},{4,20},{20... | collective-permute-start | bytes 86024 | tf_op jit(solution)/shard_map/ppermute | solution.py:545

commit v23 on v22

--- a/solution.py
+++ b/solution.py
@@ -134,8 +134,8 @@
     return blocks + [(9 * part + k, far) for k in range(9)] + [(WALL, far)]
 
 
-def first_kernel(pops_at, solid_at, table_at, index_at, own, first_out, second_out, *scratch):
-    pops, solid, table, index, messages, sems = scratch
+def first_kernel(pops_at, solid_at, table_at, index_at, own, first_out, *scratch):
+    pops, solid, table, index, sems = scratch
     groups = [(pops_at.at[pl.ds(q, 9)], pops.at[pl.ds(q, 9)]) for q in (0, 9, 18)]
     small = [(table_at, table), (index_at, index)]
     copies = [
@@ -166,31 +166,37 @@
     for z in range(NZ):
         own[pl.ds((WALL * NZ + z) * 8, 8), :] = solid[z].astype(F32)
 
-    inside = lax.rem(lanes, 4)
-    for out, edge, second, part in ((messages.at[0], 7, 6, 6), (messages.at[1], 0, 1, 0)):
-        back = 15 - part
-        for first, count, place in ((0, back, 0), (back + 3, 24 - back, back)):
-            out[pl.ds(place * NZ, count * NZ), :] = own[
-                pl.ds(first * NZ * 8 + edge, count * NZ, stride=8), :
-            ]
-        for z in range(NZ):
-            west, east, aim, flag = (
-                own[pl.ds((c * NZ + z) * 8, 8), :] for c in (back, back + 2, AIM, WALL)
-            )
-            mixed = jnp.where(inside < 2, jnp.where(inside == 0, west, aim), flag)
-            mixed = jnp.where(inside == 3, east, mixed)
-            out[pl.ds(MIXED * NZ + z, 1), :] = mixed[edge : edge + 1]
-        for a in range(3):
-            out[pl.ds((MIXED + 1 + 3 * a) * NZ, 3 * NZ), :] = own[
-                pl.ds((9 * a + part) * NZ * 8 + second, 3 * NZ, stride=8), :
-            ]
-
-    ahead = way("gz", "gy")
-    first_out[...] = messages[ahead]
-    second_out[...] = messages[1 - ahead]
-
-
-def ahead_kernel(own, two, one):
+    ahead = way("gz", "gy") == 0
+    pl.when(ahead)(lambda: pack_rows(own, first_out, True))
+    pl.when(jnp.logical_not(ahead))(lambda: pack_rows(own, first_out, False))
+
+
+def pack_rows(own, out, upward):
+    inside = lax.rem(lane_ids(), 4)
+    edge, second, part = (7, 6, 6) if upward else (0, 1, 0)
+    back = 15 - part
+    for first, count, place in ((0, back, 0), (back + 3, 24 - back, back)):
+        out[pl.ds(place * NZ, count * NZ), :] = own[
+            pl.ds(first * NZ * 8 + edge, count * NZ, stride=8), :
+        ]
+    for z in range(NZ):
+        west, east, aim, flag = (
+            own[pl.ds((c * NZ + z) * 8, 8), :] for c in (back, back + 2, AIM, WALL)
+        )
+        mixed = jnp.where(inside < 2, jnp.where(inside == 0, west, aim), flag)
+        mixed = jnp.where(inside == 3, east, mixed)
+        out[pl.ds(MIXED * NZ + z, 1), :] = mixed[edge : edge + 1]
+    for a in range(3):
+        out[pl.ds((MIXED + 1 + 3 * a) * NZ, 3 * NZ), :] = own[
+            pl.ds((9 * a + part) * NZ * 8 + second, 3 * NZ, stride=8), :
+        ]
+
+
+def ahead_kernel(own, two, one, second_out):
+    ahead = way("gz", "gy") == 0
+    pl.when(ahead)(lambda: pack_rows(own, second_out, False))
+    pl.when(jnp.logical_not(ahead))(lambda: pack_rows(own, second_out, True))
+
     def pack(zup, zdown):
         for out, first, second, part in ((zup, NZ - 1, NZ - 2, 2), (zdown, 0, 1, 0)):
             for k, (c, z) in enumerate(z_blocks(first, second, part)):
@@ -560,34 +566,33 @@
 
 
 def shards(pops, solid, profile_table, profile_index):
-    own, y_first, y_second = pl.pallas_call(
+    own, y_first = pl.pallas_call(
         first_kernel,
-        out_shape=[shape(CHANNELS * NZ * 8, 128), shape(Y_ROWS, 128), shape(Y_ROWS, 128)],
+        out_shape=[shape(CHANNELS * NZ * 8, 128), shape(Y_ROWS, 128)],
         in_specs=[HBM] * 4,
-        out_specs=[VMEM] * 3,
+        out_specs=[VMEM] * 2,
         scratch_shapes=[
             pltpu.VMEM(pops.shape, F32),
             pltpu.VMEM(solid.shape, jnp.int32),
             pltpu.SMEM(profile_table.shape[::-1], F32),
             pltpu.SMEM(profile_index.shape, jnp.int32),
-            pltpu.VMEM((2, Y_ROWS, 128), F32),
             pltpu.SemaphoreType.DMA((6,)),
         ],
         compiler_params=PARAMS,
         name="collide",
     )(*(pltpu.with_memory_space_constraint(a, pltpu.HBM) for a in (pops, solid, profile_table.T, profile_index)))
     y_first = swap_mixed(y_first, 0)
-    y_second = swap_mixed(y_second, 1)
-    own_two, own_one = pl.pallas_call(
+    own_two, own_one, y_second = pl.pallas_call(
         ahead_kernel,
-        out_shape=[shape(Z_BLOCKS * 8, 128)] * 2,
+        out_shape=[*[shape(Z_BLOCKS * 8, 128)] * 2, shape(Y_ROWS, 128)],
         in_specs=[VMEM],
-        out_specs=[VMEM] * 2,
+        out_specs=[VMEM] * 3,
         compiler_params=PARAMS,
         name="pack_own",
     )(own)
     own_two = swap(own_two, "gz", 1, False)
     own_one = swap(own_one, "gz", 0, False)
+    y_second = swap_mixed(y_second, 1)
     z_one, z_two = pl.pallas_call(
         second_kernel,
         out_shape=[shape(Z_ROWS, 128)] * 2,

time: 21.1 us -> 21.2 us (level)
  no operation moved by 1% of the time
where the time goes in v23:
time: 21.2 us; the launch traced here: 21 us
  starting transfers between devices  13.7 us (65%)
  Pallas kernels  4.46 us (21%)
  waiting for transfers between devices  2.76 us (13%)
    ppermute x5, starting transfers between devices, swap(): return lax.ppermute(value, axis, pairs(lax.axis_size(axis), turn, wrap))  9.37 us
    ppermute x2, starting transfers between devices, swap_mixed(): return lax.ppermute(value, ('gy', 'gz'), moves)  4.29 us
    ppermute x5, waiting for transfers between devices, swap(): return lax.ppermute(value, axis, pairs(lax.axis_size(axis), turn, wrap))  2.75 us
    pallas_call x1, Pallas kernels, shards(): pl.pallas_call(last_kernel, out_shape=shape(27, NZ, NY, NX), in_specs=[VM...  1.4 us
    pallas_call x1, Pallas kernels, shards(): pl.pallas_call(first_kernel, out_shape=[shape(CHANNELS * NZ * 8, 128), sh...  1.35 us
    pallas_call x1, Pallas kernels, shards(): pl.pallas_call(block_kernel, out_shape=shape(27, UNITS * 8, 128), in_spec...  0.72 us
    pallas_call x1, Pallas kernels, shards(): pl.pallas_call(third_kernel, out_shape=[shape(SLABS * ROWS, 128), shape(1...  0.44 us
  transfers between devices with their start and end apart: 7, of which 2 were waited for; matrix products, arithmetic and copies ran while one was open for 0% of the time, Pallas kernels for 6%

profile of v23, /device:TPU:1, one launch (start us, length us, event | category | flops | bytes accessed | tf_op | source)
XLA Modules:
  0.0 21.0 jit_solution(10096792609449110988)
XLA Ops:
  0.0 1.3 %collide.1 = (f32[928,128]{1,0:T(8,128)S(1)}, f32[136,128]{1,0:T(8,128)S(1)}) custom-call(f32[27,4,8,128]{3,2,1,0:T(8,128)} %pops_at.1, s32[4,8,128]{2,1,0:T(8,128)} %solid_at.1, f32[4,8]{1,0:T(4,128)} %bitcast.1, s32[8]{0:T(128)} %index_at.1), custom_call_target="tpu_custom_call" | custom-call | tf_op jit(solution)/shard_map/collide/pallas_call | solution.py:569
  1.4 4.2 %collective-permute-start = (f32[136,128]{1,0:T(8,128)S(1)}, f32[136,128]{1,0:T(8,128)S(1)}, u32[]{:S(2)}, u32[]{:S(2)}) collective-permute-start(f32[136,128]{1,0:T(8,128)S(1)} %get-tuple-element.18), channel_id=1, source_target_pairs={{0,4},{8,12},{4,0},{12,8},{5,9},{13,1},{9,5},{1,13},{2,6},{10,14},... | collective-permute-start | bytes 208904 | tf_op jit(solution)/shard_map/ppermute | solution.py:561
  5.6 0.1 collective-permute-start.1
  5.7 4.4 %collective-permute-start.2 = (f32[312,128]{1,0:T(8,128)S(1)}, f32[312,128]{1,0:T(8,128)S(1)}, u32[]{:S(2)}, u32[]{:S(2)}) collective-permute-start(f32[312,128]{1,0:T(8,128)S(1)} %get-tuple-element.20), channel_id=1, source_target_pairs={{1,2},{2,1},{5,6},{6,5},{9,10},{10,9},{13,14},{14,13},{17,18},{18,... | collective-permute-start | bytes 479240 | tf_op jit(solution)/shard_map/ppermute | solution.py:551
  10.1 0.1 collective-permute-start.3
  10.2 0.0 collective-permute-done.y_first
  10.2 0.0 collective-permute-done.1.y_second
  10.2 0.1 pack_z.1
  10.3 0.6 %collective-permute-start.4 = (f32[104,128]{1,0:T(8,128)S(1)}, f32[104,128]{1,0:T(8,128)S(1)}, u32[]{:S(2)}, u32[]{:S(2)}) collective-permute-start(f32[104,128]{1,0:T(8,128)S(1)} %get-tuple-element.24), channel_id=1, source_target_pairs={{0,1},{2,3},{1,0},{3,2},{4,5},{6,7},{5,4},{7,6},{8,9},{10,11},{9,8... | collective-permute-start | bytes 159752 | tf_op jit(solution)/shard_map/ppermute | solution.py:551
  10.9 3.0 %collective-permute-start.5 = (f32[104,128]{1,0:T(8,128)S(1)}, f32[104,128]{1,0:T(8,128)S(1)}, u32[]{:S(2)}, u32[]{:S(2)}) collective-permute-start(f32[104,128]{1,0:T(8,128)S(1)} %get-tuple-element.25), channel_id=1, source_target_pairs={{1,2},{2,1},{5,6},{6,5},{9,10},{10,9},{13,14},{14,13},{17,18},{18,... | collective-permute-start | bytes 159752 | tf_op jit(solution)/shard_map/ppermute | solution.py:551
  13.9 0.0 collective-permute-done.2.two
  13.9 0.0 collective-permute-done.3.one
  14.0 0.4 %fill.1 = (f32[3920,128]{1,0:T(8,128)S(1)}, f32[128,128]{1,0:T(8,128)S(1)}) custom-call(f32[928,128]{1,0:T(8,128)S(1)} %get-tuple-element.17.own, f32[136,128]{1,0:T(8,128)S(1)} %collective-permute-done.y_first, f32[136,128]{1,0:T(8,128)S(1)} %collective-permute-done.1.y_second, f32[312,128]{1,0:T(8,128)S(1)} %collective-permute-done.2.two, ...), custom_call_target="tpu_custom_call" | custom-call | flops 1000000 | bytes 4194304 | tf_op jit(solution)/shard_map/fill/pallas_call | solution.py:612
  14.3 0.0 collective-permute-done.4.z_one
  14.4 2.0 %collective-permute-done.5.z_two = f32[104,128]{1,0:T(8,128)S(1)} collective-permute-done((f32[104,128]{1,0:T(8,128)S(1)}, f32[104,128]{1,0:T(8,128)S(1)}, u32[]{:S(2)}, u32[]{:S(2)}) %collective-permute-start.5) | collective-permute-done | bytes 53280 | tf_op jit(solution)/shard_map/ppermute | solution.py:551
  16.3 0.4 %pack_x.1 = (f32[3920,128]{1,0:T(8,128)S(1)}, f32[128,128]{1,0:T(8,128)S(1)}, f32[144,128]{1,0:T(8,128)S(1)}, f32[56,128]{1,0:T(8,128)S(1)}) custom-call(f32[3920,128]{1,0:T(8,128)S(1)} %get-tuple-element.22.part, f32[128,128]{1,0:T(8,128)S(1)} %get-tuple-element.23.packed, ...), custom_call_target="tpu_custom_call", output_to_operand_aliasing={{0}: (0, {}), {1}: (1, {})} | custom-call | tf_op jit(solution)/shard_map/pack_x/pallas_call | solution.py:622
  16.8 1.3 %collective-permute-start.6 = (f32[56,128]{1,0:T(8,128)S(1)}, f32[56,128]{1,0:T(8,128)S(1)}, u32[]{:S(2)}, u32[]{:S(2)}) collective-permute-start(f32[56,128]{1,0:T(8,128)S(1)} %get-tuple-element.28), channel_id=1, source_target_pairs={{0,16},{16,0},{1,17},{17,1},{2,18},{18,2},{3,19},{19,3},{4,20},{20... | collective-permute-start | bytes 86024 | tf_op jit(solution)/shard_map/ppermute | solution.py:551
  18.1 0.7 %block.1 = f32[27,72,128]{2,1,0:T(8,128)S(1)} custom-call(f32[3920,128]{1,0:T(8,128)S(1)} %get-tuple-element.26.full), custom_call_target="tpu_custom_call" | custom-call | flops 4976640 | bytes 4194304 | tf_op jit(solution)/shard_map/block/pallas_call | solution.py:639
  18.8 0.8 %collective-permute-done.6.x_one.x_two = f32[56,128]{1,0:T(8,128)S(1)} collective-permute-done((f32[56,128]{1,0:T(8,128)S(1)}, f32[56,128]{1,0:T(8,128)S(1)}, u32[]{:S(2)}, u32[]{:S(2)}) %collective-permute-start.6) | collective-permute-done | bytes 28704 | tf_op jit(solution)/shard_map/ppermute | solution.py:551
  19.6 1.4 %finish.1 = f32[27,4,8,128]{3,2,1,0:T(8,128)} custom-call(f32[3920,128]{1,0:T(8,128)S(1)} %get-tuple-element.26.full, f32[27,72,128]{2,1,0:T(8,128)S(1)} %block.1, f32[144,128]{1,0:T(8,128)S(1)} %get-tuple-element.27.columns, f32[56,128]{1,0:T(8,128)S(1)} %collective-permute-done.6.x_one.x_two, f32[56,128]{1,0:T(8,128)S(1)} %collective-permute-done.6.x_one.x_two), custom_call_target="tpu_custom_call" | custom-call | tf_op jit(solution)/shard_map/finish/pallas_call | solution.py:651
  (1 shorter events, 0.0 us)
Async XLA Ops:
  1.4 8.8 %collective-permute-start = (f32[136,128]{1,0:T(8,128)S(1)}, f32[136,128]{1,0:T(8,128)S(1)}, u32[]{:S(2)}, u32[]{:S(2)}) collective-permute-start(f32[136,128]{1,0:T(8,128)S(1)} %get-tuple-element.18), channel_id=1, source_target_pairs={{0,4},{8,12},{4,0},{12,8},{5,9},{13,1},{9,5},{1,13},{2,6},{10,14},... | collective-permute-start | bytes 208904 | tf_op jit(solution)/shard_map/ppermute | solution.py:561
  5.6 4.6 %collective-permute-start.1 = (f32[136,128]{1,0:T(8,128)S(1)}, f32[136,128]{1,0:T(8,128)S(1)}, u32[]{:S(2)}, u32[]{:S(2)}) collective-permute-start(f32[136,128]{1,0:T(8,128)S(1)} %get-tuple-element.19), channel_id=1, source_target_pairs={{4,8},{12,0},{8,4},{0,12},{1,5},{9,13},{5,1},{13,9},{6,10},{14,2},... | collective-permute-start | bytes 208904 | tf_op jit(solution)/shard_map/ppermute | solution.py:561
  5.7 8.2 %collective-permute-start.2 = (f32[312,128]{1,0:T(8,128)S(1)}, f32[312,128]{1,0:T(8,128)S(1)}, u32[]{:S(2)}, u32[]{:S(2)}) collective-permute-start(f32[312,128]{1,0:T(8,128)S(1)} %get-tuple-element.20), channel_id=1, source_target_pairs={{1,2},{2,1},{5,6},{6,5},{9,10},{10,9},{13,14},{14,13},{17,18},{18,... | collective-permute-start | bytes 479240 | tf_op jit(solution)/shard_map/ppermute | solution.py:551
  10.1 3.8 %collective-permute-start.3 = (f32[312,128]{1,0:T(8,128)S(1)}, f32[312,128]{1,0:T(8,128)S(1)}, u32[]{:S(2)}, u32[]{:S(2)}) collective-permute-start(f32[312,128]{1,0:T(8,128)S(1)} %get-tuple-element.21), channel_id=1, source_target_pairs={{0,1},{2,3},{1,0},{3,2},{4,5},{6,7},{5,4},{7,6},{8,9},{10,11},{9,8... | collective-permute-start | bytes 479240 | tf_op jit(solution)/shard_map/ppermute | solution.py:551
  10.3 4.0 %collective-permute-start.4 = (f32[104,128]{1,0:T(8,128)S(1)}, f32[104,128]{1,0:T(8,128)S(1)}, u32[]{:S(2)}, u32[]{:S(2)}) collective-permute-start(f32[104,128]{1,0:T(8,128)S(1)} %get-tuple-element.24), channel_id=1, source_target_pairs={{0,1},{2,3},{1,0},{3,2},{4,5},{6,7},{5,4},{7,6},{8,9},{10,11},{9,8... | collective-permute-start | bytes 159752 | tf_op jit(solution)/shard_map/ppermute | solution.py:551
  10.9 5.4 %collective-permute-start.5 = (f32[104,128]{1,0:T(8,128)S(1)}, f32[104,128]{1,0:T(8,128)S(1)}, u32[]{:S(2)}, u32[]{:S(2)}) collective-permute-start(f32[104,128]{1,0:T(8,128)S(1)} %get-tuple-element.25), channel_id=1, source_target_pairs={{1,2},{2,1},{5,6},{6,5},{9,10},{10,9},{13,14},{14,13},{17,18},{18,... | collective-permute-start | bytes 159752 | tf_op jit(solution)/shard_map/ppermute | solution.py:551
  16.8 2.8 %collective-permute-start.6 = (f32[56,128]{1,0:T(8,128)S(1)}, f32[56,128]{1,0:T(8,128)S(1)}, u32[]{:S(2)}, u32[]{:S(2)}) collective-permute-start(f32[56,128]{1,0:T(8,128)S(1)} %get-tuple-element.28), channel_id=1, source_target_pairs={{0,16},{16,0},{1,17},{17,1},{2,18},{18,2},{3,19},{19,3},{4,20},{20... | collective-permute-start | bytes 86024 | tf_op jit(solution)/shard_map/ppermute | solution.py:551

commit v24 on v22

--- a/solution.py
+++ b/solution.py
@@ -324,7 +324,27 @@
         pack[pl.ds(8 * t, 8), :] = packed
 
 
-OWN_TILES = range(2 * PITCH // 8, (NZ + 2) * PITCH // 8)
+def pack_rim(full, pack, first):
+    slot, rows = lane_ids() // 4, row_ids()
+    parts = (rows < 2, (rows >= 2) & (rows < 6), rows >= 6)
+    packed = jnp.zeros((8, 128), F32)
+    for c in range(CHANNELS):
+        a, b, d = (full[pl.ds(c * ROWS + PAD + 8 * (first + t), 8), :] for t in range(3))
+        rim = jnp.where(parts[0], a, jnp.where(parts[1], b, d))
+        packed = jnp.where(slot == c, pltpu.roll(rim, (4 * c + 2) % 128, 1), packed)
+    for t, part in enumerate(parts):
+        tile = pl.ds(8 * (first + t), 8)
+        pack[tile, :] = jnp.where(part, packed, pack[tile, :])
+
+
+def bound_planes(full):
+    here, last = lax.axis_index("gz"), lax.axis_size("gz") - 1
+    ground = pl.ds(WALL * ROWS + plane_at(-1), PITCH)
+    full[ground, :] = jnp.where(here == 0, 1.0, full[ground, :])
+    for q in range(9):
+        above = pl.ds(q * ROWS + plane_at(NZ), PITCH)
+        mirrored = full[pl.ds((q + 18) * ROWS + plane_at(NZ - 1), PITCH), :]
+        full[above, :] = jnp.where(here == last, mirrored, full[above, :])
 
 
 def fill_kernel(own, y_first, y_second, two, one, full, pack, flags, aims):
@@ -333,25 +353,19 @@
             full[pl.ds(c * ROWS + plane_at(z) + 2, 8), :] = own[pl.ds((c * NZ + z) * 8, 8), :]
     by_roles(y_first, y_second, functools.partial(add_rows, full, flags, aims))
     by_parity("gz", one, two, functools.partial(add_own_planes, full))
-    pack_columns(full, pack, OWN_TILES)
+    bound_planes(full)
+    pack_columns(full, pack, range(FLAT // 8))
     pack[pl.ds(FLAT, 128 - FLAT), :] = jnp.zeros((128 - FLAT, 128), F32)
 
 
 def third_kernel(part, packed, z_one, z_two, full, pack, columns, message, halos):
-    here, last = lax.axis_index("gz"), lax.axis_size("gz") - 1
     ahead = way("gz")
     halos[ahead] = z_one[...]
     halos[1 - ahead] = z_two[...]
     add_planes(full, halos.at[0], halos.at[1])
-
-    ground = pl.ds(WALL * ROWS + plane_at(-1), PITCH)
-    full[ground, :] = jnp.where(here == 0, 1.0, full[ground, :])
-    for q in range(9):
-        above = pl.ds(q * ROWS + plane_at(NZ), PITCH)
-        mirrored = full[pl.ds((q + 18) * ROWS + plane_at(NZ - 1), PITCH), :]
-        full[above, :] = jnp.where(here == last, mirrored, full[above, :])
-
-    pack_columns(full, pack, [t for t in range(FLAT // 8) if t not in OWN_TILES])
+    bound_planes(full)
+    for first in (0, (NZ + 2) * PITCH // 8):
+        pack_rim(full, pack, first)
     columns[pl.ds(PAD, 128), :] = pack[...].T
 
     def row(c, i, count):

time: 21.1 us -> 21 us (level)
  transfers between devices with their start and end apart: 7 -> 7, of which waited for: 2 -> 2; matrix products, arithmetic and copies ran while one was open for 0% -> 0% of each run, Pallas kernels for 6% -> 7%
where the time goes in v24:
time: 21 us; the launch traced here: 20.8 us
  starting transfers between devices  13.6 us (65%)
  Pallas kernels  4.54 us (22%)
  waiting for transfers between devices  2.57 us (12%)
    ppermute x5, starting transfers between devices, swap(): return lax.ppermute(value, axis, pairs(lax.axis_size(axis), turn, wrap))  9.35 us
    ppermute x2, starting transfers between devices, swap_mixed(): return lax.ppermute(value, ('gy', 'gz'), moves)  4.22 us
    ppermute x5, waiting for transfers between devices, swap(): return lax.ppermute(value, axis, pairs(lax.axis_size(axis), turn, wrap))  2.57 us
    pallas_call x1, Pallas kernels, shards(): pl.pallas_call(last_kernel, out_shape=shape(27, NZ, NY, NX), in_specs=[VM...  1.4 us
    pallas_call x1, Pallas kernels, shards(): pl.pallas_call(first_kernel, out_shape=[shape(CHANNELS * NZ * 8, 128), sh...  1.37 us
    pallas_call x1, Pallas kernels, shards(): pl.pallas_call(block_kernel, out_shape=shape(27, UNITS * 8, 128), in_spec...  0.72 us
    pallas_call x1, Pallas kernels, shards(): pl.pallas_call(fill_kernel, out_shape=[shape(SLABS * ROWS, 128), shape(12...  0.57 us
  transfers between devices with their start and end apart: 7, of which 2 were waited for; matrix products, arithmetic and copies ran while one was open for 0% of the time, Pallas kernels for 7%

profile of v24, /device:TPU:1, one launch (start us, length us, event | category | flops | bytes accessed | tf_op | source)
XLA Modules:
  0.0 20.8 jit_solution(2280818158556631488)
XLA Ops:
  0.0 1.4 %collide.1 = (f32[928,128]{1,0:T(8,128)S(1)}, f32[136,128]{1,0:T(8,128)S(1)}, f32[136,128]{1,0:T(8,128)S(1)}) custom-call(f32[27,4,8,128]{3,2,1,0:T(8,128)} %pops_at.1, s32[4,8,128]{2,1,0:T(8,128)} %solid_at.1, f32[4,8]{1,0:T(4,128)} %bitcast.1, s32[8]{0:T(128)} %index_at.1), custom_call_target="tpu_custom_call" | custom-call | tf_op jit(solution)/shard_map/collide/pallas_call | solution.py:577
  1.4 4.2 %collective-permute-start = (f32[136,128]{1,0:T(8,128)S(1)}, f32[136,128]{1,0:T(8,128)S(1)}, u32[]{:S(2)}, u32[]{:S(2)}) collective-permute-start(f32[136,128]{1,0:T(8,128)S(1)} %get-tuple-element.18), channel_id=1, source_target_pairs={{0,4},{8,12},{4,0},{12,8},{5,9},{13,1},{9,5},{1,13},{2,6},{10,14},... | collective-permute-start | bytes 208904 | tf_op jit(solution)/shard_map/ppermute | solution.py:569
  5.6 0.0 collective-permute-start.1
  5.6 4.4 %collective-permute-start.2 = (f32[312,128]{1,0:T(8,128)S(1)}, f32[312,128]{1,0:T(8,128)S(1)}, u32[]{:S(2)}, u32[]{:S(2)}) collective-permute-start(f32[312,128]{1,0:T(8,128)S(1)} %get-tuple-element.20), channel_id=1, source_target_pairs={{1,2},{2,1},{5,6},{6,5},{9,10},{10,9},{13,14},{14,13},{17,18},{18,... | collective-permute-start | bytes 479240 | tf_op jit(solution)/shard_map/ppermute | solution.py:559
  10.0 0.1 collective-permute-start.3
  10.1 0.0 collective-permute-done.y_first
  10.1 0.0 collective-permute-done.1.y_second
  10.1 0.1 pack_z.1
  10.3 0.5 %collective-permute-start.4 = (f32[104,128]{1,0:T(8,128)S(1)}, f32[104,128]{1,0:T(8,128)S(1)}, u32[]{:S(2)}, u32[]{:S(2)}) collective-permute-start(f32[104,128]{1,0:T(8,128)S(1)} %get-tuple-element.24), channel_id=1, source_target_pairs={{0,1},{2,3},{1,0},{3,2},{4,5},{6,7},{5,4},{7,6},{8,9},{10,11},{9,8... | collective-permute-start | bytes 159752 | tf_op jit(solution)/shard_map/ppermute | solution.py:559
  10.8 3.0 %collective-permute-start.5 = (f32[104,128]{1,0:T(8,128)S(1)}, f32[104,128]{1,0:T(8,128)S(1)}, u32[]{:S(2)}, u32[]{:S(2)}) collective-permute-start(f32[104,128]{1,0:T(8,128)S(1)} %get-tuple-element.25), channel_id=1, source_target_pairs={{1,2},{2,1},{5,6},{6,5},{9,10},{10,9},{13,14},{14,13},{17,18},{18,... | collective-permute-start | bytes 159752 | tf_op jit(solution)/shard_map/ppermute | solution.py:559
  13.8 0.0 collective-permute-done.2.two
  13.8 0.0 collective-permute-done.3.one
  13.8 0.6 %fill.1 = (f32[3920,128]{1,0:T(8,128)S(1)}, f32[128,128]{1,0:T(8,128)S(1)}) custom-call(f32[928,128]{1,0:T(8,128)S(1)} %get-tuple-element.17.own, f32[136,128]{1,0:T(8,128)S(1)} %collective-permute-done.y_first, f32[136,128]{1,0:T(8,128)S(1)} %collective-permute-done.1.y_second, f32[312,128]{1,0:T(8,128)S(1)} %collective-permute-done.2.two, ...), custom_call_target="tpu_custom_call" | custom-call | flops 1000000 | bytes 4194304 | tf_op jit(solution)/shard_map/fill/pallas_call | solution.py:621
  14.4 0.0 collective-permute-done.4.z_one
  14.4 1.8 %collective-permute-done.5.z_two = f32[104,128]{1,0:T(8,128)S(1)} collective-permute-done((f32[104,128]{1,0:T(8,128)S(1)}, f32[104,128]{1,0:T(8,128)S(1)}, u32[]{:S(2)}, u32[]{:S(2)}) %collective-permute-start.5) | collective-permute-done | bytes 53280 | tf_op jit(solution)/shard_map/ppermute | solution.py:559
  16.2 0.3 %pack_x.1 = (f32[3920,128]{1,0:T(8,128)S(1)}, f32[128,128]{1,0:T(8,128)S(1)}, f32[144,128]{1,0:T(8,128)S(1)}, f32[56,128]{1,0:T(8,128)S(1)}) custom-call(f32[3920,128]{1,0:T(8,128)S(1)} %get-tuple-element.22.part, f32[128,128]{1,0:T(8,128)S(1)} %get-tuple-element.23.packed, ...), custom_call_target="tpu_custom_call", output_to_operand_aliasing={{0}: (0, {}), {1}: (1, {})} | custom-call | tf_op jit(solution)/shard_map/pack_x/pallas_call | solution.py:631
  16.6 1.3 %collective-permute-start.6 = (f32[56,128]{1,0:T(8,128)S(1)}, f32[56,128]{1,0:T(8,128)S(1)}, u32[]{:S(2)}, u32[]{:S(2)}) collective-permute-start(f32[56,128]{1,0:T(8,128)S(1)} %get-tuple-element.28), channel_id=1, source_target_pairs={{0,16},{16,0},{1,17},{17,1},{2,18},{18,2},{3,19},{19,3},{4,20},{20... | collective-permute-start | bytes 86024 | tf_op jit(solution)/shard_map/ppermute | solution.py:559
  17.9 0.7 %block.1 = f32[27,72,128]{2,1,0:T(8,128)S(1)} custom-call(f32[3920,128]{1,0:T(8,128)S(1)} %get-tuple-element.26.full), custom_call_target="tpu_custom_call" | custom-call | flops 4976640 | bytes 4194304 | tf_op jit(solution)/shard_map/block/pallas_call | solution.py:648
  18.6 0.8 %collective-permute-done.6.x_one.x_two = f32[56,128]{1,0:T(8,128)S(1)} collective-permute-done((f32[56,128]{1,0:T(8,128)S(1)}, f32[56,128]{1,0:T(8,128)S(1)}, u32[]{:S(2)}, u32[]{:S(2)}) %collective-permute-start.6) | collective-permute-done | bytes 28704 | tf_op jit(solution)/shard_map/ppermute | solution.py:559
  19.4 1.4 %finish.1 = f32[27,4,8,128]{3,2,1,0:T(8,128)} custom-call(f32[3920,128]{1,0:T(8,128)S(1)} %get-tuple-element.26.full, f32[27,72,128]{2,1,0:T(8,128)S(1)} %block.1, f32[144,128]{1,0:T(8,128)S(1)} %get-tuple-element.27.columns, f32[56,128]{1,0:T(8,128)S(1)} %collective-permute-done.6.x_one.x_two, f32[56,128]{1,0:T(8,128)S(1)} %collective-permute-done.6.x_one.x_two), custom_call_target="tpu_custom_call" | custom-call | tf_op jit(solution)/shard_map/finish/pallas_call | solution.py:660
  (1 shorter events, 0.0 us)
Async XLA Ops:
  1.4 8.7 %collective-permute-start = (f32[136,128]{1,0:T(8,128)S(1)}, f32[136,128]{1,0:T(8,128)S(1)}, u32[]{:S(2)}, u32[]{:S(2)}) collective-permute-start(f32[136,128]{1,0:T(8,128)S(1)} %get-tuple-element.18), channel_id=1, source_target_pairs={{0,4},{8,12},{4,0},{12,8},{5,9},{13,1},{9,5},{1,13},{2,6},{10,14},... | collective-permute-start | bytes 208904 | tf_op jit(solution)/shard_map/ppermute | solution.py:569
  5.6 4.5 %collective-permute-start.1 = (f32[136,128]{1,0:T(8,128)S(1)}, f32[136,128]{1,0:T(8,128)S(1)}, u32[]{:S(2)}, u32[]{:S(2)}) collective-permute-start(f32[136,128]{1,0:T(8,128)S(1)} %get-tuple-element.19), channel_id=1, source_target_pairs={{4,8},{12,0},{8,4},{0,12},{1,5},{9,13},{5,1},{13,9},{6,10},{14,2},... | collective-permute-start | bytes 208904 | tf_op jit(solution)/shard_map/ppermute | solution.py:569
  5.6 8.2 %collective-permute-start.2 = (f32[312,128]{1,0:T(8,128)S(1)}, f32[312,128]{1,0:T(8,128)S(1)}, u32[]{:S(2)}, u32[]{:S(2)}) collective-permute-start(f32[312,128]{1,0:T(8,128)S(1)} %get-tuple-element.20), channel_id=1, source_target_pairs={{1,2},{2,1},{5,6},{6,5},{9,10},{10,9},{13,14},{14,13},{17,18},{18,... | collective-permute-start | bytes 479240 | tf_op jit(solution)/shard_map/ppermute | solution.py:559
  10.0 3.8 %collective-permute-start.3 = (f32[312,128]{1,0:T(8,128)S(1)}, f32[312,128]{1,0:T(8,128)S(1)}, u32[]{:S(2)}, u32[]{:S(2)}) collective-permute-start(f32[312,128]{1,0:T(8,128)S(1)} %get-tuple-element.21), channel_id=1, source_target_pairs={{0,1},{2,3},{1,0},{3,2},{4,5},{6,7},{5,4},{7,6},{8,9},{10,11},{9,8... | collective-permute-start | bytes 479240 | tf_op jit(solution)/shard_map/ppermute | solution.py:559
  10.3 4.2 %collective-permute-start.4 = (f32[104,128]{1,0:T(8,128)S(1)}, f32[104,128]{1,0:T(8,128)S(1)}, u32[]{:S(2)}, u32[]{:S(2)}) collective-permute-start(f32[104,128]{1,0:T(8,128)S(1)} %get-tuple-element.24), channel_id=1, source_target_pairs={{0,1},{2,3},{1,0},{3,2},{4,5},{6,7},{5,4},{7,6},{8,9},{10,11},{9,8... | collective-permute-start | bytes 159752 | tf_op jit(solution)/shard_map/ppermute | solution.py:559
  10.8 5.4 %collective-permute-start.5 = (f32[104,128]{1,0:T(8,128)S(1)}, f32[104,128]{1,0:T(8,128)S(1)}, u32[]{:S(2)}, u32[]{:S(2)}) collective-permute-start(f32[104,128]{1,0:T(8,128)S(1)} %get-tuple-element.25), channel_id=1, source_target_pairs={{1,2},{2,1},{5,6},{6,5},{9,10},{10,9},{13,14},{14,13},{17,18},{18,... | collective-permute-start | bytes 159752 | tf_op jit(solution)/shard_map/ppermute | solution.py:559
  16.6 2.8 %collective-permute-start.6 = (f32[56,128]{1,0:T(8,128)S(1)}, f32[56,128]{1,0:T(8,128)S(1)}, u32[]{:S(2)}, u32[]{:S(2)}) collective-permute-start(f32[56,128]{1,0:T(8,128)S(1)} %get-tuple-element.28), channel_id=1, source_target_pairs={{0,16},{16,0},{1,17},{17,1},{2,18},{18,2},{3,19},{19,3},{4,20},{20... | collective-permute-start | bytes 86024 | tf_op jit(solution)/shard_map/ppermute | solution.py:559

commit v25 on v24

--- a/solution.py
+++ b/solution.py
@@ -390,7 +390,7 @@
             message[pl.ds(2 * c + 1, 1), :] = returned(c, 2, 3)
 
 
-def block_kernel(full, post, walls):
+def block_kernel(full, base, post, walls):
     top = lax.axis_index("gz") == lax.axis_size("gz") - 1
     sponge = (lax.axis_index("gx") * NX + lane_ids()) < SPONGE
     for t in range(ROWS // 8):
@@ -421,8 +421,21 @@
         for q in range(9):
             post[q, pl.ds((NZ + 1) * PITCH, PITCH), :] = post[q + 18, pl.ds(NZ * PITCH, PITCH), :]
 
-
-def last_kernel(full, block, columns, x_one, x_two, out, west, east, column, walls, back, done, sems):
+    for z in range(NZ):
+        cell = (z + 1) * PITCH + 2
+        for q in range(27):
+            cx, cy, cz = VEL[q]
+            start = cell - PITCH * cz - cy
+            value = post[q, pl.ds(start, 8), :]
+            if cx:
+                value = pltpu.roll(value, cx % 128, 1)
+            if q != 13:
+                blocked = walls[cx + 1, pl.ds(PAD + PITCH + start, 8), :] != 0.0
+                value = jnp.where(blocked, post[26 - q, pl.ds(cell, 8), :], value)
+            base[q, z] = value
+
+
+def last_kernel(full, base, columns, x_one, x_two, out, west, east, column, walls, back, done, sems):
     here_x, size_x = lax.axis_index("gx"), lax.axis_size("gx")
     top = lax.axis_index("gz") == lax.axis_size("gz") - 1
     lanes, rows = lane_ids(), row_ids()
@@ -505,10 +518,9 @@
 
     rim = (lanes == 0) | (lanes == 127)
 
-    def rimmed(q, start):
+    def ends_at(q, start):
         k = q // 3
-        ends = column_at((8 * k + 5, 73 + 2 * k, 8 * k + 1)[q % 3], 0, PITCH + start)
-        return jnp.where(rim, ends, block[q, pl.ds(start, 8), :])
+        return column_at((8 * k + 5, 73 + 2 * k, 8 * k + 1)[q % 3], 0, PITCH + start)
 
     for u in range(UNITS):
         flags = full[pl.ds(WALL * ROWS + PAD + PITCH + 8 * u, 8), :]
@@ -526,16 +538,16 @@
         cell = cells[z]
         start = cell - PITCH * cz - cy
         if cx > 0:
-            side = column_at(8 * (q // 3) + 2, 0, PITCH + start)
-            value = jnp.where(lanes < 2, side, pltpu.roll(block[q, pl.ds(start, 8), :], 1, 1))
+            side, reach = column_at(8 * (q // 3) + 2, 0, PITCH + start), lanes < 2
         elif cx < 0:
-            side = column_at(8 * (q // 3) + 6, 126, PITCH + start)
-            value = jnp.where(lanes > 125, side, pltpu.roll(block[q, pl.ds(start, 8), :], 127, 1))
+            side, reach = column_at(8 * (q // 3) + 6, 126, PITCH + start), lanes > 125
         else:
-            value = rimmed(q, start)
+            side, reach = ends_at(q, start), rim
         if q != 13:
             blocked = walls[cx + 1, pl.ds(start, 8), :] != 0.0
-            value = jnp.where(blocked, rimmed(26 - q, cell), value)
+            side = jnp.where(blocked, ends_at(26 - q, cell), side)
+            reach = (blocked & rim) | (jnp.logical_not(blocked) & reach)
+        value = jnp.where(reach, side, base[q, z])
         return jnp.where(solids[z], WEIGHT[q], value)
 
     copies = []
@@ -645,12 +657,12 @@
     )(part, packed, z_one, z_two)
     x_one = swap(message, "gx", 0, True)
     x_two = x_one if lax.axis_size("gx") == 2 else swap(message, "gx", 1, True)
-    block = pl.pallas_call(
+    base = pl.pallas_call(
         block_kernel,
-        out_shape=shape(27, UNITS * 8, 128),
+        out_shape=shape(27, NZ, NY, NX),
         in_specs=[VMEM],
         out_specs=VMEM,
-        scratch_shapes=[pltpu.VMEM((3, ROWS, 128), F32)],
+        scratch_shapes=[pltpu.VMEM((27, UNITS * 8, 128), F32), pltpu.VMEM((3, ROWS, 128), F32)],
         compiler_params=PARAMS,
         cost_estimate=pl.CostEstimate(
             flops=27 * 20 * UNITS * 1024, bytes_accessed=2**22, transcendentals=0
@@ -673,7 +685,7 @@
         ],
         compiler_params=PARAMS,
         name="finish",
-    )(full, block, columns, x_one, x_two)
+    )(full, base, columns, x_one, x_two)
 
 
 def solution(mesh):

time: 21 us -> 21 us (level)
  no operation moved by 1% of the time
where the time goes in v25:
time: 21 us; the launch traced here: 20.8 us
  starting transfers between devices  13.6 us (65%)
  Pallas kernels  4.7 us (22%)
  waiting for transfers between devices  2.46 us (12%)
    ppermute x5, starting transfers between devices, swap(): return lax.ppermute(value, axis, pairs(lax.axis_size(axis), turn, wrap))  9.35 us
    ppermute x2, starting transfers between devices, swap_mixed(): return lax.ppermute(value, ('gy', 'gz'), moves)  4.22 us
    ppermute x5, waiting for transfers between devices, swap(): return lax.ppermute(value, axis, pairs(lax.axis_size(axis), turn, wrap))  2.46 us
    pallas_call x1, Pallas kernels, shards(): pl.pallas_call(last_kernel, out_shape=shape(27, NZ, NY, NX), in_specs=[VM...  1.45 us
    pallas_call x1, Pallas kernels, shards(): pl.pallas_call(first_kernel, out_shape=[shape(CHANNELS * NZ * 8, 128), sh...  1.37 us
    pallas_call x1, Pallas kernels, shards(): pl.pallas_call(block_kernel, out_shape=shape(27, NZ, NY, NX), in_specs=[V...  0.83 us
    pallas_call x1, Pallas kernels, shards(): pl.pallas_call(fill_kernel, out_shape=[shape(SLABS * ROWS, 128), shape(12...  0.57 us
  transfers between devices with their start and end apart: 7, of which 2 were waited for; matrix products, arithmetic and copies ran while one was open for 0% of the time, Pallas kernels for 7%

profile of v25, /device:TPU:1, one launch (start us, length us, event | category | flops | bytes accessed | tf_op | source)
XLA Modules:
  0.0 20.8 jit_solution(11161683108021810278)
XLA Ops:
  0.0 1.4 %collide.1 = (f32[928,128]{1,0:T(8,128)S(1)}, f32[136,128]{1,0:T(8,128)S(1)}, f32[136,128]{1,0:T(8,128)S(1)}) custom-call(f32[27,4,8,128]{3,2,1,0:T(8,128)} %pops_at.1, s32[4,8,128]{2,1,0:T(8,128)} %solid_at.1, f32[4,8]{1,0:T(4,128)} %bitcast.1, s32[8]{0:T(128)} %index_at.1), custom_call_target="tpu_custom_call" | custom-call | tf_op jit(solution)/shard_map/collide/pallas_call | solution.py:589
  1.4 4.2 %collective-permute-start = (f32[136,128]{1,0:T(8,128)S(1)}, f32[136,128]{1,0:T(8,128)S(1)}, u32[]{:S(2)}, u32[]{:S(2)}) collective-permute-start(f32[136,128]{1,0:T(8,128)S(1)} %get-tuple-element.18), channel_id=1, source_target_pairs={{0,4},{8,12},{4,0},{12,8},{5,9},{13,1},{9,5},{1,13},{2,6},{10,14},... | collective-permute-start | bytes 208904 | tf_op jit(solution)/shard_map/ppermute | solution.py:581
  5.6 0.0 collective-permute-start.1
  5.6 4.4 %collective-permute-start.2 = (f32[312,128]{1,0:T(8,128)S(1)}, f32[312,128]{1,0:T(8,128)S(1)}, u32[]{:S(2)}, u32[]{:S(2)}) collective-permute-start(f32[312,128]{1,0:T(8,128)S(1)} %get-tuple-element.20), channel_id=1, source_target_pairs={{1,2},{2,1},{5,6},{6,5},{9,10},{10,9},{13,14},{14,13},{17,18},{18,... | collective-permute-start | bytes 479240 | tf_op jit(solution)/shard_map/ppermute | solution.py:571
  10.0 0.1 collective-permute-start.3
  10.1 0.0 collective-permute-done.y_first
  10.1 0.0 collective-permute-done.1.y_second
  10.1 0.1 pack_z.1
  10.3 0.5 %collective-permute-start.4 = (f32[104,128]{1,0:T(8,128)S(1)}, f32[104,128]{1,0:T(8,128)S(1)}, u32[]{:S(2)}, u32[]{:S(2)}) collective-permute-start(f32[104,128]{1,0:T(8,128)S(1)} %get-tuple-element.24), channel_id=1, source_target_pairs={{0,1},{2,3},{1,0},{3,2},{4,5},{6,7},{5,4},{7,6},{8,9},{10,11},{9,8... | collective-permute-start | bytes 159752 | tf_op jit(solution)/shard_map/ppermute | solution.py:571
  10.8 3.0 %collective-permute-start.5 = (f32[104,128]{1,0:T(8,128)S(1)}, f32[104,128]{1,0:T(8,128)S(1)}, u32[]{:S(2)}, u32[]{:S(2)}) collective-permute-start(f32[104,128]{1,0:T(8,128)S(1)} %get-tuple-element.25), channel_id=1, source_target_pairs={{1,2},{2,1},{5,6},{6,5},{9,10},{10,9},{13,14},{14,13},{17,18},{18,... | collective-permute-start | bytes 159752 | tf_op jit(solution)/shard_map/ppermute | solution.py:571
  13.8 0.0 collective-permute-done.2.two
  13.8 0.0 collective-permute-done.3.one
  13.8 0.6 %fill.1 = (f32[3920,128]{1,0:T(8,128)S(1)}, f32[128,128]{1,0:T(8,128)S(1)}) custom-call(f32[928,128]{1,0:T(8,128)S(1)} %get-tuple-element.17.own, f32[136,128]{1,0:T(8,128)S(1)} %collective-permute-done.y_first, f32[136,128]{1,0:T(8,128)S(1)} %collective-permute-done.1.y_second, f32[312,128]{1,0:T(8,128)S(1)} %collective-permute-done.2.two, ...), custom_call_target="tpu_custom_call" | custom-call | flops 1000000 | bytes 4194304 | tf_op jit(solution)/shard_map/fill/pallas_call | solution.py:633
  14.4 0.0 collective-permute-done.4.z_one
  14.4 1.8 %collective-permute-done.5.z_two = f32[104,128]{1,0:T(8,128)S(1)} collective-permute-done((f32[104,128]{1,0:T(8,128)S(1)}, f32[104,128]{1,0:T(8,128)S(1)}, u32[]{:S(2)}, u32[]{:S(2)}) %collective-permute-start.5) | collective-permute-done | bytes 53280 | tf_op jit(solution)/shard_map/ppermute | solution.py:571
  16.2 0.3 %pack_x.1 = (f32[3920,128]{1,0:T(8,128)S(1)}, f32[128,128]{1,0:T(8,128)S(1)}, f32[144,128]{1,0:T(8,128)S(1)}, f32[56,128]{1,0:T(8,128)S(1)}) custom-call(f32[3920,128]{1,0:T(8,128)S(1)} %get-tuple-element.22.part, f32[128,128]{1,0:T(8,128)S(1)} %get-tuple-element.23.packed, ...), custom_call_target="tpu_custom_call", output_to_operand_aliasing={{0}: (0, {}), {1}: (1, {})} | custom-call | tf_op jit(solution)/shard_map/pack_x/pallas_call | solution.py:643
  16.6 1.3 %collective-permute-start.6 = (f32[56,128]{1,0:T(8,128)S(1)}, f32[56,128]{1,0:T(8,128)S(1)}, u32[]{:S(2)}, u32[]{:S(2)}) collective-permute-start(f32[56,128]{1,0:T(8,128)S(1)} %get-tuple-element.28), channel_id=1, source_target_pairs={{0,16},{16,0},{1,17},{17,1},{2,18},{18,2},{3,19},{19,3},{4,20},{20... | collective-permute-start | bytes 86024 | tf_op jit(solution)/shard_map/ppermute | solution.py:571
  17.9 0.8 %block.1.base = f32[27,4,8,128]{3,2,1,0:T(8,128)S(1)} custom-call(f32[3920,128]{1,0:T(8,128)S(1)} %get-tuple-element.26.full), custom_call_target="tpu_custom_call" | custom-call | flops 4976640 | bytes 4194304 | tf_op jit(solution)/shard_map/block/pallas_call | solution.py:660
  18.7 0.6 %collective-permute-done.6.x_one.x_two = f32[56,128]{1,0:T(8,128)S(1)} collective-permute-done((f32[56,128]{1,0:T(8,128)S(1)}, f32[56,128]{1,0:T(8,128)S(1)}, u32[]{:S(2)}, u32[]{:S(2)}) %collective-permute-start.6) | collective-permute-done | bytes 28704 | tf_op jit(solution)/shard_map/ppermute | solution.py:571
  19.4 1.5 %finish.1 = f32[27,4,8,128]{3,2,1,0:T(8,128)} custom-call(f32[3920,128]{1,0:T(8,128)S(1)} %get-tuple-element.26.full, f32[27,4,8,128]{3,2,1,0:T(8,128)S(1)} %block.1.base, f32[144,128]{1,0:T(8,128)S(1)} %get-tuple-element.27.columns, f32[56,128]{1,0:T(8,128)S(1)} %collective-permute-done.6.x_one.x_two, f32[56,128]{1,0:T(8,128)S(1)} %collective-permute-done.6.x_one.x_two), custom_call_target="tpu_custom_call" | custom-call | tf_op jit(solution)/shard_map/finish/pallas_call | solution.py:672
  (1 shorter events, 0.0 us)
Async XLA Ops:
  1.4 8.7 %collective-permute-start = (f32[136,128]{1,0:T(8,128)S(1)}, f32[136,128]{1,0:T(8,128)S(1)}, u32[]{:S(2)}, u32[]{:S(2)}) collective-permute-start(f32[136,128]{1,0:T(8,128)S(1)} %get-tuple-element.18), channel_id=1, source_target_pairs={{0,4},{8,12},{4,0},{12,8},{5,9},{13,1},{9,5},{1,13},{2,6},{10,14},... | collective-permute-start | bytes 208904 | tf_op jit(solution)/shard_map/ppermute | solution.py:581
  5.6 4.5 %collective-permute-start.1 = (f32[136,128]{1,0:T(8,128)S(1)}, f32[136,128]{1,0:T(8,128)S(1)}, u32[]{:S(2)}, u32[]{:S(2)}) collective-permute-start(f32[136,128]{1,0:T(8,128)S(1)} %get-tuple-element.19), channel_id=1, source_target_pairs={{4,8},{12,0},{8,4},{0,12},{1,5},{9,13},{5,1},{13,9},{6,10},{14,2},... | collective-permute-start | bytes 208904 | tf_op jit(solution)/shard_map/ppermute | solution.py:581
  5.6 8.2 %collective-permute-start.2 = (f32[312,128]{1,0:T(8,128)S(1)}, f32[312,128]{1,0:T(8,128)S(1)}, u32[]{:S(2)}, u32[]{:S(2)}) collective-permute-start(f32[312,128]{1,0:T(8,128)S(1)} %get-tuple-element.20), channel_id=1, source_target_pairs={{1,2},{2,1},{5,6},{6,5},{9,10},{10,9},{13,14},{14,13},{17,18},{18,... | collective-permute-start | bytes 479240 | tf_op jit(solution)/shard_map/ppermute | solution.py:571
  10.0 3.8 %collective-permute-start.3 = (f32[312,128]{1,0:T(8,128)S(1)}, f32[312,128]{1,0:T(8,128)S(1)}, u32[]{:S(2)}, u32[]{:S(2)}) collective-permute-start(f32[312,128]{1,0:T(8,128)S(1)} %get-tuple-element.21), channel_id=1, source_target_pairs={{0,1},{2,3},{1,0},{3,2},{4,5},{6,7},{5,4},{7,6},{8,9},{10,11},{9,8... | collective-permute-start | bytes 479240 | tf_op jit(solution)/shard_map/ppermute | solution.py:571
  10.3 4.2 %collective-permute-start.4 = (f32[104,128]{1,0:T(8,128)S(1)}, f32[104,128]{1,0:T(8,128)S(1)}, u32[]{:S(2)}, u32[]{:S(2)}) collective-permute-start(f32[104,128]{1,0:T(8,128)S(1)} %get-tuple-element.24), channel_id=1, source_target_pairs={{0,1},{2,3},{1,0},{3,2},{4,5},{6,7},{5,4},{7,6},{8,9},{10,11},{9,8... | collective-permute-start | bytes 159752 | tf_op jit(solution)/shard_map/ppermute | solution.py:571
  10.8 5.4 %collective-permute-start.5 = (f32[104,128]{1,0:T(8,128)S(1)}, f32[104,128]{1,0:T(8,128)S(1)}, u32[]{:S(2)}, u32[]{:S(2)}) collective-permute-start(f32[104,128]{1,0:T(8,128)S(1)} %get-tuple-element.25), channel_id=1, source_target_pairs={{1,2},{2,1},{5,6},{6,5},{9,10},{10,9},{13,14},{14,13},{17,18},{18,... | collective-permute-start | bytes 159752 | tf_op jit(solution)/shard_map/ppermute | solution.py:571
  16.6 2.8 %collective-permute-start.6 = (f32[56,128]{1,0:T(8,128)S(1)}, f32[56,128]{1,0:T(8,128)S(1)}, u32[]{:S(2)}, u32[]{:S(2)}) collective-permute-start(f32[56,128]{1,0:T(8,128)S(1)} %get-tuple-element.28), channel_id=1, source_target_pairs={{0,16},{16,0},{1,17},{17,1},{2,18},{18,2},{3,19},{19,3},{4,20},{20... | collective-permute-start | bytes 86024 | tf_op jit(solution)/shard_map/ppermute | solution.py:571

commit v26 on v24

--- a/solution.py
+++ b/solution.py
@@ -476,9 +476,6 @@
     place = here_x * NX + jnp.where(rows < 4, rows - 2, rows + (NX - 6))
     place = lax.rem(place + size_x * NX, size_x * NX)
     sides = relaxed(moved, place < SPONGE, strip[AIM])
-    lid = top & (lanes >= (NZ + 2) * PITCH) & (lanes < (NZ + 3) * PITCH)
-    for q in range(9):
-        sides[q] = jnp.where(lid, pltpu.roll(sides[q + 18], PITCH, 1), sides[q])
     for q, side in enumerate(sides + [strip[WALL]]):
         column[pl.ds(PAD + 8 * q, 8), :] = side
 
@@ -505,9 +502,15 @@
 
     rim = (lanes == 0) | (lanes == 127)
 
-    def rimmed(q, start):
-        k = q // 3
-        ends = column_at((8 * k + 5, 73 + 2 * k, 8 * k + 1)[q % 3], 0, PITCH + start)
+    def edge_of(q, z, start, base, lane):
+        place = 72 + 2 * (q // 3) + base if q % 3 == 1 else 8 * (q // 3) + base
+        value = column_at(place, lane, PITCH + start)
+        if z == NZ - 1 and VEL[q][2] < 0:
+            value = jnp.where(top, column_at(place + (12 if q % 3 == 1 else 48), lane, start), value)
+        return value
+
+    def rimmed(q, z, start):
+        ends = edge_of(q, z, start, (5, 1, 1)[q % 3], 0)
         return jnp.where(rim, ends, block[q, pl.ds(start, 8), :])
 
     for u in range(UNITS):
@@ -526,16 +529,16 @@
         cell = cells[z]
         start = cell - PITCH * cz - cy
         if cx > 0:
-            side = column_at(8 * (q // 3) + 2, 0, PITCH + start)
+            side = edge_of(q, z, start, 2, 0)
             value = jnp.where(lanes < 2, side, pltpu.roll(block[q, pl.ds(start, 8), :], 1, 1))
         elif cx < 0:
-            side = column_at(8 * (q // 3) + 6, 126, PITCH + start)
+            side = edge_of(q, z, start, 6, 126)
             value = jnp.where(lanes > 125, side, pltpu.roll(block[q, pl.ds(start, 8), :], 127, 1))
         else:
-            value = rimmed(q, start)
+            value = rimmed(q, z, start)
         if q != 13:
             blocked = walls[cx + 1, pl.ds(start, 8), :] != 0.0
-            value = jnp.where(blocked, rimmed(26 - q, cell), value)
+            value = jnp.where(blocked, rimmed(26 - q, None, cell), value)
         return jnp.where(solids[z], WEIGHT[q], value)
 
     copies = []

time: 21 us -> 20.9 us (level)
  no operation moved by 1% of the time
where the time goes in v26:
time: 20.9 us; the launch traced here: 20.7 us
  starting transfers between devices  13.6 us (65%)
  Pallas kernels  4.48 us (21%)
  waiting for transfers between devices  2.57 us (12%)
    ppermute x5, starting transfers between devices, swap(): return lax.ppermute(value, axis, pairs(lax.axis_size(axis), turn, wrap))  9.35 us
    ppermute x2, starting transfers between devices, swap_mixed(): return lax.ppermute(value, ('gy', 'gz'), moves)  4.22 us
    ppermute x5, waiting for transfers between devices, swap(): return lax.ppermute(value, axis, pairs(lax.axis_size(axis), turn, wrap))  2.57 us
    pallas_call x1, Pallas kernels, shards(): pl.pallas_call(first_kernel, out_shape=[shape(CHANNELS * NZ * 8, 128), sh...  1.37 us
    pallas_call x1, Pallas kernels, shards(): pl.pallas_call(last_kernel, out_shape=shape(27, NZ, NY, NX), in_specs=[VM...  1.34 us
    pallas_call x1, Pallas kernels, shards(): pl.pallas_call(block_kernel, out_shape=shape(27, UNITS * 8, 128), in_spec...  0.72 us
    pallas_call x1, Pallas kernels, shards(): pl.pallas_call(fill_kernel, out_shape=[shape(SLABS * ROWS, 128), shape(12...  0.57 us
  transfers between devices with their start and end apart: 7, of which 2 were waited for; matrix products, arithmetic and copies ran while one was open for 0% of the time, Pallas kernels for 7%

profile of v26, /device:TPU:1, one launch (start us, length us, event | category | flops | bytes accessed | tf_op | source)
XLA Modules:
  0.0 20.7 jit_solution(8727268563695425330)
XLA Ops:
  0.0 1.4 %collide.1 = (f32[928,128]{1,0:T(8,128)S(1)}, f32[136,128]{1,0:T(8,128)S(1)}, f32[136,128]{1,0:T(8,128)S(1)}) custom-call(f32[27,4,8,128]{3,2,1,0:T(8,128)} %pops_at.1, s32[4,8,128]{2,1,0:T(8,128)} %solid_at.1, f32[4,8]{1,0:T(4,128)} %bitcast.1, s32[8]{0:T(128)} %index_at.1), custom_call_target="tpu_custom_call" | custom-call | tf_op jit(solution)/shard_map/collide/pallas_call | solution.py:580
  1.4 4.2 %collective-permute-start = (f32[136,128]{1,0:T(8,128)S(1)}, f32[136,128]{1,0:T(8,128)S(1)}, u32[]{:S(2)}, u32[]{:S(2)}) collective-permute-start(f32[136,128]{1,0:T(8,128)S(1)} %get-tuple-element.18), channel_id=1, source_target_pairs={{0,4},{8,12},{4,0},{12,8},{5,9},{13,1},{9,5},{1,13},{2,6},{10,14},... | collective-permute-start | bytes 208904 | tf_op jit(solution)/shard_map/ppermute | solution.py:572
  5.6 0.0 collective-permute-start.1
  5.6 4.4 %collective-permute-start.2 = (f32[312,128]{1,0:T(8,128)S(1)}, f32[312,128]{1,0:T(8,128)S(1)}, u32[]{:S(2)}, u32[]{:S(2)}) collective-permute-start(f32[312,128]{1,0:T(8,128)S(1)} %get-tuple-element.20), channel_id=1, source_target_pairs={{1,2},{2,1},{5,6},{6,5},{9,10},{10,9},{13,14},{14,13},{17,18},{18,... | collective-permute-start | bytes 479240 | tf_op jit(solution)/shard_map/ppermute | solution.py:562
  10.0 0.1 collective-permute-start.3
  10.1 0.0 collective-permute-done.y_first
  10.1 0.0 collective-permute-done.1.y_second
  10.1 0.1 pack_z.1
  10.3 0.5 %collective-permute-start.4 = (f32[104,128]{1,0:T(8,128)S(1)}, f32[104,128]{1,0:T(8,128)S(1)}, u32[]{:S(2)}, u32[]{:S(2)}) collective-permute-start(f32[104,128]{1,0:T(8,128)S(1)} %get-tuple-element.24), channel_id=1, source_target_pairs={{0,1},{2,3},{1,0},{3,2},{4,5},{6,7},{5,4},{7,6},{8,9},{10,11},{9,8... | collective-permute-start | bytes 159752 | tf_op jit(solution)/shard_map/ppermute | solution.py:562
  10.8 3.0 %collective-permute-start.5 = (f32[104,128]{1,0:T(8,128)S(1)}, f32[104,128]{1,0:T(8,128)S(1)}, u32[]{:S(2)}, u32[]{:S(2)}) collective-permute-start(f32[104,128]{1,0:T(8,128)S(1)} %get-tuple-element.25), channel_id=1, source_target_pairs={{1,2},{2,1},{5,6},{6,5},{9,10},{10,9},{13,14},{14,13},{17,18},{18,... | collective-permute-start | bytes 159752 | tf_op jit(solution)/shard_map/ppermute | solution.py:562
  13.8 0.0 collective-permute-done.2.two
  13.8 0.0 collective-permute-done.3.one
  13.8 0.6 %fill.1 = (f32[3920,128]{1,0:T(8,128)S(1)}, f32[128,128]{1,0:T(8,128)S(1)}) custom-call(f32[928,128]{1,0:T(8,128)S(1)} %get-tuple-element.17.own, f32[136,128]{1,0:T(8,128)S(1)} %collective-permute-done.y_first, f32[136,128]{1,0:T(8,128)S(1)} %collective-permute-done.1.y_second, f32[312,128]{1,0:T(8,128)S(1)} %collective-permute-done.2.two, ...), custom_call_target="tpu_custom_call" | custom-call | flops 1000000 | bytes 4194304 | tf_op jit(solution)/shard_map/fill/pallas_call | solution.py:624
  14.4 0.0 collective-permute-done.4.z_one
  14.4 1.8 %collective-permute-done.5.z_two = f32[104,128]{1,0:T(8,128)S(1)} collective-permute-done((f32[104,128]{1,0:T(8,128)S(1)}, f32[104,128]{1,0:T(8,128)S(1)}, u32[]{:S(2)}, u32[]{:S(2)}) %collective-permute-start.5) | collective-permute-done | bytes 53280 | tf_op jit(solution)/shard_map/ppermute | solution.py:562
  16.2 0.3 %pack_x.1 = (f32[3920,128]{1,0:T(8,128)S(1)}, f32[128,128]{1,0:T(8,128)S(1)}, f32[144,128]{1,0:T(8,128)S(1)}, f32[56,128]{1,0:T(8,128)S(1)}) custom-call(f32[3920,128]{1,0:T(8,128)S(1)} %get-tuple-element.22.part, f32[128,128]{1,0:T(8,128)S(1)} %get-tuple-element.23.packed, ...), custom_call_target="tpu_custom_call", output_to_operand_aliasing={{0}: (0, {}), {1}: (1, {})} | custom-call | tf_op jit(solution)/shard_map/pack_x/pallas_call | solution.py:634
  16.6 1.3 %collective-permute-start.6 = (f32[56,128]{1,0:T(8,128)S(1)}, f32[56,128]{1,0:T(8,128)S(1)}, u32[]{:S(2)}, u32[]{:S(2)}) collective-permute-start(f32[56,128]{1,0:T(8,128)S(1)} %get-tuple-element.28), channel_id=1, source_target_pairs={{0,16},{16,0},{1,17},{17,1},{2,18},{18,2},{3,19},{19,3},{4,20},{20... | collective-permute-start | bytes 86024 | tf_op jit(solution)/shard_map/ppermute | solution.py:562
  17.9 0.7 %block.1 = f32[27,72,128]{2,1,0:T(8,128)S(1)} custom-call(f32[3920,128]{1,0:T(8,128)S(1)} %get-tuple-element.26.full), custom_call_target="tpu_custom_call" | custom-call | flops 4976640 | bytes 4194304 | tf_op jit(solution)/shard_map/block/pallas_call | solution.py:651
  18.6 0.8 %collective-permute-done.6.x_one.x_two = f32[56,128]{1,0:T(8,128)S(1)} collective-permute-done((f32[56,128]{1,0:T(8,128)S(1)}, f32[56,128]{1,0:T(8,128)S(1)}, u32[]{:S(2)}, u32[]{:S(2)}) %collective-permute-start.6) | collective-permute-done | bytes 28704 | tf_op jit(solution)/shard_map/ppermute | solution.py:562
  19.4 1.3 %finish.1 = f32[27,4,8,128]{3,2,1,0:T(8,128)} custom-call(f32[3920,128]{1,0:T(8,128)S(1)} %get-tuple-element.26.full, f32[27,72,128]{2,1,0:T(8,128)S(1)} %block.1, f32[144,128]{1,0:T(8,128)S(1)} %get-tuple-element.27.columns, f32[56,128]{1,0:T(8,128)S(1)} %collective-permute-done.6.x_one.x_two, f32[56,128]{1,0:T(8,128)S(1)} %collective-permute-done.6.x_one.x_two), custom_call_target="tpu_custom_call" | custom-call | tf_op jit(solution)/shard_map/finish/pallas_call | solution.py:663
  (1 shorter events, 0.0 us)
Async XLA Ops:
  1.4 8.7 %collective-permute-start = (f32[136,128]{1,0:T(8,128)S(1)}, f32[136,128]{1,0:T(8,128)S(1)}, u32[]{:S(2)}, u32[]{:S(2)}) collective-permute-start(f32[136,128]{1,0:T(8,128)S(1)} %get-tuple-element.18), channel_id=1, source_target_pairs={{0,4},{8,12},{4,0},{12,8},{5,9},{13,1},{9,5},{1,13},{2,6},{10,14},... | collective-permute-start | bytes 208904 | tf_op jit(solution)/shard_map/ppermute | solution.py:572
  5.6 4.5 %collective-permute-start.1 = (f32[136,128]{1,0:T(8,128)S(1)}, f32[136,128]{1,0:T(8,128)S(1)}, u32[]{:S(2)}, u32[]{:S(2)}) collective-permute-start(f32[136,128]{1,0:T(8,128)S(1)} %get-tuple-element.19), channel_id=1, source_target_pairs={{4,8},{12,0},{8,4},{0,12},{1,5},{9,13},{5,1},{13,9},{6,10},{14,2},... | collective-permute-start | bytes 208904 | tf_op jit(solution)/shard_map/ppermute | solution.py:572
  5.6 8.2 %collective-permute-start.2 = (f32[312,128]{1,0:T(8,128)S(1)}, f32[312,128]{1,0:T(8,128)S(1)}, u32[]{:S(2)}, u32[]{:S(2)}) collective-permute-start(f32[312,128]{1,0:T(8,128)S(1)} %get-tuple-element.20), channel_id=1, source_target_pairs={{1,2},{2,1},{5,6},{6,5},{9,10},{10,9},{13,14},{14,13},{17,18},{18,... | collective-permute-start | bytes 479240 | tf_op jit(solution)/shard_map/ppermute | solution.py:562
  10.0 3.8 %collective-permute-start.3 = (f32[312,128]{1,0:T(8,128)S(1)}, f32[312,128]{1,0:T(8,128)S(1)}, u32[]{:S(2)}, u32[]{:S(2)}) collective-permute-start(f32[312,128]{1,0:T(8,128)S(1)} %get-tuple-element.21), channel_id=1, source_target_pairs={{0,1},{2,3},{1,0},{3,2},{4,5},{6,7},{5,4},{7,6},{8,9},{10,11},{9,8... | collective-permute-start | bytes 479240 | tf_op jit(solution)/shard_map/ppermute | solution.py:562
  10.3 4.2 %collective-permute-start.4 = (f32[104,128]{1,0:T(8,128)S(1)}, f32[104,128]{1,0:T(8,128)S(1)}, u32[]{:S(2)}, u32[]{:S(2)}) collective-permute-start(f32[104,128]{1,0:T(8,128)S(1)} %get-tuple-element.24), channel_id=1, source_target_pairs={{0,1},{2,3},{1,0},{3,2},{4,5},{6,7},{5,4},{7,6},{8,9},{10,11},{9,8... | collective-permute-start | bytes 159752 | tf_op jit(solution)/shard_map/ppermute | solution.py:562
  10.8 5.4 %collective-permute-start.5 = (f32[104,128]{1,0:T(8,128)S(1)}, f32[104,128]{1,0:T(8,128)S(1)}, u32[]{:S(2)}, u32[]{:S(2)}) collective-permute-start(f32[104,128]{1,0:T(8,128)S(1)} %get-tuple-element.25), channel_id=1, source_target_pairs={{1,2},{2,1},{5,6},{6,5},{9,10},{10,9},{13,14},{14,13},{17,18},{18,... | collective-permute-start | bytes 159752 | tf_op jit(solution)/shard_map/ppermute | solution.py:562
  16.6 2.8 %collective-permute-start.6 = (f32[56,128]{1,0:T(8,128)S(1)}, f32[56,128]{1,0:T(8,128)S(1)}, u32[]{:S(2)}, u32[]{:S(2)}) collective-permute-start(f32[56,128]{1,0:T(8,128)S(1)} %get-tuple-element.28), channel_id=1, source_target_pairs={{0,16},{16,0},{1,17},{17,1},{2,18},{18,2},{3,19},{19,3},{4,20},{20... | collective-permute-start | bytes 86024 | tf_op jit(solution)/shard_map/ppermute | solution.py:562

commit v27 on v26

--- a/solution.py
+++ b/solution.py
@@ -327,11 +327,20 @@
 def pack_rim(full, pack, first):
     slot, rows = lane_ids() // 4, row_ids()
     parts = (rows < 2, (rows >= 2) & (rows < 6), rows >= 6)
-    packed = jnp.zeros((8, 128), F32)
-    for c in range(CHANNELS):
-        a, b, d = (full[pl.ds(c * ROWS + PAD + 8 * (first + t), 8), :] for t in range(3))
-        rim = jnp.where(parts[0], a, jnp.where(parts[1], b, d))
-        packed = jnp.where(slot == c, pltpu.roll(rim, (4 * c + 2) % 128, 1), packed)
+    chains = []
+    for base in range(0, CHANNELS, 8):
+        chain = None
+        for c in range(base, min(base + 8, CHANNELS)):
+            a, b, d = (full[pl.ds(c * ROWS + PAD + 8 * (first + t), 8), :] for t in range(3))
+            rim = jnp.where(parts[0], a, jnp.where(parts[1], b, d))
+            moved = pltpu.roll(rim, (4 * c + 2) % 128, 1)
+            chain = moved if chain is None else jnp.where(slot == c, moved, chain)
+        chains.append(chain)
+    packed = jnp.where(
+        slot < 16,
+        jnp.where(slot < 8, chains[0], chains[1]),
+        jnp.where(slot < 24, chains[2], chains[3]),
+    )
     for t, part in enumerate(parts):
         tile = pl.ds(8 * (first + t), 8)
         pack[tile, :] = jnp.where(part, packed, pack[tile, :])

time: 20.9 us -> 20.9 us (level)
  no operation moved by 1% of the time
where the time goes in v27:
time: 20.9 us; the launch traced here: 20.7 us
  starting transfers between devices  13.6 us (65%)
  Pallas kernels  4.48 us (21%)
  waiting for transfers between devices  2.57 us (12%)
    ppermute x5, starting transfers between devices, swap(): return lax.ppermute(value, axis, pairs(lax.axis_size(axis), turn, wrap))  9.35 us
    ppermute x2, starting transfers between devices, swap_mixed(): return lax.ppermute(value, ('gy', 'gz'), moves)  4.22 us
    ppermute x5, waiting for transfers between devices, swap(): return lax.ppermute(value, axis, pairs(lax.axis_size(axis), turn, wrap))  2.57 us
    pallas_call x1, Pallas kernels, shards(): pl.pallas_call(first_kernel, out_shape=[shape(CHANNELS * NZ * 8, 128), sh...  1.37 us
    pallas_call x1, Pallas kernels, shards(): pl.pallas_call(last_kernel, out_shape=shape(27, NZ, NY, NX), in_specs=[VM...  1.34 us
    pallas_call x1, Pallas kernels, shards(): pl.pallas_call(block_kernel, out_shape=shape(27, UNITS * 8, 128), in_spec...  0.72 us
    pallas_call x1, Pallas kernels, shards(): pl.pallas_call(fill_kernel, out_shape=[shape(SLABS * ROWS, 128), shape(12...  0.57 us
  transfers between devices with their start and end apart: 7, of which 2 were waited for; matrix products, arithmetic and copies ran while one was open for 0% of the time, Pallas kernels for 7%

profile of v27, /device:TPU:1, one launch (start us, length us, event | category | flops | bytes accessed | tf_op | source)
XLA Modules:
  0.0 20.7 jit_solution(17126475811849972061)
XLA Ops:
  0.0 1.4 %collide.1 = (f32[928,128]{1,0:T(8,128)S(1)}, f32[136,128]{1,0:T(8,128)S(1)}, f32[136,128]{1,0:T(8,128)S(1)}) custom-call(f32[27,4,8,128]{3,2,1,0:T(8,128)} %pops_at.1, s32[4,8,128]{2,1,0:T(8,128)} %solid_at.1, f32[4,8]{1,0:T(4,128)} %bitcast.1, s32[8]{0:T(128)} %index_at.1), custom_call_target="tpu_custom_call" | custom-call | tf_op jit(solution)/shard_map/collide/pallas_call | solution.py:589
  1.4 4.2 %collective-permute-start = (f32[136,128]{1,0:T(8,128)S(1)}, f32[136,128]{1,0:T(8,128)S(1)}, u32[]{:S(2)}, u32[]{:S(2)}) collective-permute-start(f32[136,128]{1,0:T(8,128)S(1)} %get-tuple-element.18), channel_id=1, source_target_pairs={{0,4},{8,12},{4,0},{12,8},{5,9},{13,1},{9,5},{1,13},{2,6},{10,14},... | collective-permute-start | bytes 208904 | tf_op jit(solution)/shard_map/ppermute | solution.py:581
  5.6 0.0 collective-permute-start.1
  5.6 4.4 %collective-permute-start.2 = (f32[312,128]{1,0:T(8,128)S(1)}, f32[312,128]{1,0:T(8,128)S(1)}, u32[]{:S(2)}, u32[]{:S(2)}) collective-permute-start(f32[312,128]{1,0:T(8,128)S(1)} %get-tuple-element.20), channel_id=1, source_target_pairs={{1,2},{2,1},{5,6},{6,5},{9,10},{10,9},{13,14},{14,13},{17,18},{18,... | collective-permute-start | bytes 479240 | tf_op jit(solution)/shard_map/ppermute | solution.py:571
  10.0 0.1 collective-permute-start.3
  10.1 0.0 collective-permute-done.y_first
  10.1 0.0 collective-permute-done.1.y_second
  10.1 0.1 pack_z.1
  10.3 0.5 %collective-permute-start.4 = (f32[104,128]{1,0:T(8,128)S(1)}, f32[104,128]{1,0:T(8,128)S(1)}, u32[]{:S(2)}, u32[]{:S(2)}) collective-permute-start(f32[104,128]{1,0:T(8,128)S(1)} %get-tuple-element.24), channel_id=1, source_target_pairs={{0,1},{2,3},{1,0},{3,2},{4,5},{6,7},{5,4},{7,6},{8,9},{10,11},{9,8... | collective-permute-start | bytes 159752 | tf_op jit(solution)/shard_map/ppermute | solution.py:571
  10.8 3.0 %collective-permute-start.5 = (f32[104,128]{1,0:T(8,128)S(1)}, f32[104,128]{1,0:T(8,128)S(1)}, u32[]{:S(2)}, u32[]{:S(2)}) collective-permute-start(f32[104,128]{1,0:T(8,128)S(1)} %get-tuple-element.25), channel_id=1, source_target_pairs={{1,2},{2,1},{5,6},{6,5},{9,10},{10,9},{13,14},{14,13},{17,18},{18,... | collective-permute-start | bytes 159752 | tf_op jit(solution)/shard_map/ppermute | solution.py:571
  13.8 0.0 collective-permute-done.2.two
  13.8 0.0 collective-permute-done.3.one
  13.8 0.6 %fill.1 = (f32[3920,128]{1,0:T(8,128)S(1)}, f32[128,128]{1,0:T(8,128)S(1)}) custom-call(f32[928,128]{1,0:T(8,128)S(1)} %get-tuple-element.17.own, f32[136,128]{1,0:T(8,128)S(1)} %collective-permute-done.y_first, f32[136,128]{1,0:T(8,128)S(1)} %collective-permute-done.1.y_second, f32[312,128]{1,0:T(8,128)S(1)} %collective-permute-done.2.two, ...), custom_call_target="tpu_custom_call" | custom-call | flops 1000000 | bytes 4194304 | tf_op jit(solution)/shard_map/fill/pallas_call | solution.py:633
  14.4 0.0 collective-permute-done.4.z_one
  14.4 1.8 %collective-permute-done.5.z_two = f32[104,128]{1,0:T(8,128)S(1)} collective-permute-done((f32[104,128]{1,0:T(8,128)S(1)}, f32[104,128]{1,0:T(8,128)S(1)}, u32[]{:S(2)}, u32[]{:S(2)}) %collective-permute-start.5) | collective-permute-done | bytes 53280 | tf_op jit(solution)/shard_map/ppermute | solution.py:571
  16.2 0.3 %pack_x.1 = (f32[3920,128]{1,0:T(8,128)S(1)}, f32[128,128]{1,0:T(8,128)S(1)}, f32[144,128]{1,0:T(8,128)S(1)}, f32[56,128]{1,0:T(8,128)S(1)}) custom-call(f32[3920,128]{1,0:T(8,128)S(1)} %get-tuple-element.22.part, f32[128,128]{1,0:T(8,128)S(1)} %get-tuple-element.23.packed, ...), custom_call_target="tpu_custom_call", output_to_operand_aliasing={{0}: (0, {}), {1}: (1, {})} | custom-call | tf_op jit(solution)/shard_map/pack_x/pallas_call | solution.py:643
  16.6 1.3 %collective-permute-start.6 = (f32[56,128]{1,0:T(8,128)S(1)}, f32[56,128]{1,0:T(8,128)S(1)}, u32[]{:S(2)}, u32[]{:S(2)}) collective-permute-start(f32[56,128]{1,0:T(8,128)S(1)} %get-tuple-element.28), channel_id=1, source_target_pairs={{0,16},{16,0},{1,17},{17,1},{2,18},{18,2},{3,19},{19,3},{4,20},{20... | collective-permute-start | bytes 86024 | tf_op jit(solution)/shard_map/ppermute | solution.py:571
  17.9 0.7 %block.1 = f32[27,72,128]{2,1,0:T(8,128)S(1)} custom-call(f32[3920,128]{1,0:T(8,128)S(1)} %get-tuple-element.26.full), custom_call_target="tpu_custom_call" | custom-call | flops 4976640 | bytes 4194304 | tf_op jit(solution)/shard_map/block/pallas_call | solution.py:660
  18.6 0.8 %collective-permute-done.6.x_one.x_two = f32[56,128]{1,0:T(8,128)S(1)} collective-permute-done((f32[56,128]{1,0:T(8,128)S(1)}, f32[56,128]{1,0:T(8,128)S(1)}, u32[]{:S(2)}, u32[]{:S(2)}) %collective-permute-start.6) | collective-permute-done | bytes 28704 | tf_op jit(solution)/shard_map/ppermute | solution.py:571
  19.4 1.3 %finish.1 = f32[27,4,8,128]{3,2,1,0:T(8,128)} custom-call(f32[3920,128]{1,0:T(8,128)S(1)} %get-tuple-element.26.full, f32[27,72,128]{2,1,0:T(8,128)S(1)} %block.1, f32[144,128]{1,0:T(8,128)S(1)} %get-tuple-element.27.columns, f32[56,128]{1,0:T(8,128)S(1)} %collective-permute-done.6.x_one.x_two, f32[56,128]{1,0:T(8,128)S(1)} %collective-permute-done.6.x_one.x_two), custom_call_target="tpu_custom_call" | custom-call | tf_op jit(solution)/shard_map/finish/pallas_call | solution.py:672
  (1 shorter events, 0.0 us)
Async XLA Ops:
  1.4 8.7 %collective-permute-start = (f32[136,128]{1,0:T(8,128)S(1)}, f32[136,128]{1,0:T(8,128)S(1)}, u32[]{:S(2)}, u32[]{:S(2)}) collective-permute-start(f32[136,128]{1,0:T(8,128)S(1)} %get-tuple-element.18), channel_id=1, source_target_pairs={{0,4},{8,12},{4,0},{12,8},{5,9},{13,1},{9,5},{1,13},{2,6},{10,14},... | collective-permute-start | bytes 208904 | tf_op jit(solution)/shard_map/ppermute | solution.py:581
  5.6 4.5 %collective-permute-start.1 = (f32[136,128]{1,0:T(8,128)S(1)}, f32[136,128]{1,0:T(8,128)S(1)}, u32[]{:S(2)}, u32[]{:S(2)}) collective-permute-start(f32[136,128]{1,0:T(8,128)S(1)} %get-tuple-element.19), channel_id=1, source_target_pairs={{4,8},{12,0},{8,4},{0,12},{1,5},{9,13},{5,1},{13,9},{6,10},{14,2},... | collective-permute-start | bytes 208904 | tf_op jit(solution)/shard_map/ppermute | solution.py:581
  5.6 8.2 %collective-permute-start.2 = (f32[312,128]{1,0:T(8,128)S(1)}, f32[312,128]{1,0:T(8,128)S(1)}, u32[]{:S(2)}, u32[]{:S(2)}) collective-permute-start(f32[312,128]{1,0:T(8,128)S(1)} %get-tuple-element.20), channel_id=1, source_target_pairs={{1,2},{2,1},{5,6},{6,5},{9,10},{10,9},{13,14},{14,13},{17,18},{18,... | collective-permute-start | bytes 479240 | tf_op jit(solution)/shard_map/ppermute | solution.py:571
  10.0 3.8 %collective-permute-start.3 = (f32[312,128]{1,0:T(8,128)S(1)}, f32[312,128]{1,0:T(8,128)S(1)}, u32[]{:S(2)}, u32[]{:S(2)}) collective-permute-start(f32[312,128]{1,0:T(8,128)S(1)} %get-tuple-element.21), channel_id=1, source_target_pairs={{0,1},{2,3},{1,0},{3,2},{4,5},{6,7},{5,4},{7,6},{8,9},{10,11},{9,8... | collective-permute-start | bytes 479240 | tf_op jit(solution)/shard_map/ppermute | solution.py:571
  10.3 4.2 %collective-permute-start.4 = (f32[104,128]{1,0:T(8,128)S(1)}, f32[104,128]{1,0:T(8,128)S(1)}, u32[]{:S(2)}, u32[]{:S(2)}) collective-permute-start(f32[104,128]{1,0:T(8,128)S(1)} %get-tuple-element.24), channel_id=1, source_target_pairs={{0,1},{2,3},{1,0},{3,2},{4,5},{6,7},{5,4},{7,6},{8,9},{10,11},{9,8... | collective-permute-start | bytes 159752 | tf_op jit(solution)/shard_map/ppermute | solution.py:571
  10.8 5.4 %collective-permute-start.5 = (f32[104,128]{1,0:T(8,128)S(1)}, f32[104,128]{1,0:T(8,128)S(1)}, u32[]{:S(2)}, u32[]{:S(2)}) collective-permute-start(f32[104,128]{1,0:T(8,128)S(1)} %get-tuple-element.25), channel_id=1, source_target_pairs={{1,2},{2,1},{5,6},{6,5},{9,10},{10,9},{13,14},{14,13},{17,18},{18,... | collective-permute-start | bytes 159752 | tf_op jit(solution)/shard_map/ppermute | solution.py:571
  16.6 2.8 %collective-permute-start.6 = (f32[56,128]{1,0:T(8,128)S(1)}, f32[56,128]{1,0:T(8,128)S(1)}, u32[]{:S(2)}, u32[]{:S(2)}) collective-permute-start(f32[56,128]{1,0:T(8,128)S(1)} %get-tuple-element.28), channel_id=1, source_target_pairs={{0,16},{16,0},{1,17},{17,1},{2,18},{18,2},{3,19},{19,3},{4,20},{20... | collective-permute-start | bytes 86024 | tf_op jit(solution)/shard_map/ppermute | solution.py:571
